TPU v7x, 32 devices: a whole 2x2x4 slice. The times are simulated.
32 devices in a mesh: rows: 16 (over z, x, core), feat: 2 (over y).
Axes of the slice: x: 2, y: 2, z: 4, core: 2. Of those that a mesh axis runs over, the one named last changes fastest.
Arguments:
- features: bfloat16 [256, 32768], P('feat', 'rows'), may hold values from -8 to 8
- adjacency: bfloat16 [256, 12, 128, 128], P('rows'), may hold values from 0 to 1, as said below
- tile_cols: int32 [256, 12], P('rows'), may hold values from 0 to 255, as said below
- self_weight: bfloat16 [256, 256], P('feat'), may hold values from -0.375 to 0.375
- neigh_weight: bfloat16 [256, 256], P('feat'), may hold values from -0.375 to 0.375
- bias_vector: float32 [256], P('feat'), may hold values from -3 to 3
- grad_output: bfloat16 [256, 32768], P('feat', 'rows'), may hold values from -8 to 8
Outputs:
- activation: bfloat16 [256, 32768], P('feat', 'rows')
- grad_features: bfloat16 [256, 32768], P('feat', 'rows')
- grad_self: float32 [256, 256], P('feat')
- grad_neigh: float32 [256, 256], P('feat')
- grad_bias: float32 [256], P('feat')
Inputs may be any that keep to these rules, and one draw needn't show every extreme that they name: `tile_cols`: row blocks b with the same b // 16 form one group; among the 192 tiles of one group, at most 12 have source blocks c with the same c // 16, and in every group some c // 16 is reached by exactly 12 tiles. `adjacency`: the first tile of every row block has all its diagonal entries at 0.5 or more.
All inputs are finite; a program needn't handle non-finite values.
Results may differ from a plain program's by a relative error of at most 0.0034.
Values may be sent and summed in bfloat16 or wider, within the bound.
No kernel may reach another device: no remote copies, remote signals or barrier semaphores. Data moves between devices by JAX's collectives and lax.ppermute only.
A program may use at most 128 MiB of HBM per device.

v0:
```python
import jax
import jax.numpy as jnp
from jax import lax
from jax.sharding import PartitionSpec as P


def left_product(weights, values):
    return lax.dot_general(
        weights, values, (((0,), (0,)), ((), ())), preferred_element_type=jnp.float32
    )


def right_product(values, grads):
    return lax.dot_general(
        values, grads, (((1,), (1,)), ((), ())), preferred_element_type=jnp.float32
    )


def shards(features, adjacency, tile_cols, self_weight, neigh_weight, bias_vector, grad_output):
    hid_dev, nodes_dev = features.shape
    blocks_dev, per_block, tile_size, unused = adjacency.shape
    degree = jnp.sum(adjacency, axis=(1, 3), dtype=jnp.float32)
    inverse = (1.0 / degree).reshape(nodes_dev)
    gathered = lax.all_gather(features, "rows", axis=1, tiled=True)
    all_nodes = gathered.shape[1]
    blocked = gathered.reshape(hid_dev, all_nodes // tile_size, tile_size)
    picked = jnp.take(blocked, tile_cols, axis=1)
    summed = jnp.einsum("hbtj,btij->hbi", picked, adjacency, preferred_element_type=jnp.float32)
    aggregate = (summed.reshape(hid_dev, nodes_dev) * inverse[None, :]).astype(jnp.bfloat16)
    preact = lax.psum_scatter(
        left_product(self_weight, features) + left_product(neigh_weight, aggregate),
        "feat",
        scatter_dimension=0,
        tiled=True,
    )
    preact = preact + bias_vector[:, None]
    activation = jnp.where(preact > 0, preact, jnp.expm1(jnp.minimum(preact, 0.0))).astype(
        jnp.bfloat16
    )
    slopes = jnp.where(preact > 0, 1.0, jnp.exp(jnp.minimum(preact, 0.0)))
    grad_pre = (grad_output.astype(jnp.float32) * slopes).astype(jnp.bfloat16)
    grad_full = lax.all_gather(grad_pre, "feat", axis=0, tiled=True)
    local_self = right_product(features, grad_full)
    local_neigh = right_product(aggregate, grad_full)
    local_bias = jnp.sum(grad_pre, axis=1, dtype=jnp.float32)
    grad_self, grad_neigh, grad_bias = lax.psum((local_self, local_neigh, local_bias), "rows")
    scaled = (
        jnp.dot(neigh_weight, grad_full, preferred_element_type=jnp.float32) * inverse[None, :]
    ).astype(jnp.bfloat16)
    self_term = jnp.dot(self_weight, grad_full, preferred_element_type=jnp.float32)
    contribs = jnp.einsum(
        "hbi,btij->hbtj",
        scaled.reshape(hid_dev, blocks_dev, tile_size),
        adjacency,
        preferred_element_type=jnp.float32,
    )
    tile_count = blocks_dev * per_block
    contribs = contribs.reshape(hid_dev, tile_count, tile_size)
    flat_cols = tile_cols.reshape(tile_count)
    spread_sum = jnp.zeros((hid_dev, all_nodes // tile_size, tile_size), jnp.float32)
    spread_sum = spread_sum.at[:, flat_cols, :].add(contribs)
    backward_sum = lax.psum_scatter(
        spread_sum.reshape(hid_dev, all_nodes), "rows", scatter_dimension=1, tiled=True
    )
    grad_features = (self_term + backward_sum).astype(jnp.bfloat16)
    return (activation, grad_features, grad_self, grad_neigh, grad_bias)


def solution(mesh):
    in_specs = (
        P("feat", "rows"),
        P("rows", None, None, None),
        P("rows", None),
        P("feat", None),
        P("feat", None),
        P("feat"),
        P("feat", "rows"),
    )
    out_specs = (P("feat", "rows"), P("feat", "rows"), P("feat", None), P("feat", None), P("feat"))
    return jax.shard_map(shards, mesh=mesh, in_specs=in_specs, out_specs=out_specs, check_vma=False)
```

profile of v0, /device:TPU:0, one launch (start us, length us, event | category | flops | bytes accessed | tf_op | source)
XLA Modules:
  0.0 463.5 jit_solution(4787259881096156086)
XLA Ops:
  7.2 2.1 copy.23
  10.2 0.7 compare_and_fusion
  10.9 3.7 convert_reduce_fusion
  15.1 73.3 %all-gather.3.cloned.1.call-done = bf16[128,32768]{0,1:T(8,128)(2,1)} async-done(((bf16[128,2048]{0,1:T(8,128)(2,1)}), bf16[128,32768]{0,1:T(8,128)(2,1)}) %all-gather.3.cloned.1.call-update) | async-done | bytes 8388624 | tf_op jit(solution)/shard_map/all_gather | solution.py:24
  88.4 12.0 %copy.24 = bf16[128,256,128]{2,0,1:T(8,128)(2,1)} copy(bf16[128,256,128]{0,2,1:T(8,128)(2,1)} %bitcast.60) | data formatting | bytes 16777216 | tf_op jit(solution)/shard_map/reshape | solution.py:26
  100.4 11.5 %gather_fusion = bf16[192,128,128]{2,1,0:T(8,128)(2,1)} fusion(bf16[128,256,128]{2,0,1:T(8,128)(2,1)} %copy.24, s32[1024]{0:T(1024)S(1)} %pad_clamp_fusion), kind=kCustom, calls=%fused_computation | custom fusion | bytes 12583680 | tf_op jit(solution)/shard_map/jit(_take)/gather | solution.py:27
  111.8 6.5 %fusion = f32[16,128,128,1]{1,2,3,0:T(8,128)S(1)} fusion(bf16[16,12,128,128]{3,2,1,0:T(8,128)(2,1)} %param.8, bf16[16,12,128,128]{3,2,1,0:T(8,128)(2,1)} %bitcast.59, pred[16,12]{1,0:T(8,128)(4,1)S(1)} %compare_and_fusion), kind=kOutput, calls=%fused_computation.3 | convolution fusion | flops 808452096 | bytes 13631680 | tf_op jit(solution)/shard_map/hbtj,btij->hbi/dot_general | solution.py:28
  118.7 1.8 fusion.5
  120.6 30.2 %reduce-scatter.3.cloned.1.call-done = f32[128,2048]{1,0:T(8,128)} async-done(((f32[256,2048]{1,0:T(8,128)}), f32[128,2048]{1,0:T(8,128)}) %reduce-scatter.3.cloned.1.call-update) | async-done | bytes 1048592 | tf_op jit(solution)/shard_map/reduce_scatter | solution.py:30
  150.8 3.0 convert_reduce_fusion.1
  154.0 21.3 %all-gather.5.cloned.1.call-done = bf16[256,2048]{1,0:T(8,128)(2,1)} async-done(((bf16[128,2048]{1,0:T(8,128)(2,1)}), bf16[256,2048]{1,0:T(8,128)(2,1)}) %all-gather.5.cloned.1.call-update) | async-done | bytes 1048592 | tf_op jit(solution)/shard_map/all_gather | solution.py:42
  175.2 2.4 fusion.17
  177.6 2.3 convolution_bitcast_fusion.2
  180.2 1.9 fusion.7
  182.1 9.2 %fusion.16 = f32[16,128,12,128]{3,1,2,0:T(8,128)} fusion(bf16[128,16,128,1]{0,2,3,1:T(8,128)(2,1)S(1)} %bitcast.61, bf16[16,12,128,128]{3,2,1,0:T(8,128)(2,1)} %param.8), kind=kOutput, calls=%fused_computation.31 | convolution fusion | flops 805306368 | bytes 19398656 | tf_op jit(solution)/shard_map/hbi,btij->hbtj/dot_general | solution.py:51
  191.2 7.8 %broadcast_in_dim.25 = f32[128,256,128]{2,0,1:T(8,128)} broadcast(f32[]{:T(128)} %constant.11.clone.1), dimensions={} | broadcast | bytes 16777220 | tf_op jit(solution)/shard_map/broadcast_in_dim | solution.py:60
  199.1 40.1 %scatter_fusion = f32[128,256,128]{2,0,1:T(8,128)} fusion(f32[128,256,128]{2,0,1:T(8,128)} %broadcast_in_dim.25, s32[192]{0:T(256)S(1)} %bitcast.62, f32[192,128,128]{2,1,0:T(8,128)} %bitcast.57), kind=kCustom, calls=%fused_computation.1 | custom fusion | flops 3145728 | bytes 37749504 | tf_op jit(solution)/shard_map/scatter-add | solution.py:61
  239.1 17.4 %copy.27 = f32[128,256,128]{0,2,1:T(8,128)} copy(f32[128,256,128]{2,0,1:T(8,128)} %scatter_fusion) | data formatting | bytes 33554432 | tf_op jit(solution)/shard_map/scatter-add | solution.py:61
  256.6 33.9 %psum.23 = f32[128]{0:T(128)} all-reduce(f32[128]{0:T(128)S(1)} %get-tuple-element.22), channel_id=1, replica_groups=mesh['rows'=16,'feat'=2] {'rows'}, use_global_device_ids=true, to_apply=%region_7.8 | all-reduce | flops 128 | bytes 1024 | tf_op jit(solution)/shard_map/psum | solution.py:46
  290.5 1.7 copy.29
  292.1 160.5 %reduce-scatter.5.cloned.1.call-done = f32[128,2048]{0,1:T(8,128)} async-done(((f32[128,32768]{0,1:T(8,128)}), f32[128,2048]{0,1:T(8,128)}) %reduce-scatter.5.cloned.1.call-update) | async-done | bytes 1048592 | tf_op jit(solution)/shard_map/reduce_scatter | solution.py:62
  452.7 1.7 fusion.8
  454.4 1.0 copy.28
  455.4 1.6 copy.38
  (33 shorter events, 2.2 us)
Async XLA Ops:
  7.2 111.5 %copy-start = (bf16[128,256]{1,0:T(8,128)(2,1)S(1)}, bf16[128,256]{1,0:T(8,128)(2,1)}, u32[]{:S(2)}) copy-start(bf16[128,256]{1,0:T(8,128)(2,1)} %param.11) | copy-start | bytes 196612
  7.2 7.4 %copy-start.3 = (bf16[128,2048]{1,0:T(8,128)(2,1)S(1)}, bf16[128,2048]{1,0:T(8,128)(2,1)}, u32[]{:S(2)}) copy-start(bf16[128,2048]{1,0:T(8,128)(2,1)} %param.7) | copy-start | bytes 1572868
  7.2 7.4 %copy-start.4 = (bf16[128,256]{1,0:T(8,128)(2,1)S(1)}, bf16[128,256]{1,0:T(8,128)(2,1)}, u32[]{:S(2)}) copy-start(bf16[128,256]{1,0:T(8,128)(2,1)} %param.10) | copy-start | bytes 196612
  7.2 81.2 %all-gather.3.cloned.1.call-start = ((), (), s32[]{:S(2)}) async-start(), calls=%async_computation.2 | async-start | bytes 8912896 | tf_op jit(solution)/shard_map/all_gather | solution.py:24
  9.4 141.4 %reduce-scatter.3.cloned.1.call-start = ((), (), s32[]{:S(2)}) async-start(), calls=%async_computation.3 | async-start | bytes 3145728 | tf_op jit(solution)/shard_map/reduce_scatter | solution.py:30
  118.3 32.4 %copy-start.6 = (f32[128]{0:T(128)S(1)}, f32[128]{0:T(128)}, u32[]{:S(2)}) copy-start(f32[128]{0:T(128)} %param.12) | copy-start | bytes 1540
  118.3 35.5 %copy-start.5 = (s32[16,12]{1,0:T(8,128)S(1)}, s32[16,12]{1,0:T(8,128)}, u32[]{:S(2)}) copy-start(s32[16,12]{1,0:T(8,128)} %param.9) | copy-start | bytes 2308
  120.5 54.7 %all-gather.5.cloned.1.call-start = ((), (), s32[]{:S(2)}) async-start(), calls=%async_computation.4 | async-start | bytes 1572864 | tf_op jit(solution)/shard_map/all_gather | solution.py:42
  153.8 136.7 %all-reduce.3.cloned.1.call-start = ((), (), s32[]{:S(2)}) async-start(), calls=%async_computation.6 | async-start | bytes 524288 | tf_op jit(solution)/shard_map/psum | solution.py:46
  180.0 272.7 %reduce-scatter.5.cloned.1.call-start = ((), (), s32[]{:S(2)}) async-start(), calls=%async_computation.5 | async-start | bytes 17825792 | tf_op jit(solution)/shard_map/reduce_scatter | solution.py:62
  256.6 196.1 %copy-start.2 = (bf16[256,2048]{1,0:T(8,128)(2,1)S(1)}, bf16[256,2048]{1,0:T(8,128)(2,1)}, u32[]{:S(2)}) copy-start(bf16[256,2048]{1,0:T(8,128)(2,1)} %all-gather.5.cloned.1.call-done) | copy-start | bytes 3145732
  256.6 200.4 %copy-start.1 = (bf16[128,256]{1,0:T(8,128)(2,1)S(1)}, bf16[128,256]{1,0:T(8,128)(2,1)}, u32[]{:S(2)}) copy-start(bf16[128,256]{1,0:T(8,128)(2,1)} %param.11) | copy-start | bytes 196612
Sparse Core Ops, SparseCore 0:
  10.8 77.5 all-gather.2
  120.7 30.0 reduce-scatter.2
  153.9 21.2 all-gather.4
  180.1 88.9 all-reduce.2
  273.6 179.0 reduce-scatter.4
where the time goes:
time: 465 us; the launch traced here: 464 us
  waiting for transfers between devices  285 us (61%)
  local copies, waits for them, and re-layouts  55.3 us (12%)
  other arithmetic  48.5 us (10%)
  blocking collectives  33.9 us (7%)
  matrix products  26.2 us (6%)
  between operations  13.9 us (3%)
    reduce_scatter x1, waiting for transfers between devices, shards(): lax.psum_scatter(spread_sum.reshape(hid_dev, all_nodes), 'rows', scatter_...  161 us
    all_gather x1, waiting for transfers between devices, shards(): gathered = lax.all_gather(features, 'rows', axis=1, tiled=True)  73.3 us
    scatter-add x1, other arithmetic, shards(): spread_sum = spread_sum.at[:, flat_cols, :].add(contribs)  40.1 us
    psum x1, blocking collectives, shards(): lax.psum((local_self, local_neigh, local_bias), 'rows')  33.9 us
    reduce_scatter x1, waiting for transfers between devices, shards(): lax.psum_scatter(left_product(self_weight, features) + left_product(neigh...  30.2 us
    all_gather x1, waiting for transfers between devices, shards(): grad_full = lax.all_gather(grad_pre, 'feat', axis=0, tiled=True)  21.3 us
    scatter-add x1, local copies, waits for them, and re-layouts, shards(): spread_sum = spread_sum.at[:, flat_cols, :].add(contribs)  17.4 us
    reshape x1, local copies, waits for them, and re-layouts, shards(): blocked = gathered.reshape(hid_dev, all_nodes // tile_size, tile_size)  12 us
  transfers between devices with their start and end apart: 5, of which 4 were waited for; matrix products, arithmetic and copies ran while one was open for 18% of the time, Pallas kernels for 0%

commit v1 on v0

v1 whole, which is shorter than its diff:
```python
import functools

import jax
import jax.numpy as jnp
from jax import lax
from jax.experimental import pallas as pl
from jax.experimental.pallas import tpu as pltpu
from jax.sharding import PartitionSpec as P

CAP = 12
VMEM_BYTES = 40 * 1024 * 1024
HBM = pl.BlockSpec(memory_space=pl.ANY)
VMEM = pl.BlockSpec(memory_space=pltpu.VMEM)
SMEM = pl.BlockSpec(memory_space=pltpu.SMEM)


def params():
    return pltpu.CompilerParams(vmem_limit_bytes=VMEM_BYTES)


def cost(flops, moved):
    return pl.CostEstimate(flops=flops, bytes_accessed=moved, transcendentals=0)


def ring_pairs(rows, step):
    levels, chips = rows // 4, rows // 2
    order = [2 * z for z in range(levels)] + [2 * z + 1 for z in reversed(range(levels))]
    return [
        (2 * order[p] + core, 2 * order[(p + step) % chips] + core)
        for p in range(chips)
        for core in range(2)
    ]


def ring_row(row, offset, rows):
    levels, chips = rows // 4, rows // 2
    z, x, core = row // 4, (row // 2) % 2, row % 2
    target = ((z if x == 0 else chips - 1 - z) + offset) % chips
    chip = 2 * target if target < levels else 2 * (chips - 1 - target) + 1
    return 2 * chip + core


def places(spot, row, wanted, rows):
    table = [[ring_row(r, offset, rows) ^ flip for offset, flip in wanted] for r in range(rows)]
    mine = lax.dynamic_index_in_dim(jnp.array(table, jnp.int32), row, 0, keepdims=False)
    return jnp.concatenate([jnp.reshape(spot, (1,)).astype(jnp.int32), mine])


def swap_cores(value, rows):
    return lax.ppermute(value, "rows", [(r, r ^ 1) for r in range(rows)])


def exchange(pieces, feats):
    got = [pieces[0]]
    for k in range(1, feats):
        got.append(lax.ppermute(pieces[k], "feat", [(i, (i + k) % feats) for i in range(feats)]))
    return got


def aggregate_kernel(plan, here, cols, adj, *refs):
    feats, count, hid, half, width, per_block, tile = plan
    blocks = width // tile
    part = blocks // feats
    sources, refs = refs[:count], refs[count:]
    aggs, inverse, held, tiles, sems, tile_sems = refs[:feats], *refs[feats:]
    spot = here[0]
    copies = []
    for n in range(count):
        row = here[1 + n]
        if sources[n].shape[0] == hid:
            target = held.at[row]
        else:
            target = held.at[row, pl.ds((n % 2) * half, half)]
        copies.append(pltpu.make_async_copy(sources[n], target, sems.at[n]))
    for copy in copies:
        copy.start()

    def fetch(block):
        return pltpu.make_async_copy(adj.at[block], tiles.at[block], tile_sems.at[block])

    for block in range(blocks):
        fetch(block).start()
    for copy in copies:
        copy.wait()
    ones = jnp.ones((16, 2 * tile), jnp.bfloat16)
    for k in range(feats):
        where = lax.rem(spot + k, feats)

        def step(local, carry):
            block = where * part + local
            fetch(block).wait()
            total = None
            for t in range(0, per_block, 2):
                left, right = [], []
                for u in (t, t + 1):
                    col = cols[block, u]
                    row = col // blocks
                    lane = pl.multiple_of((col - row * blocks) * tile, tile)
                    left.append(held[row, :, pl.ds(lane, tile)])
                    right.append(tiles[block, u])
                term = lax.dot_general(
                    jnp.concatenate([jnp.concatenate(left, axis=1), ones], axis=0),
                    jnp.concatenate(right, axis=1),
                    (((1,), (1,)), ((), ())),
                    preferred_element_type=jnp.float32,
                )
                total = term if total is None else total + term
            factor = 1.0 / total[hid : hid + 1]
            lane = pl.ds(pl.multiple_of(local * tile, tile), tile)
            aggs[k][:, lane] = (total[:hid] * factor).astype(jnp.bfloat16)
            inverse[where, :, lane] = factor
            return carry

        lax.fori_loop(0, part, step, 0, unroll=2 if part % 2 == 0 else 1)


def middle_kernel(plan, here, wt, wn, bias, inverse, *refs):
    feats, hid, span, chunk = plan
    xs, gos, aggs = refs[:feats], refs[feats : 2 * feats], refs[2 * feats : 3 * feats]
    refs = refs[3 * feats :]
    scaled, acts, grad = refs[:feats], refs[feats : 2 * feats], refs[2 * feats]
    both, cot = refs[2 * feats + 1 :]
    spot = here[0]
    for k in range(feats):
        at = pl.multiple_of(lax.rem(spot - k + feats, feats) * hid, hid)
        both[pl.ds(at, hid)] = xs[k][...]
        both[pl.ds(feats * hid + at, hid)] = aggs[k][...]
        cot[pl.ds(at, hid)] = gos[k][...]
    for c in range(0, span, chunk):
        lane = pl.ds(c, chunk)
        values = both[:, lane]
        for k in range(feats):
            at = pl.ds(pl.multiple_of(lax.rem(spot + k, feats) * hid, hid), hid)
            pre = jnp.dot(wt[at], values, preferred_element_type=jnp.float32) + bias[at]
            slope = jnp.exp(jnp.minimum(pre, 0.0))
            acts[k][:, lane] = jnp.where(pre > 0, pre, slope - 1.0).astype(jnp.bfloat16)
            grad[at, lane] = (cot[at, lane].astype(jnp.float32) * slope).astype(jnp.bfloat16)
        for k in range(feats):
            at = pl.ds(pl.multiple_of(lax.rem(spot + k, feats) * hid, hid), hid)
            back = jnp.dot(wn[at], grad[:, lane], preferred_element_type=jnp.float32)
            scaled[k][:, lane] = (back * inverse[spot, :, lane]).astype(jnp.bfloat16)


def weights_kernel(plan, here, ws, grad, *refs):
    feats, hid, span = plan
    xs, aggs, refs = refs[:feats], refs[feats : 2 * feats], refs[2 * feats :]
    selfs, grads = refs[:feats], refs[feats:]
    spot = here[0]
    every = feats * hid
    g = grad[...]
    contract = (((1,), (1,)), ((), ()))
    sums = lax.dot_general(
        jnp.ones((8, span), jnp.bfloat16), g, contract, preferred_element_type=jnp.float32
    )
    for k in range(feats):
        at = pl.ds(pl.multiple_of(lax.rem(spot + k, feats) * hid, hid), hid)
        selfs[k][...] = jnp.dot(ws[at], g, preferred_element_type=jnp.float32)
        back = (feats - k) % feats
        grads[k][:hid, :every] = lax.dot_general(
            xs[back][...], g, contract, preferred_element_type=jnp.float32
        )
        grads[k][:hid, every:] = lax.dot_general(
            aggs[back][...], g, contract, preferred_element_type=jnp.float32
        )
        grads[k][hid:, :every] = sums
        grads[k][hid:, every:] = sums


def spread_kernel(plan, here, slots, lanes, adj, pair, *refs):
    feats, hid, span, tile, blocks, per_block, outs, with_self = plan
    own, other, refs = refs[:feats], refs[feats : 2 * feats], refs[2 * feats :]
    if with_self:
        selfs, refs = refs[:feats], refs[feats:]
    results, (held, tiles, total, sems) = refs[: 2 * len(outs)], refs[2 * len(outs) :]
    spot = here[0]
    half = hid // 2
    copies = []
    for d in range(len(outs)):
        first = here[1 + d] * CAP
        for side, source in enumerate((adj, pair)):
            for s in range(CAP):
                found = jnp.maximum(slots[side, first + s], 0)
                block = found // per_block
                n = (d * 2 + side) * CAP + s
                copy = pltpu.make_async_copy(
                    source.at[block, found - block * per_block], tiles.at[n], sems.at[n]
                )
                copy.start()
                copies.append(copy)
    for side, pieces in enumerate((own, other)):
        held[side, blocks] = jnp.zeros((hid, tile), jnp.bfloat16)
        for k in range(feats):
            base = lax.rem(spot - k + feats, feats) * (span // tile)
            for local in range(span // tile):
                held[side, base + local] = pieces[k][:, local * tile : (local + 1) * tile]
    for d, kinds in enumerate(outs):
        if with_self:
            for k in range(feats):
                at = pl.multiple_of(lax.rem(spot - k + feats, feats) * span, span)
                total[:, pl.ds(at, span)] = selfs[k][...]
        else:
            total[...] = jnp.zeros_like(total)
        first = here[1 + d] * CAP
        for side in range(2):
            for s0 in range(0, CAP, 6):
                terms = []
                for s in range(s0, s0 + 6):
                    n = (d * 2 + side) * CAP + s
                    copies[n].wait()
                    found = slots[side, first + s]
                    block = jnp.where(found < 0, blocks, found // per_block)
                    term = jnp.dot(
                        held[side, block], tiles[n], preferred_element_type=jnp.float32
                    )
                    terms.append(term)
                for i, term in enumerate(terms):
                    lane = pl.multiple_of(lanes[side, first + s0 + i] * tile, tile)
                    total[:, pl.ds(lane, tile)] += term
        for part, kind in enumerate(kinds):
            value = total[part * half : (part + 1) * half]
            results[2 * d + part][...] = value.astype(kind)


def finish_kernel(base_low, base_high, a_low, b_low, a_high, b_high, out):
    half = a_low.shape[0]
    out[:half] = (
        base_low[...] + a_low[...].astype(jnp.float32) + b_low[...].astype(jnp.float32)
    ).astype(jnp.bfloat16)
    out[half:] = (
        base_high[...] + a_high[...].astype(jnp.float32) + b_high[...].astype(jnp.float32)
    ).astype(jnp.bfloat16)


def place_kernel(feats, here, *refs):
    out = refs[-1]
    span = refs[0].shape[1]
    for k in range(feats):
        at = pl.multiple_of(lax.rem(here[0] - k + feats, feats) * span, span)
        out[:, pl.ds(at, span)] = refs[k][...]


def slot_table(cols, rows, blocks):
    flat = cols.reshape(-1)
    group = flat // blocks
    ids = lax.iota(jnp.int32, flat.shape[0])
    earlier = (group[None, :] == group[:, None]) & (ids[None, :] < ids[:, None])
    spot = group * CAP + jnp.sum(earlier.astype(jnp.int32), axis=1)
    hit = spot[None, :] == lax.iota(jnp.int32, rows * CAP)[:, None]
    slots = jnp.max(jnp.where(hit, ids[None, :], -1), axis=1)
    lanes = jnp.sum(jnp.where(hit, (flat % blocks)[None, :], 0), axis=1)
    return slots, lanes


def shards(rows, feats, features, adjacency, tile_cols, self_weight, neigh_weight, bias_vector, grad_output):
    hid, width = features.shape
    blocks, per_block, tile, unused = adjacency.shape
    half, span = hid // 2, width // feats
    every = hid * feats
    top = rows // 4
    row, spot = lax.axis_index("rows"), lax.axis_index("feat")
    spot_only = jnp.reshape(spot, (1,)).astype(jnp.int32)
    forward, backward = ring_pairs(rows, 1), ring_pairs(rows, -1)

    sources, wanted = [features, swap_cores(features, rows)], [(0, 0), (0, 1)]
    up = [features[:half], features[half:]]
    down = list(up)
    for step in range(1, top + 1):
        arrived = {}
        for part in range(2):
            if step < top or part == 0:
                up[part] = lax.ppermute(up[part], "rows", forward)
                arrived[-step, part] = up[part]
            if step < top or part == 1:
                down[part] = lax.ppermute(down[part], "rows", backward)
                arrived[step, part] = down[part]
        if step == top:
            arrived = {(step, 0): up[0], (step, 1): down[1]}
        for offset in sorted({key[0] for key in arrived}):
            for flip in range(2):
                for part in range(2):
                    piece = arrived[offset, part]
                    sources.append(swap_cores(piece, rows) if flip else piece)
                    wanted.append((offset, flip))

    def sections(value):
        return [
            lax.dynamic_slice_in_dim(value, ((spot + k) % feats) * span, span, axis=1)
            for k in range(feats)
        ]

    xs = exchange(sections(features), feats)
    gos = exchange(sections(grad_output), feats)
    weights = lax.all_gather(jnp.stack([self_weight, neigh_weight]), "feat", axis=1, tiled=True)
    bias = lax.all_gather(bias_vector, "feat", axis=0, tiled=True).reshape(every, 1)
    turned = weights.reshape(2 * every, every).T
    pair_adjacency = swap_cores(adjacency, rows)
    tables = [slot_table(c, rows, blocks) for c in (tile_cols, swap_cores(tile_cols, rows))]
    slots = jnp.stack([t[0] for t in tables])
    lanes = jnp.stack([t[1] for t in tables])

    count = len(sources)
    here = places(spot, row, wanted, rows)
    shape = jax.ShapeDtypeStruct
    *aggs, inverse = pl.pallas_call(
        functools.partial(aggregate_kernel, (feats, count, hid, half, width, per_block, tile)),
        out_shape=[shape((hid, span), jnp.bfloat16)] * feats
        + [shape((feats, 1, span), jnp.float32)],
        in_specs=[SMEM, SMEM, HBM] + [HBM] * count,
        out_specs=[VMEM] * (feats + 1),
        scratch_shapes=[
            pltpu.VMEM((rows, hid, width), jnp.bfloat16),
            pltpu.VMEM(adjacency.shape, jnp.bfloat16),
            pltpu.SemaphoreType.DMA((count,)),
            pltpu.SemaphoreType.DMA((blocks,)),
        ],
        compiler_params=params(),
        cost_estimate=cost(2 * hid * adjacency.size, 2 * adjacency.size + 2 * rows * hid * width),
        name="aggregate",
    )(here, tile_cols, adjacency, *sources)
    aggs = exchange(aggs, feats)

    chunk = min(span, 256)
    outs = pl.pallas_call(
        functools.partial(middle_kernel, (feats, hid, span, chunk)),
        out_shape=[shape((hid, span), jnp.bfloat16)] * (2 * feats)
        + [shape((every, span), jnp.bfloat16)],
        in_specs=[SMEM] + [VMEM] * (4 + 3 * feats),
        out_specs=[VMEM] * (2 * feats + 1),
        scratch_shapes=[
            pltpu.VMEM((2 * every, span), jnp.bfloat16),
            pltpu.VMEM((every, span), jnp.bfloat16),
        ],
        compiler_params=params(),
        cost_estimate=cost(6 * every * every * span, 14 * every * span),
        name="middle",
    )(spot_only, turned, weights[1], bias, inverse, *xs, *gos, *aggs)
    scaled, acts, grad = outs[:feats], outs[feats : 2 * feats], outs[2 * feats]
    scaled = exchange(scaled, feats)
    scaled_pair = [swap_cores(piece, rows) for piece in scaled]

    outs = pl.pallas_call(
        functools.partial(weights_kernel, (feats, hid, span)),
        out_shape=[shape((hid, span), jnp.float32)] * feats
        + [shape((hid + 8, 2 * every), jnp.float32)] * feats,
        in_specs=[SMEM] + [VMEM] * (2 + 2 * feats),
        out_specs=[VMEM] * (2 * feats),
        compiler_params=params(),
        cost_estimate=cost(6 * every * every * span, 10 * every * span),
        name="weights",
    )(spot_only, weights[0], grad, *xs, *aggs)
    selfs, grads = exchange(outs[:feats], feats), exchange(outs[feats:], feats)
    acts = exchange(acts, feats)
    activation = pl.pallas_call(
        functools.partial(place_kernel, feats),
        out_shape=shape((hid, width), jnp.bfloat16),
        in_specs=[SMEM] + [VMEM] * feats,
        out_specs=VMEM,
        compiler_params=params(),
        cost_estimate=cost(0, 4 * hid * width),
        name="place",
    )(spot_only, *acts)
    grads = lax.psum(sum(grads[1:], grads[0]), "rows")
    grad_self, grad_neigh = grads[:hid, :every], grads[:hid, every:]
    grad_bias = lax.dynamic_slice_in_dim(grads[hid, :every], spot * hid, hid)

    def spread(offsets, kinds, extra=()):
        dests = places(spot, row, [(offset, 0) for offset in offsets], rows)
        n = len(offsets) * 2 * CAP
        return pl.pallas_call(
            functools.partial(
                spread_kernel,
                (feats, hid, span, tile, blocks, per_block, kinds, bool(extra)),
            ),
            out_shape=[shape((half, width), kind) for pair in kinds for kind in pair],
            in_specs=[SMEM] * 3 + [HBM] * 2 + [VMEM] * (2 * feats + len(extra)),
            out_specs=[VMEM] * (2 * len(offsets)),
            scratch_shapes=[
                pltpu.VMEM((2, blocks + 1, hid, tile), jnp.bfloat16),
                pltpu.VMEM((n, tile, tile), jnp.bfloat16),
                pltpu.VMEM((hid, width), jnp.float32),
                pltpu.SemaphoreType.DMA((n,)),
            ],
            compiler_params=params(),
            cost_estimate=cost(2 * n * hid * tile * tile, 2 * n * tile * tile + 8 * hid * width),
            name="spread",
        )(dests, slots, lanes, adjacency, pair_adjacency, *scaled, *scaled_pair, *extra)

    narrow, wide = jnp.bfloat16, jnp.float32
    up, down = [None, None], [None, None]

    def joined(arrived, mine):
        if arrived is None:
            return mine
        return (arrived.astype(jnp.float32) + mine).astype(jnp.bfloat16)

    for level in range(top, 0, -1):
        if level == top:
            low, high = spread([top], [(narrow, narrow)])
            up[0] = lax.ppermute(low, "rows", forward)
            down[1] = lax.ppermute(high, "rows", backward)
            continue
        kinds = [
            tuple(narrow if arrived is None else wide for arrived in way) for way in (up, down)
        ]
        mine = spread([level, -level], kinds)
        up = [lax.ppermute(joined(up[i], mine[i]), "rows", forward) for i in range(2)]
        down = [lax.ppermute(joined(down[i], mine[2 + i]), "rows", backward) for i in range(2)]
    low, high = spread([0], [(wide, wide)], extra=tuple(selfs))
    grad_features = pl.pallas_call(
        finish_kernel,
        out_shape=shape((hid, width), jnp.bfloat16),
        in_specs=[VMEM] * 6,
        out_specs=VMEM,
        compiler_params=params(),
        cost_estimate=cost(0, 8 * hid * width),
        name="finish",
    )(low, high, up[0], down[0], up[1], down[1])
    return (activation, grad_features, grad_self, grad_neigh, grad_bias)


def solution(mesh):
    in_specs = (
        P("feat", "rows"),
        P("rows", None, None, None),
        P("rows", None),
        P("feat", None),
        P("feat", None),
        P("feat"),
        P("feat", "rows"),
    )
    out_specs = (P("feat", "rows"), P("feat", "rows"), P("feat", None), P("feat", None), P("feat"))
    body = functools.partial(shards, mesh.shape["rows"], mesh.shape["feat"])
    return jax.shard_map(body, mesh=mesh, in_specs=in_specs, out_specs=out_specs, check_vma=False)
```

time: 465 us -> 298 us (0.64)
  waiting for transfers between devices: 285 us -> 129 us
  Pallas kernels: 0 us -> 58.9 us
  starting transfers between devices: 0.39 us -> 43.9 us
  other arithmetic: 48.5 us -> 5.5 us
  matrix products: 26.2 us -> 0 us
  blocking collectives: 33.9 us -> 11.6 us
  local copies, waits for them, and re-layouts: 55.3 us -> 33.7 us
    reduce_scatter x2 -> x0, waiting for transfers between devices: 191 us -> none  [the longest x1 161 us: shards(): lax.psum_scatter(spread_sum.reshape(hid_dev, all_nodes), 'rows', scatter_...]
    all_gather x2 -> x0, waiting for transfers between devices: 94.6 us -> none  [the longest x1 73.3 us: shards(): gathered = lax.all_gather(features, 'rows', axis=1, tiled=True)]
    psum x1, waiting for transfers between devices: 0.01 us -> 78 us  [shards(): grads = lax.psum(sum(grads[1:], grads[0]), 'rows')]
    pallas_call x0 -> x10, Pallas kernels: none -> 58.9 us  [the longest x5 42.7 us: spread(): pl.pallas_call(functools.partial(spread_kernel, (feats, hid, span, tile,...]
    ppermute x0 -> x54, waiting for transfers between devices: none -> 51 us  [the longest x7 24.1 us: shards(): down[part] = lax.ppermute(down[part], 'rows', backward)]
    ppermute x0 -> x54, starting transfers between devices: none -> 43.9 us  [the longest x7 12.3 us: shards(): down[part] = lax.ppermute(down[part], 'rows', backward)]
    scatter-add x1 -> x0, other arithmetic: 40.1 us -> none  [shards(): spread_sum = spread_sum.at[:, flat_cols, :].add(contribs)]
    psum x1 -> x0, blocking collectives: 33.9 us -> none  [shards(): lax.psum((local_self, local_neigh, local_bias), 'rows')]
  transfers between devices with their start and end apart: 5 -> 55, of which waited for: 4 -> 15; matrix products, arithmetic and copies ran while one was open for 18% -> 7% of each run, Pallas kernels for 0% -> 19%
where the time goes in v1:
time: 298 us; the launch traced here: 297 us
  waiting for transfers between devices  129 us (43%)
  Pallas kernels  58.9 us (20%)
  starting transfers between devices  43.9 us (15%)
  local copies, waits for them, and re-layouts  33.7 us (11%)
  between operations  14.4 us (5%)
  blocking collectives  11.6 us (4%)
  other arithmetic  5.5 us (2%)
    psum x1, waiting for transfers between devices, shards(): grads = lax.psum(sum(grads[1:], grads[0]), 'rows')  78 us
    pallas_call x5, Pallas kernels, spread(): pl.pallas_call(functools.partial(spread_kernel, (feats, hid, span, tile,...  42.7 us
    ppermute x7, waiting for transfers between devices, shards(): down[part] = lax.ppermute(down[part], 'rows', backward)  24.1 us
    unnamed x60, local copies, waits for them, and re-layouts  19.4 us
    ppermute x7, starting transfers between devices, shards(): down[part] = lax.ppermute(down[part], 'rows', backward)  12.3 us
    ppermute x7, starting transfers between devices, exchange(): lax.ppermute(pieces[k], 'feat', [(i, (i + k) % feats) for i in range(feat...  10.4 us
    pallas_call x1, Pallas kernels, shards(): pl.pallas_call(functools.partial(aggregate_kernel, (feats, count, hid, ha...  9.73 us
    ppermute x6, waiting for transfers between devices, shards(): lax.ppermute(joined(down[i], mine[2 + i]), 'rows', backward)  9.38 us
  transfers between devices with their start and end apart: 55, of which 15 were waited for; matrix products, arithmetic and copies ran while one was open for 7% of the time, Pallas kernels for 19%

profile of v1, /device:TPU:0, one launch (start us, length us, event | category | flops | bytes accessed | tf_op | source)
XLA Modules:
  0.0 297.1 jit_solution(4203128010379805381)
XLA Ops:
  8.8 2.6 collective-permute-start.6
  13.5 5.1 %collective-permute-done.6.refs_7_ = bf16[64,2048]{1,0:T(8,128)(2,1)S(1)} collective-permute-done((bf16[64,2048]{1,0:T(8,128)(2,1)S(1)}, bf16[64,2048]{1,0:T(8,128)(2,1)S(1)}, u32[]{:S(2)}, u32[]{:S(2)}) %collective-permute-start.6) | collective-permute-done | bytes 262176 | tf_op jit(solution)/shard_map/ppermute | solution.py:274
  20.5 3.7 %collective-permute-done.5.refs_6_ = bf16[64,2048]{1,0:T(8,128)(2,1)S(1)} collective-permute-done((bf16[64,2048]{1,0:T(8,128)(2,1)S(1)}, bf16[64,2048]{1,0:T(8,128)(2,1)S(1)}, u32[]{:S(2)}, u32[]{:S(2)}) %collective-permute-start.5) | collective-permute-done | bytes 262176 | tf_op jit(solution)/shard_map/ppermute | solution.py:274
  26.2 3.5 %collective-permute-done.14.refs_15_ = bf16[64,2048]{1,0:T(8,128)(2,1)S(1)} collective-permute-done((bf16[64,2048]{1,0:T(8,128)(2,1)S(1)}, bf16[64,2048]{1,0:T(8,128)(2,1)S(1)}, u32[]{:S(2)}, u32[]{:S(2)}) %collective-permute-start.14) | collective-permute-done | bytes 262176 | tf_op jit(solution)/shard_map/ppermute | solution.py:274
  34.6 3.2 %collective-permute-done.13.refs_14_ = bf16[64,2048]{1,0:T(8,128)(2,1)S(1)} collective-permute-done((bf16[64,2048]{1,0:T(8,128)(2,1)S(1)}, bf16[64,2048]{1,0:T(8,128)(2,1)S(1)}, u32[]{:S(2)}, u32[]{:S(2)}) %collective-permute-start.13) | collective-permute-done | bytes 262176 | tf_op jit(solution)/shard_map/ppermute | solution.py:274
  45.2 4.7 %collective-permute-done.22.refs_23_ = bf16[64,2048]{1,0:T(8,128)(2,1)S(1)} collective-permute-done((bf16[64,2048]{1,0:T(8,128)(2,1)S(1)}, bf16[64,2048]{1,0:T(8,128)(2,1)S(1)}, u32[]{:S(2)}, u32[]{:S(2)}) %collective-permute-start.22) | collective-permute-done | bytes 262176 | tf_op jit(solution)/shard_map/ppermute | solution.py:274
  62.7 3.8 %collective-permute-done.26.refs_27_ = bf16[64,2048]{1,0:T(8,128)(2,1)S(1)} collective-permute-done((bf16[64,2048]{1,0:T(8,128)(2,1)}, bf16[64,2048]{1,0:T(8,128)(2,1)S(1)}, u32[]{:S(2)}, u32[]{:S(2)}) %collective-permute-start.26) | collective-permute-done | bytes 262176 | tf_op jit(solution)/shard_map/ppermute | solution.py:274
  67.1 2.8 collective-permute-done.25.refs_26_
  69.9 6.6 %all_gather.6 = bf16[2,256,256]{2,1,0:T(8,128)(2,1)S(1)} all-gather(bf16[2,128,256]{2,1,0:T(8,128)(2,1)S(1)} %pad_maximum_fusion), channel_id=1, replica_groups=mesh['rows'=16,'feat'=2] {'feat'}, dimensions={1}, use_global_device_ids=true | all-gather | bytes 393216 | tf_op jit(solution)/shard_map/all_gather | solution.py:293
  89.7 9.7 %aggregate.1 = (bf16[128,1024]{1,0:T(8,128)(2,1)S(1)}, bf16[128,1024]{1,0:T(8,128)(2,1)}, f32[2,1,1024]{2,1,0:T(1,128)S(1)}) custom-call(s32[31]{0:T(128)S(1)} %copy-done.24, s32[16,12]{1,0:T(8,128)S(1)} %copy-done.23, bf16[16,12,128,128]{3,2,1,0:T(8,128)(2,1)} %adj.11, bf16[128,2048]{1,0:T(8,128)(2,1)S(1)} %copy-done.2, ...), custom_call_target="tpu_custom_call" | custom-call | flops 805306368 | bytes 14680064 | tf_op jit(solution)/shard_map/aggregate/pallas_call | solution.py:304
  103.5 5.1 %all-gather = f32[2,1,128]{2,1,0:T(1,128)S(1)} all-gather(f32[1,1,128]{2,1,0:T(1,128)S(1)} %bitcast.36), channel_id=1, replica_groups=mesh['rows'=16,'feat'=2] {'feat'}, dimensions={0}, use_global_device_ids=true | all-gather | bytes 1536 | tf_op jit(solution)/shard_map/all_gather | solution.py:294
  110.0 3.0 %middle.1 = (bf16[128,1024]{1,0:T(8,128)(2,1)S(1)}, bf16[128,1024]{1,0:T(8,128)(2,1)S(1)}, bf16[128,1024]{1,0:T(8,128)(2,1)S(1)}, bf16[128,1024]{1,0:T(8,128)(2,1)}, bf16[256,1024]{1,0:T(8,128)(2,1)S(1)}) custom-call(s32[1]{0:T(128)} %bitcast.here, bf16[256,512]{1,0:T(8,128)(2,1)S(1)} %bitcast.27, bf16[256,256]{1,0:T(8,128)(2,1)S(1)} %get-tuple-element.74.wn, ...), custom_call_target="tpu_custom_call" | custom-call | flops 402653184 | bytes 3670016 | tf_op jit(solution)/shard_map/middle/pallas_call | solution.py:323
  117.6 4.4 %collective-permute-done.35.refs_1_ = bf16[128,1024]{1,0:T(8,128)(2,1)S(1)} collective-permute-done((bf16[128,1024]{1,0:T(8,128)(2,1)S(1)}, bf16[128,1024]{1,0:T(8,128)(2,1)S(1)}, u32[]{:S(2)}, u32[]{:S(2)}) %collective-permute-start.35) | collective-permute-done | bytes 262176 | tf_op jit(solution)/shard_map/ppermute | solution.py:56
  124.8 3.2 %collective-permute-done.53 = f32[136,512]{1,0:T(8,128)S(1)} collective-permute-done((f32[136,512]{1,0:T(8,128)S(1)}, f32[136,512]{1,0:T(8,128)S(1)}, u32[]{:S(2)}, u32[]{:S(2)}) %collective-permute-start.53) | collective-permute-done | bytes 278560 | tf_op jit(solution)/shard_map/ppermute | solution.py:56
  128.8 2.8 copy-done
  131.5 6.3 %spread.6 = (bf16[64,2048]{1,0:T(8,128)(2,1)}, bf16[64,2048]{1,0:T(8,128)(2,1)}) custom-call(s32[2]{0:T(128)S(1)} %get-tuple-element.80.here, s32[2,192]{1,0:T(2,128)S(1)} %get-tuple-element.83.slots, s32[2,192]{1,0:T(2,128)S(1)} %get-tuple-element.84.lanes, bf16[16,12,128,128]{3,2,1,0:T(8,128)(2,1)S(1)} %copy-done, ...), custom_call_target="tpu_custom_call" | custom-call | flops 100663296 | bytes 2883584 | tf_op jit(solution)/shard_map/spread/pallas_call | solution.py:369
  140.6 78.0 %all-reduce.2.cloned.1.call-done = f32[136,512]{1,0:T(8,128)} async-done(((f32[136,512]{1,0:T(8,128)}), f32[136,512]{1,0:T(8,128)}) %all-reduce.2.cloned.1.call-update) | async-done | bytes 278544 | tf_op jit(solution)/shard_map/psum | solution.py:362
  220.7 2.8 copy-done.1
  223.5 10.3 %spread.7 = (f32[64,2048]{1,0:T(8,128)S(1)}, bf16[64,2048]{1,0:T(8,128)(2,1)S(1)}, bf16[64,2048]{1,0:T(8,128)(2,1)S(1)}, f32[64,2048]{1,0:T(8,128)S(1)}) custom-call(s32[3]{0:T(128)S(1)} %get-tuple-element.81.here, s32[2,192]{1,0:T(2,128)S(1)} %get-tuple-element.83.slots, s32[2,192]{1,0:T(2,128)S(1)} %get-tuple-element.84.lanes, ...), custom_call_target="tpu_custom_call" | custom-call | flops 201326592 | bytes 3670016 | tf_op jit(solution)/shard_map/spread/pallas_call | solution.py:369
  235.9 10.3 %spread.9 = (f32[64,2048]{1,0:T(8,128)S(1)}, f32[64,2048]{1,0:T(8,128)S(1)}, f32[64,2048]{1,0:T(8,128)S(1)}, f32[64,2048]{1,0:T(8,128)S(1)}) custom-call(s32[3]{0:T(128)S(1)} %pad_add_fusion.7.here, s32[2,192]{1,0:T(2,128)S(1)} %get-tuple-element.83.slots, s32[2,192]{1,0:T(2,128)S(1)} %get-tuple-element.84.lanes, bf16[16,12,128,128]{3,2,1,0:T(8,128)(2,1)S(1)} %copy-done.1, ...), custom_call_target="tpu_custom_call" | custom-call | flops 201326592 | bytes 3670016 | tf_op jit(solution)/shard_map/spread/pallas_call | solution.py:369
  246.2 10.3 %spread.8 = (f32[64,2048]{1,0:T(8,128)S(1)}, f32[64,2048]{1,0:T(8,128)S(1)}, f32[64,2048]{1,0:T(8,128)S(1)}, f32[64,2048]{1,0:T(8,128)S(1)}) custom-call(s32[3]{0:T(128)S(1)} %get-tuple-element.82.here, s32[2,192]{1,0:T(2,128)S(1)} %get-tuple-element.83.slots, s32[2,192]{1,0:T(2,128)S(1)} %get-tuple-element.84.lanes, ...), custom_call_target="tpu_custom_call" | custom-call | flops 201326592 | bytes 3670016 | tf_op jit(solution)/shard_map/spread/pallas_call | solution.py:369
  261.0 8.9 %collective-permute-done.44 = bf16[64,2048]{1,0:T(8,128)(2,1)S(1)} collective-permute-done((bf16[64,2048]{1,0:T(8,128)(2,1)S(1)}, bf16[64,2048]{1,0:T(8,128)(2,1)S(1)}, u32[]{:S(2)}, u32[]{:S(2)}) %collective-permute-start.44) | collective-permute-done | bytes 262176 | tf_op jit(solution)/shard_map/ppermute | solution.py:407
  274.4 5.5 %collective-permute-done.41 = bf16[64,2048]{1,0:T(8,128)(2,1)S(1)} collective-permute-done((bf16[64,2048]{1,0:T(8,128)(2,1)S(1)}, bf16[64,2048]{1,0:T(8,128)(2,1)S(1)}, u32[]{:S(2)}, u32[]{:S(2)}) %collective-permute-start.41) | collective-permute-done | bytes 262176 | tf_op jit(solution)/shard_map/ppermute | solution.py:406
  283.8 5.5 %spread.5 = (f32[64,2048]{1,0:T(8,128)S(1)}, f32[64,2048]{1,0:T(8,128)S(1)}) custom-call(s32[2]{0:T(128)S(1)} %get-tuple-element.79.here, s32[2,192]{1,0:T(2,128)S(1)} %get-tuple-element.83.slots, s32[2,192]{1,0:T(2,128)S(1)} %get-tuple-element.84.lanes, bf16[16,12,128,128]{3,2,1,0:T(8,128)(2,1)S(1)} %copy-done.1, ...), custom_call_target="tpu_custom_call" | custom-call | flops 100663296 | bytes 2883584 | tf_op jit(solution)/shard_map/spread/pallas_call | solution.py:369
  (201 shorter events, 80.8 us)
Async XLA Ops:
  7.2 211.4 %all-reduce.2.cloned.1.call-start = ((), (), s32[]{:S(2)}) async-start(), calls=%async_computation | async-start | bytes 557056 | tf_op jit(solution)/shard_map/psum | solution.py:362
  7.2 121.5 %collective-permute-start.34 = (bf16[16,12,128,128]{3,2,1,0:T(8,128)(2,1)}, bf16[16,12,128,128]{3,2,1,0:T(8,128)(2,1)}, u32[]{:S(2)}, u32[]{:S(2)}) collective-permute-start(bf16[16,12,128,128]{3,2,1,0:T(8,128)(2,1)} %adj.11), channel_id=1, source_target_pairs={{0,2},{2,0},{4,6},{6,4},{8,10},{10,8},{12,14},{14,12},{16,18},{18,... | collective-permute-start | bytes 18874376 | tf_op jit(solution)/shard_map/ppermute | solution.py:50
  11.5 12.7 %collective-permute-start.5 = (bf16[64,2048]{1,0:T(8,128)(2,1)S(1)}, bf16[64,2048]{1,0:T(8,128)(2,1)S(1)}, u32[]{:S(2)}, u32[]{:S(2)}) collective-permute-start(bf16[64,2048]{1,0:T(8,128)(2,1)S(1)} %get-tuple-element.70), channel_id=1, source_target_pairs={{0,4},{2,6},{8,0},{10,2},{16,8},{18,10},{24,16},{26,18},{28,24},{3... | collective-permute-start | bytes 786440 | tf_op jit(solution)/shard_map/ppermute | solution.py:274
  13.4 12.8 %collective-permute-start.1 = (bf16[64,2048]{1,0:T(8,128)(2,1)S(1)}, bf16[64,2048]{1,0:T(8,128)(2,1)S(1)}, u32[]{:S(2)}, u32[]{:S(2)}) collective-permute-start(bf16[64,2048]{1,0:T(8,128)(2,1)S(1)} %get-tuple-element.70), channel_id=1, source_target_pairs={{0,8},{2,10},{8,16},{10,18},{16,24},{18,26},{24,28},{26,30},{28,20... | collective-permute-start | bytes 786440 | tf_op jit(solution)/shard_map/ppermute | solution.py:271
  18.6 11.0 %collective-permute-start.14 = (bf16[64,2048]{1,0:T(8,128)(2,1)S(1)}, bf16[64,2048]{1,0:T(8,128)(2,1)S(1)}, u32[]{:S(2)}, u32[]{:S(2)}) collective-permute-start(bf16[64,2048]{1,0:T(8,128)(2,1)S(1)} %collective-permute-done.6.refs_7_), channel_id=1, source_target_pairs={{0,4},{2,6},{8,0},{10,2},{16,8},{18,10},{24,16},{26,18},{28,24},{3... | collective-permute-start | bytes 786440 | tf_op jit(solution)/shard_map/ppermute | solution.py:274
  20.5 10.8 %collective-permute-start.8 = (bf16[64,2048]{1,0:T(8,128)(2,1)S(1)}, bf16[64,2048]{1,0:T(8,128)(2,1)S(1)}, u32[]{:S(2)}, u32[]{:S(2)}) collective-permute-start(bf16[64,2048]{1,0:T(8,128)(2,1)S(1)} %collective-permute-done.6.refs_7_), channel_id=1, source_target_pairs={{0,2},{2,0},{4,6},{6,4},{8,10},{10,8},{12,14},{14,12},{16,18},{18,... | collective-permute-start | bytes 786440 | tf_op jit(solution)/shard_map/ppermute | solution.py:50
  31.3 12.2 %collective-permute-start = (bf16[128,2048]{1,0:T(8,128)(2,1)}, bf16[128,2048]{1,0:T(8,128)(2,1)S(1)}, u32[]{:S(2)}, u32[]{:S(2)}) collective-permute-start(bf16[128,2048]{1,0:T(8,128)(2,1)} %refs_0_.1), channel_id=1, source_target_pairs={{0,2},{2,0},{4,6},{6,4},{8,10},{10,8},{12,14},{14,12},{16,18},{18,... | collective-permute-start | bytes 1572872 | tf_op jit(solution)/shard_map/ppermute | solution.py:50
  67.0 11.1 %collective-permute-start.28 = (bf16[64,2048]{1,0:T(8,128)(2,1)S(1)}, bf16[64,2048]{1,0:T(8,128)(2,1)S(1)}, u32[]{:S(2)}, u32[]{:S(2)}) collective-permute-start(bf16[64,2048]{1,0:T(8,128)(2,1)S(1)} %collective-permute-done.26.refs_27_), channel_id=1, source_target_pairs={{0,2},{2,0},{4,6},{6,4},{8,10},{10,8},{12,14},{14,12},{16,18},{18,... | collective-permute-start | bytes 786440 | tf_op jit(solution)/shard_map/ppermute | solution.py:50
  76.5 33.4 %collective-permute-start.33 = (s32[16,12]{1,0:T(8,128)}, s32[16,12]{1,0:T(8,128)S(1)}, u32[]{:S(2)}, u32[]{:S(2)}) collective-permute-start(s32[16,12]{1,0:T(8,128)} %cols.1), channel_id=1, source_target_pairs={{0,2},{2,0},{4,6},{6,4},{8,10},{10,8},{12,14},{14,12},{16,18},{18,... | collective-permute-start | bytes 2312 | tf_op jit(solution)/shard_map/ppermute | solution.py:50
  76.6 33.4 %collective-permute-start.30 = (bf16[128,1024]{1,0:T(8,128)(2,1)}, bf16[128,1024]{1,0:T(8,128)(2,1)}, u32[]{:S(2)}, u32[]{:S(2)}) collective-permute-start(bf16[128,1024]{1,0:T(8,128)(2,1)} %get-tuple-element.65), channel_id=1, source_target_pairs={{0,1},{1,0},{2,3},{3,2},{4,5},{5,4},{6,7},{7,6},{8,9},{9,8},{10,11... | collective-permute-start | bytes 786440 | tf_op jit(solution)/shard_map/ppermute | solution.py:56
  78.2 31.8 %collective-permute-start.29 = (bf16[128,1024]{1,0:T(8,128)(2,1)}, bf16[128,1024]{1,0:T(8,128)(2,1)S(1)}, u32[]{:S(2)}, u32[]{:S(2)}) collective-permute-start(bf16[128,1024]{1,0:T(8,128)(2,1)} %get-tuple-element.67), channel_id=1, source_target_pairs={{0,1},{1,0},{2,3},{3,2},{4,5},{5,4},{6,7},{7,6},{8,9},{9,8},{10,11... | collective-permute-start | bytes 786440 | tf_op jit(solution)/shard_map/ppermute | solution.py:56
  115.7 13.0 %collective-permute-start.36 = (bf16[128,1024]{1,0:T(8,128)(2,1)S(1)}, bf16[128,1024]{1,0:T(8,128)(2,1)S(1)}, u32[]{:S(2)}, u32[]{:S(2)}) collective-permute-start(bf16[128,1024]{1,0:T(8,128)(2,1)S(1)} %get-tuple-element.38.refs_0_), channel_id=1, source_target_pairs={{0,2},{2,0},{4,6},{6,4},{8,10},{10,8},{12,14},{14,12},{16,18},{18,... | collective-permute-start | bytes 786440 | tf_op jit(solution)/shard_map/ppermute | solution.py:50
  122.2 17.5 %collective-permute-start.32 = (bf16[128,1024]{1,0:T(8,128)(2,1)}, bf16[128,1024]{1,0:T(8,128)(2,1)S(1)}, u32[]{:S(2)}, u32[]{:S(2)}) collective-permute-start(bf16[128,1024]{1,0:T(8,128)(2,1)} %get-tuple-element.37), channel_id=1, source_target_pairs={{0,1},{1,0},{2,3},{3,2},{4,5},{5,4},{6,7},{7,6},{8,9},{9,8},{10,11... | collective-permute-start | bytes 786440 | tf_op jit(solution)/shard_map/ppermute | solution.py:56
  137.8 118.7 %collective-permute-start.39 = (bf16[64,2048]{1,0:T(8,128)(2,1)}, bf16[64,2048]{1,0:T(8,128)(2,1)S(1)}, u32[]{:S(2)}, u32[]{:S(2)}) collective-permute-start(bf16[64,2048]{1,0:T(8,128)(2,1)} %get-tuple-element.45), channel_id=1, source_target_pairs={{0,8},{2,10},{8,16},{10,18},{16,24},{18,26},{24,28},{26,30},{28,20... | collective-permute-start | bytes 786440 | tf_op jit(solution)/shard_map/ppermute | solution.py:399
  138.6 145.2 %collective-permute-start.38 = (f32[128,1024]{1,0:T(8,128)}, f32[128,1024]{1,0:T(8,128)S(1)}, u32[]{:S(2)}, u32[]{:S(2)}) collective-permute-start(f32[128,1024]{1,0:T(8,128)} %get-tuple-element.42), channel_id=1, source_target_pairs={{0,1},{1,0},{2,3},{3,2},{4,5},{5,4},{6,7},{7,6},{8,9},{9,8},{10,11... | collective-permute-start | bytes 1572872 | tf_op jit(solution)/shard_map/ppermute | solution.py:56
  219.3 38.3 %collective-permute-start.49 = (bf16[64,2048]{1,0:T(8,128)(2,1)}, bf16[64,2048]{1,0:T(8,128)(2,1)S(1)}, u32[]{:S(2)}, u32[]{:S(2)}) collective-permute-start(bf16[64,2048]{1,0:T(8,128)(2,1)} %get-tuple-element.55), channel_id=1, source_target_pairs={{0,4},{2,6},{8,0},{10,2},{16,8},{18,10},{24,16},{26,18},{28,24},{3... | collective-permute-start | bytes 786440 | tf_op jit(solution)/shard_map/ppermute | solution.py:400
  233.8 25.0 %collective-permute-start.43 = (bf16[64,2048]{1,0:T(8,128)(2,1)S(1)}, bf16[64,2048]{1,0:T(8,128)(2,1)S(1)}, u32[]{:S(2)}, u32[]{:S(2)}) collective-permute-start(bf16[64,2048]{1,0:T(8,128)(2,1)S(1)} %get-tuple-element.49), channel_id=1, source_target_pairs={{0,4},{2,6},{8,0},{10,2},{16,8},{18,10},{24,16},{26,18},{28,24},{3... | collective-permute-start | bytes 786440 | tf_op jit(solution)/shard_map/ppermute | solution.py:407
  235.2 25.1 %collective-permute-start.46 = (bf16[64,2048]{1,0:T(8,128)(2,1)S(1)}, bf16[64,2048]{1,0:T(8,128)(2,1)S(1)}, u32[]{:S(2)}, u32[]{:S(2)}) collective-permute-start(bf16[64,2048]{1,0:T(8,128)(2,1)S(1)} %get-tuple-element.52), channel_id=1, source_target_pairs={{0,8},{2,10},{8,16},{10,18},{16,24},{18,26},{24,28},{26,30},{28,20... | collective-permute-start | bytes 786440 | tf_op jit(solution)/shard_map/ppermute | solution.py:406
  256.6 14.0 %collective-permute-start.40 = (bf16[64,2048]{1,0:T(8,128)(2,1)S(1)}, bf16[64,2048]{1,0:T(8,128)(2,1)S(1)}, u32[]{:S(2)}, u32[]{:S(2)}) collective-permute-start(bf16[64,2048]{1,0:T(8,128)(2,1)S(1)} %add_convert_fusion.9), channel_id=1, source_target_pairs={{0,8},{2,10},{8,16},{10,18},{16,24},{18,26},{24,28},{26,30},{28,20... | collective-permute-start | bytes 786440 | tf_op jit(solution)/shard_map/ppermute | solution.py:406
  257.6 15.5 %collective-permute-start.50 = (bf16[64,2048]{1,0:T(8,128)(2,1)S(1)}, bf16[64,2048]{1,0:T(8,128)(2,1)S(1)}, u32[]{:S(2)}, u32[]{:S(2)}) collective-permute-start(bf16[64,2048]{1,0:T(8,128)(2,1)S(1)} %add_convert_fusion.2), channel_id=1, source_target_pairs={{0,4},{2,6},{8,0},{10,2},{16,8},{18,10},{24,16},{26,18},{28,24},{3... | collective-permute-start | bytes 786440 | tf_op jit(solution)/shard_map/ppermute | solution.py:407
  258.8 11.1 %collective-permute-start.44 = (bf16[64,2048]{1,0:T(8,128)(2,1)S(1)}, bf16[64,2048]{1,0:T(8,128)(2,1)S(1)}, u32[]{:S(2)}, u32[]{:S(2)}) collective-permute-start(bf16[64,2048]{1,0:T(8,128)(2,1)S(1)} %add_convert_fusion.6), channel_id=1, source_target_pairs={{0,4},{2,6},{8,0},{10,2},{16,8},{18,10},{24,16},{26,18},{28,24},{3... | collective-permute-start | bytes 786440 | tf_op jit(solution)/shard_map/ppermute | solution.py:407
  260.4 11.8 %collective-permute-start.47 = (bf16[64,2048]{1,0:T(8,128)(2,1)S(1)}, bf16[64,2048]{1,0:T(8,128)(2,1)S(1)}, u32[]{:S(2)}, u32[]{:S(2)}) collective-permute-start(bf16[64,2048]{1,0:T(8,128)(2,1)S(1)} %add_convert_fusion.4), channel_id=1, source_target_pairs={{0,8},{2,10},{8,16},{10,18},{16,24},{18,26},{24,28},{26,30},{28,20... | collective-permute-start | bytes 786440 | tf_op jit(solution)/shard_map/ppermute | solution.py:406
  270.0 19.3 %collective-permute-start.45 = (bf16[64,2048]{1,0:T(8,128)(2,1)S(1)}, bf16[64,2048]{1,0:T(8,128)(2,1)S(1)}, u32[]{:S(2)}, u32[]{:S(2)}) collective-permute-start(bf16[64,2048]{1,0:T(8,128)(2,1)S(1)} %add_convert_fusion.5), channel_id=1, source_target_pairs={{0,4},{2,6},{8,0},{10,2},{16,8},{18,10},{24,16},{26,18},{28,24},{3... | collective-permute-start | bytes 786440 | tf_op jit(solution)/shard_map/ppermute | solution.py:407
  272.2 17.1 %collective-permute-start.48 = (bf16[64,2048]{1,0:T(8,128)(2,1)S(1)}, bf16[64,2048]{1,0:T(8,128)(2,1)S(1)}, u32[]{:S(2)}, u32[]{:S(2)}) collective-permute-start(bf16[64,2048]{1,0:T(8,128)(2,1)S(1)} %add_convert_fusion.3), channel_id=1, source_target_pairs={{0,8},{2,10},{8,16},{10,18},{16,24},{18,26},{24,28},{26,30},{28,20... | collective-permute-start | bytes 786440 | tf_op jit(solution)/shard_map/ppermute | solution.py:406
  (61 other events, 513.2 us)
Sparse Core Ops, SparseCore 0:
  128.8 89.6 all-reduce.1

commit v2 on v0

v2 whole, which is shorter than its diff:
```python
import functools

import jax
import jax.numpy as jnp
from jax import lax
from jax.experimental import pallas as pl
from jax.experimental.pallas import tpu as pltpu
from jax.sharding import PartitionSpec as P

CAP = 12
MIB = 1024 * 1024
HBM = pl.BlockSpec(memory_space=pltpu.HBM)
VMEM = pl.BlockSpec(memory_space=pltpu.VMEM)
SMEM = pl.BlockSpec(memory_space=pltpu.SMEM)
LAST = (((1,), (1,)), ((), ()))


def params(mib):
    return pltpu.CompilerParams(vmem_limit_bytes=mib * MIB)


def cost(flops, moved):
    return pl.CostEstimate(flops=flops, bytes_accessed=moved, transcendentals=0)


def product(left, right, dims=(((1,), (0,)), ((), ()))):
    return lax.dot_general(left, right, dims, preferred_element_type=jnp.float32)


def ring_pairs(rows, step):
    levels, chips = rows // 4, rows // 2
    order = [2 * z for z in range(levels)] + [2 * z + 1 for z in reversed(range(levels))]
    return [
        (2 * order[p] + core, 2 * order[(p + step) % chips] + core)
        for p in range(chips)
        for core in range(2)
    ]


def ring_row(row, offset, rows):
    levels, chips = rows // 4, rows // 2
    z, x, core = row // 4, lax.rem(row // 2, 2), lax.rem(row, 2)
    target = lax.rem(jnp.where(x == 0, z, chips - 1 - z) + (offset + chips), chips)
    low = target < levels
    return 2 * jnp.where(low, 2 * target, 2 * (chips - 1 - target) + 1) + core


def swap(value, rows, bit=1):
    return lax.ppermute(value, "rows", [(r, r ^ bit) for r in range(rows)])


def exchange(pieces, feats):
    got = [pieces[0]]
    for k in range(1, feats):
        got.append(lax.ppermute(pieces[k], "feat", [(i, (i + k) % feats) for i in range(feats)]))
    return got


def ahead(k, feats, size):
    return pl.multiple_of(lax.rem(lax.axis_index("feat") + k, feats) * size, size)


def behind(k, feats, size):
    return pl.multiple_of(lax.rem(lax.axis_index("feat") - k + feats, feats) * size, size)


def pack_kernel(feats, feature, grad_output, ws, wn, bias, *outs):
    hid, every = ws.shape
    span = feature.shape[1] // feats
    line = lax.broadcasted_iota(jnp.int32, (hid, hid), 0)
    lane = lax.broadcasted_iota(jnp.int32, (hid, hid), 1)
    column = jnp.sum(jnp.where(line == lane, bias[...], 0.0), axis=1, keepdims=True)
    high = column.astype(jnp.bfloat16).astype(jnp.float32)
    middle = (column - high).astype(jnp.bfloat16).astype(jnp.float32)
    spread = lax.broadcasted_iota(jnp.int32, (hid, 128), 1)
    parts = jnp.where(
        spread == 0, high, jnp.where(spread == 1, middle, jnp.where(spread == 2, column - high - middle, 0.0))
    )
    for k in range(feats):
        at = pl.ds(ahead(k, feats, span), span)
        outs[k][:, :span] = feature[:, at]
        outs[k][:, span : 2 * span] = grad_output[:, at]
        outs[k][:, 2 * span : 2 * span + every] = ws[...]
        outs[k][:, 2 * span + every : 2 * span + 2 * every] = wn[...]
        outs[k][:, 2 * span + 2 * every :] = parts.astype(jnp.bfloat16)


def unpack_kernel(feats, *refs):
    packs, (turned, ws_all, wn_all, bias_all, x_all, cot_all, both) = refs[:feats], refs[feats:]
    hid, span = packs[0].shape[0], x_all.shape[1]
    every = feats * hid
    for k in range(feats):
        at = pl.ds(behind(k, feats, hid), hid)
        pack = packs[k]
        x_all[at] = pack[:, :span]
        cot_all[at] = pack[:, span : 2 * span]
        ws_all[at] = pack[:, 2 * span : 2 * span + every]
        wn_all[at] = pack[:, 2 * span + every : 2 * span + 2 * every]
        parts = pack[:, 2 * span + 2 * every :].astype(jnp.float32)
        bias_all[at] = jnp.sum(parts, axis=1, keepdims=True)
    both[:every] = ws_all[...].astype(jnp.float32)
    both[every:] = wn_all[...].astype(jnp.float32)
    turned[...] = both[...].T.astype(jnp.bfloat16)


def table_kernel(cols, table, counts):
    blocks, per_block = cols.shape
    size = table.shape[0]

    def clear(i, carry):
        table[i] = -1
        return carry

    def reset(i, carry):
        counts[i] = 0
        return carry

    lax.fori_loop(0, size, clear, 0)
    lax.fori_loop(0, size // CAP, reset, 0)

    def step(block, carry):
        for t in range(per_block):
            col = cols[block, t]
            group = col // blocks
            seen = counts[group]
            table[group * CAP + seen] = (block * per_block + t) * 256 + (col - group * blocks)
            counts[group] = seen + 1
        return carry

    lax.fori_loop(0, blocks, step, 0)


def aggregate_kernel(plan, cols, adj, *refs):
    feats, wanted, rows, hid, half, width, per_block, tile = plan
    count = len(wanted)
    blocks = width // tile
    part = blocks // feats
    sources, refs = refs[:count], refs[count:]
    aggs, inverse, held, sems = refs[:feats], *refs[feats:]
    row = lax.axis_index("rows")
    copies = []
    for n, (offset, flip, side) in enumerate(wanted):
        place = ring_row(row, offset, rows)
        if flip:
            place = place + 1 - 2 * lax.rem(place, 2)
        target = held.at[place]
        if side is not None:
            target = held.at[place, pl.ds(side * half, half)]
        copies.append(pltpu.make_async_copy(sources[n], target, sems.at[n]))
    for copy in copies:
        copy.start()
    for copy in copies:
        copy.wait()
    ones = jnp.ones((16, 2 * tile), jnp.bfloat16)
    for k in range(feats):
        where = lax.rem(lax.axis_index("feat") + k, feats)

        def step(local, carry):
            block = where * part + local
            total = None
            for t in range(0, per_block, 2):
                left, right = [], []
                for u in (t, t + 1):
                    col = cols[block, u]
                    source = col // blocks
                    lane = pl.multiple_of((col - source * blocks) * tile, tile)
                    left.append(held[source, :, pl.ds(lane, tile)])
                    right.append(adj[block, u])
                term = product(
                    jnp.concatenate([jnp.concatenate(left, axis=1), ones], axis=0),
                    jnp.concatenate(right, axis=1),
                    LAST,
                )
                total = term if total is None else total + term
            factor = 1.0 / total[hid : hid + 1]
            lane = pl.ds(pl.multiple_of(local * tile, tile), tile)
            aggs[k][:, lane] = (total[:hid] * factor).astype(jnp.bfloat16)
            inverse[where, :, lane] = factor
            return carry

        lax.fori_loop(0, part, step, 0, unroll=2 if part % 2 == 0 else 1)


def middle_kernel(plan, turned, wn, bias, inverse, x_all, cot, *refs):
    feats, hid, span, chunk = plan
    aggs, refs = refs[:feats], refs[feats:]
    scaled, acts, grad, both = refs[:feats], refs[feats : 2 * feats], *refs[2 * feats :]
    every = feats * hid
    both[:every] = x_all[...]
    for k in range(feats):
        both[pl.ds(every + behind(k, feats, hid), hid)] = aggs[k][...]
    for c in range(0, span, chunk):
        lane = pl.ds(c, chunk)
        for k in range(feats):
            at = pl.ds(ahead(k, feats, hid), hid)
            pre = product(turned[at], both[:, lane]) + bias[at]
            slope = jnp.exp(jnp.minimum(pre, 0.0))
            acts[k][:, lane] = jnp.where(pre > 0, pre, slope - 1.0).astype(jnp.bfloat16)
            grad[at, lane] = (cot[at, lane].astype(jnp.float32) * slope).astype(jnp.bfloat16)
        for k in range(feats):
            at = pl.ds(ahead(k, feats, hid), hid)
            back = product(wn[at], grad[:, lane])
            factor = inverse[lax.axis_index("feat"), :, lane]
            scaled[k][:, lane] = (back * factor).astype(jnp.bfloat16)


def own_quarter():
    row = lax.axis_index("rows")
    return 2 * lax.rem(row, 2) + lax.rem(row // 2, 2)


def turned_quarter(mine, index):
    both = (index // 2, index % 2)
    core = both[0] + mine // 2 - 2 * both[0] * (mine // 2)
    x = both[1] + lax.rem(mine, 2) - 2 * both[1] * lax.rem(mine, 2)
    return 2 * core + x


def weights_kernel(feats, ws, x_all, grad, *refs):
    aggs, refs = refs[:feats], refs[feats:]
    selfs, grads = refs[:feats], refs[feats:]
    every, span = grad.shape
    hid = every // feats
    wide = every // 2
    mine = own_quarter()
    g = grad[...]
    sums = product(jnp.ones((8, span), jnp.bfloat16), g, LAST)
    for k in range(feats):
        at = pl.ds(ahead(k, feats, hid), hid)
        selfs[k][...] = product(ws[at], g)
        values = [product(x_all[at], g, LAST), product(aggs[(feats - k) % feats][...], g, LAST)]
        for quarter in range(4):
            slot = turned_quarter(mine, quarter)
            lane = slice(quarter % 2 * wide, (quarter % 2 + 1) * wide)
            grads[k][slot, :hid] = values[quarter // 2][:, lane]
            grads[k][slot, hid:] = sums[:, lane]


def collect_kernel(pair, pair_far, grad_self, grad_neigh, sums):
    hid, every = grad_self.shape
    wide = every // 2
    mine = own_quarter()
    for slot in range(4):
        value = (pair, pair_far)[slot // 2][slot % 2]
        quarter = turned_quarter(mine, slot)
        for q, out in enumerate((grad_self, grad_self, grad_neigh, grad_neigh)):

            @pl.when(quarter == q)
            def _():
                lane = slice(q % 2 * wide, (q % 2 + 1) * wide)
                out[:, lane] = value[:hid]
                if q < 2:
                    sums[:, lane] = value[hid:]


def arrange_kernel(feats, tile, *refs):
    pieces, held = refs[:-1], refs[-1]
    hid, span = pieces[0].shape
    part = span // tile
    for side in range(2):
        held[side, feats * part] = jnp.zeros((hid, tile), jnp.bfloat16)
        for k in range(feats):
            base = lax.rem(lax.axis_index("feat") - k + feats, feats) * part
            for local in range(part):
                held[side, base + local] = pieces[side * feats + k][:, local * tile : (local + 1) * tile]


def spread_kernel(plan, table, table_pair, adj, pair, held, *refs):
    feats, rows, offsets, kinds = plan
    selfs = refs[:feats] if offsets == (0,) else ()
    refs = refs[len(selfs) :]
    results, total = refs[:-1], refs[-1]
    blocks, per_block, tile, unused = adj.shape
    half = total.shape[0] // 2
    for d, offset in enumerate(offsets):
        if selfs:
            span = selfs[0].shape[1]
            for k in range(feats):
                total[:, pl.ds(behind(k, feats, span), span)] = selfs[k][...]
        else:
            total[...] = jnp.zeros_like(total)
        first = ring_row(lax.axis_index("rows"), offset, rows) * CAP
        for side, (slots, tiles) in enumerate(((table, adj), (table_pair, pair))):
            for s0 in range(0, CAP, 4):
                terms = []
                for s in range(s0, s0 + 4):
                    entry = slots[first + s]
                    index = jnp.maximum(entry, 0) // 256
                    block = index // per_block
                    place = jnp.where(entry < 0, blocks, block)
                    lane = lax.rem(jnp.maximum(entry, 0), 256) * tile
                    term = product(held[side, place], tiles[block, index - block * per_block])
                    terms.append((pl.multiple_of(lane, tile), term))
                for lane, term in terms:
                    total[:, pl.ds(lane, tile)] += term
        for part in range(2):
            value = total[part * half : (part + 1) * half]
            results[2 * d + part][...] = value.astype(kinds[2 * d + part])


def finish_kernel(base_low, base_high, a_low, b_low, a_high, b_high, out):
    half = a_low.shape[0]
    low = base_low[...] + a_low[...].astype(jnp.float32) + b_low[...].astype(jnp.float32)
    out[:half] = low.astype(jnp.bfloat16)
    high = base_high[...] + a_high[...].astype(jnp.float32) + b_high[...].astype(jnp.float32)
    out[half:] = high.astype(jnp.bfloat16)


def place_kernel(feats, *refs):
    out = refs[-1]
    span = refs[0].shape[1]
    for k in range(feats):
        out[:, pl.ds(behind(k, feats, span), span)] = refs[k][...]


def call(kernel, name, outs, ins, out_specs, scratch, mib, flops, moved, *args):
    return pl.pallas_call(
        kernel,
        out_shape=[jax.ShapeDtypeStruct(shape, kind) for shape, kind in outs],
        in_specs=ins,
        out_specs=out_specs,
        scratch_shapes=scratch,
        compiler_params=params(mib),
        cost_estimate=cost(flops, moved),
        name=name,
    )(*args)


def shards(rows, feats, features, adjacency, tile_cols, self_weight, neigh_weight, bias_vector, grad_output):
    hid, width = features.shape
    blocks, per_block, tile, unused = adjacency.shape
    half, span = hid // 2, width // feats
    every = hid * feats
    top = rows // 4
    narrow, wide = jnp.bfloat16, jnp.float32
    forward, backward = ring_pairs(rows, 1), ring_pairs(rows, -1)
    bind = functools.partial

    sources, wanted = [features, swap(features, rows)], [(0, 0, None), (0, 1, None)]
    up = [features[:half], features[half:]]
    down = list(up)
    for step in range(1, top + 1):
        for side in range(2):
            arrived = []
            if step < top or side == 0:
                up[side] = lax.ppermute(up[side], "rows", forward)
                arrived.append((-step, up[side]))
            if step < top or side == 1:
                down[side] = lax.ppermute(down[side], "rows", backward)
                arrived.append((step, down[side]))
            for offset, piece in arrived:
                sources += [piece, swap(piece, rows)]
                wanted += [(offset, 0, side), (offset, 1, side)]

    packed = 2 * span + 2 * every + 128
    packs = call(
        bind(pack_kernel, feats), "pack", [((hid, packed), narrow)] * feats, [VMEM] * 5,
        [VMEM] * feats, [], 8, 0, 4 * hid * packed * feats,
        features, grad_output, self_weight, neigh_weight, bias_vector.reshape(1, hid),
    )
    packs = exchange(packs, feats)
    turned, ws_all, wn_all, bias_all, x_all, cot_all = call(
        bind(unpack_kernel, feats), "unpack",
        [((every, 2 * every), narrow), ((every, every), narrow), ((every, every), narrow),
         ((every, 1), wide), ((every, span), narrow), ((every, span), narrow)],
        [VMEM] * feats, [VMEM] * 6, [pltpu.VMEM((2 * every, every), wide)], 8, 0,
        4 * every * packed, *packs,
    )
    (table,) = call(
        table_kernel, "table", [((rows * CAP,), jnp.int32)], [SMEM], [SMEM],
        [pltpu.SMEM((rows,), jnp.int32)], 4, 0, 8 * rows * CAP, tile_cols,
    )
    table_pair = swap(table, rows)
    pair = swap(adjacency, rows)

    count = len(sources)
    *aggs, inverse = call(
        bind(aggregate_kernel, (feats, tuple(wanted), rows, hid, half, width, per_block, tile)),
        "aggregate", [((hid, span), narrow)] * feats + [((feats, 1, span), wide)],
        [SMEM, VMEM] + [HBM] * count, [VMEM] * (feats + 1),
        [pltpu.VMEM((rows, hid, width), narrow), pltpu.SemaphoreType.DMA((count,))], 20,
        2 * hid * adjacency.size, 2 * adjacency.size + 2 * rows * hid * width,
        tile_cols, adjacency, *sources,
    )
    aggs = exchange(aggs, feats)

    outs = call(
        bind(middle_kernel, (feats, hid, span, min(span, 256))), "middle",
        [((hid, span), narrow)] * (2 * feats) + [((every, span), narrow)],
        [VMEM] * (6 + feats), [VMEM] * (2 * feats + 1),
        [pltpu.VMEM((2 * every, span), narrow)], 12,
        6 * every * every * span, 14 * every * span,
        turned, wn_all, bias_all, inverse, x_all, cot_all, *aggs,
    )
    scaled, acts, grad = outs[:feats], outs[feats : 2 * feats], outs[2 * feats]
    scaled = exchange(scaled, feats)
    scaled_pair = [swap(piece, rows) for piece in scaled]

    outs = call(
        bind(weights_kernel, feats), "weights",
        [((hid, span), wide)] * feats + [((4, hid + 8, every // 2), wide)] * feats,
        [VMEM] * (3 + feats), [VMEM] * (2 * feats), [], 12,
        6 * every * every * span, 10 * every * span,
        ws_all, x_all, grad, *aggs,
    )
    selfs, grads = exchange(outs[:feats], feats), exchange(outs[feats:], feats)
    acts = exchange(acts, feats)
    (activation,) = call(
        bind(place_kernel, feats), "place", [((hid, width), narrow)], [VMEM] * feats, [VMEM], [], 8,
        0, 4 * hid * width, *acts,
    )

    grads = sum(grads[1:], grads[0])
    grads = grads[:2] + swap(grads[2:], rows, 1)
    grads = grads[0] + swap(grads[1], rows, 2)
    bit = 4
    while bit < rows:
        grads = grads + swap(grads, rows, bit)
        bit *= 2
    near = jnp.stack([grads, swap(grads, rows, 2)])
    far = swap(near, rows, 1)
    grad_self, grad_neigh, sums = call(
        collect_kernel, "collect",
        [((hid, every), wide), ((hid, every), wide), ((8, every), wide)],
        [VMEM] * 2, [VMEM] * 3, [], 8, 0, 16 * hid * every, near, far,
    )
    grad_bias = lax.dynamic_slice_in_dim(sums[0], lax.axis_index("feat") * hid, hid)

    (held,) = call(
        bind(arrange_kernel, feats, tile), "arrange", [((2, blocks + 1, hid, tile), narrow)],
        [VMEM] * (2 * feats), [VMEM], [], 8, 0, 8 * hid * width, *scaled, *scaled_pair,
    )

    def spread(offsets, kinds, extra=()):
        return call(
            bind(spread_kernel, (feats, rows, offsets, kinds)), "spread",
            [((half, width), kind) for kind in kinds],
            [SMEM] * 2 + [VMEM] * (3 + len(extra)), [VMEM] * len(kinds),
            [pltpu.VMEM((hid, width), wide)], 8,
            4 * CAP * len(offsets) * hid * tile * tile, 8 * hid * width * len(offsets),
            table, table_pair, adjacency, pair, held, *extra,
        )

    up, down = [None, None], [None, None]

    def joined(arrived, mine):
        if arrived is None:
            return mine
        return (arrived.astype(jnp.float32) + mine).astype(jnp.bfloat16)

    for level in range(top, 0, -1):
        if level == top:
            low, high = spread((top,), (narrow, narrow))
            up[0] = lax.ppermute(low, "rows", forward)
            down[1] = lax.ppermute(high, "rows", backward)
            continue
        kinds = tuple(narrow if arrived is None else wide for arrived in up + down)
        mine = spread((level, -level), kinds)
        up = [lax.ppermute(joined(up[i], mine[i]), "rows", forward) for i in range(2)]
        down = [lax.ppermute(joined(down[i], mine[2 + i]), "rows", backward) for i in range(2)]
    low, high = spread((0,), (wide, wide), extra=tuple(selfs))
    (grad_features,) = call(
        finish_kernel, "finish", [((hid, width), narrow)], [VMEM] * 6, [VMEM], [], 8, 0,
        8 * hid * width, low, high, up[0], down[0], up[1], down[1],
    )
    return (activation, grad_features, grad_self, grad_neigh, grad_bias)


def solution(mesh):
    in_specs = (
        P("feat", "rows"),
        P("rows", None, None, None),
        P("rows", None),
        P("feat", None),
        P("feat", None),
        P("feat"),
        P("feat", "rows"),
    )
    out_specs = (P("feat", "rows"), P("feat", "rows"), P("feat", None), P("feat", None), P("feat"))
    body = functools.partial(shards, mesh.shape["rows"], mesh.shape["feat"])
    return jax.shard_map(body, mesh=mesh, in_specs=in_specs, out_specs=out_specs, check_vma=False)
```

time: 465 us -> 196 us (0.42)
  waiting for transfers between devices: 285 us -> 98.2 us
  starting transfers between devices: 0.39 us -> 50.5 us
  other arithmetic: 48.5 us -> 3.49 us
  local copies, waits for them, and re-layouts: 55.3 us -> 19.4 us
  blocking collectives: 33.9 us -> 0 us
  matrix products: 26.2 us -> 0 us
  Pallas kernels: 0 us -> 23.1 us
  between operations: 13.9 us -> 0.98 us
    reduce_scatter x2 -> x0, waiting for transfers between devices: 191 us -> none  [the longest x1 161 us: shards(): lax.psum_scatter(spread_sum.reshape(hid_dev, all_nodes), 'rows', scatter_...]
    ppermute x0 -> x59, waiting for transfers between devices: none -> 98.2 us  [the longest x7 26.9 us: shards(): down[side] = lax.ppermute(down[side], 'rows', backward)]
    all_gather x2 -> x0, waiting for transfers between devices: 94.6 us -> none  [the longest x1 73.3 us: shards(): gathered = lax.all_gather(features, 'rows', axis=1, tiled=True)]
    ppermute x0 -> x59, starting transfers between devices: none -> 50.5 us  [the longest x7 12.3 us: shards(): down[side] = lax.ppermute(down[side], 'rows', backward)]
    scatter-add x1 -> x0, other arithmetic: 40.1 us -> none  [shards(): spread_sum = spread_sum.at[:, flat_cols, :].add(contribs)]
    psum x1 -> x0, blocking collectives: 33.9 us -> none  [shards(): lax.psum((local_self, local_neigh, local_bias), 'rows')]
    dot_general x8 -> x0, matrix products: 26.2 us -> none  [the longest x1 9.17 us: shards(): jnp.einsum('hbi,btij->hbtj', scaled.reshape(hid_dev, blocks_dev, tile_siz...]
    pallas_call x0 -> x15, Pallas kernels: none -> 23.1 us  [call(): pl.pallas_call(kernel, out_shape=[jax.ShapeDtypeStruct(shape, kind) for s...]
  transfers between devices with their start and end apart: 5 -> 59, of which waited for: 4 -> 29; matrix products, arithmetic and copies ran while one was open for 18% -> 3% of each run, Pallas kernels for 0% -> 11%
where the time goes in v2:
time: 196 us
  waiting for transfers between devices  98.2 us (50%)
  starting transfers between devices  50.5 us (26%)
  Pallas kernels  23.1 us (12%)
  local copies, waits for them, and re-layouts  19.4 us (10%)
  other arithmetic  3.49 us (2%)
    ppermute x7, waiting for transfers between devices, shards(): down[side] = lax.ppermute(down[side], 'rows', backward)  26.9 us
    pallas_call x15, Pallas kernels, call(): pl.pallas_call(kernel, out_shape=[jax.ShapeDtypeStruct(shape, kind) for s...  23.1 us
    ppermute x6, waiting for transfers between devices, exchange(): lax.ppermute(pieces[k], 'feat', [(i, (i + k) % feats) for i in range(feat...  21.8 us
    unnamed x32, local copies, waits for them, and re-layouts  17.8 us
    ppermute x6, waiting for transfers between devices, shards(): lax.ppermute(joined(up[i], mine[i]), 'rows', forward)  17.5 us
    ppermute x6, waiting for transfers between devices, shards(): lax.ppermute(joined(down[i], mine[2 + i]), 'rows', backward)  14.6 us
    ppermute x7, starting transfers between devices, shards(): down[side] = lax.ppermute(down[side], 'rows', backward)  12.3 us
    ppermute x25, waiting for transfers between devices, swap(): return lax.ppermute(value, 'rows', [(r, r ^ bit) for r in range(rows)])  10.3 us
  transfers between devices with their start and end apart: 59, of which 29 were waited for; matrix products, arithmetic and copies ran while one was open for 3% of the time, Pallas kernels for 11%

profile of v2, /device:TPU:0, one launch (start us, length us, event | category | flops | bytes accessed | tf_op | source)
XLA Modules:
  0.0 195.7 jit_solution(2585807809062738988)
XLA Ops:
  7.0 5.1 %collective-permute-done.8.refs_8_ = bf16[64,2048]{1,0:T(8,128)(2,1)S(1)} collective-permute-done((bf16[64,2048]{1,0:T(8,128)(2,1)S(1)}, bf16[64,2048]{1,0:T(8,128)(2,1)S(1)}, u32[]{:S(2)}, u32[]{:S(2)}) %collective-permute-start.8) | collective-permute-done | bytes 262176 | tf_op jit(solution)/shard_map/ppermute | solution.py:349
  13.9 3.7 %collective-permute-done.4.refs_4_ = bf16[64,2048]{1,0:T(8,128)(2,1)S(1)} collective-permute-done((bf16[64,2048]{1,0:T(8,128)(2,1)S(1)}, bf16[64,2048]{1,0:T(8,128)(2,1)S(1)}, u32[]{:S(2)}, u32[]{:S(2)}) %collective-permute-start.4) | collective-permute-done | bytes 262176 | tf_op jit(solution)/shard_map/ppermute | solution.py:349
  19.6 3.5 %collective-permute-done.16.refs_16_ = bf16[64,2048]{1,0:T(8,128)(2,1)S(1)} collective-permute-done((bf16[64,2048]{1,0:T(8,128)(2,1)S(1)}, bf16[64,2048]{1,0:T(8,128)(2,1)S(1)}, u32[]{:S(2)}, u32[]{:S(2)}) %collective-permute-start.16) | collective-permute-done | bytes 262176 | tf_op jit(solution)/shard_map/ppermute | solution.py:349
  27.1 4.1 %collective-permute-done.12.refs_12_ = bf16[64,2048]{1,0:T(8,128)(2,1)S(1)} collective-permute-done((bf16[64,2048]{1,0:T(8,128)(2,1)S(1)}, bf16[64,2048]{1,0:T(8,128)(2,1)S(1)}, u32[]{:S(2)}, u32[]{:S(2)}) %collective-permute-start.12) | collective-permute-done | bytes 262176 | tf_op jit(solution)/shard_map/ppermute | solution.py:349
  36.1 3.8 %collective-permute-done.24.refs_24_ = bf16[64,2048]{1,0:T(8,128)(2,1)S(1)} collective-permute-done((bf16[64,2048]{1,0:T(8,128)(2,1)S(1)}, bf16[64,2048]{1,0:T(8,128)(2,1)S(1)}, u32[]{:S(2)}, u32[]{:S(2)}) %collective-permute-start.24) | collective-permute-done | bytes 262176 | tf_op jit(solution)/shard_map/ppermute | solution.py:349
  44.6 3.3 %collective-permute-done.20.refs_20_ = bf16[64,2048]{1,0:T(8,128)(2,1)S(1)} collective-permute-done((bf16[64,2048]{1,0:T(8,128)(2,1)S(1)}, bf16[64,2048]{1,0:T(8,128)(2,1)S(1)}, u32[]{:S(2)}, u32[]{:S(2)}) %collective-permute-start.20) | collective-permute-done | bytes 262176 | tf_op jit(solution)/shard_map/ppermute | solution.py:349
  51.5 3.4 %collective-permute-done.28.refs_28_ = bf16[64,2048]{1,0:T(8,128)(2,1)S(1)} collective-permute-done((bf16[64,2048]{1,0:T(8,128)(2,1)S(1)}, bf16[64,2048]{1,0:T(8,128)(2,1)S(1)}, u32[]{:S(2)}, u32[]{:S(2)}) %collective-permute-start.28) | collective-permute-done | bytes 262176 | tf_op jit(solution)/shard_map/ppermute | solution.py:349
  64.8 2.8 %copy-done = bf16[16,12,128,128]{3,2,1,0:T(8,128)(2,1)S(1)} copy-done((bf16[16,12,128,128]{3,2,1,0:T(8,128)(2,1)S(1)}, bf16[16,12,128,128]{3,2,1,0:T(8,128)(2,1)}, u32[]{:S(2)}) %copy-start) | copy-done | bytes 6291480
  69.4 5.1 %aggregate.1 = (bf16[128,1024]{1,0:T(8,128)(2,1)S(1)}, bf16[128,1024]{1,0:T(8,128)(2,1)S(1)}, f32[2,1,1024]{2,1,0:T(1,128)S(1)}) custom-call(s32[16,12]{1,0:T(8,128)S(1)} %copy-done.14, bf16[16,12,128,128]{3,2,1,0:T(8,128)(2,1)S(1)} %copy-done, bf16[128,2048]{1,0:T(8,128)(2,1)S(1)} %copy-done.6, bf16[128,2048]{1,0:T(8,128)(2,1)S(1)} %collective-permute-done.1.refs_1_, ...), custom_call_target="tpu_custom_call" | custom-call | flops 805306368 | bytes 14680064 | tf_op jit(solution)/shard_map/aggregate/pallas_call | solution.py:317
  76.3 6.7 %collective-permute-done.30.refs_1_ = bf16[128,1024]{1,0:T(8,128)(2,1)S(1)} collective-permute-done((bf16[128,1024]{1,0:T(8,128)(2,1)S(1)}, bf16[128,1024]{1,0:T(8,128)(2,1)S(1)}, u32[]{:S(2)}, u32[]{:S(2)}) %collective-permute-start.30) | collective-permute-done | bytes 262176 | tf_op jit(solution)/shard_map/ppermute | solution.py:55
  87.2 7.4 %collective-permute-done.52 = f32[4,136,128]{2,1,0:T(8,128)S(1)} collective-permute-done((f32[4,136,128]{2,1,0:T(8,128)S(1)}, f32[4,136,128]{2,1,0:T(8,128)S(1)}, u32[]{:S(2)}, u32[]{:S(2)}) %collective-permute-start.52) | collective-permute-done | bytes 278560 | tf_op jit(solution)/shard_map/ppermute | solution.py:55
  96.6 6.8 %collective-permute-done.34.refs_1_ = bf16[128,1024]{1,0:T(8,128)(2,1)S(1)} collective-permute-done((bf16[128,1024]{1,0:T(8,128)(2,1)S(1)}, bf16[128,1024]{1,0:T(8,128)(2,1)S(1)}, u32[]{:S(2)}, u32[]{:S(2)}) %collective-permute-start.34) | collective-permute-done | bytes 262176 | tf_op jit(solution)/shard_map/ppermute | solution.py:55
  105.1 3.1 %collective-permute-done.55 = f32[136,128]{1,0:T(8,128)S(1)} collective-permute-done((f32[136,128]{1,0:T(8,128)S(1)}, f32[136,128]{1,0:T(8,128)S(1)}, u32[]{:S(2)}, u32[]{:S(2)}) %collective-permute-start.55) | collective-permute-done | bytes 69664 | tf_op jit(solution)/shard_map/ppermute | solution.py:49
  110.9 4.2 %table.1 = s32[192]{0:T(256)S(1)} custom-call(s32[16,12]{1,0:T(8,128)S(1)} %copy-done.14), custom_call_target="tpu_custom_call" | custom-call | bytes 1536 | tf_op jit(solution)/shard_map/table/pallas_call | solution.py:317
  121.5 3.7 %collective-permute-done.57 = f32[136,128]{1,0:T(8,128)S(1)} collective-permute-done((f32[136,128]{1,0:T(8,128)S(1)}, f32[136,128]{1,0:T(8,128)S(1)}, u32[]{:S(2)}, u32[]{:S(2)}) %collective-permute-start.57) | collective-permute-done | bytes 69664 | tf_op jit(solution)/shard_map/ppermute | solution.py:49
  134.8 7.9 %collective-permute-done.45 = bf16[64,2048]{1,0:T(8,128)(2,1)S(1)} collective-permute-done((bf16[64,2048]{1,0:T(8,128)(2,1)S(1)}, bf16[64,2048]{1,0:T(8,128)(2,1)S(1)}, u32[]{:S(2)}, u32[]{:S(2)}) %collective-permute-start.45) | collective-permute-done | bytes 262176 | tf_op jit(solution)/shard_map/ppermute | solution.py:459
  144.9 5.3 %collective-permute-done.49 = bf16[64,2048]{1,0:T(8,128)(2,1)S(1)} collective-permute-done((bf16[64,2048]{1,0:T(8,128)(2,1)S(1)}, bf16[64,2048]{1,0:T(8,128)(2,1)S(1)}, u32[]{:S(2)}, u32[]{:S(2)}) %collective-permute-start.49) | collective-permute-done | bytes 262176 | tf_op jit(solution)/shard_map/ppermute | solution.py:460
  151.7 4.9 %collective-permute-done.43 = bf16[64,2048]{1,0:T(8,128)(2,1)S(1)} collective-permute-done((bf16[64,2048]{1,0:T(8,128)(2,1)S(1)}, bf16[64,2048]{1,0:T(8,128)(2,1)S(1)}, u32[]{:S(2)}, u32[]{:S(2)}) %collective-permute-start.43) | collective-permute-done | bytes 262176 | tf_op jit(solution)/shard_map/ppermute | solution.py:460
  159.5 5.2 %collective-permute-done.46 = bf16[64,2048]{1,0:T(8,128)(2,1)S(1)} collective-permute-done((bf16[64,2048]{1,0:T(8,128)(2,1)S(1)}, bf16[64,2048]{1,0:T(8,128)(2,1)S(1)}, u32[]{:S(2)}, u32[]{:S(2)}) %collective-permute-start.46) | collective-permute-done | bytes 262176 | tf_op jit(solution)/shard_map/ppermute | solution.py:459
  166.7 4.3 %collective-permute-done.40 = bf16[64,2048]{1,0:T(8,128)(2,1)S(1)} collective-permute-done((bf16[64,2048]{1,0:T(8,128)(2,1)S(1)}, bf16[64,2048]{1,0:T(8,128)(2,1)S(1)}, u32[]{:S(2)}, u32[]{:S(2)}) %collective-permute-start.40) | collective-permute-done | bytes 262176 | tf_op jit(solution)/shard_map/ppermute | solution.py:459
  173.6 4.4 %collective-permute-done.50 = bf16[64,2048]{1,0:T(8,128)(2,1)S(1)} collective-permute-done((bf16[64,2048]{1,0:T(8,128)(2,1)S(1)}, bf16[64,2048]{1,0:T(8,128)(2,1)S(1)}, u32[]{:S(2)}, u32[]{:S(2)}) %collective-permute-start.50) | collective-permute-done | bytes 262176 | tf_op jit(solution)/shard_map/ppermute | solution.py:460
  180.4 3.4 %collective-permute-start.41 = (bf16[64,2048]{1,0:T(8,128)(2,1)}, bf16[64,2048]{1,0:T(8,128)(2,1)S(1)}, u32[]{:S(2)}, u32[]{:S(2)}) collective-permute-start(bf16[64,2048]{1,0:T(8,128)(2,1)} %add_convert_fusion.7), channel_id=1, source_target_pairs={{0,8},{2,10},{8,16},{10,18},{16,24},{18,26},{24,28},{26,30},{28,20... | collective-permute-start | bytes 786440 | tf_op jit(solution)/shard_map/ppermute | solution.py:459
  187.9 2.8 %copy-done.2 = bf16[16,12,128,128]{3,2,1,0:T(8,128)(2,1)S(1)} copy-done((bf16[16,12,128,128]{3,2,1,0:T(8,128)(2,1)S(1)}, bf16[16,12,128,128]{3,2,1,0:T(8,128)(2,1)}, u32[]{:S(2)}) %copy-start.2) | copy-done | bytes 6291480
  190.7 2.8 %copy-done.4 = bf16[16,12,128,128]{3,2,1,0:T(8,128)(2,1)S(1)} copy-done((bf16[16,12,128,128]{3,2,1,0:T(8,128)(2,1)S(1)}, bf16[16,12,128,128]{3,2,1,0:T(8,128)(2,1)}, u32[]{:S(2)}) %copy-start.4) | copy-done | bytes 6291480
  (162 shorter events, 87.0 us)
Async XLA Ops:
  0.6 115.6 %collective-permute-start.33 = (bf16[16,12,128,128]{3,2,1,0:T(8,128)(2,1)}, bf16[16,12,128,128]{3,2,1,0:T(8,128)(2,1)S(1)}, u32[]{:S(2)}, u32[]{:S(2)}) collective-permute-start(bf16[16,12,128,128]{3,2,1,0:T(8,128)(2,1)} %adj.11), channel_id=1, source_target_pairs={{0,2},{2,0},{4,6},{6,4},{8,10},{10,8},{12,14},{14,12},{16,18},{18,... | collective-permute-start | bytes 18874376 | tf_op jit(solution)/shard_map/ppermute | solution.py:49
  2.2 9.8 %collective-permute-start.8 = (bf16[64,2048]{1,0:T(8,128)(2,1)S(1)}, bf16[64,2048]{1,0:T(8,128)(2,1)S(1)}, u32[]{:S(2)}, u32[]{:S(2)}) collective-permute-start(bf16[64,2048]{1,0:T(8,128)(2,1)S(1)} %get-tuple-element.83), channel_id=1, source_target_pairs={{0,4},{2,6},{8,0},{10,2},{16,8},{18,10},{24,16},{26,18},{28,24},{3... | collective-permute-start | bytes 786440 | tf_op jit(solution)/shard_map/ppermute | solution.py:349
  4.9 12.7 %collective-permute-start.4 = (bf16[64,2048]{1,0:T(8,128)(2,1)S(1)}, bf16[64,2048]{1,0:T(8,128)(2,1)S(1)}, u32[]{:S(2)}, u32[]{:S(2)}) collective-permute-start(bf16[64,2048]{1,0:T(8,128)(2,1)S(1)} %get-tuple-element.84), channel_id=1, source_target_pairs={{0,4},{2,6},{8,0},{10,2},{16,8},{18,10},{24,16},{26,18},{28,24},{3... | collective-permute-start | bytes 786440 | tf_op jit(solution)/shard_map/ppermute | solution.py:349
  6.8 12.8 %collective-permute-start.2 = (bf16[64,2048]{1,0:T(8,128)(2,1)S(1)}, bf16[64,2048]{1,0:T(8,128)(2,1)S(1)}, u32[]{:S(2)}, u32[]{:S(2)}) collective-permute-start(bf16[64,2048]{1,0:T(8,128)(2,1)S(1)} %get-tuple-element.84), channel_id=1, source_target_pairs={{0,8},{2,10},{8,16},{10,18},{16,24},{18,26},{24,28},{26,30},{28,20... | collective-permute-start | bytes 786440 | tf_op jit(solution)/shard_map/ppermute | solution.py:346
  12.0 11.0 %collective-permute-start.16 = (bf16[64,2048]{1,0:T(8,128)(2,1)S(1)}, bf16[64,2048]{1,0:T(8,128)(2,1)S(1)}, u32[]{:S(2)}, u32[]{:S(2)}) collective-permute-start(bf16[64,2048]{1,0:T(8,128)(2,1)S(1)} %collective-permute-done.8.refs_8_), channel_id=1, source_target_pairs={{0,4},{2,6},{8,0},{10,2},{16,8},{18,10},{24,16},{26,18},{28,24},{3... | collective-permute-start | bytes 786440 | tf_op jit(solution)/shard_map/ppermute | solution.py:349
  13.9 10.8 %collective-permute-start.9 = (bf16[64,2048]{1,0:T(8,128)(2,1)S(1)}, bf16[64,2048]{1,0:T(8,128)(2,1)S(1)}, u32[]{:S(2)}, u32[]{:S(2)}) collective-permute-start(bf16[64,2048]{1,0:T(8,128)(2,1)S(1)} %collective-permute-done.8.refs_8_), channel_id=1, source_target_pairs={{0,2},{2,0},{4,6},{6,4},{8,10},{10,8},{12,14},{14,12},{16,18},{18,... | collective-permute-start | bytes 786440 | tf_op jit(solution)/shard_map/ppermute | solution.py:49
  24.7 11.1 %collective-permute-start.1 = (bf16[128,2048]{1,0:T(8,128)(2,1)}, bf16[128,2048]{1,0:T(8,128)(2,1)S(1)}, u32[]{:S(2)}, u32[]{:S(2)}) collective-permute-start(bf16[128,2048]{1,0:T(8,128)(2,1)} %refs_0_.1), channel_id=1, source_target_pairs={{0,2},{2,0},{4,6},{6,4},{8,10},{10,8},{12,14},{14,12},{16,18},{18,... | collective-permute-start | bytes 1572872 | tf_op jit(solution)/shard_map/ppermute | solution.py:49
  49.3 11.7 %collective-permute-start.25 = (bf16[64,2048]{1,0:T(8,128)(2,1)S(1)}, bf16[64,2048]{1,0:T(8,128)(2,1)S(1)}, u32[]{:S(2)}, u32[]{:S(2)}) collective-permute-start(bf16[64,2048]{1,0:T(8,128)(2,1)S(1)} %collective-permute-done.24.refs_24_), channel_id=1, source_target_pairs={{0,2},{2,0},{4,6},{6,4},{8,10},{10,8},{12,14},{14,12},{16,18},{18,... | collective-permute-start | bytes 786440 | tf_op jit(solution)/shard_map/ppermute | solution.py:49
  51.0 11.6 %collective-permute-start.23 = (bf16[64,2048]{1,0:T(8,128)(2,1)S(1)}, bf16[64,2048]{1,0:T(8,128)(2,1)S(1)}, u32[]{:S(2)}, u32[]{:S(2)}) collective-permute-start(bf16[64,2048]{1,0:T(8,128)(2,1)S(1)} %collective-permute-done.22.refs_22_), channel_id=1, source_target_pairs={{0,2},{2,0},{4,6},{6,4},{8,10},{10,8},{12,14},{14,12},{16,18},{18,... | collective-permute-start | bytes 786440 | tf_op jit(solution)/shard_map/ppermute | solution.py:49
  51.0 11.6 %collective-permute-start.21 = (bf16[64,2048]{1,0:T(8,128)(2,1)S(1)}, bf16[64,2048]{1,0:T(8,128)(2,1)S(1)}, u32[]{:S(2)}, u32[]{:S(2)}) collective-permute-start(bf16[64,2048]{1,0:T(8,128)(2,1)S(1)} %collective-permute-done.20.refs_20_), channel_id=1, source_target_pairs={{0,2},{2,0},{4,6},{6,4},{8,10},{10,8},{12,14},{14,12},{16,18},{18,... | collective-permute-start | bytes 786440 | tf_op jit(solution)/shard_map/ppermute | solution.py:49
  61.0 15.0 %collective-permute-start = (bf16[128,2688]{1,0:T(8,128)(2,1)S(1)}, bf16[128,2688]{1,0:T(8,128)(2,1)S(1)}, u32[]{:S(2)}, u32[]{:S(2)}) collective-permute-start(bf16[128,2688]{1,0:T(8,128)(2,1)S(1)} %get-tuple-element.45), channel_id=1, source_target_pairs={{0,1},{1,0},{2,3},{3,2},{4,5},{5,4},{6,7},{7,6},{8,9},{9,8},{10,11... | collective-permute-start | bytes 2064392 | tf_op jit(solution)/shard_map/ppermute | solution.py:55
  96.6 18.5 %collective-permute-start.35 = (bf16[128,1024]{1,0:T(8,128)(2,1)S(1)}, bf16[128,1024]{1,0:T(8,128)(2,1)S(1)}, u32[]{:S(2)}, u32[]{:S(2)}) collective-permute-start(bf16[128,1024]{1,0:T(8,128)(2,1)S(1)} %get-tuple-element.56.refs_0_), channel_id=1, source_target_pairs={{0,2},{2,0},{4,6},{6,4},{8,10},{10,8},{12,14},{14,12},{16,18},{18,... | collective-permute-start | bytes 786440 | tf_op jit(solution)/shard_map/ppermute | solution.py:49
  103.5 11.6 %collective-permute-start.36 = (bf16[128,1024]{1,0:T(8,128)(2,1)S(1)}, bf16[128,1024]{1,0:T(8,128)(2,1)S(1)}, u32[]{:S(2)}, u32[]{:S(2)}) collective-permute-start(bf16[128,1024]{1,0:T(8,128)(2,1)S(1)} %collective-permute-done.34.refs_1_), channel_id=1, source_target_pairs={{0,2},{2,0},{4,6},{6,4},{8,10},{10,8},{12,14},{14,12},{16,18},{18,... | collective-permute-start | bytes 786440 | tf_op jit(solution)/shard_map/ppermute | solution.py:49
  108.2 9.6 %collective-permute-start.56 = (f32[136,128]{1,0:T(8,128)S(1)}, f32[136,128]{1,0:T(8,128)S(1)}, u32[]{:S(2)}, u32[]{:S(2)}) collective-permute-start(f32[136,128]{1,0:T(8,128)S(1)} %add.61), channel_id=1, source_target_pairs={{0,16},{2,18},{4,20},{6,22},{8,24},{10,26},{12,28},{14,30},{16,0},... | collective-permute-start | bytes 208904 | tf_op jit(solution)/shard_map/ppermute | solution.py:49
  117.4 13.4 %collective-permute-start.48 = (bf16[64,2048]{1,0:T(8,128)(2,1)S(1)}, bf16[64,2048]{1,0:T(8,128)(2,1)S(1)}, u32[]{:S(2)}, u32[]{:S(2)}) collective-permute-start(bf16[64,2048]{1,0:T(8,128)(2,1)S(1)} %get-tuple-element.74), channel_id=1, source_target_pairs={{0,4},{2,6},{8,0},{10,2},{16,8},{18,10},{24,16},{26,18},{28,24},{3... | collective-permute-start | bytes 786440 | tf_op jit(solution)/shard_map/ppermute | solution.py:455
  119.4 60.3 %collective-permute-start.31 = (bf16[128,1024]{1,0:T(8,128)(2,1)S(1)}, bf16[128,1024]{1,0:T(8,128)(2,1)S(1)}, u32[]{:S(2)}, u32[]{:S(2)}) collective-permute-start(bf16[128,1024]{1,0:T(8,128)(2,1)S(1)} %get-tuple-element.55), channel_id=1, source_target_pairs={{0,1},{1,0},{2,3},{3,2},{4,5},{5,4},{6,7},{7,6},{8,9},{9,8},{10,11... | collective-permute-start | bytes 786440 | tf_op jit(solution)/shard_map/ppermute | solution.py:55
  120.0 67.9 %collective-permute-start.37 = (f32[128,1024]{1,0:T(8,128)}, f32[128,1024]{1,0:T(8,128)S(1)}, u32[]{:S(2)}, u32[]{:S(2)}) collective-permute-start(f32[128,1024]{1,0:T(8,128)} %get-tuple-element.61), channel_id=1, source_target_pairs={{0,1},{1,0},{2,3},{3,2},{4,5},{5,4},{6,7},{7,6},{8,9},{9,8},{10,11... | collective-permute-start | bytes 1572872 | tf_op jit(solution)/shard_map/ppermute | solution.py:55
  125.2 58.6 %collective-permute-start.58 = (f32[2,136,128]{2,1,0:T(8,128)S(1)}, f32[2,136,128]{2,1,0:T(8,128)S(1)}, u32[]{:S(2)}, u32[]{:S(2)}) collective-permute-start(f32[2,136,128]{2,1,0:T(8,128)S(1)} %pad_maximum_fusion.pair), channel_id=1, source_target_pairs={{0,2},{2,0},{4,6},{6,4},{8,10},{10,8},{12,14},{14,12},{16,18},{18,... | collective-permute-start | bytes 417800 | tf_op jit(solution)/shard_map/ppermute | solution.py:49
  130.8 12.2 %collective-permute-start.42 = (bf16[64,2048]{1,0:T(8,128)(2,1)S(1)}, bf16[64,2048]{1,0:T(8,128)(2,1)S(1)}, u32[]{:S(2)}, u32[]{:S(2)}) collective-permute-start(bf16[64,2048]{1,0:T(8,128)(2,1)S(1)} %get-tuple-element.68), channel_id=1, source_target_pairs={{0,4},{2,6},{8,0},{10,2},{16,8},{18,10},{24,16},{26,18},{28,24},{3... | collective-permute-start | bytes 786440 | tf_op jit(solution)/shard_map/ppermute | solution.py:460
  142.7 15.5 %collective-permute-start.39 = (bf16[64,2048]{1,0:T(8,128)(2,1)S(1)}, bf16[64,2048]{1,0:T(8,128)(2,1)S(1)}, u32[]{:S(2)}, u32[]{:S(2)}) collective-permute-start(bf16[64,2048]{1,0:T(8,128)(2,1)S(1)} %add_convert_fusion.9), channel_id=1, source_target_pairs={{0,8},{2,10},{8,16},{10,18},{16,24},{18,26},{24,28},{26,30},{28,20... | collective-permute-start | bytes 786440 | tf_op jit(solution)/shard_map/ppermute | solution.py:459
  158.2 36.5 %collective-permute-start.44 = (bf16[64,2048]{1,0:T(8,128)(2,1)}, bf16[64,2048]{1,0:T(8,128)(2,1)S(1)}, u32[]{:S(2)}, u32[]{:S(2)}) collective-permute-start(bf16[64,2048]{1,0:T(8,128)(2,1)} %add_convert_fusion.5), channel_id=1, source_target_pairs={{0,4},{2,6},{8,0},{10,2},{16,8},{18,10},{24,16},{26,18},{28,24},{3... | collective-permute-start | bytes 786440 | tf_op jit(solution)/shard_map/ppermute | solution.py:460
  178.0 16.8 %collective-permute-start.47 = (bf16[64,2048]{1,0:T(8,128)(2,1)}, bf16[64,2048]{1,0:T(8,128)(2,1)S(1)}, u32[]{:S(2)}, u32[]{:S(2)}) collective-permute-start(bf16[64,2048]{1,0:T(8,128)(2,1)} %add_convert_fusion.3), channel_id=1, source_target_pairs={{0,8},{2,10},{8,16},{10,18},{16,24},{18,26},{24,28},{26,30},{28,20... | collective-permute-start | bytes 786440 | tf_op jit(solution)/shard_map/ppermute | solution.py:459
  180.4 14.3 %collective-permute-start.41 = (bf16[64,2048]{1,0:T(8,128)(2,1)}, bf16[64,2048]{1,0:T(8,128)(2,1)S(1)}, u32[]{:S(2)}, u32[]{:S(2)}) collective-permute-start(bf16[64,2048]{1,0:T(8,128)(2,1)} %add_convert_fusion.7), channel_id=1, source_target_pairs={{0,8},{2,10},{8,16},{10,18},{16,24},{18,26},{24,28},{26,30},{28,20... | collective-permute-start | bytes 786440 | tf_op jit(solution)/shard_map/ppermute | solution.py:459
  183.9 10.9 %collective-permute-start.51 = (bf16[64,2048]{1,0:T(8,128)(2,1)}, bf16[64,2048]{1,0:T(8,128)(2,1)S(1)}, u32[]{:S(2)}, u32[]{:S(2)}) collective-permute-start(bf16[64,2048]{1,0:T(8,128)(2,1)} %add_convert_fusion), channel_id=1, source_target_pairs={{0,4},{2,6},{8,0},{10,2},{16,8},{18,10},{24,16},{26,18},{28,24},{3... | collective-permute-start | bytes 786440 | tf_op jit(solution)/shard_map/ppermute | solution.py:460
  (51 other events, 304.2 us)

commit v3 on v2

v3 whole, which is shorter than its diff:
```python
import functools

import jax
import jax.numpy as jnp
from jax import lax
from jax.experimental import pallas as pl
from jax.experimental.pallas import tpu as pltpu
from jax.sharding import PartitionSpec as P

CAP = 12
MIB = 1024 * 1024
WHOLE = 60
HBM = pl.BlockSpec(memory_space=pltpu.HBM)
VMEM = pl.BlockSpec(memory_space=pltpu.VMEM)
SMEM = pl.BlockSpec(memory_space=pltpu.SMEM)
LAST = (((1,), (1,)), ((), ()))


def params(mib):
    return pltpu.CompilerParams(vmem_limit_bytes=mib * MIB)


def cost(flops, moved):
    return pl.CostEstimate(flops=flops, bytes_accessed=moved, transcendentals=0)


def product(left, right, dims=(((1,), (0,)), ((), ()))):
    return lax.dot_general(left, right, dims, preferred_element_type=jnp.float32)


def ring_pairs(rows, step, flip=0):
    levels, chips = rows // 4, rows // 2
    order = [2 * z for z in range(levels)] + [2 * z + 1 for z in reversed(range(levels))]
    return [
        (2 * order[p] + core, 2 * order[(p + step) % chips] + (core ^ flip))
        for p in range(chips)
        for core in range(2)
    ]


def ring_row(row, offset, rows):
    levels, chips = rows // 4, rows // 2
    z, x, core = row // 4, lax.rem(row // 2, 2), lax.rem(row, 2)
    target = lax.rem(jnp.where(x == 0, z, chips - 1 - z) + (offset + chips), chips)
    low = target < levels
    return 2 * jnp.where(low, 2 * target, 2 * (chips - 1 - target) + 1) + core


def swap(value, rows, bit=1):
    return lax.ppermute(value, "rows", [(r, r ^ bit) for r in range(rows)])


def exchange(pieces, feats):
    got = [pieces[0]]
    for k in range(1, feats):
        got.append(lax.ppermute(pieces[k], "feat", [(i, (i + k) % feats) for i in range(feats)]))
    return got


def after(value, *others):
    return lax.optimization_barrier((value, *others))[0]


def ahead(k, feats, size):
    return pl.multiple_of(lax.rem(lax.axis_index("feat") + k, feats) * size, size)


def behind(k, feats, size):
    return pl.multiple_of(lax.rem(lax.axis_index("feat") - k + feats, feats) * size, size)


def pack_kernel(feats, feature, grad_output, ws, wn, bias, *refs):
    outs, (parts, sems) = refs[:feats], refs[feats:]
    hid, every = ws.shape
    span = feature.shape[1] // feats
    copies = []
    for k in range(feats):
        at = pl.ds(ahead(k, feats, span), span)
        for source, low, size in (
            (feature.at[:, at], 0, span),
            (grad_output.at[:, at], span, span),
            (ws, 2 * span, every),
            (wn, 2 * span + every, every),
            (parts, 2 * span + 2 * every, 128),
        ):
            place = outs[k].at[:, pl.ds(low, size)]
            copies.append(pltpu.make_async_copy(source, place, sems.at[len(copies)]))
    line = lax.broadcasted_iota(jnp.int32, (hid, hid), 0)
    lane = lax.broadcasted_iota(jnp.int32, (hid, hid), 1)
    column = jnp.sum(jnp.where(line == lane, bias[...], 0.0), axis=1, keepdims=True)
    high = column.astype(jnp.bfloat16).astype(jnp.float32)
    middle = (column - high).astype(jnp.bfloat16).astype(jnp.float32)
    low = column - high - middle
    at = lax.broadcasted_iota(jnp.int32, (hid, 128), 1)
    value = jnp.where(at == 0, high, jnp.where(at == 1, middle, jnp.where(at == 2, low, 0.0)))
    parts[...] = value.astype(jnp.bfloat16)
    for copy in copies:
        copy.start()
    for copy in copies:
        copy.wait()


def unpack_kernel(feats, *refs):
    packs, (turned, ws_all, wn_all, bias_all, x_all, cot_all, both) = refs[:feats], refs[feats:]
    hid, span = packs[0].shape[0], x_all.shape[1]
    every = feats * hid
    for k in range(feats):
        at = pl.ds(behind(k, feats, hid), hid)
        pack = packs[k]
        x_all[at] = pack[:, :span]
        cot_all[at] = pack[:, span : 2 * span]
        ws_all[at] = pack[:, 2 * span : 2 * span + every]
        wn_all[at] = pack[:, 2 * span + every : 2 * span + 2 * every]
        parts = pack[:, 2 * span + 2 * every :].astype(jnp.float32)
        bias_all[at] = jnp.sum(parts, axis=1, keepdims=True)
    both[:every] = ws_all[...].astype(jnp.float32)
    both[every:] = wn_all[...].astype(jnp.float32)
    turned[...] = both[...].T.astype(jnp.bfloat16)


def table_kernel(cols, table, counts):
    blocks, per_block = cols.shape
    base = blocks * per_block
    groups = counts.shape[0]

    def clear(i, carry):
        counts[i] = 0
        for s in range(CAP):
            table[base + i * CAP + s] = -1
        return carry

    lax.fori_loop(0, groups, clear, 0)

    def step(block, carry):
        for t in range(per_block):
            col = cols[block, t]
            group = col // blocks
            seen = counts[group]
            counts[group] = seen + 1
            index = block * per_block + t
            table[index] = col
            table[base + group * CAP + seen] = index * 256 + (col - group * blocks)
        return carry

    lax.fori_loop(0, blocks, step, 0)


def aggregate_kernel(plan, table, table_pair, adj, pair, *refs):
    feats, parts, wanted, rows = plan
    count, taken = len(wanted), len(parts)
    blocks, per_block, tile, unused = adj.shape
    part = blocks // feats
    half = refs[0].shape[0]
    sources, refs = refs[:count], refs[count:]
    near, far, inverse, (held, tiles, sems, tile_sems) = (
        refs[:taken],
        refs[taken : 2 * taken],
        refs[2 * taken],
        refs[2 * taken + 1 :],
    )
    row = lax.axis_index("rows")
    copies = []
    for n, (offset, side) in enumerate(wanted):
        place = ring_row(row, offset, rows)
        if side:
            place = place + 1 - 2 * lax.rem(place, 2)
        copies.append(pltpu.make_async_copy(sources[n], held.at[place], sems.at[n]))

    def fetch(slot, local, side):
        where = lax.rem(lax.axis_index("feat") + parts[slot], feats)
        return pltpu.make_async_copy(
            (adj, pair)[side].at[where * part + local],
            tiles.at[slot, local, side],
            tile_sems.at[slot, local, side],
        )

    for copy in copies:
        copy.start()
    for slot in range(taken):
        for local in range(part):
            for side in range(2):
                fetch(slot, local, side).start()
    for copy in copies:
        copy.wait()
    ones = jnp.ones((16, 2 * tile), jnp.bfloat16)
    for slot in range(taken):
        where = lax.rem(lax.axis_index("feat") + parts[slot], feats)

        def step(local, carry):
            lane = pl.ds(pl.multiple_of(local * tile, tile), tile)
            for side in range(2):
                fetch(slot, local, side).wait()
            for side in range(2):
                first = (where * part + local) * per_block
                total = None
                for t in range(0, per_block, 2):
                    left, right = [], []
                    for u in (t, t + 1):
                        col = (table, table_pair)[side][first + u]
                        source = col // blocks
                        at = pl.multiple_of((col - source * blocks) * tile, tile)
                        left.append(held[source, :, pl.ds(at, tile)])
                        right.append(tiles[slot, local, side, u])
                    term = product(
                        jnp.concatenate([jnp.concatenate(left, axis=1), ones], axis=0),
                        jnp.concatenate(right, axis=1),
                        LAST,
                    )
                    total = term if total is None else total + term
                factor = 1.0 / total[half : half + 1]
                value = (total[:half] * factor).astype(jnp.bfloat16)
                (near, far)[side][slot][:, lane] = value
                if side == 0:
                    inverse[slot, :, lane] = factor
            return carry

        lax.fori_loop(0, part, step, 0)


def middle_kernel(plan, turned, wn, bias, inverse, x_all, cot, *refs):
    feats, hid, span, chunk = plan
    near, far, refs = refs[:feats], refs[feats : 2 * feats], refs[2 * feats :]
    scaled, acts, grad, agg = refs[:feats], refs[feats : 2 * feats], refs[2 * feats], refs[2 * feats + 1]
    half = hid // 2
    core = lax.rem(lax.axis_index("rows"), 2)
    for k in range(feats):
        base = behind(k, feats, hid)
        agg[pl.ds(pl.multiple_of(base + core * half, half), half)] = near[k][...]
        agg[pl.ds(pl.multiple_of(base + (1 - core) * half, half), half)] = far[k][...]
    every = feats * hid
    for c in range(0, span, chunk):
        lane = pl.ds(c, chunk)
        for k in range(feats):
            at = pl.ds(ahead(k, feats, hid), hid)
            pre = product(turned[at, :every], x_all[:, lane])
            pre = pre + product(turned[at, every:], agg[:, lane]) + bias[at]
            slope = jnp.exp(jnp.minimum(pre, 0.0))
            acts[k][:, lane] = jnp.where(pre > 0, pre, slope - 1.0).astype(jnp.bfloat16)
            grad[at, lane] = (cot[at, lane].astype(jnp.float32) * slope).astype(jnp.bfloat16)
        for k in range(feats):
            at = pl.ds(ahead(k, feats, hid), hid)
            back = product(wn[at], grad[:, lane])
            scaled[k][:, lane] = (back * inverse[0, :, lane]).astype(jnp.bfloat16)


def own_quarter():
    row = lax.axis_index("rows")
    return 2 * lax.rem(row, 2) + lax.rem(row // 2, 2)


def turned_quarter(mine, index):
    both = (index // 2, index % 2)
    core = both[0] + mine // 2 - 2 * both[0] * (mine // 2)
    x = both[1] + lax.rem(mine, 2) - 2 * both[1] * lax.rem(mine, 2)
    return 2 * core + x


def weights_kernel(feats, ws, x_all, agg, grad, *refs):
    acts, (first, *sent), grads = refs[:feats], refs[feats : 2 * feats], refs[2 * feats :]
    every, span = grad.shape
    hid = every // feats
    wide = every // 2
    mine = own_quarter()
    g = grad[...]
    sums = product(jnp.ones((8, span), jnp.bfloat16), g, LAST)
    for k in range(feats):
        at = pl.ds(ahead(k, feats, hid), hid)
        own = product(ws[at], g)
        if k == 0:
            first[...] = own
        else:
            high = own.astype(jnp.bfloat16)
            sent[k - 1][:, :span] = acts[k][...]
            sent[k - 1][:, span : 2 * span] = high
            sent[k - 1][:, 2 * span :] = (own - high.astype(jnp.float32)).astype(jnp.bfloat16)
        values = [product(x_all[at], g, LAST), product(agg[at], g, LAST)]
        for quarter in range(4):
            slot = turned_quarter(mine, quarter)
            lane = slice(quarter % 2 * wide, (quarter % 2 + 1) * wide)
            grads[k][slot, :hid] = values[quarter // 2][:, lane]
            grads[k][slot, hid:] = sums[:, lane]


def collect_kernel(pair, pair_far, grad_self, grad_neigh, sums):
    hid, every = grad_self.shape
    wide = every // 2
    mine = own_quarter()
    for slot in range(4):
        value = (pair, pair_far)[slot // 2][slot % 2]
        quarter = turned_quarter(mine, slot)
        for q, out in enumerate((grad_self, grad_self, grad_neigh, grad_neigh)):

            @pl.when(quarter == q)
            def _():
                lane = slice(q % 2 * wide, (q % 2 + 1) * wide)
                out[:, lane] = value[:hid]
                if q < 2:
                    sums[:, lane] = value[hid:]


def arrange_kernel(feats, tile, *refs):
    pieces, held = refs[:-1], refs[-1]
    hid, span = pieces[0].shape
    part = span // tile
    for side in range(2):
        held[side, feats * part] = jnp.zeros((hid, tile), jnp.bfloat16)
        for k in range(feats):
            base = lax.rem(lax.axis_index("feat") - k + feats, feats) * part
            for local in range(part):
                held[side, base + local] = pieces[side * feats + k][:, local * tile : (local + 1) * tile]


def spread_kernel(plan, table, table_pair, adj, pair, held, *refs):
    rows, offsets, kinds = plan
    results, (total, tiles, sems) = refs[: len(kinds)], refs[len(kinds) :]
    blocks, per_block, tile, unused = adj.shape
    half = total.shape[0] // 2
    row = lax.axis_index("rows")
    firsts = [blocks * per_block + ring_row(row, offset, rows) * CAP for offset in offsets]
    sides = ((table, adj), (table_pair, pair))
    copies = []
    for d in range(len(offsets)):
        for side, (slots, source) in enumerate(sides):
            for s in range(CAP):
                index = jnp.maximum(slots[firsts[d] + s], 0) // 256
                block = index // per_block
                n = (2 * d + side) * CAP + s
                tiled = source.at[block, index - block * per_block]
                copies.append(pltpu.make_async_copy(tiled, tiles.at[n], sems.at[n]))
                copies[-1].start()
    for d in range(len(offsets)):
        total[...] = jnp.zeros_like(total)
        for copy in copies[2 * d * CAP : 2 * (d + 1) * CAP]:
            copy.wait()
        for side, (slots, source) in enumerate(sides):
            for s0 in range(0, CAP, 4):
                terms = []
                for s in range(s0, s0 + 4):
                    entry = slots[firsts[d] + s]
                    index = jnp.maximum(entry, 0) // 256
                    place = jnp.where(entry < 0, blocks, index // per_block)
                    lane = lax.rem(jnp.maximum(entry, 0), 256) * tile
                    term = product(held[side, place], tiles[(2 * d + side) * CAP + s])
                    terms.append((pl.multiple_of(lane, tile), term))
                for lane, term in terms:
                    total[:, pl.ds(lane, tile)] += term
        for part in range(2):
            value = total[part * half : (part + 1) * half]
            results[2 * d + part][...] = value.astype(kinds[2 * d + part])


def finish_kernel(feats, base_low, base_high, a_low, b_low, a_high, b_high, *refs):
    (own, *sent), out = refs[:feats], refs[feats]
    half, span = a_low.shape[0], own.shape[1]
    for k in range(feats):
        at = behind(k, feats, span)
        nodes = pl.ds(at, span)
        for part, (base, a, b) in enumerate(((base_low, a_low, b_low), (base_high, a_high, b_high))):
            lines = slice(part * half, (part + 1) * half)
            if k == 0:
                value = own[lines]
            else:
                value = sent[k - 1][lines, span : 2 * span].astype(jnp.float32)
                value = value + sent[k - 1][lines, 2 * span :].astype(jnp.float32)
            value = value + base[:, nodes] + a[:, nodes].astype(jnp.float32)
            out[lines, nodes] = (value + b[:, nodes].astype(jnp.float32)).astype(jnp.bfloat16)


def place_kernel(feats, *refs):
    (own, *sent), out = refs[:feats], refs[feats]
    span = own.shape[1]
    out[:, pl.ds(behind(0, feats, span), span)] = own[...]
    for k in range(1, feats):
        out[:, pl.ds(behind(k, feats, span), span)] = sent[k - 1][:, :span]


def call(kernel, name, outs, ins, out_specs, scratch, mib, flops, moved, *args):
    return pl.pallas_call(
        kernel,
        out_shape=[jax.ShapeDtypeStruct(shape, kind) for shape, kind in outs],
        in_specs=ins,
        out_specs=out_specs,
        scratch_shapes=scratch,
        compiler_params=params(mib),
        cost_estimate=cost(flops, moved),
        name=name,
    )(*args)


def shards(rows, feats, features, adjacency, tile_cols, self_weight, neigh_weight, bias_vector, grad_output):
    hid, width = features.shape
    blocks, per_block, tile, unused = adjacency.shape
    half, span = hid // 2, width // feats
    every = hid * feats
    top = rows // 4
    narrow, wide = jnp.bfloat16, jnp.float32
    forward, backward = ring_pairs(rows, 1), ring_pairs(rows, -1)
    bind = functools.partial

    core = lax.rem(lax.axis_index("rows"), 2)
    mine = lax.dynamic_slice_in_dim(features, core * half, half)
    away = lax.dynamic_slice_in_dim(features, (1 - core) * half, half)
    sources, wanted = [mine], [(0, 0)]
    up, down = [mine, away], [mine, away]
    (table,) = call(
        table_kernel, "table", [((tile_cols.size + rows * CAP,), jnp.int32)], [SMEM], [SMEM],
        [pltpu.SMEM((rows,), jnp.int32)], 4, 0, 8 * rows * CAP, tile_cols,
    )
    packed = 2 * span + 2 * every + 128
    packs = call(
        bind(pack_kernel, feats), "pack", [((hid, packed), narrow)] * feats, [HBM] * 4 + [VMEM],
        [HBM] * feats,
        [pltpu.VMEM((hid, 128), narrow), pltpu.SemaphoreType.DMA((5 * feats,))], WHOLE, 0,
        4 * hid * packed * feats,
        features, grad_output, self_weight, neigh_weight, bias_vector.reshape(1, hid),
    )
    for step in range(1, top + 1):
        if step == 2:
            pair = swap(after(adjacency, up[0], down[0]), rows)
        if step == top - 1:
            up[0], pair, table, packs = lax.optimization_barrier((up[0], pair, table, packs))
            table_pair = swap(table, rows)
            packs = exchange(packs, feats)
        if step == top:
            sources.append(swap(after(away, up[0], down[0]), rows))
            wanted.append((0, 1))
        for side in range(2):
            flip = side if step == 1 else 0
            forward, backward = ring_pairs(rows, 1, flip), ring_pairs(rows, -1, flip)
            if step < top or side == 0:
                up[side] = lax.ppermute(up[side], "rows", forward)
                sources.append(up[side])
                wanted.append((-step, side))
            if step < top or side == 1:
                down[side] = lax.ppermute(down[side], "rows", backward)
                sources.append(down[side])
                wanted.append((step, side))

    turned, ws_all, wn_all, bias_all, x_all, cot_all = call(
        bind(unpack_kernel, feats), "unpack",
        [((every, 2 * every), narrow), ((every, every), narrow), ((every, every), narrow),
         ((every, 1), wide), ((every, span), narrow), ((every, span), narrow)],
        [VMEM] * feats, [VMEM] * 6, [pltpu.VMEM((2 * every, every), wide)], 8, 0,
        4 * every * packed, *packs,
    )

    count = len(sources)

    def aggregate(parts):
        n = len(parts)
        outs = call(
            bind(aggregate_kernel, (feats, parts, tuple(wanted), rows)), "aggregate",
            [((half, span), narrow)] * (2 * n) + [((n, 1, span), wide)],
            [SMEM] * 2 + [HBM] * (2 + count), [VMEM] * (2 * n + 1),
            [
                pltpu.VMEM((rows, half, width), narrow),
                pltpu.VMEM((n, blocks // feats, 2, per_block, tile, tile), narrow),
                pltpu.SemaphoreType.DMA((count,)),
                pltpu.SemaphoreType.DMA((n, blocks // feats, 2)),
            ],
            WHOLE, 2 * hid * adjacency.size, 2 * adjacency.size + rows * hid * width,
            table, table_pair, adjacency, pair, *sources,
        )
        return outs[:n], outs[n : 2 * n], outs[2 * n]

    def send(value, k, flip):
        pairs = [
            (r * feats + i, (r ^ flip) * feats + (i + k) % feats)
            for r in range(rows)
            for i in range(feats)
        ]
        return lax.ppermute(value, ("rows", "feat"), pairs)

    there, there_far, unused_inverse = aggregate(tuple(range(1, feats)))
    near = [send(there[k - 1], k, 0) for k in range(1, feats)]
    far = [send(there_far[k - 1], k, 1) for k in range(1, feats)]
    here, here_far, inverse = aggregate((0,))
    near, far = [here[0]] + near, [send(here_far[0], 0, 1)] + far

    outs = call(
        bind(middle_kernel, (feats, hid, span, min(span, 256))), "middle",
        [((hid, span), narrow)] * (2 * feats) + [((every, span), narrow)] * 2,
        [VMEM] * (6 + 2 * feats), [VMEM] * (2 * feats + 2), [], 12,
        6 * every * every * span, 14 * every * span,
        turned, wn_all, bias_all, inverse, x_all, cot_all, *near, *far,
    )
    scaled, acts, grad, agg = outs[:feats], outs[feats : 2 * feats], outs[-2], outs[-1]
    scaled = exchange(scaled, feats)
    scaled_pair = [swap(piece, rows) for piece in scaled]

    outs = call(
        bind(weights_kernel, feats), "weights",
        [((hid, span), wide)] + [((hid, 3 * span), narrow)] * (feats - 1)
        + [((4, hid + 8, every // 2), wide)] * feats,
        [VMEM] * (4 + feats), [VMEM] * (2 * feats), [], 12,
        6 * every * every * span, 10 * every * span,
        ws_all, x_all, agg, grad, *acts,
    )
    parcels, grads = outs[:feats], outs[feats:]

    (held,) = call(
        bind(arrange_kernel, feats, tile), "arrange", [((2, blocks + 1, hid, tile), narrow)],
        [VMEM] * (2 * feats), [VMEM], [], 8, 0, 8 * hid * width, *scaled, *scaled_pair,
    )

    def spread(offsets, kinds):
        n = 2 * CAP * len(offsets)
        return call(
            bind(spread_kernel, (rows, offsets, kinds)), "spread",
            [((half, width), kind) for kind in kinds],
            [SMEM] * 2 + [HBM] * 2 + [VMEM], [VMEM] * len(kinds),
            [
                pltpu.VMEM((hid, width), wide),
                pltpu.VMEM((n, tile, tile), narrow),
                pltpu.SemaphoreType.DMA((n,)),
            ],
            12, 2 * n * hid * tile * tile, 8 * hid * width * len(offsets),
            table, table_pair, adjacency, pair, held,
        )

    up, down = [None, None], [None, None]

    def joined(arrived, mine):
        if arrived is None:
            return mine
        return (arrived.astype(jnp.float32) + mine).astype(jnp.bfloat16)

    for level in range(top, 0, -1):
        if level == top:
            low, high = spread((top,), (narrow, narrow))
            grads, low = lax.optimization_barrier((grads, low))
            up[0] = lax.ppermute(low, "rows", forward)
            down[1] = lax.ppermute(high, "rows", backward)
            continue
        kinds = tuple(narrow if arrived is None else wide for arrived in up + down)
        offsets = (level, -level)
        if level == 1:
            offsets, kinds = (1, -1, 0), kinds + (wide, wide)
        mine = spread(offsets, kinds)
        up = [lax.ppermute(joined(up[i], mine[i]), "rows", forward) for i in range(2)]
        down = [lax.ppermute(joined(down[i], mine[2 + i]), "rows", backward) for i in range(2)]

    grads = exchange(grads, feats)
    grads = sum(grads[1:], grads[0])
    grads = grads[:2] + swap(grads[2:], rows, 1)
    grads = grads[0] + swap(grads[1], rows, 2)
    bit = 4
    while bit < rows:
        grads = grads + swap(grads, rows, bit)
        bit *= 2
    near = jnp.stack([grads, swap(grads, rows, 2)])
    far = swap(near, rows, 1)
    far, parcels = lax.optimization_barrier((far, parcels))
    parcels = exchange(parcels, feats)
    grad_self, grad_neigh, sums = call(
        collect_kernel, "collect",
        [((hid, every), wide), ((hid, every), wide), ((8, every), wide)],
        [VMEM] * 2, [VMEM] * 3, [], 8, 0, 16 * hid * every, near, far,
    )
    grad_bias = lax.dynamic_slice_in_dim(sums[0], lax.axis_index("feat") * hid, hid)
    (activation,) = call(
        bind(place_kernel, feats), "place", [((hid, width), narrow)], [VMEM] * feats, [VMEM], [], 8,
        0, 4 * hid * width, acts[0], *parcels[1:],
    )
    (grad_features,) = call(
        bind(finish_kernel, feats), "finish", [((hid, width), narrow)], [VMEM] * (6 + feats),
        [VMEM], [], 8, 0, 8 * hid * width,
        mine[4], mine[5], up[0], down[0], up[1], down[1], *parcels,
    )
    return (activation, grad_features, grad_self, grad_neigh, grad_bias)


def solution(mesh):
    in_specs = (
        P("feat", "rows"),
        P("rows", None, None, None),
        P("rows", None),
        P("feat", None),
        P("feat", None),
        P("feat"),
        P("feat", "rows"),
    )
    out_specs = (P("feat", "rows"), P("feat", "rows"), P("feat", None), P("feat", None), P("feat"))
    body = functools.partial(shards, mesh.shape["rows"], mesh.shape["feat"])
    return jax.shard_map(body, mesh=mesh, in_specs=in_specs, out_specs=out_specs, check_vma=False)
```

time: 196 us -> 212 us (1.082)
  Pallas kernels: 23.1 us -> 88.1 us
  waiting for transfers between devices: 98.2 us -> 63 us
  local copies, waits for them, and re-layouts: 19.4 us -> 9 us
  starting transfers between devices: 50.5 us -> 46.5 us
    pallas_call x15, Pallas kernels: 23.1 us -> 88.1 us  [call(): pl.pallas_call(kernel, out_shape=[jax.ShapeDtypeStruct(shape, kind) for s...]
    ppermute x6, waiting for transfers between devices: 14.6 us -> 0.02 us  [shards(): lax.ppermute(joined(down[i], mine[2 + i]), 'rows', backward)]
    ppermute x6, waiting for transfers between devices: 17.5 us -> 5.17 us  [shards(): lax.ppermute(joined(up[i], mine[i]), 'rows', forward)]
    unnamed x32 -> x52, local copies, waits for them, and re-layouts: 17.8 us -> 7.39 us
    ppermute x7, starting transfers between devices: 12.3 us -> 3.23 us  [shards(): down[side] = lax.ppermute(down[side], 'rows', backward)]
    ppermute x6 -> x4, waiting for transfers between devices: 21.8 us -> 15.1 us  [exchange(): lax.ppermute(pieces[k], 'feat', [(i, (i + k) % feats) for i in range(feat...]
    ppermute x7, waiting for transfers between devices: 26.9 us -> 21.2 us  [shards(): down[side] = lax.ppermute(down[side], 'rows', backward)]
    ppermute x25 -> x11, waiting for transfers between devices: 10.3 us -> 14.1 us  [swap(): return lax.ppermute(value, 'rows', [(r, r ^ bit) for r in range(rows)])]
  transfers between devices with their start and end apart: 59 -> 46, of which waited for: 29 -> 16; matrix products, arithmetic and copies ran while one was open for 3% -> 2% of each run, Pallas kernels for 11% -> 39%
where the time goes in v3:
time: 212 us; the launch traced here: 211 us
  Pallas kernels  88.1 us (42%)
  waiting for transfers between devices  63 us (30%)
  starting transfers between devices  46.5 us (22%)
  local copies, waits for them, and re-layouts  9 us (4%)
  other arithmetic  3.43 us (2%)
    pallas_call x15, Pallas kernels, call(): pl.pallas_call(kernel, out_shape=[jax.ShapeDtypeStruct(shape, kind) for s...  88.1 us
    ppermute x7, waiting for transfers between devices, shards(): down[side] = lax.ppermute(down[side], 'rows', backward)  21.2 us
    ppermute x4, waiting for transfers between devices, exchange(): lax.ppermute(pieces[k], 'feat', [(i, (i + k) % feats) for i in range(feat...  15.1 us
    ppermute x11, waiting for transfers between devices, swap(): return lax.ppermute(value, 'rows', [(r, r ^ bit) for r in range(rows)])  14.1 us
    ppermute x7, starting transfers between devices, shards(): up[side] = lax.ppermute(up[side], 'rows', forward)  11.8 us
    ppermute x6, starting transfers between devices, shards(): lax.ppermute(joined(up[i], mine[i]), 'rows', forward)  9.28 us
    unnamed x52, local copies, waits for them, and re-layouts  7.39 us
    ppermute x6, starting transfers between devices, shards(): lax.ppermute(joined(down[i], mine[2 + i]), 'rows', backward)  6.94 us
  transfers between devices with their start and end apart: 46, of which 16 were waited for; matrix products, arithmetic and copies ran while one was open for 2% of the time, Pallas kernels for 39%

profile of v3, /device:TPU:0, one launch (start us, length us, event | category | flops | bytes accessed | tf_op | source)
XLA Modules:
  0.0 211.2 jit_solution(12776385468045646570)
XLA Ops:
  1.7 3.1 %collective-permute-start = (bf16[64,2048]{1,0:T(8,128)(2,1)S(1)}, bf16[64,2048]{1,0:T(8,128)(2,1)S(1)}, u32[]{:S(2)}, u32[]{:S(2)}) collective-permute-start(bf16[64,2048]{1,0:T(8,128)(2,1)S(1)} %get-tuple-element.116.refs_0_), channel_id=1, source_target_pairs={{0,8},{2,10},{8,16},{10,18},{16,24},{18,26},{24,28},{26,30},{28,20... | collective-permute-start | bytes 786440 | tf_op jit(solution)/shard_map/ppermute | solution.py:431
  4.8 6.2 %collective-permute-done.refs_1_ = bf16[64,2048]{1,0:T(8,128)(2,1)S(1)} collective-permute-done((bf16[64,2048]{1,0:T(8,128)(2,1)S(1)}, bf16[64,2048]{1,0:T(8,128)(2,1)S(1)}, u32[]{:S(2)}, u32[]{:S(2)}) %collective-permute-start) | collective-permute-done | bytes 262176 | tf_op jit(solution)/shard_map/ppermute | solution.py:431
  14.7 5.8 %collective-permute-done.7.refs_4_ = bf16[64,2048]{1,0:T(8,128)(2,1)S(1)} collective-permute-done((bf16[64,2048]{1,0:T(8,128)(2,1)S(1)}, bf16[64,2048]{1,0:T(8,128)(2,1)S(1)}, u32[]{:S(2)}, u32[]{:S(2)}) %collective-permute-start.7) | collective-permute-done | bytes 262176 | tf_op jit(solution)/shard_map/ppermute | solution.py:435
  24.9 3.2 %table.1 = s32[384]{0:T(512)S(1)} custom-call(s32[16,12]{1,0:T(8,128)S(1)} %copy-done.9), custom_call_target="tpu_custom_call" | custom-call | bytes 1536 | tf_op jit(solution)/shard_map/table/pallas_call | solution.py:378
  28.1 41.7 %pack.1 = (bf16[128,2688]{1,0:T(8,128)(2,1)}, bf16[128,2688]{1,0:T(8,128)(2,1)}) custom-call(bf16[128,2048]{1,0:T(8,128)(2,1)} %feature.1, bf16[128,2048]{1,0:T(8,128)(2,1)} %grad_output.1, bf16[128,256]{1,0:T(8,128)(2,1)} %ws.1, bf16[128,256]{1,0:T(8,128)(2,1)} %wn.1, f32[1,128]{1,0:T(1,128)} %bitcast.13), custom_call_target="tpu_custom_call" | custom-call | bytes 2752512 | tf_op jit(solution)/shard_map/pack/pallas_call | solution.py:378
  75.5 8.5 %collective-permute-done.14.refs_12_ = bf16[64,2048]{1,0:T(8,128)(2,1)S(1)} collective-permute-done((bf16[64,2048]{1,0:T(8,128)(2,1)S(1)}, bf16[64,2048]{1,0:T(8,128)(2,1)S(1)}, u32[]{:S(2)}, u32[]{:S(2)}) %collective-permute-start.14) | collective-permute-done | bytes 262176 | tf_op jit(solution)/shard_map/ppermute | solution.py:435
  86.3 5.4 %collective-permute-done.17.refs_15_ = bf16[64,2048]{1,0:T(8,128)(2,1)S(1)} collective-permute-done((bf16[64,2048]{1,0:T(8,128)(2,1)S(1)}, bf16[64,2048]{1,0:T(8,128)(2,1)S(1)}, u32[]{:S(2)}, u32[]{:S(2)}) %collective-permute-start.17) | collective-permute-done | bytes 262176 | tf_op jit(solution)/shard_map/ppermute | solution.py:435
  93.4 9.0 %aggregate.3 = (bf16[64,1024]{1,0:T(8,128)(2,1)}, bf16[64,1024]{1,0:T(8,128)(2,1)}, f32[1,1,1024]{2,1,0:T(1,128)}) custom-call(s32[384]{0:T(512)} %copy-done.5, s32[384]{0:T(512)} %copy-done.7, bf16[16,12,128,128]{3,2,1,0:T(8,128)(2,1)} %adj.11, bf16[16,12,128,128]{3,2,1,0:T(8,128)(2,1)} %collective-permute-done.3.pair, bf16[64,2048]{1,0:T(8,128)(2,1)} %copy-done.11, ...), custom_call_target="tpu_custom_call" | custom-call | flops 805306368 | bytes 10485760 | tf_op jit(solution)/shard_map/aggregate/pallas_call | solution.py:378
  104.1 9.2 %aggregate.2 = (bf16[64,1024]{1,0:T(8,128)(2,1)}, bf16[64,1024]{1,0:T(8,128)(2,1)}, f32[1,1,1024]{2,1,0:T(1,128)}) custom-call(s32[384]{0:T(512)} %copy-done.5, s32[384]{0:T(512)} %copy-done.7, bf16[16,12,128,128]{3,2,1,0:T(8,128)(2,1)} %adj.11, bf16[16,12,128,128]{3,2,1,0:T(8,128)(2,1)} %collective-permute-done.3.pair, bf16[64,2048]{1,0:T(8,128)(2,1)} %copy-done.11, ...), custom_call_target="tpu_custom_call" | custom-call | flops 805306368 | bytes 10485760 | tf_op jit(solution)/shard_map/aggregate/pallas_call | solution.py:378
  119.7 6.9 %collective-permute-done.21.refs_1_ = bf16[128,1024]{1,0:T(8,128)(2,1)S(1)} collective-permute-done((bf16[128,1024]{1,0:T(8,128)(2,1)S(1)}, bf16[128,1024]{1,0:T(8,128)(2,1)S(1)}, u32[]{:S(2)}, u32[]{:S(2)}) %collective-permute-start.21) | collective-permute-done | bytes 262176 | tf_op jit(solution)/shard_map/ppermute | solution.py:56
  128.4 2.8 %copy-done = bf16[16,12,128,128]{3,2,1,0:T(8,128)(2,1)S(1)} copy-done((bf16[16,12,128,128]{3,2,1,0:T(8,128)(2,1)S(1)}, bf16[16,12,128,128]{3,2,1,0:T(8,128)(2,1)}, u32[]{:S(2)}) %copy-start) | copy-done | bytes 6291480
  131.2 3.1 %spread.4 = (bf16[64,2048]{1,0:T(8,128)(2,1)S(1)}, bf16[64,2048]{1,0:T(8,128)(2,1)S(1)}) custom-call(s32[384]{0:T(512)S(1)} %copy-done.6, s32[384]{0:T(512)S(1)} %copy-done.8, bf16[16,12,128,128]{3,2,1,0:T(8,128)(2,1)S(1)} %copy-done, bf16[16,12,128,128]{3,2,1,0:T(8,128)(2,1)} %collective-permute-done.3.pair, bf16[2,17,128,128]{3,2,1,0:T(8,128)(2,1)S(1)} %arrange.1.held), custom_call_target="tpu_custom_call" | custom-call | flops 100663296 | bytes 2097152 | tf_op jit(solution)/shard_map/spread/pallas_call | solution.py:378
  135.0 1.9 weights.1
  138.5 4.3 %spread.6 = (f32[64,2048]{1,0:T(8,128)S(1)}, bf16[64,2048]{1,0:T(8,128)(2,1)S(1)}, bf16[64,2048]{1,0:T(8,128)(2,1)S(1)}, f32[64,2048]{1,0:T(8,128)S(1)}) custom-call(s32[384]{0:T(512)S(1)} %copy-done.6, s32[384]{0:T(512)S(1)} %copy-done.8, bf16[16,12,128,128]{3,2,1,0:T(8,128)(2,1)S(1)} %copy-done, bf16[16,12,128,128]{3,2,1,0:T(8,128)(2,1)} %collective-permute-done.3.pair, ...), custom_call_target="tpu_custom_call" | custom-call | flops 201326592 | bytes 4194304 | tf_op jit(solution)/shard_map/spread/pallas_call | solution.py:378
  146.2 4.3 %spread.7 = (f32[64,2048]{1,0:T(8,128)S(1)}, f32[64,2048]{1,0:T(8,128)S(1)}, f32[64,2048]{1,0:T(8,128)S(1)}, f32[64,2048]{1,0:T(8,128)S(1)}) custom-call(s32[384]{0:T(512)S(1)} %copy-done.6, s32[384]{0:T(512)S(1)} %copy-done.8, bf16[16,12,128,128]{3,2,1,0:T(8,128)(2,1)S(1)} %copy-done, bf16[16,12,128,128]{3,2,1,0:T(8,128)(2,1)} %collective-permute-done.3.pair, ...), custom_call_target="tpu_custom_call" | custom-call | flops 201326592 | bytes 4194304 | tf_op jit(solution)/shard_map/spread/pallas_call | solution.py:378
  150.5 6.0 %spread.5 = (f32[64,2048]{1,0:T(8,128)S(1)}, f32[64,2048]{1,0:T(8,128)S(1)}, f32[64,2048]{1,0:T(8,128)S(1)}, f32[64,2048]{1,0:T(8,128)S(1)}, f32[64,2048]{1,0:T(8,128)S(1)}, /*index=5*/f32[64,2048]{1,0:T(8,128)S(1)}) custom-call(s32[384]{0:T(512)S(1)} %copy-done.6, s32[384]{0:T(512)S(1)} %copy-done.8, bf16[16,12,128,128]{3,2,1,0:T(8,128)(2,1)S(1)} %copy-done, ...), custom_call_target="tpu_custom_call" | custom-call | flops 301989888 | bytes 6291456 | tf_op jit(solution)/shard_map/spread/pallas_call | solution.py:378
  163.0 5.9 %collective-permute-done.26 = f32[136,128]{1,0:T(8,128)S(1)} collective-permute-done((f32[136,128]{1,0:T(8,128)S(1)}, f32[136,128]{1,0:T(8,128)S(1)}, u32[]{:S(2)}, u32[]{:S(2)}) %collective-permute-start.26) | collective-permute-done | bytes 69664 | tf_op jit(solution)/shard_map/ppermute | solution.py:50
  169.1 2.5 %collective-permute-start.44 = (bf16[64,2048]{1,0:T(8,128)(2,1)S(1)}, bf16[64,2048]{1,0:T(8,128)(2,1)S(1)}, u32[]{:S(2)}, u32[]{:S(2)}) collective-permute-start(bf16[64,2048]{1,0:T(8,128)(2,1)S(1)} %add_convert_fusion.1), channel_id=1, source_target_pairs={{0,4},{2,6},{8,0},{10,2},{16,8},{18,10},{24,16},{26,18},{28,24},{3... | collective-permute-start | bytes 786440 | tf_op jit(solution)/shard_map/ppermute | solution.py:541
  171.6 2.5 %collective-permute-done.27 = f32[136,128]{1,0:T(8,128)S(1)} collective-permute-done((f32[136,128]{1,0:T(8,128)S(1)}, f32[136,128]{1,0:T(8,128)S(1)}, u32[]{:S(2)}, u32[]{:S(2)}) %collective-permute-start.27) | collective-permute-done | bytes 69664 | tf_op jit(solution)/shard_map/ppermute | solution.py:50
  174.1 3.8 %collective-permute-start.28 = (f32[136,128]{1,0:T(8,128)S(1)}, f32[136,128]{1,0:T(8,128)S(1)}, u32[]{:S(2)}, u32[]{:S(2)}) collective-permute-start(f32[136,128]{1,0:T(8,128)S(1)} %add.59), channel_id=1, source_target_pairs={{0,16},{2,18},{4,20},{6,22},{8,24},{10,26},{12,28},{14,30},{16,0},... | collective-permute-start | bytes 208904 | tf_op jit(solution)/shard_map/ppermute | solution.py:50
  180.1 2.1 collective-permute-done.28
  190.3 5.2 %collective-permute-done.34 = bf16[64,2048]{1,0:T(8,128)(2,1)S(1)} collective-permute-done((bf16[64,2048]{1,0:T(8,128)(2,1)S(1)}, bf16[64,2048]{1,0:T(8,128)(2,1)S(1)}, u32[]{:S(2)}, u32[]{:S(2)}) %collective-permute-start.34) | collective-permute-done | bytes 262176 | tf_op jit(solution)/shard_map/ppermute | solution.py:540
  200.2 8.2 %collective-permute-done.31.refs_1_ = bf16[128,3072]{1,0:T(8,128)(2,1)S(1)} collective-permute-done((bf16[128,3072]{1,0:T(8,128)(2,1)}, bf16[128,3072]{1,0:T(8,128)(2,1)S(1)}, u32[]{:S(2)}, u32[]{:S(2)}) %collective-permute-start.31) | collective-permute-done | bytes 786464 | tf_op jit(solution)/shard_map/ppermute | solution.py:56
  209.2 2.0 finish.1
  (156 shorter events, 56.6 us)
Async XLA Ops:
  12.6 58.5 %collective-permute-start.3 = (bf16[16,12,128,128]{3,2,1,0:T(8,128)(2,1)}, bf16[16,12,128,128]{3,2,1,0:T(8,128)(2,1)}, u32[]{:S(2)}, u32[]{:S(2)}) collective-permute-start(bf16[16,12,128,128]{3,2,1,0:T(8,128)(2,1)} %adj.11), channel_id=1, source_target_pairs={{0,2},{2,0},{4,6},{6,4},{8,10},{10,8},{12,14},{14,12},{16,18},{18,... | collective-permute-start | bytes 18874376 | tf_op jit(solution)/shard_map/ppermute | solution.py:50
  14.3 55.4 %collective-permute-start.8 = (bf16[64,2048]{1,0:T(8,128)(2,1)S(1)}, bf16[64,2048]{1,0:T(8,128)(2,1)S(1)}, u32[]{:S(2)}, u32[]{:S(2)}) collective-permute-start(bf16[64,2048]{1,0:T(8,128)(2,1)S(1)} %collective-permute-done.2.refs_2_), channel_id=1, source_target_pairs={{0,4},{2,6},{8,0},{10,2},{16,8},{18,10},{24,16},{26,18},{28,24},{3... | collective-permute-start | bytes 786440 | tf_op jit(solution)/shard_map/ppermute | solution.py:435
  20.5 49.7 %collective-permute-start.10 = (bf16[64,2048]{1,0:T(8,128)(2,1)S(1)}, bf16[64,2048]{1,0:T(8,128)(2,1)S(1)}, u32[]{:S(2)}, u32[]{:S(2)}) collective-permute-start(bf16[64,2048]{1,0:T(8,128)(2,1)S(1)} %collective-permute-done.7.refs_4_), channel_id=1, source_target_pairs={{0,4},{2,6},{8,0},{10,2},{16,8},{18,10},{24,16},{26,18},{28,24},{3... | collective-permute-start | bytes 786440 | tf_op jit(solution)/shard_map/ppermute | solution.py:435
  21.3 49.7 %collective-permute-start.1 = (bf16[64,2048]{1,0:T(8,128)(2,1)S(1)}, bf16[64,2048]{1,0:T(8,128)(2,1)S(1)}, u32[]{:S(2)}, u32[]{:S(2)}) collective-permute-start(bf16[64,2048]{1,0:T(8,128)(2,1)S(1)} %collective-permute-done.refs_1_), channel_id=1, source_target_pairs={{0,8},{2,10},{8,16},{10,18},{16,24},{18,26},{24,28},{26,30},{28,20... | collective-permute-start | bytes 786440 | tf_op jit(solution)/shard_map/ppermute | solution.py:431
  22.6 51.3 %collective-permute-start.9 = (bf16[64,2048]{1,0:T(8,128)(2,1)S(1)}, bf16[64,2048]{1,0:T(8,128)(2,1)S(1)}, u32[]{:S(2)}, u32[]{:S(2)}) collective-permute-start(bf16[64,2048]{1,0:T(8,128)(2,1)S(1)} %collective-permute-done.6.refs_3_), channel_id=1, source_target_pairs={{0,8},{2,10},{8,16},{10,18},{16,24},{18,26},{24,28},{26,30},{28,20... | collective-permute-start | bytes 786440 | tf_op jit(solution)/shard_map/ppermute | solution.py:431
  69.8 14.6 %collective-permute-start.12 = (bf16[64,2048]{1,0:T(8,128)(2,1)S(1)}, bf16[64,2048]{1,0:T(8,128)(2,1)S(1)}, u32[]{:S(2)}, u32[]{:S(2)}) collective-permute-start(bf16[64,2048]{1,0:T(8,128)(2,1)S(1)} %collective-permute-done.8.refs_6_), channel_id=1, source_target_pairs={{0,4},{2,6},{8,0},{10,2},{16,8},{18,10},{24,16},{26,18},{28,24},{3... | collective-permute-start | bytes 786440 | tf_op jit(solution)/shard_map/ppermute | solution.py:435
  70.3 13.7 %collective-permute-start.14 = (bf16[64,2048]{1,0:T(8,128)(2,1)S(1)}, bf16[64,2048]{1,0:T(8,128)(2,1)S(1)}, u32[]{:S(2)}, u32[]{:S(2)}) collective-permute-start(bf16[64,2048]{1,0:T(8,128)(2,1)S(1)} %collective-permute-done.10.refs_8_), channel_id=1, source_target_pairs={{0,4},{2,6},{8,0},{10,2},{16,8},{18,10},{24,16},{26,18},{28,24},{3... | collective-permute-start | bytes 786440 | tf_op jit(solution)/shard_map/ppermute | solution.py:435
  71.0 13.3 %collective-permute-start.11 = (bf16[64,2048]{1,0:T(8,128)(2,1)S(1)}, bf16[64,2048]{1,0:T(8,128)(2,1)S(1)}, u32[]{:S(2)}, u32[]{:S(2)}) collective-permute-start(bf16[64,2048]{1,0:T(8,128)(2,1)S(1)} %collective-permute-done.1.refs_5_), channel_id=1, source_target_pairs={{0,8},{2,10},{8,16},{10,18},{16,24},{18,26},{24,28},{26,30},{28,20... | collective-permute-start | bytes 786440 | tf_op jit(solution)/shard_map/ppermute | solution.py:431
  72.4 41.4 %collective-permute-start.4 = (bf16[128,2688]{1,0:T(8,128)(2,1)}, bf16[128,2688]{1,0:T(8,128)(2,1)S(1)}, u32[]{:S(2)}, u32[]{:S(2)}) collective-permute-start(bf16[128,2688]{1,0:T(8,128)(2,1)} %get-tuple-element.64), channel_id=1, source_target_pairs={{0,1},{1,0},{2,3},{3,2},{4,5},{5,4},{6,7},{7,6},{8,9},{9,8},{10,11... | collective-permute-start | bytes 2064392 | tf_op jit(solution)/shard_map/ppermute | solution.py:56
  134.3 22.2 %collective-permute-start.42 = (bf16[64,2048]{1,0:T(8,128)(2,1)S(1)}, bf16[64,2048]{1,0:T(8,128)(2,1)S(1)}, u32[]{:S(2)}, u32[]{:S(2)}) collective-permute-start(bf16[64,2048]{1,0:T(8,128)(2,1)S(1)} %get-tuple-element.106), channel_id=1, source_target_pairs={{0,4},{2,6},{8,0},{10,2},{16,8},{18,10},{24,16},{26,18},{28,24},{3... | collective-permute-start | bytes 786440 | tf_op jit(solution)/shard_map/ppermute | solution.py:533
  136.9 21.8 %collective-permute-start.24 = (f32[4,136,128]{2,1,0:T(8,128)S(1)}, f32[4,136,128]{2,1,0:T(8,128)S(1)}, u32[]{:S(2)}, u32[]{:S(2)}) collective-permute-start(f32[4,136,128]{2,1,0:T(8,128)S(1)} %get-tuple-element.90), channel_id=1, source_target_pairs={{0,1},{1,0},{2,3},{3,2},{4,5},{5,4},{6,7},{7,6},{8,9},{9,8},{10,11... | collective-permute-start | bytes 835592 | tf_op jit(solution)/shard_map/ppermute | solution.py:56
  142.8 14.5 %collective-permute-start.39 = (bf16[64,2048]{1,0:T(8,128)(2,1)S(1)}, bf16[64,2048]{1,0:T(8,128)(2,1)S(1)}, u32[]{:S(2)}, u32[]{:S(2)}) collective-permute-start(bf16[64,2048]{1,0:T(8,128)(2,1)S(1)} %get-tuple-element.103), channel_id=1, source_target_pairs={{0,8},{2,10},{8,16},{10,18},{16,24},{18,26},{24,28},{26,30},{28,20... | collective-permute-start | bytes 786440 | tf_op jit(solution)/shard_map/ppermute | solution.py:540
  144.2 14.7 %collective-permute-start.36 = (bf16[64,2048]{1,0:T(8,128)(2,1)S(1)}, bf16[64,2048]{1,0:T(8,128)(2,1)S(1)}, u32[]{:S(2)}, u32[]{:S(2)}) collective-permute-start(bf16[64,2048]{1,0:T(8,128)(2,1)S(1)} %get-tuple-element.100), channel_id=1, source_target_pairs={{0,4},{2,6},{8,0},{10,2},{16,8},{18,10},{24,16},{26,18},{28,24},{3... | collective-permute-start | bytes 786440 | tf_op jit(solution)/shard_map/ppermute | solution.py:541
  144.9 16.4 %collective-permute-start.32 = (bf16[64,2048]{1,0:T(8,128)(2,1)S(1)}, bf16[64,2048]{1,0:T(8,128)(2,1)S(1)}, u32[]{:S(2)}, u32[]{:S(2)}) collective-permute-start(bf16[64,2048]{1,0:T(8,128)(2,1)S(1)} %get-tuple-element.96), channel_id=1, source_target_pairs={{0,8},{2,10},{8,16},{10,18},{16,24},{18,26},{24,28},{26,30},{28,20... | collective-permute-start | bytes 786440 | tf_op jit(solution)/shard_map/ppermute | solution.py:532
  156.5 12.4 %collective-permute-start.43 = (bf16[64,2048]{1,0:T(8,128)(2,1)S(1)}, bf16[64,2048]{1,0:T(8,128)(2,1)S(1)}, u32[]{:S(2)}, u32[]{:S(2)}) collective-permute-start(bf16[64,2048]{1,0:T(8,128)(2,1)S(1)} %add_convert_fusion.2), channel_id=1, source_target_pairs={{0,4},{2,6},{8,0},{10,2},{16,8},{18,10},{24,16},{26,18},{28,24},{3... | collective-permute-start | bytes 786440 | tf_op jit(solution)/shard_map/ppermute | solution.py:541
  157.4 20.6 %collective-permute-start.40 = (bf16[64,2048]{1,0:T(8,128)(2,1)S(1)}, bf16[64,2048]{1,0:T(8,128)(2,1)S(1)}, u32[]{:S(2)}, u32[]{:S(2)}) collective-permute-start(bf16[64,2048]{1,0:T(8,128)(2,1)S(1)} %add_convert_fusion.4), channel_id=1, source_target_pairs={{0,8},{2,10},{8,16},{10,18},{16,24},{18,26},{24,28},{26,30},{28,20... | collective-permute-start | bytes 786440 | tf_op jit(solution)/shard_map/ppermute | solution.py:540
  158.9 23.7 %collective-permute-start.37 = (bf16[64,2048]{1,0:T(8,128)(2,1)S(1)}, bf16[64,2048]{1,0:T(8,128)(2,1)S(1)}, u32[]{:S(2)}, u32[]{:S(2)}) collective-permute-start(bf16[64,2048]{1,0:T(8,128)(2,1)S(1)} %add_convert_fusion.6), channel_id=1, source_target_pairs={{0,4},{2,6},{8,0},{10,2},{16,8},{18,10},{24,16},{26,18},{28,24},{3... | collective-permute-start | bytes 786440 | tf_op jit(solution)/shard_map/ppermute | solution.py:541
  161.4 25.3 %collective-permute-start.33 = (bf16[64,2048]{1,0:T(8,128)(2,1)S(1)}, bf16[64,2048]{1,0:T(8,128)(2,1)S(1)}, u32[]{:S(2)}, u32[]{:S(2)}) collective-permute-start(bf16[64,2048]{1,0:T(8,128)(2,1)S(1)} %add_convert_fusion.9), channel_id=1, source_target_pairs={{0,8},{2,10},{8,16},{10,18},{16,24},{18,26},{24,28},{26,30},{28,20... | collective-permute-start | bytes 786440 | tf_op jit(solution)/shard_map/ppermute | solution.py:540
  169.1 20.0 %collective-permute-start.44 = (bf16[64,2048]{1,0:T(8,128)(2,1)S(1)}, bf16[64,2048]{1,0:T(8,128)(2,1)S(1)}, u32[]{:S(2)}, u32[]{:S(2)}) collective-permute-start(bf16[64,2048]{1,0:T(8,128)(2,1)S(1)} %add_convert_fusion.1), channel_id=1, source_target_pairs={{0,4},{2,6},{8,0},{10,2},{16,8},{18,10},{24,16},{26,18},{28,24},{3... | collective-permute-start | bytes 786440 | tf_op jit(solution)/shard_map/ppermute | solution.py:541
  178.7 30.5 %collective-permute-start.41 = (bf16[64,2048]{1,0:T(8,128)(2,1)}, bf16[64,2048]{1,0:T(8,128)(2,1)S(1)}, u32[]{:S(2)}, u32[]{:S(2)}) collective-permute-start(bf16[64,2048]{1,0:T(8,128)(2,1)} %add_convert_fusion.3), channel_id=1, source_target_pairs={{0,8},{2,10},{8,16},{10,18},{16,24},{18,26},{24,28},{26,30},{28,20... | collective-permute-start | bytes 786440 | tf_op jit(solution)/shard_map/ppermute | solution.py:540
  183.4 25.8 %collective-permute-start.38 = (bf16[64,2048]{1,0:T(8,128)(2,1)}, bf16[64,2048]{1,0:T(8,128)(2,1)S(1)}, u32[]{:S(2)}, u32[]{:S(2)}) collective-permute-start(bf16[64,2048]{1,0:T(8,128)(2,1)} %add_convert_fusion.5), channel_id=1, source_target_pairs={{0,4},{2,6},{8,0},{10,2},{16,8},{18,10},{24,16},{26,18},{28,24},{3... | collective-permute-start | bytes 786440 | tf_op jit(solution)/shard_map/ppermute | solution.py:541
  188.5 19.9 %collective-permute-start.31 = (bf16[128,3072]{1,0:T(8,128)(2,1)}, bf16[128,3072]{1,0:T(8,128)(2,1)S(1)}, u32[]{:S(2)}, u32[]{:S(2)}) collective-permute-start(bf16[128,3072]{1,0:T(8,128)(2,1)} %get-tuple-element.93), channel_id=1, source_target_pairs={{0,1},{1,0},{2,3},{3,2},{4,5},{5,4},{6,7},{7,6},{8,9},{9,8},{10,11... | collective-permute-start | bytes 2359304 | tf_op jit(solution)/shard_map/ppermute | solution.py:56
  189.8 19.4 %collective-permute-start.45 = (bf16[64,2048]{1,0:T(8,128)(2,1)}, bf16[64,2048]{1,0:T(8,128)(2,1)S(1)}, u32[]{:S(2)}, u32[]{:S(2)}) collective-permute-start(bf16[64,2048]{1,0:T(8,128)(2,1)} %add_convert_fusion), channel_id=1, source_target_pairs={{0,4},{2,6},{8,0},{10,2},{16,8},{18,10},{24,16},{26,18},{28,24},{3... | collective-permute-start | bytes 786440 | tf_op jit(solution)/shard_map/ppermute | solution.py:541
  196.2 13.0 %collective-permute-start.35 = (bf16[64,2048]{1,0:T(8,128)(2,1)}, bf16[64,2048]{1,0:T(8,128)(2,1)}, u32[]{:S(2)}, u32[]{:S(2)}) collective-permute-start(bf16[64,2048]{1,0:T(8,128)(2,1)} %add_convert_fusion.7), channel_id=1, source_target_pairs={{0,8},{2,10},{8,16},{10,18},{16,24},{18,26},{24,28},{26,30},{28,20... | collective-permute-start | bytes 786440 | tf_op jit(solution)/shard_map/ppermute | solution.py:540
  (48 other events, 814.7 us)

commit v4 on v3

--- a/solution.py
+++ b/solution.py
@@ -9,7 +9,6 @@
 
 CAP = 12
 MIB = 1024 * 1024
-WHOLE = 60
 HBM = pl.BlockSpec(memory_space=pltpu.HBM)
 VMEM = pl.BlockSpec(memory_space=pltpu.VMEM)
 SMEM = pl.BlockSpec(memory_space=pltpu.SMEM)
@@ -145,6 +144,12 @@
     lax.fori_loop(0, blocks, step, 0)
 
 
+def load_kernel(source, out, sem):
+    copy = pltpu.make_async_copy(source, out, sem)
+    copy.start()
+    copy.wait()
+
+
 def aggregate_kernel(plan, table, table_pair, adj, pair, *refs):
     feats, parts, wanted, rows = plan
     count, taken = len(wanted), len(parts)
@@ -152,7 +157,7 @@
     part = blocks // feats
     half = refs[0].shape[0]
     sources, refs = refs[:count], refs[count:]
-    near, far, inverse, (held, tiles, sems, tile_sems) = (
+    near, far, inverse, (held, sems) = (
         refs[:taken],
         refs[taken : 2 * taken],
         refs[2 * taken],
@@ -166,20 +171,8 @@
             place = place + 1 - 2 * lax.rem(place, 2)
         copies.append(pltpu.make_async_copy(sources[n], held.at[place], sems.at[n]))
 
-    def fetch(slot, local, side):
-        where = lax.rem(lax.axis_index("feat") + parts[slot], feats)
-        return pltpu.make_async_copy(
-            (adj, pair)[side].at[where * part + local],
-            tiles.at[slot, local, side],
-            tile_sems.at[slot, local, side],
-        )
-
     for copy in copies:
         copy.start()
-    for slot in range(taken):
-        for local in range(part):
-            for side in range(2):
-                fetch(slot, local, side).start()
     for copy in copies:
         copy.wait()
     ones = jnp.ones((16, 2 * tile), jnp.bfloat16)
@@ -189,9 +182,8 @@
         def step(local, carry):
             lane = pl.ds(pl.multiple_of(local * tile, tile), tile)
             for side in range(2):
-                fetch(slot, local, side).wait()
-            for side in range(2):
-                first = (where * part + local) * per_block
+                block = where * part + local
+                first = block * per_block
                 total = None
                 for t in range(0, per_block, 2):
                     left, right = [], []
@@ -200,7 +192,7 @@
                         source = col // blocks
                         at = pl.multiple_of((col - source * blocks) * tile, tile)
                         left.append(held[source, :, pl.ds(at, tile)])
-                        right.append(tiles[slot, local, side, u])
+                        right.append((adj, pair)[side][block, u])
                     term = product(
                         jnp.concatenate([jnp.concatenate(left, axis=1), ones], axis=0),
                         jnp.concatenate(right, axis=1),
@@ -214,7 +206,7 @@
                     inverse[slot, :, lane] = factor
             return carry
 
-        lax.fori_loop(0, part, step, 0)
+        lax.fori_loop(0, part, step, 0, unroll=2 if part % 2 == 0 else 1)
 
 
 def middle_kernel(plan, turned, wn, bias, inverse, x_all, cot, *refs):
@@ -312,58 +304,57 @@
 
 def spread_kernel(plan, table, table_pair, adj, pair, held, *refs):
     rows, offsets, kinds = plan
-    results, (total, tiles, sems) = refs[: len(kinds)], refs[len(kinds) :]
+    results, total = refs[:-1], refs[-1]
     blocks, per_block, tile, unused = adj.shape
     half = total.shape[0] // 2
     row = lax.axis_index("rows")
     firsts = [blocks * per_block + ring_row(row, offset, rows) * CAP for offset in offsets]
-    sides = ((table, adj), (table_pair, pair))
-    copies = []
-    for d in range(len(offsets)):
-        for side, (slots, source) in enumerate(sides):
-            for s in range(CAP):
-                index = jnp.maximum(slots[firsts[d] + s], 0) // 256
-                block = index // per_block
-                n = (2 * d + side) * CAP + s
-                tiled = source.at[block, index - block * per_block]
-                copies.append(pltpu.make_async_copy(tiled, tiles.at[n], sems.at[n]))
-                copies[-1].start()
     for d in range(len(offsets)):
         total[...] = jnp.zeros_like(total)
-        for copy in copies[2 * d * CAP : 2 * (d + 1) * CAP]:
-            copy.wait()
-        for side, (slots, source) in enumerate(sides):
+        for side, (slots, tiles) in enumerate(((table, adj), (table_pair, pair))):
             for s0 in range(0, CAP, 4):
                 terms = []
                 for s in range(s0, s0 + 4):
                     entry = slots[firsts[d] + s]
                     index = jnp.maximum(entry, 0) // 256
-                    place = jnp.where(entry < 0, blocks, index // per_block)
+                    block = index // per_block
+                    place = jnp.where(entry < 0, blocks, block)
                     lane = lax.rem(jnp.maximum(entry, 0), 256) * tile
-                    term = product(held[side, place], tiles[(2 * d + side) * CAP + s])
+                    term = product(held[side, place], tiles[block, index - block * per_block])
                     terms.append((pl.multiple_of(lane, tile), term))
                 for lane, term in terms:
                     total[:, pl.ds(lane, tile)] += term
-        for part in range(2):
-            value = total[part * half : (part + 1) * half]
-            results[2 * d + part][...] = value.astype(kinds[2 * d + part])
-
-
-def finish_kernel(feats, base_low, base_high, a_low, b_low, a_high, b_high, *refs):
+        if len(kinds) == 2 * len(offsets):
+            for part in range(2):
+                value = total[part * half : (part + 1) * half]
+                results[2 * d + part][...] = value.astype(kinds[2 * d + part])
+        else:
+            results[d][...] = total[...]
+
+
+def join_kernel(name, arrived, mine, out):
+    half = mine.shape[0] // 2
+    if arrived.shape[0] == half:
+        lines = slice(0, half) if name == "low" else slice(half, 2 * half)
+        rest = slice(half, 2 * half) if name == "low" else slice(0, half)
+        out[rest] = mine[rest].astype(jnp.bfloat16)
+    else:
+        lines = slice(0, 2 * half)
+    out[lines] = (arrived[...].astype(jnp.float32) + mine[lines]).astype(jnp.bfloat16)
+
+
+def finish_kernel(feats, base, a, b, *refs):
     (own, *sent), out = refs[:feats], refs[feats]
-    half, span = a_low.shape[0], own.shape[1]
+    span = own.shape[1]
     for k in range(feats):
-        at = behind(k, feats, span)
-        nodes = pl.ds(at, span)
-        for part, (base, a, b) in enumerate(((base_low, a_low, b_low), (base_high, a_high, b_high))):
-            lines = slice(part * half, (part + 1) * half)
-            if k == 0:
-                value = own[lines]
-            else:
-                value = sent[k - 1][lines, span : 2 * span].astype(jnp.float32)
-                value = value + sent[k - 1][lines, 2 * span :].astype(jnp.float32)
-            value = value + base[:, nodes] + a[:, nodes].astype(jnp.float32)
-            out[lines, nodes] = (value + b[:, nodes].astype(jnp.float32)).astype(jnp.bfloat16)
+        nodes = pl.ds(behind(k, feats, span), span)
+        if k == 0:
+            value = own[...]
+        else:
+            value = sent[k - 1][:, span : 2 * span].astype(jnp.float32)
+            value = value + sent[k - 1][:, 2 * span :].astype(jnp.float32)
+        value = value + base[:, nodes] + a[:, nodes].astype(jnp.float32)
+        out[:, nodes] = (value + b[:, nodes].astype(jnp.float32)).astype(jnp.bfloat16)
 
 
 def place_kernel(feats, *refs):
@@ -409,13 +400,18 @@
     packed = 2 * span + 2 * every + 128
     packs = call(
         bind(pack_kernel, feats), "pack", [((hid, packed), narrow)] * feats, [HBM] * 4 + [VMEM],
-        [HBM] * feats,
-        [pltpu.VMEM((hid, 128), narrow), pltpu.SemaphoreType.DMA((5 * feats,))], WHOLE, 0,
+        [VMEM] * feats,
+        [pltpu.VMEM((hid, 128), narrow), pltpu.SemaphoreType.DMA((5 * feats,))], 6, 0,
         4 * hid * packed * feats,
         features, grad_output, self_weight, neigh_weight, bias_vector.reshape(1, hid),
     )
+    (tiles,) = call(
+        load_kernel, "load", [(adjacency.shape, narrow)], [HBM], [VMEM],
+        [pltpu.SemaphoreType.DMA], 4, 0, 4 * adjacency.size, adjacency,
+    )
     for step in range(1, top + 1):
         if step == 2:
+            down[1], tiles = lax.optimization_barrier((down[1], tiles))
             pair = swap(after(adjacency, up[0], down[0]), rows)
         if step == top - 1:
             up[0], pair, table, packs = lax.optimization_barrier((up[0], pair, table, packs))
@@ -451,15 +447,10 @@
         outs = call(
             bind(aggregate_kernel, (feats, parts, tuple(wanted), rows)), "aggregate",
             [((half, span), narrow)] * (2 * n) + [((n, 1, span), wide)],
-            [SMEM] * 2 + [HBM] * (2 + count), [VMEM] * (2 * n + 1),
-            [
-                pltpu.VMEM((rows, half, width), narrow),
-                pltpu.VMEM((n, blocks // feats, 2, per_block, tile, tile), narrow),
-                pltpu.SemaphoreType.DMA((count,)),
-                pltpu.SemaphoreType.DMA((n, blocks // feats, 2)),
-            ],
-            WHOLE, 2 * hid * adjacency.size, 2 * adjacency.size + rows * hid * width,
-            table, table_pair, adjacency, pair, *sources,
+            [SMEM] * 2 + [VMEM] * 2 + [HBM] * count, [VMEM] * (2 * n + 1),
+            [pltpu.VMEM((rows, half, width), narrow), pltpu.SemaphoreType.DMA((count,))],
+            12, 2 * hid * adjacency.size, 2 * adjacency.size + rows * hid * width,
+            table, table_pair, tiles, pair, *sources,
         )
         return outs[:n], outs[n : 2 * n], outs[2 * n]
 
@@ -503,44 +494,38 @@
         [VMEM] * (2 * feats), [VMEM], [], 8, 0, 8 * hid * width, *scaled, *scaled_pair,
     )
 
-    def spread(offsets, kinds):
+    def spread(offsets, halves=False):
         n = 2 * CAP * len(offsets)
+        outs = [((half, width), narrow)] * 2 if halves else [((hid, width), wide)] * len(offsets)
         return call(
-            bind(spread_kernel, (rows, offsets, kinds)), "spread",
-            [((half, width), kind) for kind in kinds],
-            [SMEM] * 2 + [HBM] * 2 + [VMEM], [VMEM] * len(kinds),
-            [
-                pltpu.VMEM((hid, width), wide),
-                pltpu.VMEM((n, tile, tile), narrow),
-                pltpu.SemaphoreType.DMA((n,)),
-            ],
-            12, 2 * n * hid * tile * tile, 8 * hid * width * len(offsets),
-            table, table_pair, adjacency, pair, held,
+            bind(spread_kernel, (rows, offsets, tuple(kind for shape, kind in outs))), "spread", outs,
+            [SMEM] * 2 + [VMEM] * 3, [VMEM] * len(outs), [pltpu.VMEM((hid, width), wide)],
+            8, 2 * n * hid * tile * tile, 8 * hid * width * len(offsets),
+            table, table_pair, tiles, pair, held,
         )
 
-    up, down = [None, None], [None, None]
-
-    def joined(arrived, mine):
-        if arrived is None:
-            return mine
-        return (arrived.astype(jnp.float32) + mine).astype(jnp.bfloat16)
-
-    for level in range(top, 0, -1):
-        if level == top:
-            low, high = spread((top,), (narrow, narrow))
-            grads, low = lax.optimization_barrier((grads, low))
-            up[0] = lax.ppermute(low, "rows", forward)
-            down[1] = lax.ppermute(high, "rows", backward)
-            continue
-        kinds = tuple(narrow if arrived is None else wide for arrived in up + down)
-        offsets = (level, -level)
-        if level == 1:
-            offsets, kinds = (1, -1, 0), kinds + (wide, wide)
-        mine = spread(offsets, kinds)
-        up = [lax.ppermute(joined(up[i], mine[i]), "rows", forward) for i in range(2)]
-        down = [lax.ppermute(joined(down[i], mine[2 + i]), "rows", backward) for i in range(2)]
+    forward, backward = ring_pairs(rows, 1), ring_pairs(rows, -1)
+    low, high = spread((top,), True)
+    grads, low = lax.optimization_barrier((grads, low))
+    up, down = lax.ppermute(low, "rows", forward), lax.ppermute(high, "rows", backward)
+    for level in range(top - 1, 0, -1):
+        offsets = (level, -level, 0) if level == 1 else (level, -level)
+        mine = spread(offsets)
+
+        def joined(name, arrived, value):
+            (out,) = call(
+                bind(join_kernel, name), "join", [((hid, width), narrow)], [VMEM] * 2, [VMEM], [], 8,
+                0, 8 * hid * width, arrived, value,
+            )
+            return out
+
+        up = lax.ppermute(joined("low", up, mine[0]), "rows", forward)
+        down = lax.ppermute(joined("high", down, mine[1]), "rows", backward)
 
     grads = exchange(grads, feats)
+    first, parcels = lax.optimization_barrier((grads[-1], parcels))
+    grads = grads[:-1] + [first]
+    parcels = exchange(parcels, feats)
     grads = sum(grads[1:], grads[0])
     grads = grads[:2] + swap(grads[2:], rows, 1)
     grads = grads[0] + swap(grads[1], rows, 2)
@@ -550,8 +535,6 @@
         bit *= 2
     near = jnp.stack([grads, swap(grads, rows, 2)])
     far = swap(near, rows, 1)
-    far, parcels = lax.optimization_barrier((far, parcels))
-    parcels = exchange(parcels, feats)
     grad_self, grad_neigh, sums = call(
         collect_kernel, "collect",
         [((hid, every), wide), ((hid, every), wide), ((8, every), wide)],
@@ -563,9 +546,8 @@
         0, 4 * hid * width, acts[0], *parcels[1:],
     )
     (grad_features,) = call(
-        bind(finish_kernel, feats), "finish", [((hid, width), narrow)], [VMEM] * (6 + feats),
-        [VMEM], [], 8, 0, 8 * hid * width,
-        mine[4], mine[5], up[0], down[0], up[1], down[1], *parcels,
+        bind(finish_kernel, feats), "finish", [((hid, width), narrow)], [VMEM] * (3 + feats),
+        [VMEM], [], 8, 0, 8 * hid * width, mine[2], up, down, *parcels,
     )
     return (activation, grad_features, grad_self, grad_neigh, grad_bias)
 

time: 212 us -> 151 us (0.71)
  Pallas kernels: 88.1 us -> 29.1 us
  waiting for transfers between devices: 63 us -> 75.2 us
  starting transfers between devices: 46.5 us -> 40.6 us
  local copies, waits for them, and re-layouts: 9 us -> 4.41 us
  other arithmetic: 3.43 us -> 0.09 us
    pallas_call x15 -> x22, Pallas kernels: 88.1 us -> 29.1 us  [call(): pl.pallas_call(kernel, out_shape=[jax.ShapeDtypeStruct(shape, kind) for s...]
    ppermute x11, waiting for transfers between devices: 14.1 us -> 24.2 us  [swap(): return lax.ppermute(value, 'rows', [(r, r ^ bit) for r in range(rows)])]
    ppermute x14 -> x8, starting transfers between devices: 18.2 us -> 8.54 us  [the longest x3 3.29 us: shards(): down = lax.ppermute(joined('high', down, mine[1]), 'rows', backward)]
    ppermute x4, waiting for transfers between devices: 15.1 us -> 6.92 us  [exchange(): lax.ppermute(pieces[k], 'feat', [(i, (i + k) % feats) for i in range(feat...]
    ppermute x14 -> x8, waiting for transfers between devices: 5.19 us -> 12.8 us  [the longest x3 9.44 us: shards(): down = lax.ppermute(joined('high', down, mine[1]), 'rows', backward)]
    unnamed x52 -> x14, local copies, waits for them, and re-layouts: 7.39 us -> 2.81 us
    convert_element_type x10 -> x0, other arithmetic: 3.34 us -> none  [joined(): return (arrived.astype(jnp.float32) + mine).astype(jnp.bfloat16)]
    ppermute x11, starting transfers between devices: 5.85 us -> 8.77 us  [swap(): return lax.ppermute(value, 'rows', [(r, r ^ bit) for r in range(rows)])]
  transfers between devices with their start and end apart: 46 -> 40, of which waited for: 16 -> 17; matrix products, arithmetic and copies ran while one was open for 2% -> 0% of each run, Pallas kernels for 39% -> 16%
where the time goes in v4:
time: 151 us; the launch traced here: 150 us
  waiting for transfers between devices  75.2 us (50%)
  starting transfers between devices  40.6 us (27%)
  Pallas kernels  29.1 us (19%)
  local copies, waits for them, and re-layouts  4.41 us (3%)
    pallas_call x22, Pallas kernels, call(): pl.pallas_call(kernel, out_shape=[jax.ShapeDtypeStruct(shape, kind) for s...  29.1 us
    ppermute x11, waiting for transfers between devices, swap(): return lax.ppermute(value, 'rows', [(r, r ^ bit) for r in range(rows)])  24.2 us
    ppermute x7, waiting for transfers between devices, shards(): down[side] = lax.ppermute(down[side], 'rows', backward)  22.6 us
    ppermute x7, starting transfers between devices, shards(): up[side] = lax.ppermute(up[side], 'rows', forward)  11.3 us
    ppermute x3, waiting for transfers between devices, shards(): down = lax.ppermute(joined('high', down, mine[1]), 'rows', backward)  9.44 us
    ppermute x11, starting transfers between devices, swap(): return lax.ppermute(value, 'rows', [(r, r ^ bit) for r in range(rows)])  8.77 us
    ppermute x7, waiting for transfers between devices, shards(): up[side] = lax.ppermute(up[side], 'rows', forward)  7.7 us
    ppermute x4, waiting for transfers between devices, exchange(): lax.ppermute(pieces[k], 'feat', [(i, (i + k) % feats) for i in range(feat...  6.92 us
  transfers between devices with their start and end apart: 40, of which 17 were waited for; matrix products, arithmetic and copies ran while one was open for 0% of the time, Pallas kernels for 16%

profile of v4, /device:TPU:0, one launch (start us, length us, event | category | flops | bytes accessed | tf_op | source)
XLA Modules:
  0.0 150.3 jit_solution(11840075541463351925)
XLA Ops:
  1.7 3.1 %collective-permute-start = (bf16[64,2048]{1,0:T(8,128)(2,1)S(1)}, bf16[64,2048]{1,0:T(8,128)(2,1)S(1)}, u32[]{:S(2)}, u32[]{:S(2)}) collective-permute-start(bf16[64,2048]{1,0:T(8,128)(2,1)S(1)} %get-tuple-element.106.refs_0_), channel_id=1, source_target_pairs={{0,8},{2,10},{8,16},{10,18},{16,24},{18,26},{24,28},{26,30},{28,20... | collective-permute-start | bytes 786440 | tf_op jit(solution)/shard_map/ppermute | solution.py:427
  4.8 6.2 %collective-permute-done.refs_1_ = bf16[64,2048]{1,0:T(8,128)(2,1)S(1)} collective-permute-done((bf16[64,2048]{1,0:T(8,128)(2,1)S(1)}, bf16[64,2048]{1,0:T(8,128)(2,1)S(1)}, u32[]{:S(2)}, u32[]{:S(2)}) %collective-permute-start) | collective-permute-done | bytes 262176 | tf_op jit(solution)/shard_map/ppermute | solution.py:427
  14.3 2.8 %copy-done = bf16[16,12,128,128]{3,2,1,0:T(8,128)(2,1)S(1)} copy-done((bf16[16,12,128,128]{3,2,1,0:T(8,128)(2,1)S(1)}, bf16[16,12,128,128]{3,2,1,0:T(8,128)(2,1)}, u32[]{:S(2)}) %copy-start) | copy-done | bytes 6291480
  17.6 3.0 %collective-permute-done.6.refs_4_ = bf16[64,2048]{1,0:T(8,128)(2,1)S(1)} collective-permute-done((bf16[64,2048]{1,0:T(8,128)(2,1)S(1)}, bf16[64,2048]{1,0:T(8,128)(2,1)S(1)}, u32[]{:S(2)}, u32[]{:S(2)}) %collective-permute-start.6) | collective-permute-done | bytes 262176 | tf_op jit(solution)/shard_map/ppermute | solution.py:431
  24.6 3.2 %table.1 = s32[384]{0:T(512)S(1)} custom-call(s32[16,12]{1,0:T(8,128)S(1)} %copy-done.5), custom_call_target="tpu_custom_call" | custom-call | bytes 1536 | tf_op jit(solution)/shard_map/table/pallas_call | solution.py:369
  30.2 5.1 %collective-permute-done.10.refs_8_ = bf16[64,2048]{1,0:T(8,128)(2,1)S(1)} collective-permute-done((bf16[64,2048]{1,0:T(8,128)(2,1)S(1)}, bf16[64,2048]{1,0:T(8,128)(2,1)S(1)}, u32[]{:S(2)}, u32[]{:S(2)}) %collective-permute-start.10) | collective-permute-done | bytes 262176 | tf_op jit(solution)/shard_map/ppermute | solution.py:431
  40.5 5.9 %collective-permute-done.14.refs_12_ = bf16[64,2048]{1,0:T(8,128)(2,1)S(1)} collective-permute-done((bf16[64,2048]{1,0:T(8,128)(2,1)S(1)}, bf16[64,2048]{1,0:T(8,128)(2,1)S(1)}, u32[]{:S(2)}, u32[]{:S(2)}) %collective-permute-start.14) | collective-permute-done | bytes 262176 | tf_op jit(solution)/shard_map/ppermute | solution.py:431
  48.9 5.5 %collective-permute-done.17.refs_15_ = bf16[64,2048]{1,0:T(8,128)(2,1)S(1)} collective-permute-done((bf16[64,2048]{1,0:T(8,128)(2,1)S(1)}, bf16[64,2048]{1,0:T(8,128)(2,1)S(1)}, u32[]{:S(2)}, u32[]{:S(2)}) %collective-permute-start.17) | collective-permute-done | bytes 262176 | tf_op jit(solution)/shard_map/ppermute | solution.py:431
  55.5 4.5 %aggregate.3 = (bf16[64,1024]{1,0:T(8,128)(2,1)S(1)}, bf16[64,1024]{1,0:T(8,128)(2,1)S(1)}, f32[1,1,1024]{2,1,0:T(1,128)}) custom-call(s32[384]{0:T(512)S(1)} %table.1, s32[384]{0:T(512)S(1)} %collective-permute-done.5.table_pair, bf16[16,12,128,128]{3,2,1,0:T(8,128)(2,1)S(1)} %load.1.adj, bf16[16,12,128,128]{3,2,1,0:T(8,128)(2,1)S(1)} %collective-permute-done.3.pair, ...), custom_call_target="tpu_custom_call" | custom-call | flops 805306368 | bytes 10485760 | tf_op jit(solution)/shard_map/aggregate/pallas_call | solution.py:369
  61.6 3.9 %aggregate.2 = (bf16[64,1024]{1,0:T(8,128)(2,1)S(1)}, bf16[64,1024]{1,0:T(8,128)(2,1)S(1)}, f32[1,1,1024]{2,1,0:T(1,128)S(1)}) custom-call(s32[384]{0:T(512)S(1)} %table.1, s32[384]{0:T(512)S(1)} %collective-permute-done.5.table_pair, bf16[16,12,128,128]{3,2,1,0:T(8,128)(2,1)S(1)} %load.1.adj, bf16[16,12,128,128]{3,2,1,0:T(8,128)(2,1)S(1)} %collective-permute-done.3.pair, ...), custom_call_target="tpu_custom_call" | custom-call | flops 805306368 | bytes 10485760 | tf_op jit(solution)/shard_map/aggregate/pallas_call | solution.py:369
  70.6 6.9 %collective-permute-done.21.refs_1_ = bf16[128,1024]{1,0:T(8,128)(2,1)S(1)} collective-permute-done((bf16[128,1024]{1,0:T(8,128)(2,1)S(1)}, bf16[128,1024]{1,0:T(8,128)(2,1)S(1)}, u32[]{:S(2)}, u32[]{:S(2)}) %collective-permute-start.21) | collective-permute-done | bytes 262176 | tf_op jit(solution)/shard_map/ppermute | solution.py:55
  77.5 1.9 %weights.1 = (f32[128,1024]{1,0:T(8,128)S(1)}, bf16[128,3072]{1,0:T(8,128)(2,1)}, f32[4,136,128]{2,1,0:T(8,128)S(1)}, f32[4,136,128]{2,1,0:T(8,128)S(1)}) custom-call(bf16[256,256]{1,0:T(8,128)(2,1)S(1)} %get-tuple-element.77.ws, bf16[256,1024]{1,0:T(8,128)(2,1)S(1)} %get-tuple-element.70.x_all, bf16[256,1024]{1,0:T(8,128)(2,1)S(1)} %get-tuple-element.78.agg, ...), custom_call_target="tpu_custom_call" | custom-call | flops 402653184 | bytes 2621440 | tf_op jit(solution)/shard_map/weights/pallas_call | solution.py:369
  84.4 1.8 %spread.6 = (f32[128,2048]{1,0:T(8,128)S(1)}, f32[128,2048]{1,0:T(8,128)S(1)}) custom-call(s32[384]{0:T(512)S(1)} %table.1, s32[384]{0:T(512)S(1)} %collective-permute-done.5.table_pair, bf16[16,12,128,128]{3,2,1,0:T(8,128)(2,1)S(1)} %load.1.adj, bf16[16,12,128,128]{3,2,1,0:T(8,128)(2,1)S(1)} %collective-permute-done.3.pair, ...), custom_call_target="tpu_custom_call" | custom-call | flops 201326592 | bytes 4194304 | tf_op jit(solution)/shard_map/spread/pallas_call | solution.py:369
  86.2 3.3 %collective-permute-done.30.arrived = bf16[64,2048]{1,0:T(8,128)(2,1)S(1)} collective-permute-done((bf16[64,2048]{1,0:T(8,128)(2,1)S(1)}, bf16[64,2048]{1,0:T(8,128)(2,1)S(1)}, u32[]{:S(2)}, u32[]{:S(2)}) %collective-permute-start.30) | collective-permute-done | bytes 262176 | tf_op jit(solution)/shard_map/ppermute | solution.py:510
  92.0 1.8 %spread.7 = (f32[128,2048]{1,0:T(8,128)S(1)}, f32[128,2048]{1,0:T(8,128)S(1)}) custom-call(s32[384]{0:T(512)S(1)} %table.1, s32[384]{0:T(512)S(1)} %collective-permute-done.5.table_pair, bf16[16,12,128,128]{3,2,1,0:T(8,128)(2,1)S(1)} %load.1.adj, bf16[16,12,128,128]{3,2,1,0:T(8,128)(2,1)S(1)} %collective-permute-done.3.pair, ...), custom_call_target="tpu_custom_call" | custom-call | flops 201326592 | bytes 4194304 | tf_op jit(solution)/shard_map/spread/pallas_call | solution.py:369
  93.8 9.4 %collective-permute-done.31.arrived = bf16[128,2048]{1,0:T(8,128)(2,1)S(1)} collective-permute-done((bf16[128,2048]{1,0:T(8,128)(2,1)S(1)}, bf16[128,2048]{1,0:T(8,128)(2,1)S(1)}, u32[]{:S(2)}, u32[]{:S(2)}) %collective-permute-start.31) | collective-permute-done | bytes 524320 | tf_op jit(solution)/shard_map/ppermute | solution.py:523
  108.8 10.3 %collective-permute-done.35 = f32[136,128]{1,0:T(8,128)S(1)} collective-permute-done((f32[136,128]{1,0:T(8,128)S(1)}, f32[136,128]{1,0:T(8,128)S(1)}, u32[]{:S(2)}, u32[]{:S(2)}) %collective-permute-start.35) | collective-permute-done | bytes 69664 | tf_op jit(solution)/shard_map/ppermute | solution.py:49
  119.3 2.3 %spread.5 = (f32[128,2048]{1,0:T(8,128)S(1)}, f32[128,2048]{1,0:T(8,128)S(1)}, f32[128,2048]{1,0:T(8,128)S(1)}) custom-call(s32[384]{0:T(512)S(1)} %table.1, s32[384]{0:T(512)S(1)} %collective-permute-done.5.table_pair, bf16[16,12,128,128]{3,2,1,0:T(8,128)(2,1)S(1)} %load.1.adj, bf16[16,12,128,128]{3,2,1,0:T(8,128)(2,1)S(1)} %collective-permute-done.3.pair, ...), custom_call_target="tpu_custom_call" | custom-call | flops 301989888 | bytes 6291456 | tf_op jit(solution)/shard_map/spread/pallas_call | solution.py:369
  123.5 2.0 %collective-permute-start.29 = (bf16[128,2048]{1,0:T(8,128)(2,1)}, bf16[128,2048]{1,0:T(8,128)(2,1)}, u32[]{:S(2)}, u32[]{:S(2)}) collective-permute-start(bf16[128,2048]{1,0:T(8,128)(2,1)} %join.8), channel_id=1, source_target_pairs={{0,8},{2,10},{8,16},{10,18},{16,24},{18,26},{24,28},{26,30},{28,20... | collective-permute-start | bytes 1572872 | tf_op jit(solution)/shard_map/ppermute | solution.py:522
  125.5 2.7 %collective-permute-start.37 = (f32[136,128]{1,0:T(8,128)S(1)}, f32[136,128]{1,0:T(8,128)S(1)}, u32[]{:S(2)}, u32[]{:S(2)}) collective-permute-start(f32[136,128]{1,0:T(8,128)S(1)} %add.29), channel_id=1, source_target_pairs={{0,16},{2,18},{4,20},{6,22},{8,24},{10,26},{12,28},{14,30},{16,0},... | collective-permute-start | bytes 208904 | tf_op jit(solution)/shard_map/ppermute | solution.py:49
  128.2 10.2 %collective-permute-done.37 = f32[136,128]{1,0:T(8,128)S(1)} collective-permute-done((f32[136,128]{1,0:T(8,128)S(1)}, f32[136,128]{1,0:T(8,128)S(1)}, u32[]{:S(2)}, u32[]{:S(2)}) %collective-permute-start.37) | collective-permute-done | bytes 69664 | tf_op jit(solution)/shard_map/ppermute | solution.py:49
  138.4 3.9 %collective-permute-start.38 = (f32[136,128]{1,0:T(8,128)S(1)}, f32[136,128]{1,0:T(8,128)S(1)}, u32[]{:S(2)}, u32[]{:S(2)}) collective-permute-start(f32[136,128]{1,0:T(8,128)S(1)} %add.30), channel_id=1, source_target_pairs={{0,4},{2,6},{4,0},{6,2},{8,12},{10,14},{12,8},{14,10},{16,20},{18,... | collective-permute-start | bytes 208904 | tf_op jit(solution)/shard_map/ppermute | solution.py:49
  142.3 2.3 %collective-permute-done.38 = f32[136,128]{1,0:T(8,128)S(1)} collective-permute-done((f32[136,128]{1,0:T(8,128)S(1)}, f32[136,128]{1,0:T(8,128)S(1)}, u32[]{:S(2)}, u32[]{:S(2)}) %collective-permute-start.38) | collective-permute-done | bytes 69664 | tf_op jit(solution)/shard_map/ppermute | solution.py:49
  148.2 2.1 %finish.1 = bf16[128,2048]{1,0:T(8,128)(2,1)} custom-call(f32[128,2048]{1,0:T(8,128)S(1)} %get-tuple-element.90.base, bf16[128,2048]{1,0:T(8,128)(2,1)} %collective-permute-done.29.a, bf16[128,2048]{1,0:T(8,128)(2,1)S(1)} %collective-permute-done.33.b, f32[128,1024]{1,0:T(8,128)S(1)} %get-tuple-element.99.refs_0_, ...), custom_call_target="tpu_custom_call" | custom-call | bytes 2097152 | tf_op jit(solution)/shard_map/finish/pallas_call | solution.py:369
  (103 shorter events, 45.3 us)
Async XLA Ops:
  1.7 9.3 %collective-permute-start = (bf16[64,2048]{1,0:T(8,128)(2,1)S(1)}, bf16[64,2048]{1,0:T(8,128)(2,1)S(1)}, u32[]{:S(2)}, u32[]{:S(2)}) collective-permute-start(bf16[64,2048]{1,0:T(8,128)(2,1)S(1)} %get-tuple-element.106.refs_0_), channel_id=1, source_target_pairs={{0,8},{2,10},{8,16},{10,18},{16,24},{18,26},{24,28},{26,30},{28,20... | collective-permute-start | bytes 786440 | tf_op jit(solution)/shard_map/ppermute | solution.py:427
  12.6 23.3 %collective-permute-start.3 = (bf16[16,12,128,128]{3,2,1,0:T(8,128)(2,1)}, bf16[16,12,128,128]{3,2,1,0:T(8,128)(2,1)S(1)}, u32[]{:S(2)}, u32[]{:S(2)}) collective-permute-start(bf16[16,12,128,128]{3,2,1,0:T(8,128)(2,1)} %source.1), channel_id=1, source_target_pairs={{0,2},{2,0},{4,6},{6,4},{8,10},{10,8},{12,14},{14,12},{16,18},{18,... | collective-permute-start | bytes 18874376 | tf_op jit(solution)/shard_map/ppermute | solution.py:49
  13.0 10.1 %collective-permute-start.7 = (bf16[64,2048]{1,0:T(8,128)(2,1)S(1)}, bf16[64,2048]{1,0:T(8,128)(2,1)S(1)}, u32[]{:S(2)}, u32[]{:S(2)}) collective-permute-start(bf16[64,2048]{1,0:T(8,128)(2,1)S(1)} %get-tuple-element.68), channel_id=1, source_target_pairs={{0,10},{2,8},{8,18},{10,16},{16,26},{18,24},{24,30},{26,28},{28,22... | collective-permute-start | bytes 786440 | tf_op jit(solution)/shard_map/ppermute | solution.py:427
  20.5 9.2 %collective-permute-start.8 = (bf16[64,2048]{1,0:T(8,128)(2,1)S(1)}, bf16[64,2048]{1,0:T(8,128)(2,1)S(1)}, u32[]{:S(2)}, u32[]{:S(2)}) collective-permute-start(bf16[64,2048]{1,0:T(8,128)(2,1)S(1)} %collective-permute-done.2.refs_2_), channel_id=1, source_target_pairs={{0,4},{2,6},{8,0},{10,2},{16,8},{18,10},{24,16},{26,18},{28,24},{3... | collective-permute-start | bytes 786440 | tf_op jit(solution)/shard_map/ppermute | solution.py:431
  21.0 14.3 %collective-permute-start.10 = (bf16[64,2048]{1,0:T(8,128)(2,1)S(1)}, bf16[64,2048]{1,0:T(8,128)(2,1)S(1)}, u32[]{:S(2)}, u32[]{:S(2)}) collective-permute-start(bf16[64,2048]{1,0:T(8,128)(2,1)S(1)} %collective-permute-done.6.refs_4_), channel_id=1, source_target_pairs={{0,4},{2,6},{8,0},{10,2},{16,8},{18,10},{24,16},{26,18},{28,24},{3... | collective-permute-start | bytes 786440 | tf_op jit(solution)/shard_map/ppermute | solution.py:431
  22.5 13.4 %collective-permute-start.1 = (bf16[64,2048]{1,0:T(8,128)(2,1)S(1)}, bf16[64,2048]{1,0:T(8,128)(2,1)S(1)}, u32[]{:S(2)}, u32[]{:S(2)}) collective-permute-start(bf16[64,2048]{1,0:T(8,128)(2,1)S(1)} %collective-permute-done.refs_1_), channel_id=1, source_target_pairs={{0,8},{2,10},{8,16},{10,18},{16,24},{18,26},{24,28},{26,30},{28,20... | collective-permute-start | bytes 786440 | tf_op jit(solution)/shard_map/ppermute | solution.py:427
  23.1 15.8 %collective-permute-start.9 = (bf16[64,2048]{1,0:T(8,128)(2,1)S(1)}, bf16[64,2048]{1,0:T(8,128)(2,1)S(1)}, u32[]{:S(2)}, u32[]{:S(2)}) collective-permute-start(bf16[64,2048]{1,0:T(8,128)(2,1)S(1)} %collective-permute-done.7.refs_3_), channel_id=1, source_target_pairs={{0,8},{2,10},{8,16},{10,18},{16,24},{18,26},{24,28},{26,30},{28,20... | collective-permute-start | bytes 786440 | tf_op jit(solution)/shard_map/ppermute | solution.py:427
  29.7 17.0 %collective-permute-start.12 = (bf16[64,2048]{1,0:T(8,128)(2,1)S(1)}, bf16[64,2048]{1,0:T(8,128)(2,1)S(1)}, u32[]{:S(2)}, u32[]{:S(2)}) collective-permute-start(bf16[64,2048]{1,0:T(8,128)(2,1)S(1)} %collective-permute-done.8.refs_6_), channel_id=1, source_target_pairs={{0,4},{2,6},{8,0},{10,2},{16,8},{18,10},{24,16},{26,18},{28,24},{3... | collective-permute-start | bytes 786440 | tf_op jit(solution)/shard_map/ppermute | solution.py:431
  35.3 11.0 %collective-permute-start.14 = (bf16[64,2048]{1,0:T(8,128)(2,1)S(1)}, bf16[64,2048]{1,0:T(8,128)(2,1)S(1)}, u32[]{:S(2)}, u32[]{:S(2)}) collective-permute-start(bf16[64,2048]{1,0:T(8,128)(2,1)S(1)} %collective-permute-done.10.refs_8_), channel_id=1, source_target_pairs={{0,4},{2,6},{8,0},{10,2},{16,8},{18,10},{24,16},{26,18},{28,24},{3... | collective-permute-start | bytes 786440 | tf_op jit(solution)/shard_map/ppermute | solution.py:431
  35.9 10.9 %collective-permute-start.11 = (bf16[64,2048]{1,0:T(8,128)(2,1)S(1)}, bf16[64,2048]{1,0:T(8,128)(2,1)S(1)}, u32[]{:S(2)}, u32[]{:S(2)}) collective-permute-start(bf16[64,2048]{1,0:T(8,128)(2,1)S(1)} %collective-permute-done.1.refs_5_), channel_id=1, source_target_pairs={{0,8},{2,10},{8,16},{10,18},{16,24},{18,26},{24,28},{26,30},{28,20... | collective-permute-start | bytes 786440 | tf_op jit(solution)/shard_map/ppermute | solution.py:427
  37.4 28.7 %collective-permute-start.4 = (bf16[128,2688]{1,0:T(8,128)(2,1)S(1)}, bf16[128,2688]{1,0:T(8,128)(2,1)S(1)}, u32[]{:S(2)}, u32[]{:S(2)}) collective-permute-start(bf16[128,2688]{1,0:T(8,128)(2,1)S(1)} %get-tuple-element.59), channel_id=1, source_target_pairs={{0,1},{1,0},{2,3},{3,2},{4,5},{5,4},{6,7},{7,6},{8,9},{9,8},{10,11... | collective-permute-start | bytes 2064392 | tf_op jit(solution)/shard_map/ppermute | solution.py:55
  38.9 10.0 %collective-permute-start.13 = (bf16[64,2048]{1,0:T(8,128)(2,1)S(1)}, bf16[64,2048]{1,0:T(8,128)(2,1)S(1)}, u32[]{:S(2)}, u32[]{:S(2)}) collective-permute-start(bf16[64,2048]{1,0:T(8,128)(2,1)S(1)} %collective-permute-done.9.refs_7_), channel_id=1, source_target_pairs={{0,8},{2,10},{8,16},{10,18},{16,24},{18,26},{24,28},{26,30},{28,20... | collective-permute-start | bytes 786440 | tf_op jit(solution)/shard_map/ppermute | solution.py:427
  70.2 9.2 %collective-permute-start.22 = (bf16[128,1024]{1,0:T(8,128)(2,1)S(1)}, bf16[128,1024]{1,0:T(8,128)(2,1)S(1)}, u32[]{:S(2)}, u32[]{:S(2)}) collective-permute-start(bf16[128,1024]{1,0:T(8,128)(2,1)S(1)} %get-tuple-element.83.refs_0_), channel_id=1, source_target_pairs={{0,2},{2,0},{4,6},{6,4},{8,10},{10,8},{12,14},{14,12},{16,18},{18,... | collective-permute-start | bytes 786440 | tf_op jit(solution)/shard_map/ppermute | solution.py:49
  82.4 8.8 %collective-permute-start.26 = (bf16[64,2048]{1,0:T(8,128)(2,1)S(1)}, bf16[64,2048]{1,0:T(8,128)(2,1)S(1)}, u32[]{:S(2)}, u32[]{:S(2)}) collective-permute-start(bf16[64,2048]{1,0:T(8,128)(2,1)S(1)} %get-tuple-element.91), channel_id=1, source_target_pairs={{0,8},{2,10},{8,16},{10,18},{16,24},{18,26},{24,28},{26,30},{28,20... | collective-permute-start | bytes 786440 | tf_op jit(solution)/shard_map/ppermute | solution.py:510
  82.9 9.0 %collective-permute-start.24 = (f32[4,136,128]{2,1,0:T(8,128)S(1)}, f32[4,136,128]{2,1,0:T(8,128)S(1)}, u32[]{:S(2)}, u32[]{:S(2)}) collective-permute-start(f32[4,136,128]{2,1,0:T(8,128)S(1)} %get-tuple-element.86), channel_id=1, source_target_pairs={{0,1},{1,0},{2,3},{3,2},{4,5},{5,4},{6,7},{7,6},{8,9},{9,8},{10,11... | collective-permute-start | bytes 835592 | tf_op jit(solution)/shard_map/ppermute | solution.py:55
  89.6 13.6 %collective-permute-start.31 = (bf16[128,2048]{1,0:T(8,128)(2,1)S(1)}, bf16[128,2048]{1,0:T(8,128)(2,1)S(1)}, u32[]{:S(2)}, u32[]{:S(2)}) collective-permute-start(bf16[128,2048]{1,0:T(8,128)(2,1)S(1)} %join.9), channel_id=1, source_target_pairs={{0,4},{2,6},{8,0},{10,2},{16,8},{18,10},{24,16},{26,18},{28,24},{3... | collective-permute-start | bytes 1572872 | tf_op jit(solution)/shard_map/ppermute | solution.py:523
  91.4 13.6 %collective-permute-start.27 = (bf16[128,2048]{1,0:T(8,128)(2,1)S(1)}, bf16[128,2048]{1,0:T(8,128)(2,1)S(1)}, u32[]{:S(2)}, u32[]{:S(2)}) collective-permute-start(bf16[128,2048]{1,0:T(8,128)(2,1)S(1)} %join.6), channel_id=1, source_target_pairs={{0,8},{2,10},{8,16},{10,18},{16,24},{18,26},{24,28},{26,30},{28,20... | collective-permute-start | bytes 1572872 | tf_op jit(solution)/shard_map/ppermute | solution.py:522
  103.3 18.3 %collective-permute-start.32 = (bf16[128,2048]{1,0:T(8,128)(2,1)S(1)}, bf16[128,2048]{1,0:T(8,128)(2,1)S(1)}, u32[]{:S(2)}, u32[]{:S(2)}) collective-permute-start(bf16[128,2048]{1,0:T(8,128)(2,1)S(1)} %join.10), channel_id=1, source_target_pairs={{0,4},{2,6},{8,0},{10,2},{16,8},{18,10},{24,16},{26,18},{28,24},{3... | collective-permute-start | bytes 1572872 | tf_op jit(solution)/shard_map/ppermute | solution.py:523
  105.1 17.5 %collective-permute-start.28 = (bf16[128,2048]{1,0:T(8,128)(2,1)S(1)}, bf16[128,2048]{1,0:T(8,128)(2,1)S(1)}, u32[]{:S(2)}, u32[]{:S(2)}) collective-permute-start(bf16[128,2048]{1,0:T(8,128)(2,1)S(1)} %join.7), channel_id=1, source_target_pairs={{0,8},{2,10},{8,16},{10,18},{16,24},{18,26},{24,28},{26,30},{28,20... | collective-permute-start | bytes 1572872 | tf_op jit(solution)/shard_map/ppermute | solution.py:522
  105.7 13.4 %collective-permute-start.35 = (f32[136,128]{1,0:T(8,128)S(1)}, f32[136,128]{1,0:T(8,128)S(1)}, u32[]{:S(2)}, u32[]{:S(2)}) collective-permute-start(f32[136,128]{1,0:T(8,128)S(1)} %slice_bitcast_fusion), channel_id=1, source_target_pairs={{0,4},{2,6},{4,0},{6,2},{8,12},{10,14},{12,8},{14,10},{16,20},{18,... | collective-permute-start | bytes 208904 | tf_op jit(solution)/shard_map/ppermute | solution.py:49
  107.3 40.0 %collective-permute-start.25 = (bf16[128,3072]{1,0:T(8,128)(2,1)}, bf16[128,3072]{1,0:T(8,128)(2,1)S(1)}, u32[]{:S(2)}, u32[]{:S(2)}) collective-permute-start(bf16[128,3072]{1,0:T(8,128)(2,1)} %get-tuple-element.89), channel_id=1, source_target_pairs={{0,1},{1,0},{2,3},{3,2},{4,5},{5,4},{6,7},{7,6},{8,9},{9,8},{10,11... | collective-permute-start | bytes 2359304 | tf_op jit(solution)/shard_map/ppermute | solution.py:55
  122.5 25.7 %collective-permute-start.33 = (bf16[128,2048]{1,0:T(8,128)(2,1)}, bf16[128,2048]{1,0:T(8,128)(2,1)S(1)}, u32[]{:S(2)}, u32[]{:S(2)}) collective-permute-start(bf16[128,2048]{1,0:T(8,128)(2,1)} %join.11), channel_id=1, source_target_pairs={{0,4},{2,6},{8,0},{10,2},{16,8},{18,10},{24,16},{26,18},{28,24},{3... | collective-permute-start | bytes 1572872 | tf_op jit(solution)/shard_map/ppermute | solution.py:523
  123.5 24.7 %collective-permute-start.29 = (bf16[128,2048]{1,0:T(8,128)(2,1)}, bf16[128,2048]{1,0:T(8,128)(2,1)}, u32[]{:S(2)}, u32[]{:S(2)}) collective-permute-start(bf16[128,2048]{1,0:T(8,128)(2,1)} %join.8), channel_id=1, source_target_pairs={{0,8},{2,10},{8,16},{10,18},{16,24},{18,26},{24,28},{26,30},{28,20... | collective-permute-start | bytes 1572872 | tf_op jit(solution)/shard_map/ppermute | solution.py:522
  125.5 12.9 %collective-permute-start.37 = (f32[136,128]{1,0:T(8,128)S(1)}, f32[136,128]{1,0:T(8,128)S(1)}, u32[]{:S(2)}, u32[]{:S(2)}) collective-permute-start(f32[136,128]{1,0:T(8,128)S(1)} %add.29), channel_id=1, source_target_pairs={{0,16},{2,18},{4,20},{6,22},{8,24},{10,26},{12,28},{14,30},{16,0},... | collective-permute-start | bytes 208904 | tf_op jit(solution)/shard_map/ppermute | solution.py:49
  (23 other events, 163.5 us)

commit v5 on v0

v5 whole, which is shorter than its diff:
```python
import functools

import jax
import jax.numpy as jnp
from jax import lax
from jax.experimental import pallas as pl
from jax.experimental.pallas import tpu as pltpu
from jax.sharding import PartitionSpec as P

CAP = 12
MIB = 1024 * 1024
HBM = pl.BlockSpec(memory_space=pltpu.HBM)
VMEM = pl.BlockSpec(memory_space=pltpu.VMEM)
SMEM = pl.BlockSpec(memory_space=pltpu.SMEM)
LAST = (((1,), (1,)), ((), ()))


def params(mib):
    return pltpu.CompilerParams(vmem_limit_bytes=mib * MIB)


def cost(flops, moved):
    return pl.CostEstimate(flops=flops, bytes_accessed=moved, transcendentals=0)


def product(left, right, dims=(((1,), (0,)), ((), ()))):
    return lax.dot_general(left, right, dims, preferred_element_type=jnp.float32)


def ring_pairs(rows, step, flip=0):
    levels, chips = rows // 4, rows // 2
    order = [2 * z for z in range(levels)] + [2 * z + 1 for z in reversed(range(levels))]
    return [
        (2 * order[p] + core, 2 * order[(p + step) % chips] + (core ^ flip))
        for p in range(chips)
        for core in range(2)
    ]


def ring_row(row, offset, rows):
    levels, chips = rows // 4, rows // 2
    z, x, core = row // 4, lax.rem(row // 2, 2), lax.rem(row, 2)
    target = lax.rem(jnp.where(x == 0, z, chips - 1 - z) + (offset + chips), chips)
    low = target < levels
    return 2 * jnp.where(low, 2 * target, 2 * (chips - 1 - target) + 1) + core


def swap(value, rows, bit=1):
    return lax.ppermute(value, "rows", [(r, r ^ bit) for r in range(rows)])


def send(value, k, flip, rows, feats):
    pairs = [
        (r * feats + i, (r ^ flip) * feats + (i + k) % feats)
        for r in range(rows)
        for i in range(feats)
    ]
    return lax.ppermute(value, ("rows", "feat"), pairs)


def after(value, *others):
    return lax.optimization_barrier((value, *others))[0]


def behind(k, feats, size):
    return pl.multiple_of(lax.rem(lax.axis_index("feat") - k + feats, feats) * size, size)


def pack_kernel(feature, grad_output, ws, wn, bias, out, parts, sems):
    hid, every = ws.shape
    width = feature.shape[1]
    copies = []
    for source, low, size in (
        (feature, 0, width),
        (grad_output, width, width),
        (ws, 2 * width, every),
        (wn, 2 * width + every, every),
        (parts, 2 * width + 2 * every, 128),
    ):
        place = out.at[:, pl.ds(low, size)]
        copies.append(pltpu.make_async_copy(source, place, sems.at[len(copies)]))
    line = lax.broadcasted_iota(jnp.int32, (hid, hid), 0)
    lane = lax.broadcasted_iota(jnp.int32, (hid, hid), 1)
    column = jnp.sum(jnp.where(line == lane, bias[...], 0.0), axis=1, keepdims=True)
    high = column.astype(jnp.bfloat16).astype(jnp.float32)
    middle = (column - high).astype(jnp.bfloat16).astype(jnp.float32)
    low = column - high - middle
    at = lax.broadcasted_iota(jnp.int32, (hid, 128), 1)
    value = jnp.where(at == 0, high, jnp.where(at == 1, middle, jnp.where(at == 2, low, 0.0)))
    parts[...] = value.astype(jnp.bfloat16)
    for copy in copies:
        copy.start()
    for copy in copies:
        copy.wait()


def prepare_kernel(feats, *refs):
    packs, (turned, cot_all, base), (weights, bias, x_all) = refs[:feats], refs[feats:-3], refs[-3:]
    hid, width = packs[0].shape[0], x_all.shape[1]
    every = feats * hid
    for k in range(feats):
        at = pl.ds(behind(k, feats, hid), hid)
        pack = packs[k]
        x_all[at] = pack[:, :width]
        cot_all[at] = pack[:, width : 2 * width]
        weights[at] = pack[:, 2 * width : 2 * width + 2 * every].astype(jnp.float32)
        parts = pack[:, 2 * width + 2 * every :].astype(jnp.float32)
        bias[at] = jnp.sum(parts, axis=1, keepdims=True)
    own = weights[:, :every].T.astype(jnp.bfloat16)
    turned[...] = weights[:, every:].T.astype(jnp.bfloat16)
    chunk = min(width, 512)
    for c in range(0, width, chunk):
        lane = pl.ds(c, chunk)
        base[:, lane] = product(own, x_all[:, lane]) + bias[...]


def table_kernel(cols, table, counts):
    blocks, per_block = cols.shape
    base = blocks * per_block
    groups = counts.shape[0]

    def clear(i, carry):
        counts[i] = 0
        for s in range(CAP):
            table[base + i * CAP + s] = -1
        return carry

    lax.fori_loop(0, groups, clear, 0)

    def step(block, carry):
        for t in range(per_block):
            col = cols[block, t]
            group = col // blocks
            seen = counts[group]
            counts[group] = seen + 1
            index = block * per_block + t
            table[index] = col
            table[base + group * CAP + seen] = index * 256 + (col - group * blocks)
        return carry

    lax.fori_loop(0, blocks, step, 0)


def load_kernel(source, out, sem):
    copy = pltpu.make_async_copy(source, out, sem)
    copy.start()
    copy.wait()


def aggregate_kernel(wanted, rows, table, tiles, *refs):
    count = len(wanted)
    blocks, per_block, tile, unused = tiles.shape
    half = refs[0].shape[0]
    sources, (out, inverse, held, sems) = refs[:count], refs[count:]
    row = lax.axis_index("rows")
    copies = []
    for n, (offset, side) in enumerate(wanted):
        place = ring_row(row, offset, rows)
        if side:
            place = place + 1 - 2 * lax.rem(place, 2)
        copies.append(pltpu.make_async_copy(sources[n], held.at[place], sems.at[n]))
    for copy in copies:
        copy.start()
    for copy in copies:
        copy.wait()
    ones = jnp.ones((16, 2 * tile), jnp.bfloat16)

    def step(block, carry):
        total = None
        for t in range(0, per_block, 2):
            left, right = [], []
            for u in (t, t + 1):
                col = table[block * per_block + u]
                source = col // blocks
                at = pl.multiple_of((col - source * blocks) * tile, tile)
                left.append(held[source, :, pl.ds(at, tile)])
                right.append(tiles[block, u])
            term = product(
                jnp.concatenate([jnp.concatenate(left, axis=1), ones], axis=0),
                jnp.concatenate(right, axis=1),
                LAST,
            )
            total = term if total is None else total + term
        factor = 1.0 / total[half : half + 1]
        lane = pl.ds(pl.multiple_of(block * tile, tile), tile)
        out[:, lane] = (total[:half] * factor).astype(jnp.bfloat16)
        inverse[:, lane] = factor
        return carry

    lax.fori_loop(0, blocks, step, 0, unroll=4)


def middle_kernel(feats, turned, wn, inverse, base, cot, *refs):
    near, far, refs = refs[:feats], refs[feats : 2 * feats], refs[2 * feats :]
    act, grad, scaled, agg_own, agg, value = refs
    hid, width = act.shape
    half = hid // 2
    core = lax.rem(lax.axis_index("rows"), 2)
    for k in range(feats):
        first = behind(k, feats, hid)
        agg[pl.ds(pl.multiple_of(first + core * half, half), half)] = near[k][...]
        agg[pl.ds(pl.multiple_of(first + (1 - core) * half, half), half)] = far[k][...]
    own = pl.ds(behind(0, feats, hid), hid)
    agg_own[...] = agg[own]
    chunk = min(width, 256)
    for c in range(0, width, chunk):
        lane = pl.ds(c, chunk)
        pre = product(turned[...], agg[:, lane]) + base[:, lane]
        slope = jnp.exp(jnp.minimum(pre, 0.0))
        grad[:, lane] = (cot[:, lane].astype(jnp.float32) * slope).astype(jnp.bfloat16)
        value[...] = jnp.where(pre > 0, pre, slope - 1.0)
        back = product(wn[...], grad[:, lane])
        scaled[:, lane] = (back * inverse[:, lane]).astype(jnp.bfloat16)
        act[:, lane] = value[own].astype(jnp.bfloat16)


def weights_kernel(ws, x_own, agg_own, grad, self_own, sums):
    hid, every = ws.shape
    g = grad[...]
    self_own[...] = product(ws[...], g)
    sums[:hid, :every] = product(x_own[...], g, LAST)
    sums[:hid, every:] = product(agg_own[...], g, LAST)
    total = product(jnp.ones((8, g.shape[1]), jnp.bfloat16), g, LAST)
    sums[hid:, :every] = total
    sums[hid:, every:] = total


def arrange_kernel(own, other, held):
    hid, tile = held.shape[2:]
    blocks = held.shape[1] - 1
    for side, source in enumerate((own, other)):
        held[side, blocks] = jnp.zeros((hid, tile), jnp.bfloat16)
        for block in range(blocks):
            held[side, block] = source[:, block * tile : (block + 1) * tile]


def spread_kernel(plan, table, table_pair, adj, pair, held, *refs):
    rows, offsets, kinds = plan
    results, total = refs[:-1], refs[-1]
    blocks, per_block, tile, unused = adj.shape
    half = total.shape[0] // 2
    row = lax.axis_index("rows")
    firsts = [blocks * per_block + ring_row(row, offset, rows) * CAP for offset in offsets]
    for d in range(len(offsets)):
        total[...] = jnp.zeros_like(total)
        for side, (slots, tiles) in enumerate(((table, adj), (table_pair, pair))):
            for s0 in range(0, CAP, 4):
                terms = []
                for s in range(s0, s0 + 4):
                    entry = slots[firsts[d] + s]
                    index = jnp.maximum(entry, 0) // 256
                    block = index // per_block
                    place = jnp.where(entry < 0, blocks, block)
                    lane = lax.rem(jnp.maximum(entry, 0), 256) * tile
                    term = product(held[side, place], tiles[block, index - block * per_block])
                    terms.append((pl.multiple_of(lane, tile), term))
                for lane, term in terms:
                    total[:, pl.ds(lane, tile)] += term
        for part in range(2):
            value = total[part * half : (part + 1) * half]
            results[2 * d + part][...] = value.astype(kinds[2 * d + part])


def join_kernel(arrived, mine, out):
    out[...] = (arrived[...].astype(jnp.float32) + mine[...]).astype(jnp.bfloat16)


def finish_kernel(own, base_low, base_high, a_low, b_low, a_high, b_high, out):
    half = a_low.shape[0]
    for part, (base, a, b) in enumerate(((base_low, a_low, b_low), (base_high, a_high, b_high))):
        lines = slice(part * half, (part + 1) * half)
        value = own[lines] + base[...] + a[...].astype(jnp.float32)
        out[lines] = (value + b[...].astype(jnp.float32)).astype(jnp.bfloat16)


def call(kernel, name, outs, ins, out_specs, scratch, mib, flops, moved, *args):
    return pl.pallas_call(
        kernel,
        out_shape=[jax.ShapeDtypeStruct(shape, kind) for shape, kind in outs],
        in_specs=ins,
        out_specs=out_specs,
        scratch_shapes=scratch,
        compiler_params=params(mib),
        cost_estimate=cost(flops, moved),
        name=name,
    )(*args)


def shards(rows, feats, features, adjacency, tile_cols, self_weight, neigh_weight, bias_vector, grad_output):
    hid, width = features.shape
    blocks, per_block, tile, unused = adjacency.shape
    half = hid // 2
    every = hid * feats
    top = rows // 4
    narrow, wide = jnp.bfloat16, jnp.float32
    bind = functools.partial

    core = lax.rem(lax.axis_index("rows"), 2)
    mine = lax.dynamic_slice_in_dim(features, core * half, half)
    away = lax.dynamic_slice_in_dim(features, (1 - core) * half, half)
    sources, wanted = [mine], [(0, 0)]
    up, down = [mine, away], [mine, away]
    pair = swap(adjacency, rows)
    (table,) = call(
        table_kernel, "table", [((tile_cols.size + rows * CAP,), jnp.int32)], [SMEM], [SMEM],
        [pltpu.SMEM((rows,), jnp.int32)], 4, 0, 8 * rows * CAP, tile_cols,
    )
    packed = 2 * width + 2 * every + 128
    (pack,) = call(
        pack_kernel, "pack", [((hid, packed), narrow)], [HBM] * 4 + [VMEM], [VMEM],
        [pltpu.VMEM((hid, 128), narrow), pltpu.SemaphoreType.DMA((5,))], 6, 0,
        4 * hid * packed,
        features, grad_output, self_weight, neigh_weight, bias_vector.reshape(1, hid),
    )
    (tiles,) = call(
        load_kernel, "load", [(adjacency.shape, narrow)], [HBM], [VMEM],
        [pltpu.SemaphoreType.DMA], 4, 0, 4 * adjacency.size, adjacency,
    )
    for step in range(1, top + 1):
        if step == 2:
            up, down, pair, table, pack = lax.optimization_barrier((up, down, pair, table, pack))
            table_pair = swap(table, rows)
            packs = [pack] + [send(pack, k, 0, rows, feats) for k in range(1, feats)]
        if step == top:
            sources.append(swap(after(away, up[0], down[0], tiles), rows))
            wanted.append((0, 1))
        for side in range(2):
            flip = side if step == 1 else 0
            forward, backward = ring_pairs(rows, 1, flip), ring_pairs(rows, -1, flip)
            if step < top or side == 0:
                up[side] = lax.ppermute(up[side], "rows", forward)
                sources.append(up[side])
                wanted.append((-step, side))
            if step < top or side == 1:
                down[side] = lax.ppermute(down[side], "rows", backward)
                sources.append(down[side])
                wanted.append((step, side))

    def aggregate(columns, values):
        return call(
            bind(aggregate_kernel, tuple(wanted), rows), "aggregate",
            [((half, width), narrow), ((1, width), wide)],
            [SMEM, VMEM] + [HBM] * len(sources), [VMEM] * 2,
            [pltpu.VMEM((rows, half, width), narrow), pltpu.SemaphoreType.DMA((len(sources),))],
            12, hid * adjacency.size, 2 * adjacency.size + rows * hid * width,
            columns, values, *sources,
        )

    value, unused_inverse = aggregate(table_pair, pair)
    far = [send(value, k, 1, rows, feats) for k in reversed(range(feats))][::-1]
    value, inverse = aggregate(table, tiles)
    near = [value] + [send(value, k, 0, rows, feats) for k in range(1, feats)]

    turned, cot_all, base = call(
        bind(prepare_kernel, feats), "prepare",
        [((every, every), narrow), ((every, width), narrow), ((every, width), wide)],
        [VMEM] * feats, [VMEM] * 3,
        [
            pltpu.VMEM((every, 2 * every), wide),
            pltpu.VMEM((every, 1), wide),
            pltpu.VMEM((every, width), narrow),
        ],
        12, 2 * every * every * width, 4 * every * packed, *packs,
    )
    activation, grad, scaled, agg_own = call(
        bind(middle_kernel, feats), "middle",
        [((hid, width), narrow), ((every, width), narrow)] + [((hid, width), narrow)] * 2,
        [VMEM] * (5 + 2 * feats), [VMEM] * 4,
        [pltpu.VMEM((every, width), narrow), pltpu.VMEM((every, min(width, 256)), wide)], 12,
        3 * every * every * width, 14 * every * width,
        turned, neigh_weight, inverse, base, cot_all, *near, *far,
    )
    scaled_pair = swap(scaled, rows)
    self_own, sums = call(
        weights_kernel, "weights", [((hid, width), wide), ((hid + 8, 2 * every), wide)],
        [VMEM] * 4, [VMEM] * 2, [], 12, 6 * hid * every * width, 10 * every * width,
        self_weight, features, agg_own, grad,
    )
    (held,) = call(
        arrange_kernel, "arrange", [((2, blocks + 1, hid, tile), narrow)],
        [VMEM] * 2, [VMEM], [], 8, 0, 8 * hid * width, scaled, scaled_pair,
    )

    def spread(offsets, kinds):
        n = 2 * CAP * len(offsets)
        return call(
            bind(spread_kernel, (rows, offsets, kinds)), "spread",
            [((half, width), kind) for kind in kinds],
            [SMEM] * 2 + [VMEM] * 3, [VMEM] * len(kinds), [pltpu.VMEM((hid, width), wide)],
            8, 2 * n * hid * tile * tile, 8 * hid * width * len(offsets),
            table, table_pair, tiles, pair, held,
        )

    def joined(arrived, mine):
        if arrived is None:
            return mine
        (out,) = call(
            join_kernel, "join", [((half, width), narrow)], [VMEM] * 2, [VMEM], [], 8,
            0, 4 * hid * width, arrived, mine,
        )
        return out

    up, down = [None, None], [None, None]
    forward, backward = ring_pairs(rows, 1), ring_pairs(rows, -1)
    for level in range(top, 0, -1):
        if level == top:
            low, high = spread((top,), (narrow, narrow))
            up[0] = lax.ppermute(low, "rows", forward)
            down[1] = lax.ppermute(high, "rows", backward)
            continue
        kinds = tuple(narrow if arrived is None else wide for arrived in up + down)
        offsets = (level, -level)
        if level == 1:
            offsets, kinds = (1, -1, 0), kinds + (wide, wide)
        mine = spread(offsets, kinds)
        if level == top // 2:
            marker = joined(down[1], mine[3])
            mine = list(mine[:3]) + [marker]
            down[1] = None
        up = [lax.ppermute(joined(up[i], mine[i]), "rows", forward) for i in range(2)]
        down = [lax.ppermute(joined(down[i], mine[2 + i]), "rows", backward) for i in range(2)]
    planes = [[4 * z + i for i in range(4)] for z in range(rows // 4)]
    lines = [[4 * z + i for z in range(rows // 4)] for i in range(4)]
    sums = after(lax.psum(sums, "rows", axis_index_groups=planes), marker)
    sums = lax.psum(sums, "rows", axis_index_groups=lines)
    grad_self, grad_neigh = sums[:hid, :every], sums[:hid, every:]
    grad_bias = lax.dynamic_slice_in_dim(sums[hid, :every], lax.axis_index("feat") * hid, hid)
    (grad_features,) = call(
        finish_kernel, "finish", [((hid, width), narrow)], [VMEM] * 7, [VMEM], [], 8, 0,
        8 * hid * width, self_own, mine[4], mine[5], up[0], down[0], up[1], down[1],
    )
    return (activation, grad_features, grad_self, grad_neigh, grad_bias)


def solution(mesh):
    in_specs = (
        P("feat", "rows"),
        P("rows", None, None, None),
        P("rows", None),
        P("feat", None),
        P("feat", None),
        P("feat"),
        P("feat", "rows"),
    )
    out_specs = (P("feat", "rows"), P("feat", "rows"), P("feat", None), P("feat", None), P("feat"))
    body = functools.partial(shards, mesh.shape["rows"], mesh.shape["feat"])
    return jax.shard_map(body, mesh=mesh, in_specs=in_specs, out_specs=out_specs, check_vma=False)
```

time: 465 us -> 189 us (0.41)
  waiting for transfers between devices: 285 us -> 70.2 us
  Pallas kernels: 0 us -> 51.2 us
  other arithmetic: 48.5 us -> 0 us
  local copies, waits for them, and re-layouts: 55.3 us -> 19.3 us
  blocking collectives: 33.9 us -> 0 us
  starting transfers between devices: 0.39 us -> 33.3 us
  matrix products: 26.2 us -> 0 us
    reduce_scatter x2 -> x0, waiting for transfers between devices: 191 us -> none  [the longest x1 161 us: shards(): lax.psum_scatter(spread_sum.reshape(hid_dev, all_nodes), 'rows', scatter_...]
    all_gather x2 -> x0, waiting for transfers between devices: 94.6 us -> none  [the longest x1 73.3 us: shards(): gathered = lax.all_gather(features, 'rows', axis=1, tiled=True)]
    pallas_call x0 -> x24, Pallas kernels: none -> 51.2 us  [call(): pl.pallas_call(kernel, out_shape=[jax.ShapeDtypeStruct(shape, kind) for s...]
    scatter-add x1 -> x0, other arithmetic: 40.1 us -> none  [shards(): spread_sum = spread_sum.at[:, flat_cols, :].add(contribs)]
    ppermute x0 -> x36, waiting for transfers between devices: none -> 36 us  [the longest x7 14.3 us: shards(): up[side] = lax.ppermute(up[side], 'rows', forward)]
    psum x1 -> x2, waiting for transfers between devices: 0.01 us -> 34.2 us  [the longest x1 22.5 us: shards(): sums = after(lax.psum(sums, 'rows', axis_index_groups=planes), marker)]
    psum x1 -> x0, blocking collectives: 33.9 us -> none  [shards(): lax.psum((local_self, local_neigh, local_bias), 'rows')]
    ppermute x0 -> x36, starting transfers between devices: none -> 33.2 us  [the longest x7 12.1 us: shards(): up[side] = lax.ppermute(up[side], 'rows', forward)]
  transfers between devices with their start and end apart: 5 -> 38, of which waited for: 4 -> 15; matrix products, arithmetic and copies ran while one was open for 18% -> 2% of each run, Pallas kernels for 0% -> 23%
where the time goes in v5:
time: 189 us; the launch traced here: 188 us
  waiting for transfers between devices  70.2 us (37%)
  Pallas kernels  51.2 us (27%)
  starting transfers between devices  33.3 us (18%)
  local copies, waits for them, and re-layouts  19.3 us (10%)
  between operations  14.3 us (8%)
    pallas_call x24, Pallas kernels, call(): pl.pallas_call(kernel, out_shape=[jax.ShapeDtypeStruct(shape, kind) for s...  51.2 us
    psum x1, waiting for transfers between devices, shards(): sums = after(lax.psum(sums, 'rows', axis_index_groups=planes), marker)  22.5 us
    unnamed x30, local copies, waits for them, and re-layouts  15.3 us
    ppermute x7, waiting for transfers between devices, shards(): up[side] = lax.ppermute(up[side], 'rows', forward)  14.3 us
    ppermute x7, starting transfers between devices, shards(): up[side] = lax.ppermute(up[side], 'rows', forward)  12.1 us
    psum x1, waiting for transfers between devices, shards(): sums = lax.psum(sums, 'rows', axis_index_groups=lines)  11.7 us
    ppermute x7, waiting for transfers between devices, shards(): down[side] = lax.ppermute(down[side], 'rows', backward)  9.6 us
    ppermute x6, starting transfers between devices, shards(): lax.ppermute(joined(up[i], mine[i]), 'rows', forward)  9.53 us
  transfers between devices with their start and end apart: 38, of which 15 were waited for; matrix products, arithmetic and copies ran while one was open for 2% of the time, Pallas kernels for 23%

profile of v5, /device:TPU:0, one launch (start us, length us, event | category | flops | bytes accessed | tf_op | source)
XLA Modules:
  0.0 188.3 jit_solution(3751198715839428226)
XLA Ops:
  8.8 2.7 %collective-permute-start = (bf16[64,2048]{1,0:T(8,128)(2,1)S(1)}, bf16[64,2048]{1,0:T(8,128)(2,1)S(1)}, u32[]{:S(2)}, u32[]{:S(2)}) collective-permute-start(bf16[64,2048]{1,0:T(8,128)(2,1)S(1)} %get-tuple-element.80.refs_0_), channel_id=1, source_target_pairs={{0,8},{2,10},{8,16},{10,18},{16,24},{18,26},{24,28},{26,30},{28,20... | collective-permute-start | bytes 786440 | tf_op jit(solution)/shard_map/ppermute | solution.py:331
  13.9 3.2 %table.1 = s32[384]{0:T(512)S(1)} custom-call(s32[16,12]{1,0:T(8,128)S(1)} %copy-done.13), custom_call_target="tpu_custom_call" | custom-call | bytes 1536 | tf_op jit(solution)/shard_map/table/pallas_call | solution.py:277
  21.8 1.9 %collective-permute-done.1.refs_3_ = bf16[64,2048]{1,0:T(8,128)(2,1)S(1)} collective-permute-done((bf16[64,2048]{1,0:T(8,128)(2,1)S(1)}, bf16[64,2048]{1,0:T(8,128)(2,1)S(1)}, u32[]{:S(2)}, u32[]{:S(2)}) %collective-permute-start.1) | collective-permute-done | bytes 262176 | tf_op jit(solution)/shard_map/ppermute | solution.py:331
  30.3 5.1 %collective-permute-done.6.refs_5_ = bf16[64,2048]{1,0:T(8,128)(2,1)S(1)} collective-permute-done((bf16[64,2048]{1,0:T(8,128)(2,1)S(1)}, bf16[64,2048]{1,0:T(8,128)(2,1)S(1)}, u32[]{:S(2)}, u32[]{:S(2)}) %collective-permute-start.6) | collective-permute-done | bytes 262176 | tf_op jit(solution)/shard_map/ppermute | solution.py:331
  37.5 5.2 %collective-permute-done.9.refs_8_ = bf16[64,2048]{1,0:T(8,128)(2,1)S(1)} collective-permute-done((bf16[64,2048]{1,0:T(8,128)(2,1)S(1)}, bf16[64,2048]{1,0:T(8,128)(2,1)S(1)}, u32[]{:S(2)}, u32[]{:S(2)}) %collective-permute-start.9) | collective-permute-done | bytes 262176 | tf_op jit(solution)/shard_map/ppermute | solution.py:335
  43.1 2.8 %copy-done.3 = bf16[16,12,128,128]{3,2,1,0:T(8,128)(2,1)S(1)} copy-done((bf16[16,12,128,128]{3,2,1,0:T(8,128)(2,1)S(1)}, bf16[16,12,128,128]{3,2,1,0:T(8,128)(2,1)}, u32[]{:S(2)}) %copy-start.3) | copy-done | bytes 6291480
  49.8 3.1 %collective-permute-done.13.refs_12_ = bf16[64,2048]{1,0:T(8,128)(2,1)S(1)} collective-permute-done((bf16[64,2048]{1,0:T(8,128)(2,1)S(1)}, bf16[64,2048]{1,0:T(8,128)(2,1)S(1)}, u32[]{:S(2)}, u32[]{:S(2)}) %collective-permute-start.13) | collective-permute-done | bytes 262176 | tf_op jit(solution)/shard_map/ppermute | solution.py:335
  53.4 2.1 %collective-permute-done.12.refs_11_ = bf16[64,2048]{1,0:T(8,128)(2,1)S(1)} collective-permute-done((bf16[64,2048]{1,0:T(8,128)(2,1)S(1)}, bf16[64,2048]{1,0:T(8,128)(2,1)S(1)}, u32[]{:S(2)}, u32[]{:S(2)}) %collective-permute-start.12) | collective-permute-done | bytes 262176 | tf_op jit(solution)/shard_map/ppermute | solution.py:331
  55.5 5.2 %collective-permute-done.15.refs_14_ = bf16[64,2048]{1,0:T(8,128)(2,1)S(1)} collective-permute-done((bf16[64,2048]{1,0:T(8,128)(2,1)S(1)}, bf16[64,2048]{1,0:T(8,128)(2,1)S(1)}, u32[]{:S(2)}, u32[]{:S(2)}) %collective-permute-start.15) | collective-permute-done | bytes 262176 | tf_op jit(solution)/shard_map/ppermute | solution.py:331
  60.7 6.7 %aggregate.3 = (bf16[64,2048]{1,0:T(8,128)(2,1)S(1)}, f32[1,2048]{1,0:T(1,128)}) custom-call(s32[384]{0:T(512)S(1)} %collective-permute-done.18.table.table_pair, bf16[16,12,128,128]{3,2,1,0:T(8,128)(2,1)} %collective-permute-done.4.tiles.pair, bf16[64,2048]{1,0:T(8,128)(2,1)S(1)} %get-tuple-element.80.refs_0_, ...), custom_call_target="tpu_custom_call" | custom-call | flops 402653184 | bytes 10485760 | tf_op jit(solution)/shard_map/aggregate/pallas_call | solution.py:277
  68.1 3.9 %aggregate.2 = (bf16[64,2048]{1,0:T(8,128)(2,1)S(1)}, f32[1,2048]{1,0:T(1,128)S(1)}) custom-call(s32[384]{0:T(512)S(1)} %table.1, bf16[16,12,128,128]{3,2,1,0:T(8,128)(2,1)S(1)} %load.1.tiles.adj, bf16[64,2048]{1,0:T(8,128)(2,1)S(1)} %get-tuple-element.80.refs_0_, bf16[64,2048]{1,0:T(8,128)(2,1)S(1)} %collective-permute-done.refs_1_, ...), custom_call_target="tpu_custom_call" | custom-call | flops 402653184 | bytes 10485760 | tf_op jit(solution)/shard_map/aggregate/pallas_call | solution.py:277
  75.6 6.2 %collective-permute-done.17.refs_1_ = bf16[64,2048]{1,0:T(8,128)(2,1)S(1)} collective-permute-done((bf16[64,2048]{1,0:T(8,128)(2,1)S(1)}, bf16[64,2048]{1,0:T(8,128)(2,1)S(1)}, u32[]{:S(2)}, u32[]{:S(2)}) %collective-permute-start.17) | collective-permute-done | bytes 262176 | tf_op jit(solution)/shard_map/ppermute | solution.py:58
  81.8 3.0 %middle.1 = (bf16[128,2048]{1,0:T(8,128)(2,1)}, bf16[256,2048]{1,0:T(8,128)(2,1)S(1)}, bf16[128,2048]{1,0:T(8,128)(2,1)S(1)}, bf16[128,2048]{1,0:T(8,128)(2,1)S(1)}) custom-call(bf16[256,256]{1,0:T(8,128)(2,1)S(1)} %get-tuple-element.43.turned, bf16[128,256]{1,0:T(8,128)(2,1)S(1)} %copy-done.10, f32[1,2048]{1,0:T(1,128)S(1)} %get-tuple-element.50.inverse, ...), custom_call_target="tpu_custom_call" | custom-call | flops 402653184 | bytes 7340032 | tf_op jit(solution)/shard_map/middle/pallas_call | solution.py:277
  84.8 1.9 %collective-permute-done.21.other = bf16[128,2048]{1,0:T(8,128)(2,1)S(1)} collective-permute-done((bf16[128,2048]{1,0:T(8,128)(2,1)S(1)}, bf16[128,2048]{1,0:T(8,128)(2,1)S(1)}, u32[]{:S(2)}, u32[]{:S(2)}) %collective-permute-start.21) | collective-permute-done | bytes 524320 | tf_op jit(solution)/shard_map/ppermute | solution.py:49
  86.9 3.4 %spread.5 = (bf16[64,2048]{1,0:T(8,128)(2,1)S(1)}, bf16[64,2048]{1,0:T(8,128)(2,1)S(1)}) custom-call(s32[384]{0:T(512)S(1)} %table.1, s32[384]{0:T(512)S(1)} %collective-permute-done.18.table.table_pair, bf16[16,12,128,128]{3,2,1,0:T(8,128)(2,1)S(1)} %load.1.tiles.adj, bf16[16,12,128,128]{3,2,1,0:T(8,128)(2,1)} %collective-permute-done.4.tiles.pair, ...), custom_call_target="tpu_custom_call" | custom-call | flops 100663296 | bytes 2097152 | tf_op jit(solution)/shard_map/spread/pallas_call | solution.py:277
  92.4 4.7 %spread.6 = (f32[64,2048]{1,0:T(8,128)S(1)}, bf16[64,2048]{1,0:T(8,128)(2,1)}, bf16[64,2048]{1,0:T(8,128)(2,1)}, f32[64,2048]{1,0:T(8,128)S(1)}) custom-call(s32[384]{0:T(512)S(1)} %table.1, s32[384]{0:T(512)S(1)} %collective-permute-done.18.table.table_pair, bf16[16,12,128,128]{3,2,1,0:T(8,128)(2,1)S(1)} %load.1.tiles.adj, ...), custom_call_target="tpu_custom_call" | custom-call | flops 201326592 | bytes 4194304 | tf_op jit(solution)/shard_map/spread/pallas_call | solution.py:277
  103.6 1.9 %weights.1 = (f32[128,2048]{1,0:T(8,128)S(1)}, f32[136,512]{1,0:T(8,128)}) custom-call(bf16[128,256]{1,0:T(8,128)(2,1)S(1)} %copy-done.12, bf16[128,2048]{1,0:T(8,128)(2,1)S(1)} %copy-done.5, bf16[128,2048]{1,0:T(8,128)(2,1)S(1)} %get-tuple-element.57.agg_own, bf16[256,2048]{1,0:T(8,128)(2,1)S(1)} %get-tuple-element.58.grad), custom_call_target="tpu_custom_call" | custom-call | flops 402653184 | bytes 5242880 | tf_op jit(solution)/shard_map/weights/pallas_call | solution.py:277
  105.6 2.8 %copy-done.1 = bf16[16,12,128,128]{3,2,1,0:T(8,128)(2,1)S(1)} copy-done((bf16[16,12,128,128]{3,2,1,0:T(8,128)(2,1)S(1)}, bf16[16,12,128,128]{3,2,1,0:T(8,128)(2,1)}, u32[]{:S(2)}) %copy-start.1) | copy-done | bytes 6291480
  108.4 4.0 %spread.7 = (f32[64,2048]{1,0:T(8,128)S(1)}, f32[64,2048]{1,0:T(8,128)S(1)}, f32[64,2048]{1,0:T(8,128)S(1)}, f32[64,2048]{1,0:T(8,128)S(1)}) custom-call(s32[384]{0:T(512)S(1)} %table.1, s32[384]{0:T(512)S(1)} %collective-permute-done.18.table.table_pair, bf16[16,12,128,128]{3,2,1,0:T(8,128)(2,1)S(1)} %copy-done.1, ...), custom_call_target="tpu_custom_call" | custom-call | flops 201326592 | bytes 4194304 | tf_op jit(solution)/shard_map/spread/pallas_call | solution.py:277
  114.2 22.5 %all-reduce.3.cloned.1.call-done = f32[136,512]{1,0:T(8,128)} async-done(((f32[136,512]{1,0:T(8,128)}), f32[136,512]{1,0:T(8,128)}) %all-reduce.3.cloned.1.call-update) | async-done | bytes 278544 | tf_op jit(solution)/shard_map/psum | solution.py:424
  147.1 2.8 %copy-done.2 = bf16[16,12,128,128]{3,2,1,0:T(8,128)(2,1)S(1)} copy-done((bf16[16,12,128,128]{3,2,1,0:T(8,128)(2,1)S(1)}, bf16[16,12,128,128]{3,2,1,0:T(8,128)(2,1)}, u32[]{:S(2)}) %copy-start.2) | copy-done | bytes 6291480
  149.8 4.6 %spread.4 = (f32[64,2048]{1,0:T(8,128)S(1)}, f32[64,2048]{1,0:T(8,128)S(1)}, f32[64,2048]{1,0:T(8,128)S(1)}, f32[64,2048]{1,0:T(8,128)S(1)}, f32[64,2048]{1,0:T(8,128)S(1)}, /*index=5*/f32[64,2048]{1,0:T(8,128)S(1)}) custom-call(s32[384]{0:T(512)S(1)} %table.1, s32[384]{0:T(512)S(1)} %collective-permute-done.18.table.table_pair, ...), custom_call_target="tpu_custom_call" | custom-call | flops 301989888 | bytes 6291456 | tf_op jit(solution)/shard_map/spread/pallas_call | solution.py:277
  163.8 2.0 %collective-permute-start.25 = (bf16[64,2048]{1,0:T(8,128)(2,1)}, bf16[64,2048]{1,0:T(8,128)(2,1)S(1)}, u32[]{:S(2)}, u32[]{:S(2)}) collective-permute-start(bf16[64,2048]{1,0:T(8,128)(2,1)} %join.12), channel_id=1, source_target_pairs={{0,8},{2,10},{8,16},{10,18},{16,24},{18,26},{24,28},{26,30},{28,20... | collective-permute-start | bytes 786440 | tf_op jit(solution)/shard_map/ppermute | solution.py:420
  165.8 11.7 %all-reduce.5.cloned.1.call-done = f32[136,512]{1,0:T(8,128)} async-done(((f32[136,512]{1,0:T(8,128)}), f32[136,512]{1,0:T(8,128)}) %all-reduce.5.cloned.1.call-update) | async-done | bytes 278544 | tf_op jit(solution)/shard_map/psum | solution.py:425
  (112 shorter events, 60.7 us)
Async XLA Ops:
  7.2 129.6 %all-reduce.3.cloned.1.call-start = ((), (), s32[]{:S(2)}) async-start(), calls=%async_computation | async-start | bytes 557056 | tf_op jit(solution)/shard_map/psum | solution.py:424
  7.2 17.5 %collective-permute-start.4 = (bf16[16,12,128,128]{3,2,1,0:T(8,128)(2,1)}, bf16[16,12,128,128]{3,2,1,0:T(8,128)(2,1)}, u32[]{:S(2)}, u32[]{:S(2)}) collective-permute-start(bf16[16,12,128,128]{3,2,1,0:T(8,128)(2,1)} %source.1), channel_id=1, source_target_pairs={{0,2},{2,0},{4,6},{6,4},{8,10},{10,8},{12,14},{14,12},{16,18},{18,... | collective-permute-start | bytes 18874376 | tf_op jit(solution)/shard_map/ppermute | solution.py:49
  8.8 13.0 %collective-permute-start = (bf16[64,2048]{1,0:T(8,128)(2,1)S(1)}, bf16[64,2048]{1,0:T(8,128)(2,1)S(1)}, u32[]{:S(2)}, u32[]{:S(2)}) collective-permute-start(bf16[64,2048]{1,0:T(8,128)(2,1)S(1)} %get-tuple-element.80.refs_0_), channel_id=1, source_target_pairs={{0,8},{2,10},{8,16},{10,18},{16,24},{18,26},{24,28},{26,30},{28,20... | collective-permute-start | bytes 786440 | tf_op jit(solution)/shard_map/ppermute | solution.py:331
  11.5 12.3 %collective-permute-start.1 = (bf16[64,2048]{1,0:T(8,128)(2,1)S(1)}, bf16[64,2048]{1,0:T(8,128)(2,1)S(1)}, u32[]{:S(2)}, u32[]{:S(2)}) collective-permute-start(bf16[64,2048]{1,0:T(8,128)(2,1)S(1)} %get-tuple-element.49), channel_id=1, source_target_pairs={{0,10},{2,8},{8,18},{10,16},{16,26},{18,24},{24,30},{26,28},{28,22... | collective-permute-start | bytes 786440 | tf_op jit(solution)/shard_map/ppermute | solution.py:331
  13.0 11.7 %collective-permute-start.3 = (bf16[64,2048]{1,0:T(8,128)(2,1)S(1)}, bf16[64,2048]{1,0:T(8,128)(2,1)S(1)}, u32[]{:S(2)}, u32[]{:S(2)}) collective-permute-start(bf16[64,2048]{1,0:T(8,128)(2,1)S(1)} %get-tuple-element.49), channel_id=1, source_target_pairs={{0,6},{2,4},{8,2},{10,0},{16,10},{18,8},{24,18},{26,16},{28,26},{3... | collective-permute-start | bytes 786440 | tf_op jit(solution)/shard_map/ppermute | solution.py:335
  24.7 48.8 %collective-permute-start.5 = (bf16[128,4736]{1,0:T(8,128)(2,1)S(1)}, bf16[128,4736]{1,0:T(8,128)(2,1)S(1)}, u32[]{:S(2)}, u32[]{:S(2)}) collective-permute-start(bf16[128,4736]{1,0:T(8,128)(2,1)S(1)} %pack.1.refs_0_), channel_id=1, source_target_pairs={{0,1},{1,0},{2,3},{3,2},{4,5},{5,4},{6,7},{7,6},{8,9},{9,8},{10,11... | collective-permute-start | bytes 3637256 | tf_op jit(solution)/shard_map/ppermute | solution.py:58
  28.3 14.3 %collective-permute-start.9 = (bf16[64,2048]{1,0:T(8,128)(2,1)S(1)}, bf16[64,2048]{1,0:T(8,128)(2,1)S(1)}, u32[]{:S(2)}, u32[]{:S(2)}) collective-permute-start(bf16[64,2048]{1,0:T(8,128)(2,1)S(1)} %collective-permute-done.3.refs_4_), channel_id=1, source_target_pairs={{0,4},{2,6},{8,0},{10,2},{16,8},{18,10},{24,16},{26,18},{28,24},{3... | collective-permute-start | bytes 786440 | tf_op jit(solution)/shard_map/ppermute | solution.py:335
  28.8 14.3 %collective-permute-start.8 = (bf16[64,2048]{1,0:T(8,128)(2,1)S(1)}, bf16[64,2048]{1,0:T(8,128)(2,1)S(1)}, u32[]{:S(2)}, u32[]{:S(2)}) collective-permute-start(bf16[64,2048]{1,0:T(8,128)(2,1)S(1)} %collective-permute-done.1.refs_3_), channel_id=1, source_target_pairs={{0,8},{2,10},{8,16},{10,18},{16,24},{18,26},{24,28},{26,30},{28,20... | collective-permute-start | bytes 786440 | tf_op jit(solution)/shard_map/ppermute | solution.py:331
  35.4 10.9 %collective-permute-start.10 = (bf16[64,2048]{1,0:T(8,128)(2,1)S(1)}, bf16[64,2048]{1,0:T(8,128)(2,1)S(1)}, u32[]{:S(2)}, u32[]{:S(2)}) collective-permute-start(bf16[64,2048]{1,0:T(8,128)(2,1)S(1)} %collective-permute-done.6.refs_5_), channel_id=1, source_target_pairs={{0,8},{2,10},{8,16},{10,18},{16,24},{18,26},{24,28},{26,30},{28,20... | collective-permute-start | bytes 786440 | tf_op jit(solution)/shard_map/ppermute | solution.py:331
  37.0 11.2 %collective-permute-start.11 = (bf16[64,2048]{1,0:T(8,128)(2,1)S(1)}, bf16[64,2048]{1,0:T(8,128)(2,1)S(1)}, u32[]{:S(2)}, u32[]{:S(2)}) collective-permute-start(bf16[64,2048]{1,0:T(8,128)(2,1)S(1)} %collective-permute-done.7.refs_6_), channel_id=1, source_target_pairs={{0,4},{2,6},{8,0},{10,2},{16,8},{18,10},{24,16},{26,18},{28,24},{3... | collective-permute-start | bytes 786440 | tf_op jit(solution)/shard_map/ppermute | solution.py:335
  48.2 12.5 %collective-permute-start.15 = (bf16[64,2048]{1,0:T(8,128)(2,1)S(1)}, bf16[64,2048]{1,0:T(8,128)(2,1)S(1)}, u32[]{:S(2)}, u32[]{:S(2)}) collective-permute-start(bf16[64,2048]{1,0:T(8,128)(2,1)S(1)} %collective-permute-done.10.refs_9_), channel_id=1, source_target_pairs={{0,8},{2,10},{8,16},{10,18},{16,24},{18,26},{24,28},{26,30},{28,20... | collective-permute-start | bytes 786440 | tf_op jit(solution)/shard_map/ppermute | solution.py:331
  98.8 14.5 %collective-permute-start.33 = (bf16[64,2048]{1,0:T(8,128)(2,1)S(1)}, bf16[64,2048]{1,0:T(8,128)(2,1)}, u32[]{:S(2)}, u32[]{:S(2)}) collective-permute-start(bf16[64,2048]{1,0:T(8,128)(2,1)S(1)} %join.17), channel_id=1, source_target_pairs={{0,4},{2,6},{8,0},{10,2},{16,8},{18,10},{24,16},{26,18},{28,24},{3... | collective-permute-start | bytes 786440 | tf_op jit(solution)/shard_map/ppermute | solution.py:421
  99.3 37.4 %collective-permute-start.29 = (bf16[64,2048]{1,0:T(8,128)(2,1)}, bf16[64,2048]{1,0:T(8,128)(2,1)}, u32[]{:S(2)}, u32[]{:S(2)}) collective-permute-start(bf16[64,2048]{1,0:T(8,128)(2,1)} %get-tuple-element.70), channel_id=1, source_target_pairs={{0,8},{2,10},{8,16},{10,18},{16,24},{18,26},{24,28},{26,30},{28,20... | collective-permute-start | bytes 786440 | tf_op jit(solution)/shard_map/ppermute | solution.py:420
  100.8 40.2 %collective-permute-start.26 = (bf16[64,2048]{1,0:T(8,128)(2,1)}, bf16[64,2048]{1,0:T(8,128)(2,1)}, u32[]{:S(2)}, u32[]{:S(2)}) collective-permute-start(bf16[64,2048]{1,0:T(8,128)(2,1)} %get-tuple-element.67), channel_id=1, source_target_pairs={{0,4},{2,6},{8,0},{10,2},{16,8},{18,10},{24,16},{26,18},{28,24},{3... | collective-permute-start | bytes 786440 | tf_op jit(solution)/shard_map/ppermute | solution.py:421
  102.1 41.7 %collective-permute-start.23 = (bf16[64,2048]{1,0:T(8,128)(2,1)}, bf16[64,2048]{1,0:T(8,128)(2,1)}, u32[]{:S(2)}, u32[]{:S(2)}) collective-permute-start(bf16[64,2048]{1,0:T(8,128)(2,1)} %join.10), channel_id=1, source_target_pairs={{0,8},{2,10},{8,16},{10,18},{16,24},{18,26},{24,28},{26,30},{28,20... | collective-permute-start | bytes 786440 | tf_op jit(solution)/shard_map/ppermute | solution.py:420
  105.5 72.0 %all-reduce.5.cloned.1.call-start = ((), (), s32[]{:S(2)}) async-start(), calls=%async_computation.1 | async-start | bytes 557056 | tf_op jit(solution)/shard_map/psum | solution.py:425
  139.6 14.9 %collective-permute-start.30 = (bf16[64,2048]{1,0:T(8,128)(2,1)}, bf16[64,2048]{1,0:T(8,128)(2,1)}, u32[]{:S(2)}, u32[]{:S(2)}) collective-permute-start(bf16[64,2048]{1,0:T(8,128)(2,1)} %join.15), channel_id=1, source_target_pairs={{0,8},{2,10},{8,16},{10,18},{16,24},{18,26},{24,28},{26,30},{28,20... | collective-permute-start | bytes 786440 | tf_op jit(solution)/shard_map/ppermute | solution.py:420
  142.8 14.9 %collective-permute-start.27 = (bf16[64,2048]{1,0:T(8,128)(2,1)}, bf16[64,2048]{1,0:T(8,128)(2,1)}, u32[]{:S(2)}, u32[]{:S(2)}) collective-permute-start(bf16[64,2048]{1,0:T(8,128)(2,1)} %join.13), channel_id=1, source_target_pairs={{0,4},{2,6},{8,0},{10,2},{16,8},{18,10},{24,16},{26,18},{28,24},{3... | collective-permute-start | bytes 786440 | tf_op jit(solution)/shard_map/ppermute | solution.py:421
  143.3 17.7 %collective-permute-start.34 = (bf16[64,2048]{1,0:T(8,128)(2,1)S(1)}, bf16[64,2048]{1,0:T(8,128)(2,1)}, u32[]{:S(2)}, u32[]{:S(2)}) collective-permute-start(bf16[64,2048]{1,0:T(8,128)(2,1)S(1)} %join.18), channel_id=1, source_target_pairs={{0,4},{2,6},{8,0},{10,2},{16,8},{18,10},{24,16},{26,18},{28,24},{3... | collective-permute-start | bytes 786440 | tf_op jit(solution)/shard_map/ppermute | solution.py:421
  145.5 16.6 %collective-permute-start.24 = (bf16[64,2048]{1,0:T(8,128)(2,1)}, bf16[64,2048]{1,0:T(8,128)(2,1)}, u32[]{:S(2)}, u32[]{:S(2)}) collective-permute-start(bf16[64,2048]{1,0:T(8,128)(2,1)} %join.11), channel_id=1, source_target_pairs={{0,8},{2,10},{8,16},{10,18},{16,24},{18,26},{24,28},{26,30},{28,20... | collective-permute-start | bytes 786440 | tf_op jit(solution)/shard_map/ppermute | solution.py:420
  156.2 24.3 %collective-permute-start.31 = (bf16[64,2048]{1,0:T(8,128)(2,1)}, bf16[64,2048]{1,0:T(8,128)(2,1)S(1)}, u32[]{:S(2)}, u32[]{:S(2)}) collective-permute-start(bf16[64,2048]{1,0:T(8,128)(2,1)} %join.16), channel_id=1, source_target_pairs={{0,8},{2,10},{8,16},{10,18},{16,24},{18,26},{24,28},{26,30},{28,20... | collective-permute-start | bytes 786440 | tf_op jit(solution)/shard_map/ppermute | solution.py:420
  159.4 21.0 %collective-permute-start.28 = (bf16[64,2048]{1,0:T(8,128)(2,1)}, bf16[64,2048]{1,0:T(8,128)(2,1)S(1)}, u32[]{:S(2)}, u32[]{:S(2)}) collective-permute-start(bf16[64,2048]{1,0:T(8,128)(2,1)} %join.14), channel_id=1, source_target_pairs={{0,4},{2,6},{8,0},{10,2},{16,8},{18,10},{24,16},{26,18},{28,24},{3... | collective-permute-start | bytes 786440 | tf_op jit(solution)/shard_map/ppermute | solution.py:421
  162.0 18.4 %collective-permute-start.35 = (bf16[64,2048]{1,0:T(8,128)(2,1)S(1)}, bf16[64,2048]{1,0:T(8,128)(2,1)S(1)}, u32[]{:S(2)}, u32[]{:S(2)}) collective-permute-start(bf16[64,2048]{1,0:T(8,128)(2,1)S(1)} %join.19), channel_id=1, source_target_pairs={{0,4},{2,6},{8,0},{10,2},{16,8},{18,10},{24,16},{26,18},{28,24},{3... | collective-permute-start | bytes 786440 | tf_op jit(solution)/shard_map/ppermute | solution.py:421
  163.8 16.6 %collective-permute-start.25 = (bf16[64,2048]{1,0:T(8,128)(2,1)}, bf16[64,2048]{1,0:T(8,128)(2,1)S(1)}, u32[]{:S(2)}, u32[]{:S(2)}) collective-permute-start(bf16[64,2048]{1,0:T(8,128)(2,1)} %join.12), channel_id=1, source_target_pairs={{0,8},{2,10},{8,16},{10,18},{16,24},{18,26},{24,28},{26,30},{28,20... | collective-permute-start | bytes 786440 | tf_op jit(solution)/shard_map/ppermute | solution.py:420
  (29 other events, 198.2 us)
Sparse Core Ops, SparseCore 0:
  105.7 31.0 all-reduce.2
  139.1 38.3 all-reduce.4

commit v6 on v5

--- a/solution.py
+++ b/solution.py
@@ -214,15 +214,48 @@
         act[:, lane] = value[own].astype(jnp.bfloat16)
 
 
+def own_quarter():
+    row = lax.axis_index("rows")
+    return 2 * lax.rem(row, 2) + lax.rem(row // 2, 2)
+
+
+def turned_quarter(mine, index):
+    both = (index // 2, index % 2)
+    core = both[0] + mine // 2 - 2 * both[0] * (mine // 2)
+    x = both[1] + lax.rem(mine, 2) - 2 * both[1] * lax.rem(mine, 2)
+    return 2 * core + x
+
+
 def weights_kernel(ws, x_own, agg_own, grad, self_own, sums):
     hid, every = ws.shape
     g = grad[...]
     self_own[...] = product(ws[...], g)
-    sums[:hid, :every] = product(x_own[...], g, LAST)
-    sums[:hid, every:] = product(agg_own[...], g, LAST)
+    wide = every // 2
+    mine = own_quarter()
+    values = [product(x_own[...], g, LAST), product(agg_own[...], g, LAST)]
     total = product(jnp.ones((8, g.shape[1]), jnp.bfloat16), g, LAST)
-    sums[hid:, :every] = total
-    sums[hid:, every:] = total
+    for quarter in range(4):
+        slot = turned_quarter(mine, quarter)
+        lane = slice(quarter % 2 * wide, (quarter % 2 + 1) * wide)
+        sums[slot, :hid] = values[quarter // 2][:, lane]
+        sums[slot, hid:] = total[:, lane]
+
+
+def collect_kernel(pair, pair_far, grad_self, grad_neigh, sums):
+    hid, every = grad_self.shape
+    wide = every // 2
+    mine = own_quarter()
+    for slot in range(4):
+        value = (pair, pair_far)[slot // 2][slot % 2]
+        quarter = turned_quarter(mine, slot)
+        for q, out in enumerate((grad_self, grad_self, grad_neigh, grad_neigh)):
+
+            @pl.when(quarter == q)
+            def _():
+                lane = slice(q % 2 * wide, (q % 2 + 1) * wide)
+                out[:, lane] = value[:hid]
+                if q < 2:
+                    sums[:, lane] = value[hid:]
 
 
 def arrange_kernel(own, other, held):
@@ -303,26 +336,30 @@
     pair = swap(adjacency, rows)
     (table,) = call(
         table_kernel, "table", [((tile_cols.size + rows * CAP,), jnp.int32)], [SMEM], [SMEM],
-        [pltpu.SMEM((rows,), jnp.int32)], 4, 0, 8 * rows * CAP, tile_cols,
+        [pltpu.SMEM((rows,), jnp.int32)], 2, 0, 8 * rows * CAP, tile_cols,
     )
     packed = 2 * width + 2 * every + 128
     (pack,) = call(
         pack_kernel, "pack", [((hid, packed), narrow)], [HBM] * 4 + [VMEM], [VMEM],
-        [pltpu.VMEM((hid, 128), narrow), pltpu.SemaphoreType.DMA((5,))], 6, 0,
+        [pltpu.VMEM((hid, 128), narrow), pltpu.SemaphoreType.DMA((5,))], 4, 0,
         4 * hid * packed,
         features, grad_output, self_weight, neigh_weight, bias_vector.reshape(1, hid),
     )
     (tiles,) = call(
         load_kernel, "load", [(adjacency.shape, narrow)], [HBM], [VMEM],
-        [pltpu.SemaphoreType.DMA], 4, 0, 4 * adjacency.size, adjacency,
+        [pltpu.SemaphoreType.DMA], 2, 0, 4 * adjacency.size, adjacency,
     )
     for step in range(1, top + 1):
         if step == 2:
-            up, down, pair, table, pack = lax.optimization_barrier((up, down, pair, table, pack))
-            table_pair = swap(table, rows)
+            up[1], down[1], pair, pack, tiles = lax.optimization_barrier(
+                (up[1], down[1], pair, pack, tiles)
+            )
             packs = [pack] + [send(pack, k, 0, rows, feats) for k in range(1, feats)]
+        if step == 3:
+            up[1], table = lax.optimization_barrier((up[1], table))
         if step == top:
-            sources.append(swap(after(away, up[0], down[0], tiles), rows))
+            table_pair = swap(after(table, up[0], down[0]), rows)
+            sources.append(swap(after(away, up[0], down[0]), rows))
             wanted.append((0, 1))
         for side in range(2):
             flip = side if step == 1 else 0
@@ -342,7 +379,7 @@
             [((half, width), narrow), ((1, width), wide)],
             [SMEM, VMEM] + [HBM] * len(sources), [VMEM] * 2,
             [pltpu.VMEM((rows, half, width), narrow), pltpu.SemaphoreType.DMA((len(sources),))],
-            12, hid * adjacency.size, 2 * adjacency.size + rows * hid * width,
+            11, hid * adjacency.size, 2 * adjacency.size + rows * hid * width,
             columns, values, *sources,
         )
 
@@ -360,25 +397,25 @@
             pltpu.VMEM((every, 1), wide),
             pltpu.VMEM((every, width), narrow),
         ],
-        12, 2 * every * every * width, 4 * every * packed, *packs,
+        8, 2 * every * every * width, 4 * every * packed, *packs,
     )
     activation, grad, scaled, agg_own = call(
         bind(middle_kernel, feats), "middle",
         [((hid, width), narrow), ((every, width), narrow)] + [((hid, width), narrow)] * 2,
         [VMEM] * (5 + 2 * feats), [VMEM] * 4,
-        [pltpu.VMEM((every, width), narrow), pltpu.VMEM((every, min(width, 256)), wide)], 12,
+        [pltpu.VMEM((every, width), narrow), pltpu.VMEM((every, min(width, 256)), wide)], 9,
         3 * every * every * width, 14 * every * width,
         turned, neigh_weight, inverse, base, cot_all, *near, *far,
     )
     scaled_pair = swap(scaled, rows)
     self_own, sums = call(
-        weights_kernel, "weights", [((hid, width), wide), ((hid + 8, 2 * every), wide)],
-        [VMEM] * 4, [VMEM] * 2, [], 12, 6 * hid * every * width, 10 * every * width,
+        weights_kernel, "weights", [((hid, width), wide), ((4, hid + 8, every // 2), wide)],
+        [VMEM] * 4, [VMEM] * 2, [], 6, 6 * hid * every * width, 10 * every * width,
         self_weight, features, agg_own, grad,
     )
     (held,) = call(
         arrange_kernel, "arrange", [((2, blocks + 1, hid, tile), narrow)],
-        [VMEM] * 2, [VMEM], [], 8, 0, 8 * hid * width, scaled, scaled_pair,
+        [VMEM] * 2, [VMEM], [], 4, 0, 8 * hid * width, scaled, scaled_pair,
     )
 
     def spread(offsets, kinds):
@@ -387,7 +424,7 @@
             bind(spread_kernel, (rows, offsets, kinds)), "spread",
             [((half, width), kind) for kind in kinds],
             [SMEM] * 2 + [VMEM] * 3, [VMEM] * len(kinds), [pltpu.VMEM((hid, width), wide)],
-            8, 2 * n * hid * tile * tile, 8 * hid * width * len(offsets),
+            9, 2 * n * hid * tile * tile, 8 * hid * width * len(offsets),
             table, table_pair, tiles, pair, held,
         )
 
@@ -395,38 +432,54 @@
         if arrived is None:
             return mine
         (out,) = call(
-            join_kernel, "join", [((half, width), narrow)], [VMEM] * 2, [VMEM], [], 8,
+            join_kernel, "join", [((half, width), narrow)], [VMEM] * 2, [VMEM], [], 3,
             0, 4 * hid * width, arrived, mine,
         )
         return out
+
+    near = sums[:2] + swap(sums[2:], rows, 1)
+    total = near[0] + swap(near[1], rows, 2)
+    bit, sends = 4, 0
+
+    def ring(value, pairs):
+        nonlocal total, bit, sends
+        sends += 1
+        if sends >= 5 and sends % 4 == 1 and bit < 2 * rows:
+            value = after(value, total)
+            total = after(total, value)
+            if bit < rows:
+                total = total + swap(total, rows, bit)
+            bit *= 2
+        return lax.ppermute(value, "rows", pairs)
 
     up, down = [None, None], [None, None]
     forward, backward = ring_pairs(rows, 1), ring_pairs(rows, -1)
     for level in range(top, 0, -1):
         if level == top:
             low, high = spread((top,), (narrow, narrow))
-            up[0] = lax.ppermute(low, "rows", forward)
-            down[1] = lax.ppermute(high, "rows", backward)
+            up[0] = ring(low, forward)
+            down[1] = ring(high, backward)
             continue
         kinds = tuple(narrow if arrived is None else wide for arrived in up + down)
         offsets = (level, -level)
         if level == 1:
             offsets, kinds = (1, -1, 0), kinds + (wide, wide)
         mine = spread(offsets, kinds)
-        if level == top // 2:
-            marker = joined(down[1], mine[3])
-            mine = list(mine[:3]) + [marker]
-            down[1] = None
-        up = [lax.ppermute(joined(up[i], mine[i]), "rows", forward) for i in range(2)]
-        down = [lax.ppermute(joined(down[i], mine[2 + i]), "rows", backward) for i in range(2)]
-    planes = [[4 * z + i for i in range(4)] for z in range(rows // 4)]
-    lines = [[4 * z + i for z in range(rows // 4)] for i in range(4)]
-    sums = after(lax.psum(sums, "rows", axis_index_groups=planes), marker)
-    sums = lax.psum(sums, "rows", axis_index_groups=lines)
-    grad_self, grad_neigh = sums[:hid, :every], sums[:hid, every:]
-    grad_bias = lax.dynamic_slice_in_dim(sums[hid, :every], lax.axis_index("feat") * hid, hid)
+        first = [i for i in range(2) if up[i] is None]
+        for i in first + [i for i in range(2) if i not in first]:
+            flow = 1 - i
+            up[i] = ring(joined(up[i], mine[i]), forward)
+            down[flow] = ring(joined(down[flow], mine[2 + flow]), backward)
+    near = jnp.stack([total, swap(total, rows, 2)])
+    far = swap(near, rows, 1)
+    grad_self, grad_neigh, total = call(
+        collect_kernel, "collect",
+        [((hid, every), wide), ((hid, every), wide), ((8, every), wide)],
+        [VMEM] * 2, [VMEM] * 3, [], 4, 0, 16 * hid * every, near, far,
+    )
+    grad_bias = lax.dynamic_slice_in_dim(total[0], lax.axis_index("feat") * hid, hid)
     (grad_features,) = call(
-        finish_kernel, "finish", [((hid, width), narrow)], [VMEM] * 7, [VMEM], [], 8, 0,
+        finish_kernel, "finish", [((hid, width), narrow)], [VMEM] * 7, [VMEM], [], 6, 0,
         8 * hid * width, self_own, mine[4], mine[5], up[0], down[0], up[1], down[1],
     )
     return (activation, grad_features, grad_self, grad_neigh, grad_bias)

time: 189 us -> 138 us (0.73)
  waiting for transfers between devices: 70.2 us -> 46.8 us
  local copies, waits for them, and re-layouts: 19.3 us -> 5.13 us
  between operations: 14.3 us -> 0.92 us
  Pallas kernels: 51.2 us -> 40.9 us
  starting transfers between devices: 33.3 us -> 43.4 us
    psum x2 -> x0, waiting for transfers between devices: 34.2 us -> none  [the longest x1 22.5 us: shards(): sums = after(lax.psum(sums, 'rows', axis_index_groups=planes), marker)]
    ppermute x4 -> x10, waiting for transfers between devices: 1.92 us -> 14.2 us  [swap(): return lax.ppermute(value, 'rows', [(r, r ^ bit) for r in range(rows)])]
    unnamed x30 -> x14, local copies, waits for them, and re-layouts: 15.3 us -> 3.54 us
    pallas_call x24 -> x25, Pallas kernels: 51.2 us -> 40.9 us  [call(): pl.pallas_call(kernel, out_shape=[jax.ShapeDtypeStruct(shape, kind) for s...]
    ppermute x7, starting transfers between devices: 2.52 us -> 11.8 us  [shards(): down[side] = lax.ppermute(down[side], 'rows', backward)]
    ppermute x4 -> x10, starting transfers between devices: 0.53 us -> 6.96 us  [swap(): return lax.ppermute(value, 'rows', [(r, r ^ bit) for r in range(rows)])]
    ppermute x7, starting transfers between devices: 12.1 us -> 5.96 us  [shards(): up[side] = lax.ppermute(up[side], 'rows', forward)]
    ppermute x7, waiting for transfers between devices: 14.3 us -> 10.8 us  [shards(): up[side] = lax.ppermute(up[side], 'rows', forward)]
  transfers between devices with their start and end apart: 38 -> 42, of which waited for: 15 -> 17; matrix products, arithmetic and copies ran while one was open for 2% -> 1% of each run, Pallas kernels for 23% -> 26%
where the time goes in v6:
time: 138 us; the launch traced here: 137 us
  waiting for transfers between devices  46.8 us (34%)
  starting transfers between devices  43.4 us (31%)
  Pallas kernels  40.9 us (30%)
  local copies, waits for them, and re-layouts  5.13 us (4%)
    pallas_call x25, Pallas kernels, call(): pl.pallas_call(kernel, out_shape=[jax.ShapeDtypeStruct(shape, kind) for s...  40.9 us
    ppermute x14, starting transfers between devices, ring(): return lax.ppermute(value, 'rows', pairs)  14.8 us
    ppermute x10, waiting for transfers between devices, swap(): return lax.ppermute(value, 'rows', [(r, r ^ bit) for r in range(rows)])  14.2 us
    ppermute x7, waiting for transfers between devices, shards(): down[side] = lax.ppermute(down[side], 'rows', backward)  12.3 us
    ppermute x7, starting transfers between devices, shards(): down[side] = lax.ppermute(down[side], 'rows', backward)  11.8 us
    ppermute x7, waiting for transfers between devices, shards(): up[side] = lax.ppermute(up[side], 'rows', forward)  10.8 us
    ppermute x10, starting transfers between devices, swap(): return lax.ppermute(value, 'rows', [(r, r ^ bit) for r in range(rows)])  6.96 us
    ppermute x4, waiting for transfers between devices, send(): return lax.ppermute(value, ('rows', 'feat'), pairs)  6.88 us
  transfers between devices with their start and end apart: 42, of which 17 were waited for; matrix products, arithmetic and copies ran while one was open for 1% of the time, Pallas kernels for 26%

profile of v6, /device:TPU:0, one launch (start us, length us, event | category | flops | bytes accessed | tf_op | source)
XLA Modules:
  0.0 137.2 jit_solution(11672635166367007078)
XLA Ops:
  2.2 2.7 %collective-permute-start.1 = (bf16[64,2048]{1,0:T(8,128)(2,1)S(1)}, bf16[64,2048]{1,0:T(8,128)(2,1)S(1)}, u32[]{:S(2)}, u32[]{:S(2)}) collective-permute-start(bf16[64,2048]{1,0:T(8,128)(2,1)S(1)} %get-tuple-element.58), channel_id=1, source_target_pairs={{0,6},{2,4},{8,2},{10,0},{16,10},{18,8},{24,18},{26,16},{28,26},{3... | collective-permute-start | bytes 786440 | tf_op jit(solution)/shard_map/ppermute | solution.py:372
  7.1 2.8 %copy-done = bf16[16,12,128,128]{3,2,1,0:T(8,128)(2,1)S(1)} copy-done((bf16[16,12,128,128]{3,2,1,0:T(8,128)(2,1)S(1)}, bf16[16,12,128,128]{3,2,1,0:T(8,128)(2,1)}, u32[]{:S(2)}) %copy-start) | copy-done | bytes 6291480
  14.8 2.7 %collective-permute-done.6.refs_2_ = bf16[64,2048]{1,0:T(8,128)(2,1)S(1)} collective-permute-done((bf16[64,2048]{1,0:T(8,128)(2,1)S(1)}, bf16[64,2048]{1,0:T(8,128)(2,1)S(1)}, u32[]{:S(2)}, u32[]{:S(2)}) %collective-permute-start.6) | collective-permute-done | bytes 262176 | tf_op jit(solution)/shard_map/ppermute | solution.py:372
  21.1 5.5 %collective-permute-done.8.refs_6_ = bf16[64,2048]{1,0:T(8,128)(2,1)S(1)} collective-permute-done((bf16[64,2048]{1,0:T(8,128)(2,1)S(1)}, bf16[64,2048]{1,0:T(8,128)(2,1)S(1)}, u32[]{:S(2)}, u32[]{:S(2)}) %collective-permute-start.8) | collective-permute-done | bytes 262176 | tf_op jit(solution)/shard_map/ppermute | solution.py:372
  30.4 1.9 %collective-permute-done.9.refs_8_ = bf16[64,2048]{1,0:T(8,128)(2,1)S(1)} collective-permute-done((bf16[64,2048]{1,0:T(8,128)(2,1)S(1)}, bf16[64,2048]{1,0:T(8,128)(2,1)S(1)}, u32[]{:S(2)}, u32[]{:S(2)}) %collective-permute-start.9) | collective-permute-done | bytes 262176 | tf_op jit(solution)/shard_map/ppermute | solution.py:372
  33.9 3.2 %table.1 = s32[384]{0:T(512)S(1)} custom-call(s32[16,12]{1,0:T(8,128)S(1)} %copy-done.5), custom_call_target="tpu_custom_call" | custom-call | bytes 1536 | tf_op jit(solution)/shard_map/table/pallas_call | solution.py:310
  43.6 3.4 %collective-permute-done.15.refs_14_ = bf16[64,2048]{1,0:T(8,128)(2,1)S(1)} collective-permute-done((bf16[64,2048]{1,0:T(8,128)(2,1)S(1)}, bf16[64,2048]{1,0:T(8,128)(2,1)S(1)}, u32[]{:S(2)}, u32[]{:S(2)}) %collective-permute-start.15) | collective-permute-done | bytes 262176 | tf_op jit(solution)/shard_map/ppermute | solution.py:368
  47.0 5.2 %collective-permute-done.12.refs_11_ = bf16[64,2048]{1,0:T(8,128)(2,1)S(1)} collective-permute-done((bf16[64,2048]{1,0:T(8,128)(2,1)S(1)}, bf16[64,2048]{1,0:T(8,128)(2,1)S(1)}, u32[]{:S(2)}, u32[]{:S(2)}) %collective-permute-start.12) | collective-permute-done | bytes 262176 | tf_op jit(solution)/shard_map/ppermute | solution.py:368
  52.2 3.8 %aggregate.2 = (bf16[64,2048]{1,0:T(8,128)(2,1)S(1)}, f32[1,2048]{1,0:T(1,128)S(1)}) custom-call(s32[384]{0:T(512)S(1)} %table.1, bf16[16,12,128,128]{3,2,1,0:T(8,128)(2,1)S(1)} %load.1.tiles.adj, bf16[64,2048]{1,0:T(8,128)(2,1)S(1)} %get-tuple-element.97.refs_0_, bf16[64,2048]{1,0:T(8,128)(2,1)S(1)} %collective-permute-done.5.refs_1_, ...), custom_call_target="tpu_custom_call" | custom-call | flops 402653184 | bytes 10485760 | tf_op jit(solution)/shard_map/aggregate/pallas_call | solution.py:310
  56.1 1.7 %collective-permute-start.17 = (bf16[64,2048]{1,0:T(8,128)(2,1)S(1)}, bf16[64,2048]{1,0:T(8,128)(2,1)S(1)}, u32[]{:S(2)}, u32[]{:S(2)}) collective-permute-start(bf16[64,2048]{1,0:T(8,128)(2,1)S(1)} %get-tuple-element.62.refs_0_), channel_id=1, source_target_pairs={{0,1},{1,0},{2,3},{3,2},{4,5},{5,4},{6,7},{7,6},{8,9},{9,8},{10,11... | collective-permute-start | bytes 786440 | tf_op jit(solution)/shard_map/ppermute | solution.py:58
  57.8 6.7 %aggregate.3 = (bf16[64,2048]{1,0:T(8,128)(2,1)S(1)}, f32[1,2048]{1,0:T(1,128)}) custom-call(s32[384]{0:T(512)S(1)} %collective-permute-done.18.table.table_pair, bf16[16,12,128,128]{3,2,1,0:T(8,128)(2,1)} %collective-permute-done.2.tiles.pair, bf16[64,2048]{1,0:T(8,128)(2,1)S(1)} %get-tuple-element.97.refs_0_, ...), custom_call_target="tpu_custom_call" | custom-call | flops 402653184 | bytes 10485760 | tf_op jit(solution)/shard_map/aggregate/pallas_call | solution.py:310
  65.9 6.9 %collective-permute-done.20.refs_3_ = bf16[64,2048]{1,0:T(8,128)(2,1)S(1)} collective-permute-done((bf16[64,2048]{1,0:T(8,128)(2,1)S(1)}, bf16[64,2048]{1,0:T(8,128)(2,1)S(1)}, u32[]{:S(2)}, u32[]{:S(2)}) %collective-permute-start.20) | collective-permute-done | bytes 262176 | tf_op jit(solution)/shard_map/ppermute | solution.py:58
  72.8 3.0 %middle.1 = (bf16[128,2048]{1,0:T(8,128)(2,1)}, bf16[256,2048]{1,0:T(8,128)(2,1)S(1)}, bf16[128,2048]{1,0:T(8,128)(2,1)S(1)}, bf16[128,2048]{1,0:T(8,128)(2,1)S(1)}) custom-call(bf16[256,256]{1,0:T(8,128)(2,1)S(1)} %get-tuple-element.52.turned, bf16[128,256]{1,0:T(8,128)(2,1)S(1)} %copy-done.3, f32[1,2048]{1,0:T(1,128)S(1)} %get-tuple-element.59.inverse, ...), custom_call_target="tpu_custom_call" | custom-call | flops 402653184 | bytes 7340032 | tf_op jit(solution)/shard_map/middle/pallas_call | solution.py:310
  80.3 3.4 %spread.5 = (bf16[64,2048]{1,0:T(8,128)(2,1)S(1)}, bf16[64,2048]{1,0:T(8,128)(2,1)S(1)}) custom-call(s32[384]{0:T(512)S(1)} %table.1, s32[384]{0:T(512)S(1)} %collective-permute-done.18.table.table_pair, bf16[16,12,128,128]{3,2,1,0:T(8,128)(2,1)S(1)} %load.1.tiles.adj, bf16[16,12,128,128]{3,2,1,0:T(8,128)(2,1)} %collective-permute-done.2.tiles.pair, ...), custom_call_target="tpu_custom_call" | custom-call | flops 100663296 | bytes 2097152 | tf_op jit(solution)/shard_map/spread/pallas_call | solution.py:310
  85.8 3.9 %spread.6 = (f32[64,2048]{1,0:T(8,128)S(1)}, bf16[64,2048]{1,0:T(8,128)(2,1)S(1)}, bf16[64,2048]{1,0:T(8,128)(2,1)S(1)}, f32[64,2048]{1,0:T(8,128)S(1)}) custom-call(s32[384]{0:T(512)S(1)} %table.1, s32[384]{0:T(512)S(1)} %collective-permute-done.18.table.table_pair, bf16[16,12,128,128]{3,2,1,0:T(8,128)(2,1)S(1)} %load.1.tiles.adj, ...), custom_call_target="tpu_custom_call" | custom-call | flops 201326592 | bytes 4194304 | tf_op jit(solution)/shard_map/spread/pallas_call | solution.py:310
  95.7 4.0 %spread.7 = (f32[64,2048]{1,0:T(8,128)S(1)}, f32[64,2048]{1,0:T(8,128)S(1)}, f32[64,2048]{1,0:T(8,128)S(1)}, f32[64,2048]{1,0:T(8,128)S(1)}) custom-call(s32[384]{0:T(512)S(1)} %table.1, s32[384]{0:T(512)S(1)} %collective-permute-done.18.table.table_pair, bf16[16,12,128,128]{3,2,1,0:T(8,128)(2,1)S(1)} %load.1.tiles.adj, ...), custom_call_target="tpu_custom_call" | custom-call | flops 201326592 | bytes 4194304 | tf_op jit(solution)/shard_map/spread/pallas_call | solution.py:310
  99.7 6.1 %collective-permute-done.32 = f32[136,128]{1,0:T(8,128)S(1)} collective-permute-done((f32[136,128]{1,0:T(8,128)S(1)}, f32[136,128]{1,0:T(8,128)S(1)}, u32[]{:S(2)}, u32[]{:S(2)}) %collective-permute-start.32) | collective-permute-done | bytes 69664 | tf_op jit(solution)/shard_map/ppermute | solution.py:49
  106.2 1.8 %collective-permute-start.29 = (bf16[64,2048]{1,0:T(8,128)(2,1)S(1)}, bf16[64,2048]{1,0:T(8,128)(2,1)S(1)}, u32[]{:S(2)}, u32[]{:S(2)}) collective-permute-start(bf16[64,2048]{1,0:T(8,128)(2,1)S(1)} %join.13), channel_id=1, source_target_pairs={{0,4},{2,6},{8,0},{10,2},{16,8},{18,10},{24,16},{26,18},{28,24},{3... | collective-permute-start | bytes 786440 | tf_op jit(solution)/shard_map/ppermute | solution.py:453
  110.4 2.6 %collective-permute-start.34 = (f32[136,128]{1,0:T(8,128)S(1)}, f32[136,128]{1,0:T(8,128)S(1)}, u32[]{:S(2)}, u32[]{:S(2)}) collective-permute-start(f32[136,128]{1,0:T(8,128)S(1)} %add.25), channel_id=1, source_target_pairs={{0,16},{2,18},{4,20},{6,22},{8,24},{10,26},{12,28},{14,30},{16,0},... | collective-permute-start | bytes 208904 | tf_op jit(solution)/shard_map/ppermute | solution.py:49
  113.0 4.6 %spread.4 = (f32[64,2048]{1,0:T(8,128)S(1)}, f32[64,2048]{1,0:T(8,128)S(1)}, f32[64,2048]{1,0:T(8,128)S(1)}, f32[64,2048]{1,0:T(8,128)S(1)}, f32[64,2048]{1,0:T(8,128)S(1)}, /*index=5*/f32[64,2048]{1,0:T(8,128)S(1)}) custom-call(s32[384]{0:T(512)S(1)} %table.1, s32[384]{0:T(512)S(1)} %collective-permute-done.18.table.table_pair, ...), custom_call_target="tpu_custom_call" | custom-call | flops 301989888 | bytes 6291456 | tf_op jit(solution)/shard_map/spread/pallas_call | solution.py:310
  117.6 5.7 %collective-permute-done.34 = f32[136,128]{1,0:T(8,128)S(1)} collective-permute-done((f32[136,128]{1,0:T(8,128)S(1)}, f32[136,128]{1,0:T(8,128)S(1)}, u32[]{:S(2)}, u32[]{:S(2)}) %collective-permute-start.34) | collective-permute-done | bytes 69664 | tf_op jit(solution)/shard_map/ppermute | solution.py:49
  124.3 2.0 %collective-permute-start.30 = (bf16[64,2048]{1,0:T(8,128)(2,1)}, bf16[64,2048]{1,0:T(8,128)(2,1)S(1)}, u32[]{:S(2)}, u32[]{:S(2)}) collective-permute-start(bf16[64,2048]{1,0:T(8,128)(2,1)} %join.14), channel_id=1, source_target_pairs={{0,4},{2,6},{8,0},{10,2},{16,8},{18,10},{24,16},{26,18},{28,24},{3... | collective-permute-start | bytes 786440 | tf_op jit(solution)/shard_map/ppermute | solution.py:453
  127.8 2.0 %collective-permute-start.39 = (bf16[64,2048]{1,0:T(8,128)(2,1)}, bf16[64,2048]{1,0:T(8,128)(2,1)S(1)}, u32[]{:S(2)}, u32[]{:S(2)}) collective-permute-start(bf16[64,2048]{1,0:T(8,128)(2,1)} %join.19), channel_id=1, source_target_pairs={{0,4},{2,6},{8,0},{10,2},{16,8},{18,10},{24,16},{26,18},{28,24},{3... | collective-permute-start | bytes 786440 | tf_op jit(solution)/shard_map/ppermute | solution.py:453
  133.6 2.6 %collective-permute-done.27.a_low = bf16[64,2048]{1,0:T(8,128)(2,1)S(1)} collective-permute-done((bf16[64,2048]{1,0:T(8,128)(2,1)}, bf16[64,2048]{1,0:T(8,128)(2,1)S(1)}, u32[]{:S(2)}, u32[]{:S(2)}) %collective-permute-start.27) | collective-permute-done | bytes 262176 | tf_op jit(solution)/shard_map/ppermute | solution.py:453
  (109 shorter events, 48.1 us)
Async XLA Ops:
  0.6 12.6 %collective-permute-start.2 = (bf16[16,12,128,128]{3,2,1,0:T(8,128)(2,1)}, bf16[16,12,128,128]{3,2,1,0:T(8,128)(2,1)}, u32[]{:S(2)}, u32[]{:S(2)}) collective-permute-start(bf16[16,12,128,128]{3,2,1,0:T(8,128)(2,1)} %source.1), channel_id=1, source_target_pairs={{0,2},{2,0},{4,6},{6,4},{8,10},{10,8},{12,14},{14,12},{16,18},{18,... | collective-permute-start | bytes 18874376 | tf_op jit(solution)/shard_map/ppermute | solution.py:49
  5.0 12.4 %collective-permute-start.6 = (bf16[64,2048]{1,0:T(8,128)(2,1)S(1)}, bf16[64,2048]{1,0:T(8,128)(2,1)S(1)}, u32[]{:S(2)}, u32[]{:S(2)}) collective-permute-start(bf16[64,2048]{1,0:T(8,128)(2,1)S(1)} %get-tuple-element.97.refs_0_), channel_id=1, source_target_pairs={{0,4},{2,6},{8,0},{10,2},{16,8},{18,10},{24,16},{26,18},{28,24},{3... | collective-permute-start | bytes 786440 | tf_op jit(solution)/shard_map/ppermute | solution.py:372
  6.5 12.6 %collective-permute-start.5 = (bf16[64,2048]{1,0:T(8,128)(2,1)S(1)}, bf16[64,2048]{1,0:T(8,128)(2,1)S(1)}, u32[]{:S(2)}, u32[]{:S(2)}) collective-permute-start(bf16[64,2048]{1,0:T(8,128)(2,1)S(1)} %get-tuple-element.97.refs_0_), channel_id=1, source_target_pairs={{0,8},{2,10},{8,16},{10,18},{16,24},{18,26},{24,28},{26,30},{28,20... | collective-permute-start | bytes 786440 | tf_op jit(solution)/shard_map/ppermute | solution.py:368
  13.3 51.8 %collective-permute-start.3 = (bf16[128,4736]{1,0:T(8,128)(2,1)S(1)}, bf16[128,4736]{1,0:T(8,128)(2,1)S(1)}, u32[]{:S(2)}, u32[]{:S(2)}) collective-permute-start(bf16[128,4736]{1,0:T(8,128)(2,1)S(1)} %pack.1.refs_0_), channel_id=1, source_target_pairs={{0,1},{1,0},{2,3},{3,2},{4,5},{5,4},{6,7},{7,6},{8,9},{9,8},{10,11... | collective-permute-start | bytes 3637256 | tf_op jit(solution)/shard_map/ppermute | solution.py:58
  19.5 12.8 %collective-permute-start.9 = (bf16[64,2048]{1,0:T(8,128)(2,1)S(1)}, bf16[64,2048]{1,0:T(8,128)(2,1)S(1)}, u32[]{:S(2)}, u32[]{:S(2)}) collective-permute-start(bf16[64,2048]{1,0:T(8,128)(2,1)S(1)} %collective-permute-done.1.refs_4_), channel_id=1, source_target_pairs={{0,4},{2,6},{8,0},{10,2},{16,8},{18,10},{24,16},{26,18},{28,24},{3... | collective-permute-start | bytes 786440 | tf_op jit(solution)/shard_map/ppermute | solution.py:372
  26.6 11.2 %collective-permute-start.11 = (bf16[64,2048]{1,0:T(8,128)(2,1)S(1)}, bf16[64,2048]{1,0:T(8,128)(2,1)S(1)}, u32[]{:S(2)}, u32[]{:S(2)}) collective-permute-start(bf16[64,2048]{1,0:T(8,128)(2,1)S(1)} %collective-permute-done.8.refs_6_), channel_id=1, source_target_pairs={{0,4},{2,6},{8,0},{10,2},{16,8},{18,10},{24,16},{26,18},{28,24},{3... | collective-permute-start | bytes 786440 | tf_op jit(solution)/shard_map/ppermute | solution.py:372
  28.3 9.6 %collective-permute-start.10 = (bf16[64,2048]{1,0:T(8,128)(2,1)S(1)}, bf16[64,2048]{1,0:T(8,128)(2,1)S(1)}, u32[]{:S(2)}, u32[]{:S(2)}) collective-permute-start(bf16[64,2048]{1,0:T(8,128)(2,1)S(1)} %collective-permute-done.7.refs_5_), channel_id=1, source_target_pairs={{0,8},{2,10},{8,16},{10,18},{16,24},{18,26},{24,28},{26,30},{28,20... | collective-permute-start | bytes 786440 | tf_op jit(solution)/shard_map/ppermute | solution.py:368
  28.7 11.4 %collective-permute-start.4 = (bf16[64,2048]{1,0:T(8,128)(2,1)S(1)}, bf16[64,2048]{1,0:T(8,128)(2,1)S(1)}, u32[]{:S(2)}, u32[]{:S(2)}) collective-permute-start(bf16[64,2048]{1,0:T(8,128)(2,1)S(1)} %collective-permute-done.refs_3_), channel_id=1, source_target_pairs={{0,8},{2,10},{8,16},{10,18},{16,24},{18,26},{24,28},{26,30},{28,20... | collective-permute-start | bytes 786440 | tf_op jit(solution)/shard_map/ppermute | solution.py:368
  32.2 10.2 %collective-permute-start.13 = (bf16[64,2048]{1,0:T(8,128)(2,1)S(1)}, bf16[64,2048]{1,0:T(8,128)(2,1)S(1)}, u32[]{:S(2)}, u32[]{:S(2)}) collective-permute-start(bf16[64,2048]{1,0:T(8,128)(2,1)S(1)} %collective-permute-done.9.refs_8_), channel_id=1, source_target_pairs={{0,4},{2,6},{8,0},{10,2},{16,8},{18,10},{24,16},{26,18},{28,24},{3... | collective-permute-start | bytes 786440 | tf_op jit(solution)/shard_map/ppermute | solution.py:372
  40.1 12.1 %collective-permute-start.12 = (bf16[64,2048]{1,0:T(8,128)(2,1)S(1)}, bf16[64,2048]{1,0:T(8,128)(2,1)S(1)}, u32[]{:S(2)}, u32[]{:S(2)}) collective-permute-start(bf16[64,2048]{1,0:T(8,128)(2,1)S(1)} %collective-permute-done.4.refs_7_), channel_id=1, source_target_pairs={{0,8},{2,10},{8,16},{10,18},{16,24},{18,26},{24,28},{26,30},{28,20... | collective-permute-start | bytes 786440 | tf_op jit(solution)/shard_map/ppermute | solution.py:368
  42.4 9.8 %collective-permute-start.16 = (bf16[64,2048]{1,0:T(8,128)(2,1)S(1)}, bf16[64,2048]{1,0:T(8,128)(2,1)S(1)}, u32[]{:S(2)}, u32[]{:S(2)}) collective-permute-start(bf16[64,2048]{1,0:T(8,128)(2,1)S(1)} %collective-permute-done.13.refs_12_), channel_id=1, source_target_pairs={{0,4},{2,6},{8,0},{10,2},{16,8},{18,10},{24,16},{26,18},{28,24},{3... | collective-permute-start | bytes 786440 | tf_op jit(solution)/shard_map/ppermute | solution.py:372
  43.6 14.2 %collective-permute-start.18 = (s32[384]{0:T(512)S(1)}, s32[384]{0:T(512)S(1)}, u32[]{:S(2)}, u32[]{:S(2)}) collective-permute-start(s32[384]{0:T(512)S(1)} %table.1), channel_id=1, source_target_pairs={{0,2},{2,0},{4,6},{6,4},{8,10},{10,8},{12,14},{14,12},{16,18},{18,... | collective-permute-start | bytes 4616 | tf_op jit(solution)/shard_map/ppermute | solution.py:49
  56.1 9.8 %collective-permute-start.17 = (bf16[64,2048]{1,0:T(8,128)(2,1)S(1)}, bf16[64,2048]{1,0:T(8,128)(2,1)S(1)}, u32[]{:S(2)}, u32[]{:S(2)}) collective-permute-start(bf16[64,2048]{1,0:T(8,128)(2,1)S(1)} %get-tuple-element.62.refs_0_), channel_id=1, source_target_pairs={{0,1},{1,0},{2,3},{3,2},{4,5},{5,4},{6,7},{7,6},{8,9},{9,8},{10,11... | collective-permute-start | bytes 786440 | tf_op jit(solution)/shard_map/ppermute | solution.py:58
  78.5 12.8 %collective-permute-start.24 = (f32[136,128]{1,0:T(8,128)S(1)}, f32[136,128]{1,0:T(8,128)S(1)}, u32[]{:S(2)}, u32[]{:S(2)}) collective-permute-start(f32[136,128]{1,0:T(8,128)S(1)} %slice_bitcast_fusion), channel_id=1, source_target_pairs={{0,4},{2,6},{4,0},{6,2},{8,12},{10,14},{12,8},{14,10},{16,20},{18,... | collective-permute-start | bytes 208904 | tf_op jit(solution)/shard_map/ppermute | solution.py:49
  89.7 10.0 %collective-permute-start.31 = (bf16[64,2048]{1,0:T(8,128)(2,1)S(1)}, bf16[64,2048]{1,0:T(8,128)(2,1)S(1)}, u32[]{:S(2)}, u32[]{:S(2)}) collective-permute-start(bf16[64,2048]{1,0:T(8,128)(2,1)S(1)} %get-tuple-element.82), channel_id=1, source_target_pairs={{0,8},{2,10},{8,16},{10,18},{16,24},{18,26},{24,28},{26,30},{28,20... | collective-permute-start | bytes 786440 | tf_op jit(solution)/shard_map/ppermute | solution.py:453
  91.4 14.8 %collective-permute-start.28 = (bf16[64,2048]{1,0:T(8,128)(2,1)S(1)}, bf16[64,2048]{1,0:T(8,128)(2,1)S(1)}, u32[]{:S(2)}, u32[]{:S(2)}) collective-permute-start(bf16[64,2048]{1,0:T(8,128)(2,1)S(1)} %get-tuple-element.79), channel_id=1, source_target_pairs={{0,4},{2,6},{8,0},{10,2},{16,8},{18,10},{24,16},{26,18},{28,24},{3... | collective-permute-start | bytes 786440 | tf_op jit(solution)/shard_map/ppermute | solution.py:453
  91.9 16.1 %collective-permute-start.25 = (bf16[64,2048]{1,0:T(8,128)(2,1)S(1)}, bf16[64,2048]{1,0:T(8,128)(2,1)S(1)}, u32[]{:S(2)}, u32[]{:S(2)}) collective-permute-start(bf16[64,2048]{1,0:T(8,128)(2,1)S(1)} %join.10), channel_id=1, source_target_pairs={{0,8},{2,10},{8,16},{10,18},{16,24},{18,26},{24,28},{26,30},{28,20... | collective-permute-start | bytes 786440 | tf_op jit(solution)/shard_map/ppermute | solution.py:453
  93.6 15.9 %collective-permute-start.37 = (bf16[64,2048]{1,0:T(8,128)(2,1)S(1)}, bf16[64,2048]{1,0:T(8,128)(2,1)S(1)}, u32[]{:S(2)}, u32[]{:S(2)}) collective-permute-start(bf16[64,2048]{1,0:T(8,128)(2,1)S(1)} %join.17), channel_id=1, source_target_pairs={{0,4},{2,6},{8,0},{10,2},{16,8},{18,10},{24,16},{26,18},{28,24},{3... | collective-permute-start | bytes 786440 | tf_op jit(solution)/shard_map/ppermute | solution.py:453
  94.1 11.7 %collective-permute-start.32 = (f32[136,128]{1,0:T(8,128)S(1)}, f32[136,128]{1,0:T(8,128)S(1)}, u32[]{:S(2)}, u32[]{:S(2)}) collective-permute-start(f32[136,128]{1,0:T(8,128)S(1)} %fusion), channel_id=1, source_target_pairs={{0,8},{2,10},{4,12},{6,14},{8,0},{10,2},{12,4},{14,6},{16,24},{18,... | collective-permute-start | bytes 208904 | tf_op jit(solution)/shard_map/ppermute | solution.py:49
  105.8 17.5 %collective-permute-start.33 = (bf16[64,2048]{1,0:T(8,128)(2,1)S(1)}, bf16[64,2048]{1,0:T(8,128)(2,1)S(1)}, u32[]{:S(2)}, u32[]{:S(2)}) collective-permute-start(bf16[64,2048]{1,0:T(8,128)(2,1)S(1)} %join.15), channel_id=1, source_target_pairs={{0,8},{2,10},{8,16},{10,18},{16,24},{18,26},{24,28},{26,30},{28,20... | collective-permute-start | bytes 786440 | tf_op jit(solution)/shard_map/ppermute | solution.py:453
  106.2 17.3 %collective-permute-start.29 = (bf16[64,2048]{1,0:T(8,128)(2,1)S(1)}, bf16[64,2048]{1,0:T(8,128)(2,1)S(1)}, u32[]{:S(2)}, u32[]{:S(2)}) collective-permute-start(bf16[64,2048]{1,0:T(8,128)(2,1)S(1)} %join.13), channel_id=1, source_target_pairs={{0,4},{2,6},{8,0},{10,2},{16,8},{18,10},{24,16},{26,18},{28,24},{3... | collective-permute-start | bytes 786440 | tf_op jit(solution)/shard_map/ppermute | solution.py:453
  108.1 18.2 %collective-permute-start.26 = (bf16[64,2048]{1,0:T(8,128)(2,1)S(1)}, bf16[64,2048]{1,0:T(8,128)(2,1)S(1)}, u32[]{:S(2)}, u32[]{:S(2)}) collective-permute-start(bf16[64,2048]{1,0:T(8,128)(2,1)S(1)} %join.11), channel_id=1, source_target_pairs={{0,8},{2,10},{8,16},{10,18},{16,24},{18,26},{24,28},{26,30},{28,20... | collective-permute-start | bytes 786440 | tf_op jit(solution)/shard_map/ppermute | solution.py:453
  109.5 17.5 %collective-permute-start.38 = (bf16[64,2048]{1,0:T(8,128)(2,1)S(1)}, bf16[64,2048]{1,0:T(8,128)(2,1)S(1)}, u32[]{:S(2)}, u32[]{:S(2)}) collective-permute-start(bf16[64,2048]{1,0:T(8,128)(2,1)S(1)} %join.18), channel_id=1, source_target_pairs={{0,4},{2,6},{8,0},{10,2},{16,8},{18,10},{24,16},{26,18},{28,24},{3... | collective-permute-start | bytes 786440 | tf_op jit(solution)/shard_map/ppermute | solution.py:453
  110.4 12.9 %collective-permute-start.34 = (f32[136,128]{1,0:T(8,128)S(1)}, f32[136,128]{1,0:T(8,128)S(1)}, u32[]{:S(2)}, u32[]{:S(2)}) collective-permute-start(f32[136,128]{1,0:T(8,128)S(1)} %add.25), channel_id=1, source_target_pairs={{0,16},{2,18},{4,20},{6,22},{8,24},{10,26},{12,28},{14,30},{16,0},... | collective-permute-start | bytes 208904 | tf_op jit(solution)/shard_map/ppermute | solution.py:49
  (25 other events, 166.7 us)

commit v7 on v6

--- a/solution.py
+++ b/solution.py
@@ -333,7 +333,6 @@
     away = lax.dynamic_slice_in_dim(features, (1 - core) * half, half)
     sources, wanted = [mine], [(0, 0)]
     up, down = [mine, away], [mine, away]
-    pair = swap(adjacency, rows)
     (table,) = call(
         table_kernel, "table", [((tile_cols.size + rows * CAP,), jnp.int32)], [SMEM], [SMEM],
         [pltpu.SMEM((rows,), jnp.int32)], 2, 0, 8 * rows * CAP, tile_cols,
@@ -345,21 +344,25 @@
         4 * hid * packed,
         features, grad_output, self_weight, neigh_weight, bias_vector.reshape(1, hid),
     )
-    (tiles,) = call(
-        load_kernel, "load", [(adjacency.shape, narrow)], [HBM], [VMEM],
-        [pltpu.SemaphoreType.DMA], 2, 0, 4 * adjacency.size, adjacency,
-    )
+
+    def load(value):
+        (out,) = call(
+            load_kernel, "load", [(adjacency.shape, narrow)], [HBM], [VMEM],
+            [pltpu.SemaphoreType.DMA], 2, 0, 4 * adjacency.size, value,
+        )
+        return out
+
+    pair, tiles = swap(adjacency, rows), load(adjacency)
     for step in range(1, top + 1):
         if step == 2:
-            up[1], down[1], pair, pack, tiles = lax.optimization_barrier(
-                (up[1], down[1], pair, pack, tiles)
-            )
+            up, down, pair, pack, tiles = lax.optimization_barrier((up, down, pair, pack, tiles))
             packs = [pack] + [send(pack, k, 0, rows, feats) for k in range(1, feats)]
         if step == 3:
             up[1], table = lax.optimization_barrier((up[1], table))
         if step == top:
             table_pair = swap(after(table, up[0], down[0]), rows)
-            sources.append(swap(after(away, up[0], down[0]), rows))
+            pair = load(pair)
+            sources.append(swap(after(away, up[0], down[0], pair), rows))
             wanted.append((0, 1))
         for side in range(2):
             flip = side if step == 1 else 0
@@ -437,7 +440,7 @@
         )
         return out
 
-    near = sums[:2] + swap(sums[2:], rows, 1)
+    near = sums[:2] + swap(after(sums[2:], scaled_pair), rows, 1)
     total = near[0] + swap(near[1], rows, 2)
     bit, sends = 4, 0
 
@@ -465,8 +468,7 @@
         if level == 1:
             offsets, kinds = (1, -1, 0), kinds + (wide, wide)
         mine = spread(offsets, kinds)
-        first = [i for i in range(2) if up[i] is None]
-        for i in first + [i for i in range(2) if i not in first]:
+        for i in (1, 0):
             flow = 1 - i
             up[i] = ring(joined(up[i], mine[i]), forward)
             down[flow] = ring(joined(down[flow], mine[2 + flow]), backward)

time: 138 us -> 135 us (0.978)
  waiting for transfers between devices: 46.8 us -> 59.3 us
  Pallas kernels: 40.9 us -> 32.6 us
  starting transfers between devices: 43.4 us -> 37 us
    ppermute x7, starting transfers between devices: 11.8 us -> 2.52 us  [shards(): down[side] = lax.ppermute(down[side], 'rows', backward)]
    pallas_call x25 -> x26, Pallas kernels: 40.9 us -> 32.6 us  [call(): pl.pallas_call(kernel, out_shape=[jax.ShapeDtypeStruct(shape, kind) for s...]
    ppermute x10, waiting for transfers between devices: 14.2 us -> 21.9 us  [swap(): return lax.ppermute(value, 'rows', [(r, r ^ bit) for r in range(rows)])]
    ppermute x7, starting transfers between devices: 5.96 us -> 12.1 us  [shards(): up[side] = lax.ppermute(up[side], 'rows', forward)]
    ppermute x7, waiting for transfers between devices: 10.8 us -> 14.3 us  [shards(): up[side] = lax.ppermute(up[side], 'rows', forward)]
    ppermute x10, starting transfers between devices: 6.96 us -> 3.88 us  [swap(): return lax.ppermute(value, 'rows', [(r, r ^ bit) for r in range(rows)])]
    ppermute x14, waiting for transfers between devices: 2.63 us -> 5.64 us  [ring(): return lax.ppermute(value, 'rows', pairs)]
    ppermute x7, waiting for transfers between devices: 12.3 us -> 10 us  [shards(): down[side] = lax.ppermute(down[side], 'rows', backward)]
  transfers between devices with their start and end apart: 42 -> 42, of which waited for: 17 -> 19; matrix products, arithmetic and copies ran while one was open for 1% -> 1% of each run, Pallas kernels for 26% -> 21%
where the time goes in v7:
time: 135 us
  waiting for transfers between devices  59.3 us (44%)
  starting transfers between devices  37 us (27%)
  Pallas kernels  32.6 us (24%)
  local copies, waits for them, and re-layouts  5.14 us (4%)
    pallas_call x26, Pallas kernels, call(): pl.pallas_call(kernel, out_shape=[jax.ShapeDtypeStruct(shape, kind) for s...  32.6 us
    ppermute x10, waiting for transfers between devices, swap(): return lax.ppermute(value, 'rows', [(r, r ^ bit) for r in range(rows)])  21.9 us
    ppermute x14, starting transfers between devices, ring(): return lax.ppermute(value, 'rows', pairs)  14.7 us
    ppermute x7, waiting for transfers between devices, shards(): up[side] = lax.ppermute(up[side], 'rows', forward)  14.3 us
    ppermute x7, starting transfers between devices, shards(): up[side] = lax.ppermute(up[side], 'rows', forward)  12.1 us
    ppermute x7, waiting for transfers between devices, shards(): down[side] = lax.ppermute(down[side], 'rows', backward)  10 us
    ppermute x4, waiting for transfers between devices, send(): return lax.ppermute(value, ('rows', 'feat'), pairs)  7.36 us
    ppermute x14, waiting for transfers between devices, ring(): return lax.ppermute(value, 'rows', pairs)  5.64 us
  transfers between devices with their start and end apart: 42, of which 19 were waited for; matrix products, arithmetic and copies ran while one was open for 1% of the time, Pallas kernels for 21%

profile of v7, /device:TPU:0, one launch (start us, length us, event | category | flops | bytes accessed | tf_op | source)
XLA Modules:
  0.0 135.1 jit_solution(5679382478842647842)
XLA Ops:
  2.2 2.7 %collective-permute-start = (bf16[64,2048]{1,0:T(8,128)(2,1)S(1)}, bf16[64,2048]{1,0:T(8,128)(2,1)S(1)}, u32[]{:S(2)}, u32[]{:S(2)}) collective-permute-start(bf16[64,2048]{1,0:T(8,128)(2,1)S(1)} %get-tuple-element.104.refs_0_), channel_id=1, source_target_pairs={{0,8},{2,10},{8,16},{10,18},{16,24},{18,26},{24,28},{26,30},{28,20... | collective-permute-start | bytes 786440 | tf_op jit(solution)/shard_map/ppermute | solution.py:371
  6.6 2.8 %copy-done = bf16[16,12,128,128]{3,2,1,0:T(8,128)(2,1)S(1)} copy-done((bf16[16,12,128,128]{3,2,1,0:T(8,128)(2,1)S(1)}, bf16[16,12,128,128]{3,2,1,0:T(8,128)(2,1)}, u32[]{:S(2)}) %copy-start) | copy-done | bytes 6291480
  12.0 2.1 %collective-permute-done.2.refs_2_ = bf16[64,2048]{1,0:T(8,128)(2,1)S(1)} collective-permute-done((bf16[64,2048]{1,0:T(8,128)(2,1)S(1)}, bf16[64,2048]{1,0:T(8,128)(2,1)S(1)}, u32[]{:S(2)}, u32[]{:S(2)}) %collective-permute-start.2) | collective-permute-done | bytes 262176 | tf_op jit(solution)/shard_map/ppermute | solution.py:375
  14.0 3.1 %collective-permute-done.1.refs_3_ = bf16[64,2048]{1,0:T(8,128)(2,1)S(1)} collective-permute-done((bf16[64,2048]{1,0:T(8,128)(2,1)S(1)}, bf16[64,2048]{1,0:T(8,128)(2,1)S(1)}, u32[]{:S(2)}, u32[]{:S(2)}) %collective-permute-start.1) | collective-permute-done | bytes 262176 | tf_op jit(solution)/shard_map/ppermute | solution.py:371
  23.7 5.1 %collective-permute-done.7.refs_5_ = bf16[64,2048]{1,0:T(8,128)(2,1)S(1)} collective-permute-done((bf16[64,2048]{1,0:T(8,128)(2,1)S(1)}, bf16[64,2048]{1,0:T(8,128)(2,1)S(1)}, u32[]{:S(2)}, u32[]{:S(2)}) %collective-permute-start.7) | collective-permute-done | bytes 262176 | tf_op jit(solution)/shard_map/ppermute | solution.py:371
  30.9 5.2 %collective-permute-done.9.refs_8_ = bf16[64,2048]{1,0:T(8,128)(2,1)S(1)} collective-permute-done((bf16[64,2048]{1,0:T(8,128)(2,1)S(1)}, bf16[64,2048]{1,0:T(8,128)(2,1)S(1)}, u32[]{:S(2)}, u32[]{:S(2)}) %collective-permute-start.9) | collective-permute-done | bytes 262176 | tf_op jit(solution)/shard_map/ppermute | solution.py:375
  36.5 3.2 %table.1 = s32[384]{0:T(512)S(1)} custom-call(s32[16,12]{1,0:T(8,128)S(1)} %copy-done.5), custom_call_target="tpu_custom_call" | custom-call | bytes 1536 | tf_op jit(solution)/shard_map/table/pallas_call | solution.py:310
  41.4 2.8 %load.3.tiles.pair = bf16[16,12,128,128]{3,2,1,0:T(8,128)(2,1)S(1)} custom-call(bf16[16,12,128,128]{3,2,1,0:T(8,128)(2,1)} %collective-permute-done.4.source), custom_call_target="tpu_custom_call" | custom-call | bytes 12582912 | tf_op jit(solution)/shard_map/load/pallas_call | solution.py:310
  47.9 5.0 %collective-permute-done.15.refs_14_ = bf16[64,2048]{1,0:T(8,128)(2,1)S(1)} collective-permute-done((bf16[64,2048]{1,0:T(8,128)(2,1)S(1)}, bf16[64,2048]{1,0:T(8,128)(2,1)S(1)}, u32[]{:S(2)}, u32[]{:S(2)}) %collective-permute-start.15) | collective-permute-done | bytes 262176 | tf_op jit(solution)/shard_map/ppermute | solution.py:371
  54.3 4.4 %aggregate.3 = (bf16[64,2048]{1,0:T(8,128)(2,1)S(1)}, f32[1,2048]{1,0:T(1,128)}) custom-call(s32[384]{0:T(512)S(1)} %collective-permute-done.18.table.table_pair, bf16[16,12,128,128]{3,2,1,0:T(8,128)(2,1)S(1)} %load.3.tiles.pair, bf16[64,2048]{1,0:T(8,128)(2,1)S(1)} %get-tuple-element.104.refs_0_, bf16[64,2048]{1,0:T(8,128)(2,1)S(1)} %collective-permute-done.refs_1_, ...), custom_call_target="tpu_custom_call" | custom-call | flops 402653184 | bytes 10485760 | tf_op jit(solution)/shard_map/aggregate/pallas_call | solution.py:310
  59.4 3.9 %aggregate.2 = (bf16[64,2048]{1,0:T(8,128)(2,1)S(1)}, f32[1,2048]{1,0:T(1,128)S(1)}) custom-call(s32[384]{0:T(512)S(1)} %table.1, bf16[16,12,128,128]{3,2,1,0:T(8,128)(2,1)S(1)} %load.2.tiles.adj, bf16[64,2048]{1,0:T(8,128)(2,1)S(1)} %get-tuple-element.104.refs_0_, bf16[64,2048]{1,0:T(8,128)(2,1)S(1)} %collective-permute-done.refs_1_, ...), custom_call_target="tpu_custom_call" | custom-call | flops 402653184 | bytes 10485760 | tf_op jit(solution)/shard_map/aggregate/pallas_call | solution.py:310
  66.9 6.2 %collective-permute-done.17.refs_1_ = bf16[64,2048]{1,0:T(8,128)(2,1)S(1)} collective-permute-done((bf16[64,2048]{1,0:T(8,128)(2,1)S(1)}, bf16[64,2048]{1,0:T(8,128)(2,1)S(1)}, u32[]{:S(2)}, u32[]{:S(2)}) %collective-permute-start.17) | collective-permute-done | bytes 262176 | tf_op jit(solution)/shard_map/ppermute | solution.py:58
  73.1 3.0 %middle.1 = (bf16[128,2048]{1,0:T(8,128)(2,1)}, bf16[256,2048]{1,0:T(8,128)(2,1)S(1)}, bf16[128,2048]{1,0:T(8,128)(2,1)S(1)}, bf16[128,2048]{1,0:T(8,128)(2,1)S(1)}) custom-call(bf16[256,256]{1,0:T(8,128)(2,1)S(1)} %get-tuple-element.55.turned, bf16[128,256]{1,0:T(8,128)(2,1)S(1)} %copy-done.3, f32[1,2048]{1,0:T(1,128)S(1)} %get-tuple-element.65.inverse, ...), custom_call_target="tpu_custom_call" | custom-call | flops 402653184 | bytes 7340032 | tf_op jit(solution)/shard_map/middle/pallas_call | solution.py:310
  83.4 1.7 %spread.6 = (f32[64,2048]{1,0:T(8,128)S(1)}, bf16[64,2048]{1,0:T(8,128)(2,1)S(1)}, bf16[64,2048]{1,0:T(8,128)(2,1)S(1)}, f32[64,2048]{1,0:T(8,128)S(1)}) custom-call(s32[384]{0:T(512)S(1)} %table.1, s32[384]{0:T(512)S(1)} %collective-permute-done.18.table.table_pair, bf16[16,12,128,128]{3,2,1,0:T(8,128)(2,1)S(1)} %load.2.tiles.adj, ...), custom_call_target="tpu_custom_call" | custom-call | flops 201326592 | bytes 4194304 | tf_op jit(solution)/shard_map/spread/pallas_call | solution.py:310
  85.2 4.3 %collective-permute-done.22.arrived = bf16[64,2048]{1,0:T(8,128)(2,1)S(1)} collective-permute-done((bf16[64,2048]{1,0:T(8,128)(2,1)S(1)}, bf16[64,2048]{1,0:T(8,128)(2,1)S(1)}, u32[]{:S(2)}, u32[]{:S(2)}) %collective-permute-start.22) | collective-permute-done | bytes 262176 | tf_op jit(solution)/shard_map/ppermute | solution.py:456
  95.1 1.8 %spread.7 = (f32[64,2048]{1,0:T(8,128)S(1)}, f32[64,2048]{1,0:T(8,128)S(1)}, f32[64,2048]{1,0:T(8,128)S(1)}, f32[64,2048]{1,0:T(8,128)S(1)}) custom-call(s32[384]{0:T(512)S(1)} %table.1, s32[384]{0:T(512)S(1)} %collective-permute-done.18.table.table_pair, bf16[16,12,128,128]{3,2,1,0:T(8,128)(2,1)S(1)} %load.2.tiles.adj, ...), custom_call_target="tpu_custom_call" | custom-call | flops 201326592 | bytes 4194304 | tf_op jit(solution)/shard_map/spread/pallas_call | solution.py:310
  96.8 9.1 %collective-permute-done.26 = f32[136,128]{1,0:T(8,128)S(1)} collective-permute-done((f32[136,128]{1,0:T(8,128)S(1)}, f32[136,128]{1,0:T(8,128)S(1)}, u32[]{:S(2)}, u32[]{:S(2)}) %collective-permute-start.26) | collective-permute-done | bytes 69664 | tf_op jit(solution)/shard_map/ppermute | solution.py:49
  106.2 1.8 %collective-permute-start.34 = (bf16[64,2048]{1,0:T(8,128)(2,1)S(1)}, bf16[64,2048]{1,0:T(8,128)(2,1)S(1)}, u32[]{:S(2)}, u32[]{:S(2)}) collective-permute-start(bf16[64,2048]{1,0:T(8,128)(2,1)S(1)} %join.15), channel_id=1, source_target_pairs={{0,8},{2,10},{8,16},{10,18},{16,24},{18,26},{24,28},{26,30},{28,20... | collective-permute-start | bytes 786440 | tf_op jit(solution)/shard_map/ppermute | solution.py:456
  108.6 2.1 %collective-permute-start.38 = (bf16[64,2048]{1,0:T(8,128)(2,1)S(1)}, bf16[64,2048]{1,0:T(8,128)(2,1)S(1)}, u32[]{:S(2)}, u32[]{:S(2)}) collective-permute-start(bf16[64,2048]{1,0:T(8,128)(2,1)S(1)} %join.18), channel_id=1, source_target_pairs={{0,4},{2,6},{8,0},{10,2},{16,8},{18,10},{24,16},{26,18},{28,24},{3... | collective-permute-start | bytes 786440 | tf_op jit(solution)/shard_map/ppermute | solution.py:456
  111.8 2.3 %spread.4 = (f32[64,2048]{1,0:T(8,128)S(1)}, f32[64,2048]{1,0:T(8,128)S(1)}, f32[64,2048]{1,0:T(8,128)S(1)}, f32[64,2048]{1,0:T(8,128)S(1)}, f32[64,2048]{1,0:T(8,128)S(1)}, /*index=5*/f32[64,2048]{1,0:T(8,128)S(1)}) custom-call(s32[384]{0:T(512)S(1)} %table.1, s32[384]{0:T(512)S(1)} %collective-permute-done.18.table.table_pair, ...), custom_call_target="tpu_custom_call" | custom-call | flops 301989888 | bytes 6291456 | tf_op jit(solution)/shard_map/spread/pallas_call | solution.py:310
  114.2 8.3 %collective-permute-done.28 = f32[136,128]{1,0:T(8,128)S(1)} collective-permute-done((f32[136,128]{1,0:T(8,128)S(1)}, f32[136,128]{1,0:T(8,128)S(1)}, u32[]{:S(2)}, u32[]{:S(2)}) %collective-permute-start.28) | collective-permute-done | bytes 69664 | tf_op jit(solution)/shard_map/ppermute | solution.py:49
  124.5 1.7 %collective-permute-start.32 = (bf16[64,2048]{1,0:T(8,128)(2,1)}, bf16[64,2048]{1,0:T(8,128)(2,1)S(1)}, u32[]{:S(2)}, u32[]{:S(2)}) collective-permute-start(bf16[64,2048]{1,0:T(8,128)(2,1)} %join.14), channel_id=1, source_target_pairs={{0,4},{2,6},{8,0},{10,2},{16,8},{18,10},{24,16},{26,18},{28,24},{3... | collective-permute-start | bytes 786440 | tf_op jit(solution)/shard_map/ppermute | solution.py:456
  127.3 1.7 %collective-permute-start.39 = (bf16[64,2048]{1,0:T(8,128)(2,1)}, bf16[64,2048]{1,0:T(8,128)(2,1)S(1)}, u32[]{:S(2)}, u32[]{:S(2)}) collective-permute-start(bf16[64,2048]{1,0:T(8,128)(2,1)} %join.19), channel_id=1, source_target_pairs={{0,4},{2,6},{8,0},{10,2},{16,8},{18,10},{24,16},{26,18},{28,24},{3... | collective-permute-start | bytes 786440 | tf_op jit(solution)/shard_map/ppermute | solution.py:456
  130.5 1.7 %collect.1 = (f32[128,256]{1,0:T(8,128)}, f32[128,256]{1,0:T(8,128)}, f32[8,256]{1,0:T(8,128)S(1)}) custom-call(f32[2,136,128]{2,1,0:T(8,128)S(1)} %pad_maximum_fusion.pair, f32[2,136,128]{2,1,0:T(8,128)} %collective-permute-done.41.pair_far), custom_call_target="tpu_custom_call" | custom-call | bytes 524288 | tf_op jit(solution)/shard_map/collect/pallas_call | solution.py:310
  (110 shorter events, 48.3 us)
Async XLA Ops:
  0.6 17.5 %collective-permute-start.4 = (bf16[16,12,128,128]{3,2,1,0:T(8,128)(2,1)}, bf16[16,12,128,128]{3,2,1,0:T(8,128)(2,1)}, u32[]{:S(2)}, u32[]{:S(2)}) collective-permute-start(bf16[16,12,128,128]{3,2,1,0:T(8,128)(2,1)} %source.1), channel_id=1, source_target_pairs={{0,2},{2,0},{4,6},{6,4},{8,10},{10,8},{12,14},{14,12},{16,18},{18,... | collective-permute-start | bytes 18874376 | tf_op jit(solution)/shard_map/ppermute | solution.py:49
  2.2 9.7 %collective-permute-start = (bf16[64,2048]{1,0:T(8,128)(2,1)S(1)}, bf16[64,2048]{1,0:T(8,128)(2,1)S(1)}, u32[]{:S(2)}, u32[]{:S(2)}) collective-permute-start(bf16[64,2048]{1,0:T(8,128)(2,1)S(1)} %get-tuple-element.104.refs_0_), channel_id=1, source_target_pairs={{0,8},{2,10},{8,16},{10,18},{16,24},{18,26},{24,28},{26,30},{28,20... | collective-permute-start | bytes 786440 | tf_op jit(solution)/shard_map/ppermute | solution.py:371
  4.9 12.3 %collective-permute-start.1 = (bf16[64,2048]{1,0:T(8,128)(2,1)S(1)}, bf16[64,2048]{1,0:T(8,128)(2,1)S(1)}, u32[]{:S(2)}, u32[]{:S(2)}) collective-permute-start(bf16[64,2048]{1,0:T(8,128)(2,1)S(1)} %get-tuple-element.64), channel_id=1, source_target_pairs={{0,10},{2,8},{8,18},{10,16},{16,26},{18,24},{24,30},{26,28},{28,22... | collective-permute-start | bytes 786440 | tf_op jit(solution)/shard_map/ppermute | solution.py:371
  6.4 11.7 %collective-permute-start.3 = (bf16[64,2048]{1,0:T(8,128)(2,1)S(1)}, bf16[64,2048]{1,0:T(8,128)(2,1)S(1)}, u32[]{:S(2)}, u32[]{:S(2)}) collective-permute-start(bf16[64,2048]{1,0:T(8,128)(2,1)S(1)} %get-tuple-element.64), channel_id=1, source_target_pairs={{0,6},{2,4},{8,2},{10,0},{16,10},{18,8},{24,18},{26,16},{28,26},{3... | collective-permute-start | bytes 786440 | tf_op jit(solution)/shard_map/ppermute | solution.py:375
  18.2 46.7 %collective-permute-start.5 = (bf16[128,4736]{1,0:T(8,128)(2,1)S(1)}, bf16[128,4736]{1,0:T(8,128)(2,1)S(1)}, u32[]{:S(2)}, u32[]{:S(2)}) collective-permute-start(bf16[128,4736]{1,0:T(8,128)(2,1)S(1)} %pack.1.refs_0_), channel_id=1, source_target_pairs={{0,1},{1,0},{2,3},{3,2},{4,5},{5,4},{6,7},{7,6},{8,9},{9,8},{10,11... | collective-permute-start | bytes 3637256 | tf_op jit(solution)/shard_map/ppermute | solution.py:58
  21.3 9.2 %collective-permute-start.8 = (bf16[64,2048]{1,0:T(8,128)(2,1)S(1)}, bf16[64,2048]{1,0:T(8,128)(2,1)S(1)}, u32[]{:S(2)}, u32[]{:S(2)}) collective-permute-start(bf16[64,2048]{1,0:T(8,128)(2,1)S(1)} %collective-permute-done.2.refs_2_), channel_id=1, source_target_pairs={{0,4},{2,6},{8,0},{10,2},{16,8},{18,10},{24,16},{26,18},{28,24},{3... | collective-permute-start | bytes 786440 | tf_op jit(solution)/shard_map/ppermute | solution.py:375
  21.7 14.3 %collective-permute-start.9 = (bf16[64,2048]{1,0:T(8,128)(2,1)S(1)}, bf16[64,2048]{1,0:T(8,128)(2,1)S(1)}, u32[]{:S(2)}, u32[]{:S(2)}) collective-permute-start(bf16[64,2048]{1,0:T(8,128)(2,1)S(1)} %collective-permute-done.3.refs_4_), channel_id=1, source_target_pairs={{0,4},{2,6},{8,0},{10,2},{16,8},{18,10},{24,16},{26,18},{28,24},{3... | collective-permute-start | bytes 786440 | tf_op jit(solution)/shard_map/ppermute | solution.py:375
  22.2 17.5 %collective-permute-start.6 = (bf16[64,2048]{1,0:T(8,128)(2,1)S(1)}, bf16[64,2048]{1,0:T(8,128)(2,1)S(1)}, u32[]{:S(2)}, u32[]{:S(2)}) collective-permute-start(bf16[64,2048]{1,0:T(8,128)(2,1)S(1)} %collective-permute-done.1.refs_3_), channel_id=1, source_target_pairs={{0,8},{2,10},{8,16},{10,18},{16,24},{18,26},{24,28},{26,30},{28,20... | collective-permute-start | bytes 786440 | tf_op jit(solution)/shard_map/ppermute | solution.py:371
  28.8 15.4 %collective-permute-start.10 = (bf16[64,2048]{1,0:T(8,128)(2,1)S(1)}, bf16[64,2048]{1,0:T(8,128)(2,1)S(1)}, u32[]{:S(2)}, u32[]{:S(2)}) collective-permute-start(bf16[64,2048]{1,0:T(8,128)(2,1)S(1)} %collective-permute-done.7.refs_5_), channel_id=1, source_target_pairs={{0,8},{2,10},{8,16},{10,18},{16,24},{18,26},{24,28},{26,30},{28,20... | collective-permute-start | bytes 786440 | tf_op jit(solution)/shard_map/ppermute | solution.py:371
  30.4 13.7 %collective-permute-start.11 = (bf16[64,2048]{1,0:T(8,128)(2,1)S(1)}, bf16[64,2048]{1,0:T(8,128)(2,1)S(1)}, u32[]{:S(2)}, u32[]{:S(2)}) collective-permute-start(bf16[64,2048]{1,0:T(8,128)(2,1)S(1)} %collective-permute-done.8.refs_6_), channel_id=1, source_target_pairs={{0,4},{2,6},{8,0},{10,2},{16,8},{18,10},{24,16},{26,18},{28,24},{3... | collective-permute-start | bytes 786440 | tf_op jit(solution)/shard_map/ppermute | solution.py:375
  36.1 10.3 %collective-permute-start.13 = (bf16[64,2048]{1,0:T(8,128)(2,1)S(1)}, bf16[64,2048]{1,0:T(8,128)(2,1)S(1)}, u32[]{:S(2)}, u32[]{:S(2)}) collective-permute-start(bf16[64,2048]{1,0:T(8,128)(2,1)S(1)} %collective-permute-done.9.refs_8_), channel_id=1, source_target_pairs={{0,4},{2,6},{8,0},{10,2},{16,8},{18,10},{24,16},{26,18},{28,24},{3... | collective-permute-start | bytes 786440 | tf_op jit(solution)/shard_map/ppermute | solution.py:375
  63.3 9.8 %collective-permute-start.17 = (bf16[64,2048]{1,0:T(8,128)(2,1)S(1)}, bf16[64,2048]{1,0:T(8,128)(2,1)S(1)}, u32[]{:S(2)}, u32[]{:S(2)}) collective-permute-start(bf16[64,2048]{1,0:T(8,128)(2,1)S(1)} %get-tuple-element.68.refs_0_), channel_id=1, source_target_pairs={{0,1},{1,0},{2,3},{3,2},{4,5},{5,4},{6,7},{7,6},{8,9},{9,8},{10,11... | collective-permute-start | bytes 786440 | tf_op jit(solution)/shard_map/ppermute | solution.py:58
  82.5 10.5 %collective-permute-start.36 = (bf16[64,2048]{1,0:T(8,128)(2,1)S(1)}, bf16[64,2048]{1,0:T(8,128)(2,1)S(1)}, u32[]{:S(2)}, u32[]{:S(2)}) collective-permute-start(bf16[64,2048]{1,0:T(8,128)(2,1)S(1)} %get-tuple-element.95), channel_id=1, source_target_pairs={{0,4},{2,6},{8,0},{10,2},{16,8},{18,10},{24,16},{26,18},{28,24},{3... | collective-permute-start | bytes 786440 | tf_op jit(solution)/shard_map/ppermute | solution.py:456
  89.5 16.5 %collective-permute-start.25 = (bf16[64,2048]{1,0:T(8,128)(2,1)S(1)}, bf16[64,2048]{1,0:T(8,128)(2,1)S(1)}, u32[]{:S(2)}, u32[]{:S(2)}) collective-permute-start(bf16[64,2048]{1,0:T(8,128)(2,1)S(1)} %join.10), channel_id=1, source_target_pairs={{0,8},{2,10},{8,16},{10,18},{16,24},{18,26},{24,28},{26,30},{28,20... | collective-permute-start | bytes 786440 | tf_op jit(solution)/shard_map/ppermute | solution.py:456
  90.9 15.2 %collective-permute-start.33 = (bf16[64,2048]{1,0:T(8,128)(2,1)S(1)}, bf16[64,2048]{1,0:T(8,128)(2,1)S(1)}, u32[]{:S(2)}, u32[]{:S(2)}) collective-permute-start(bf16[64,2048]{1,0:T(8,128)(2,1)S(1)} %get-tuple-element.92), channel_id=1, source_target_pairs={{0,8},{2,10},{8,16},{10,18},{16,24},{18,26},{24,28},{26,30},{28,20... | collective-permute-start | bytes 786440 | tf_op jit(solution)/shard_map/ppermute | solution.py:456
  91.9 16.0 %collective-permute-start.30 = (bf16[64,2048]{1,0:T(8,128)(2,1)S(1)}, bf16[64,2048]{1,0:T(8,128)(2,1)S(1)}, u32[]{:S(2)}, u32[]{:S(2)}) collective-permute-start(bf16[64,2048]{1,0:T(8,128)(2,1)S(1)} %get-tuple-element.89), channel_id=1, source_target_pairs={{0,4},{2,6},{8,0},{10,2},{16,8},{18,10},{24,16},{26,18},{28,24},{3... | collective-permute-start | bytes 786440 | tf_op jit(solution)/shard_map/ppermute | solution.py:456
  93.0 15.6 %collective-permute-start.37 = (bf16[64,2048]{1,0:T(8,128)(2,1)S(1)}, bf16[64,2048]{1,0:T(8,128)(2,1)S(1)}, u32[]{:S(2)}, u32[]{:S(2)}) collective-permute-start(bf16[64,2048]{1,0:T(8,128)(2,1)S(1)} %join.17), channel_id=1, source_target_pairs={{0,4},{2,6},{8,0},{10,2},{16,8},{18,10},{24,16},{26,18},{28,24},{3... | collective-permute-start | bytes 786440 | tf_op jit(solution)/shard_map/ppermute | solution.py:456
  93.7 12.2 %collective-permute-start.26 = (f32[136,128]{1,0:T(8,128)S(1)}, f32[136,128]{1,0:T(8,128)S(1)}, u32[]{:S(2)}, u32[]{:S(2)}) collective-permute-start(f32[136,128]{1,0:T(8,128)S(1)} %fusion), channel_id=1, source_target_pairs={{0,8},{2,10},{4,12},{6,14},{8,0},{10,2},{12,4},{14,6},{16,24},{18,... | collective-permute-start | bytes 208904 | tf_op jit(solution)/shard_map/ppermute | solution.py:49
  106.1 16.4 %collective-permute-start.27 = (bf16[64,2048]{1,0:T(8,128)(2,1)S(1)}, bf16[64,2048]{1,0:T(8,128)(2,1)S(1)}, u32[]{:S(2)}, u32[]{:S(2)}) collective-permute-start(bf16[64,2048]{1,0:T(8,128)(2,1)S(1)} %join.11), channel_id=1, source_target_pairs={{0,8},{2,10},{8,16},{10,18},{16,24},{18,26},{24,28},{26,30},{28,20... | collective-permute-start | bytes 786440 | tf_op jit(solution)/shard_map/ppermute | solution.py:456
  106.2 16.4 %collective-permute-start.34 = (bf16[64,2048]{1,0:T(8,128)(2,1)S(1)}, bf16[64,2048]{1,0:T(8,128)(2,1)S(1)}, u32[]{:S(2)}, u32[]{:S(2)}) collective-permute-start(bf16[64,2048]{1,0:T(8,128)(2,1)S(1)} %join.15), channel_id=1, source_target_pairs={{0,8},{2,10},{8,16},{10,18},{16,24},{18,26},{24,28},{26,30},{28,20... | collective-permute-start | bytes 786440 | tf_op jit(solution)/shard_map/ppermute | solution.py:456
  108.0 15.7 %collective-permute-start.31 = (bf16[64,2048]{1,0:T(8,128)(2,1)S(1)}, bf16[64,2048]{1,0:T(8,128)(2,1)S(1)}, u32[]{:S(2)}, u32[]{:S(2)}) collective-permute-start(bf16[64,2048]{1,0:T(8,128)(2,1)S(1)} %join.13), channel_id=1, source_target_pairs={{0,4},{2,6},{8,0},{10,2},{16,8},{18,10},{24,16},{26,18},{28,24},{3... | collective-permute-start | bytes 786440 | tf_op jit(solution)/shard_map/ppermute | solution.py:456
  108.6 17.9 %collective-permute-start.38 = (bf16[64,2048]{1,0:T(8,128)(2,1)S(1)}, bf16[64,2048]{1,0:T(8,128)(2,1)S(1)}, u32[]{:S(2)}, u32[]{:S(2)}) collective-permute-start(bf16[64,2048]{1,0:T(8,128)(2,1)S(1)} %join.18), channel_id=1, source_target_pairs={{0,4},{2,6},{8,0},{10,2},{16,8},{18,10},{24,16},{26,18},{28,24},{3... | collective-permute-start | bytes 786440 | tf_op jit(solution)/shard_map/ppermute | solution.py:456
  110.7 11.8 %collective-permute-start.28 = (f32[136,128]{1,0:T(8,128)S(1)}, f32[136,128]{1,0:T(8,128)S(1)}, u32[]{:S(2)}, u32[]{:S(2)}) collective-permute-start(f32[136,128]{1,0:T(8,128)S(1)} %add.25), channel_id=1, source_target_pairs={{0,16},{2,18},{4,20},{6,22},{8,24},{10,26},{12,28},{14,30},{16,0},... | collective-permute-start | bytes 208904 | tf_op jit(solution)/shard_map/ppermute | solution.py:49
  123.4 9.3 %collective-permute-start.35 = (bf16[64,2048]{1,0:T(8,128)(2,1)}, bf16[64,2048]{1,0:T(8,128)(2,1)S(1)}, u32[]{:S(2)}, u32[]{:S(2)}) collective-permute-start(bf16[64,2048]{1,0:T(8,128)(2,1)} %join.16), channel_id=1, source_target_pairs={{0,8},{2,10},{8,16},{10,18},{16,24},{18,26},{24,28},{26,30},{28,20... | collective-permute-start | bytes 786440 | tf_op jit(solution)/shard_map/ppermute | solution.py:456
  (25 other events, 149.5 us)

commit v8 on v7

--- a/solution.py
+++ b/solution.py
@@ -215,15 +215,12 @@
 
 
 def own_quarter():
-    row = lax.axis_index("rows")
-    return 2 * lax.rem(row, 2) + lax.rem(row // 2, 2)
+    return 2 * lax.rem(lax.axis_index("rows"), 2)
 
 
 def turned_quarter(mine, index):
-    both = (index // 2, index % 2)
-    core = both[0] + mine // 2 - 2 * both[0] * (mine // 2)
-    x = both[1] + lax.rem(mine, 2) - 2 * both[1] * lax.rem(mine, 2)
-    return 2 * core + x
+    turned = index // 2 + mine // 2 - 2 * (index // 2) * (mine // 2)
+    return 2 * turned + index % 2
 
 
 def weights_kernel(ws, x_own, agg_own, grad, self_own, sums):
@@ -355,14 +352,17 @@
     pair, tiles = swap(adjacency, rows), load(adjacency)
     for step in range(1, top + 1):
         if step == 2:
-            up, down, pair, pack, tiles = lax.optimization_barrier((up, down, pair, pack, tiles))
+            up, down, pair, pack, tiles, table = lax.optimization_barrier(
+                (up, down, pair, pack, tiles, table)
+            )
             packs = [pack] + [send(pack, k, 0, rows, feats) for k in range(1, feats)]
         if step == 3:
-            up[1], table = lax.optimization_barrier((up[1], table))
+            pair = load(pair)
+            up = [after(value, pair) for value in up]
+            down = [after(value, pair) for value in down]
         if step == top:
             table_pair = swap(after(table, up[0], down[0]), rows)
-            pair = load(pair)
-            sources.append(swap(after(away, up[0], down[0], pair), rows))
+            sources.append(swap(after(away, up[0], down[0]), rows))
             wanted.append((0, 1))
         for side in range(2):
             flip = side if step == 1 else 0
@@ -440,14 +440,14 @@
         )
         return out
 
-    near = sums[:2] + swap(after(sums[2:], scaled_pair), rows, 1)
-    total = near[0] + swap(near[1], rows, 2)
+    total = sums[:2] + swap(after(sums[2:], scaled_pair), rows, 1)
+    total = total + swap(total, rows, 2)
     bit, sends = 4, 0
 
     def ring(value, pairs):
         nonlocal total, bit, sends
         sends += 1
-        if sends >= 5 and sends % 4 == 1 and bit < 2 * rows:
+        if sends >= 6 and sends % 4 == 2 and bit < 2 * rows:
             value = after(value, total)
             total = after(total, value)
             if bit < rows:
@@ -472,12 +472,11 @@
             flow = 1 - i
             up[i] = ring(joined(up[i], mine[i]), forward)
             down[flow] = ring(joined(down[flow], mine[2 + flow]), backward)
-    near = jnp.stack([total, swap(total, rows, 2)])
-    far = swap(near, rows, 1)
+    far = swap(total, rows, 1)
     grad_self, grad_neigh, total = call(
         collect_kernel, "collect",
         [((hid, every), wide), ((hid, every), wide), ((8, every), wide)],
-        [VMEM] * 2, [VMEM] * 3, [], 4, 0, 16 * hid * every, near, far,
+        [VMEM] * 2, [VMEM] * 3, [], 4, 0, 16 * hid * every, total, far,
     )
     grad_bias = lax.dynamic_slice_in_dim(total[0], lax.axis_index("feat") * hid, hid)
     (grad_features,) = call(

time: 135 us -> 129 us (0.956)
  waiting for transfers between devices: 59.3 us -> 53.6 us
    ppermute x7, waiting for transfers between devices: 14.3 us -> 3.85 us  [shards(): up[side] = lax.ppermute(up[side], 'rows', forward)]
    ppermute x7, waiting for transfers between devices: 10 us -> 19.7 us  [shards(): down[side] = lax.ppermute(down[side], 'rows', backward)]
    ppermute x10 -> x9, waiting for transfers between devices: 21.9 us -> 16.8 us  [swap(): return lax.ppermute(value, 'rows', [(r, r ^ bit) for r in range(rows)])]
    ppermute x10 -> x9, starting transfers between devices: 3.88 us -> 4.95 us  [swap(): return lax.ppermute(value, 'rows', [(r, r ^ bit) for r in range(rows)])]
  transfers between devices with their start and end apart: 42 -> 41, of which waited for: 19 -> 22; matrix products, arithmetic and copies ran while one was open for 1% -> 1% of each run, Pallas kernels for 21% -> 22%
where the time goes in v8:
time: 129 us
  waiting for transfers between devices  53.6 us (42%)
  starting transfers between devices  37.1 us (29%)
  Pallas kernels  32.6 us (25%)
  local copies, waits for them, and re-layouts  4.64 us (4%)
    pallas_call x26, Pallas kernels, call(): pl.pallas_call(kernel, out_shape=[jax.ShapeDtypeStruct(shape, kind) for s...  32.6 us
    ppermute x7, waiting for transfers between devices, shards(): down[side] = lax.ppermute(down[side], 'rows', backward)  19.7 us
    ppermute x9, waiting for transfers between devices, swap(): return lax.ppermute(value, 'rows', [(r, r ^ bit) for r in range(rows)])  16.8 us
    ppermute x14, starting transfers between devices, ring(): return lax.ppermute(value, 'rows', pairs)  13.8 us
    ppermute x7, starting transfers between devices, shards(): up[side] = lax.ppermute(up[side], 'rows', forward)  11.8 us
    ppermute x4, waiting for transfers between devices, send(): return lax.ppermute(value, ('rows', 'feat'), pairs)  7.37 us
    ppermute x14, waiting for transfers between devices, ring(): return lax.ppermute(value, 'rows', pairs)  5.85 us
    ppermute x9, starting transfers between devices, swap(): return lax.ppermute(value, 'rows', [(r, r ^ bit) for r in range(rows)])  4.95 us
  transfers between devices with their start and end apart: 41, of which 22 were waited for; matrix products, arithmetic and copies ran while one was open for 1% of the time, Pallas kernels for 22%

profile of v8, /device:TPU:0, one launch (start us, length us, event | category | flops | bytes accessed | tf_op | source)
XLA Modules:
  0.0 129.0 jit_solution(6673284483122817162)
XLA Ops:
  2.2 2.7 %collective-permute-start = (bf16[64,2048]{1,0:T(8,128)(2,1)S(1)}, bf16[64,2048]{1,0:T(8,128)(2,1)S(1)}, u32[]{:S(2)}, u32[]{:S(2)}) collective-permute-start(bf16[64,2048]{1,0:T(8,128)(2,1)S(1)} %get-tuple-element.110.refs_0_), channel_id=1, source_target_pairs={{0,8},{2,10},{8,16},{10,18},{16,24},{18,26},{24,28},{26,30},{28,20... | collective-permute-start | bytes 786440 | tf_op jit(solution)/shard_map/ppermute | solution.py:371
  6.6 2.8 %copy-done = bf16[16,12,128,128]{3,2,1,0:T(8,128)(2,1)S(1)} copy-done((bf16[16,12,128,128]{3,2,1,0:T(8,128)(2,1)S(1)}, bf16[16,12,128,128]{3,2,1,0:T(8,128)(2,1)}, u32[]{:S(2)}) %copy-start) | copy-done | bytes 6291480
  10.1 3.2 %table.1 = s32[384]{0:T(512)S(1)} custom-call(s32[16,12]{1,0:T(8,128)S(1)} %copy-done.5), custom_call_target="tpu_custom_call" | custom-call | bytes 1536 | tf_op jit(solution)/shard_map/table/pallas_call | solution.py:307
  14.0 3.1 %collective-permute-done.1.refs_3_ = bf16[64,2048]{1,0:T(8,128)(2,1)S(1)} collective-permute-done((bf16[64,2048]{1,0:T(8,128)(2,1)S(1)}, bf16[64,2048]{1,0:T(8,128)(2,1)S(1)}, u32[]{:S(2)}, u32[]{:S(2)}) %collective-permute-start.1) | collective-permute-done | bytes 262176 | tf_op jit(solution)/shard_map/ppermute | solution.py:371
  23.7 2.8 %load.3.tiles.pair = bf16[16,12,128,128]{3,2,1,0:T(8,128)(2,1)S(1)} custom-call(bf16[16,12,128,128]{3,2,1,0:T(8,128)(2,1)} %collective-permute-done.4.source), custom_call_target="tpu_custom_call" | custom-call | bytes 12582912 | tf_op jit(solution)/shard_map/load/pallas_call | solution.py:307
  26.5 2.3 %collective-permute-done.7.refs_6_ = bf16[64,2048]{1,0:T(8,128)(2,1)S(1)} collective-permute-done((bf16[64,2048]{1,0:T(8,128)(2,1)S(1)}, bf16[64,2048]{1,0:T(8,128)(2,1)S(1)}, u32[]{:S(2)}, u32[]{:S(2)}) %collective-permute-start.7) | collective-permute-done | bytes 262176 | tf_op jit(solution)/shard_map/ppermute | solution.py:375
  30.9 3.5 %collective-permute-done.9.refs_8_ = bf16[64,2048]{1,0:T(8,128)(2,1)S(1)} collective-permute-done((bf16[64,2048]{1,0:T(8,128)(2,1)S(1)}, bf16[64,2048]{1,0:T(8,128)(2,1)S(1)}, u32[]{:S(2)}, u32[]{:S(2)}) %collective-permute-start.9) | collective-permute-done | bytes 262176 | tf_op jit(solution)/shard_map/ppermute | solution.py:375
  36.5 3.5 %collective-permute-done.11.refs_10_ = bf16[64,2048]{1,0:T(8,128)(2,1)S(1)} collective-permute-done((bf16[64,2048]{1,0:T(8,128)(2,1)S(1)}, bf16[64,2048]{1,0:T(8,128)(2,1)S(1)}, u32[]{:S(2)}, u32[]{:S(2)}) %collective-permute-start.11) | collective-permute-done | bytes 262176 | tf_op jit(solution)/shard_map/ppermute | solution.py:375
  40.6 4.4 %collective-permute-done.13.refs_12_ = bf16[64,2048]{1,0:T(8,128)(2,1)S(1)} collective-permute-done((bf16[64,2048]{1,0:T(8,128)(2,1)S(1)}, bf16[64,2048]{1,0:T(8,128)(2,1)S(1)}, u32[]{:S(2)}, u32[]{:S(2)}) %collective-permute-start.13) | collective-permute-done | bytes 262176 | tf_op jit(solution)/shard_map/ppermute | solution.py:375
  48.2 4.5 %collective-permute-done.16.refs_15_ = bf16[64,2048]{1,0:T(8,128)(2,1)S(1)} collective-permute-done((bf16[64,2048]{1,0:T(8,128)(2,1)S(1)}, bf16[64,2048]{1,0:T(8,128)(2,1)S(1)}, u32[]{:S(2)}, u32[]{:S(2)}) %collective-permute-start.16) | collective-permute-done | bytes 262176 | tf_op jit(solution)/shard_map/ppermute | solution.py:375
  52.8 4.4 %aggregate.3 = (bf16[64,2048]{1,0:T(8,128)(2,1)S(1)}, f32[1,2048]{1,0:T(1,128)}) custom-call(s32[384]{0:T(512)S(1)} %collective-permute-done.18.table.table_pair, bf16[16,12,128,128]{3,2,1,0:T(8,128)(2,1)S(1)} %load.3.tiles.pair, bf16[64,2048]{1,0:T(8,128)(2,1)S(1)} %get-tuple-element.110.refs_0_, bf16[64,2048]{1,0:T(8,128)(2,1)S(1)} %collective-permute-done.refs_1_, ...), custom_call_target="tpu_custom_call" | custom-call | flops 402653184 | bytes 10485760 | tf_op jit(solution)/shard_map/aggregate/pallas_call | solution.py:307
  57.9 3.9 %aggregate.2 = (bf16[64,2048]{1,0:T(8,128)(2,1)S(1)}, f32[1,2048]{1,0:T(1,128)S(1)}) custom-call(s32[384]{0:T(512)S(1)} %table.1, bf16[16,12,128,128]{3,2,1,0:T(8,128)(2,1)S(1)} %load.2.tiles.adj, bf16[64,2048]{1,0:T(8,128)(2,1)S(1)} %get-tuple-element.110.refs_0_, bf16[64,2048]{1,0:T(8,128)(2,1)S(1)} %collective-permute-done.refs_1_, ...), custom_call_target="tpu_custom_call" | custom-call | flops 402653184 | bytes 10485760 | tf_op jit(solution)/shard_map/aggregate/pallas_call | solution.py:307
  65.5 6.2 %collective-permute-done.17.refs_1_ = bf16[64,2048]{1,0:T(8,128)(2,1)S(1)} collective-permute-done((bf16[64,2048]{1,0:T(8,128)(2,1)S(1)}, bf16[64,2048]{1,0:T(8,128)(2,1)S(1)}, u32[]{:S(2)}, u32[]{:S(2)}) %collective-permute-start.17) | collective-permute-done | bytes 262176 | tf_op jit(solution)/shard_map/ppermute | solution.py:58
  71.6 3.0 %middle.1 = (bf16[128,2048]{1,0:T(8,128)(2,1)}, bf16[256,2048]{1,0:T(8,128)(2,1)S(1)}, bf16[128,2048]{1,0:T(8,128)(2,1)S(1)}, bf16[128,2048]{1,0:T(8,128)(2,1)S(1)}) custom-call(bf16[256,256]{1,0:T(8,128)(2,1)S(1)} %get-tuple-element.58.turned, bf16[128,256]{1,0:T(8,128)(2,1)S(1)} %copy-done.3, f32[1,2048]{1,0:T(1,128)S(1)} %get-tuple-element.71.inverse, ...), custom_call_target="tpu_custom_call" | custom-call | flops 402653184 | bytes 7340032 | tf_op jit(solution)/shard_map/middle/pallas_call | solution.py:307
  85.5 3.2 %collective-permute-done.22.arrived = bf16[64,2048]{1,0:T(8,128)(2,1)S(1)} collective-permute-done((bf16[64,2048]{1,0:T(8,128)(2,1)S(1)}, bf16[64,2048]{1,0:T(8,128)(2,1)S(1)}, u32[]{:S(2)}, u32[]{:S(2)}) %collective-permute-start.22) | collective-permute-done | bytes 262176 | tf_op jit(solution)/shard_map/ppermute | solution.py:456
  89.5 2.2 %collective-permute-done.34 = f32[2,136,128]{2,1,0:T(8,128)S(1)} collective-permute-done((f32[2,136,128]{2,1,0:T(8,128)S(1)}, f32[2,136,128]{2,1,0:T(8,128)S(1)}, u32[]{:S(2)}, u32[]{:S(2)}) %collective-permute-start.34) | collective-permute-done | bytes 139296 | tf_op jit(solution)/shard_map/ppermute | solution.py:49
  91.8 2.0 %collective-permute-start.36 = (f32[2,136,128]{2,1,0:T(8,128)S(1)}, f32[2,136,128]{2,1,0:T(8,128)S(1)}, u32[]{:S(2)}, u32[]{:S(2)}) collective-permute-start(f32[2,136,128]{2,1,0:T(8,128)S(1)} %add.24), channel_id=1, source_target_pairs={{0,8},{2,10},{4,12},{6,14},{8,0},{10,2},{12,4},{14,6},{16,24},{18,... | collective-permute-start | bytes 417800 | tf_op jit(solution)/shard_map/ppermute | solution.py:49
  97.6 2.1 %collective-permute-start.27 = (bf16[64,2048]{1,0:T(8,128)(2,1)S(1)}, bf16[64,2048]{1,0:T(8,128)(2,1)S(1)}, u32[]{:S(2)}, u32[]{:S(2)}) collective-permute-start(bf16[64,2048]{1,0:T(8,128)(2,1)S(1)} %join.13), channel_id=1, source_target_pairs={{0,4},{2,6},{8,0},{10,2},{16,8},{18,10},{24,16},{26,18},{28,24},{3... | collective-permute-start | bytes 786440 | tf_op jit(solution)/shard_map/ppermute | solution.py:456
  99.6 4.4 %collective-permute-done.36 = f32[2,136,128]{2,1,0:T(8,128)S(1)} collective-permute-done((f32[2,136,128]{2,1,0:T(8,128)S(1)}, f32[2,136,128]{2,1,0:T(8,128)S(1)}, u32[]{:S(2)}, u32[]{:S(2)}) %collective-permute-start.36) | collective-permute-done | bytes 139296 | tf_op jit(solution)/shard_map/ppermute | solution.py:49
  104.4 2.1 %collective-permute-start.37 = (bf16[64,2048]{1,0:T(8,128)(2,1)S(1)}, bf16[64,2048]{1,0:T(8,128)(2,1)S(1)}, u32[]{:S(2)}, u32[]{:S(2)}) collective-permute-start(bf16[64,2048]{1,0:T(8,128)(2,1)S(1)} %join.18), channel_id=1, source_target_pairs={{0,4},{2,6},{8,0},{10,2},{16,8},{18,10},{24,16},{26,18},{28,24},{3... | collective-permute-start | bytes 786440 | tf_op jit(solution)/shard_map/ppermute | solution.py:456
  107.2 2.4 %spread.4 = (f32[64,2048]{1,0:T(8,128)S(1)}, f32[64,2048]{1,0:T(8,128)S(1)}, f32[64,2048]{1,0:T(8,128)S(1)}, f32[64,2048]{1,0:T(8,128)S(1)}, f32[64,2048]{1,0:T(8,128)S(1)}, /*index=5*/f32[64,2048]{1,0:T(8,128)S(1)}) custom-call(s32[384]{0:T(512)S(1)} %table.1, s32[384]{0:T(512)S(1)} %collective-permute-done.18.table.table_pair, ...), custom_call_target="tpu_custom_call" | custom-call | flops 301989888 | bytes 6291456 | tf_op jit(solution)/shard_map/spread/pallas_call | solution.py:307
  109.7 2.2 %collective-permute-start.31 = (bf16[64,2048]{1,0:T(8,128)(2,1)S(1)}, bf16[64,2048]{1,0:T(8,128)(2,1)S(1)}, u32[]{:S(2)}, u32[]{:S(2)}) collective-permute-start(bf16[64,2048]{1,0:T(8,128)(2,1)S(1)} %join.16), channel_id=1, source_target_pairs={{0,8},{2,10},{8,16},{10,18},{16,24},{18,26},{24,28},{26,30},{28,20... | collective-permute-start | bytes 786440 | tf_op jit(solution)/shard_map/ppermute | solution.py:456
  113.0 6.8 %collective-permute-done.38 = f32[2,136,128]{2,1,0:T(8,128)S(1)} collective-permute-done((f32[2,136,128]{2,1,0:T(8,128)S(1)}, f32[2,136,128]{2,1,0:T(8,128)S(1)}, u32[]{:S(2)}, u32[]{:S(2)}) %collective-permute-start.38) | collective-permute-done | bytes 139296 | tf_op jit(solution)/shard_map/ppermute | solution.py:49
  121.4 2.0 %collective-permute-start.39 = (bf16[64,2048]{1,0:T(8,128)(2,1)}, bf16[64,2048]{1,0:T(8,128)(2,1)S(1)}, u32[]{:S(2)}, u32[]{:S(2)}) collective-permute-start(bf16[64,2048]{1,0:T(8,128)(2,1)} %join.19), channel_id=1, source_target_pairs={{0,4},{2,6},{8,0},{10,2},{16,8},{18,10},{24,16},{26,18},{28,24},{3... | collective-permute-start | bytes 786440 | tf_op jit(solution)/shard_map/ppermute | solution.py:456
  (106 shorter events, 48.3 us)
Async XLA Ops:
  0.6 17.5 %collective-permute-start.4 = (bf16[16,12,128,128]{3,2,1,0:T(8,128)(2,1)}, bf16[16,12,128,128]{3,2,1,0:T(8,128)(2,1)}, u32[]{:S(2)}, u32[]{:S(2)}) collective-permute-start(bf16[16,12,128,128]{3,2,1,0:T(8,128)(2,1)} %source.1), channel_id=1, source_target_pairs={{0,2},{2,0},{4,6},{6,4},{8,10},{10,8},{12,14},{14,12},{16,18},{18,... | collective-permute-start | bytes 18874376 | tf_op jit(solution)/shard_map/ppermute | solution.py:49
  2.2 11.4 %collective-permute-start = (bf16[64,2048]{1,0:T(8,128)(2,1)S(1)}, bf16[64,2048]{1,0:T(8,128)(2,1)S(1)}, u32[]{:S(2)}, u32[]{:S(2)}) collective-permute-start(bf16[64,2048]{1,0:T(8,128)(2,1)S(1)} %get-tuple-element.110.refs_0_), channel_id=1, source_target_pairs={{0,8},{2,10},{8,16},{10,18},{16,24},{18,26},{24,28},{26,30},{28,20... | collective-permute-start | bytes 786440 | tf_op jit(solution)/shard_map/ppermute | solution.py:371
  4.9 12.3 %collective-permute-start.1 = (bf16[64,2048]{1,0:T(8,128)(2,1)S(1)}, bf16[64,2048]{1,0:T(8,128)(2,1)S(1)}, u32[]{:S(2)}, u32[]{:S(2)}) collective-permute-start(bf16[64,2048]{1,0:T(8,128)(2,1)S(1)} %get-tuple-element.70), channel_id=1, source_target_pairs={{0,10},{2,8},{8,18},{10,16},{16,26},{18,24},{24,30},{26,28},{28,22... | collective-permute-start | bytes 786440 | tf_op jit(solution)/shard_map/ppermute | solution.py:371
  6.4 11.7 %collective-permute-start.3 = (bf16[64,2048]{1,0:T(8,128)(2,1)S(1)}, bf16[64,2048]{1,0:T(8,128)(2,1)S(1)}, u32[]{:S(2)}, u32[]{:S(2)}) collective-permute-start(bf16[64,2048]{1,0:T(8,128)(2,1)S(1)} %get-tuple-element.70), channel_id=1, source_target_pairs={{0,6},{2,4},{8,2},{10,0},{16,10},{18,8},{24,18},{26,16},{28,26},{3... | collective-permute-start | bytes 786440 | tf_op jit(solution)/shard_map/ppermute | solution.py:375
  18.2 45.3 %collective-permute-start.5 = (bf16[128,4736]{1,0:T(8,128)(2,1)S(1)}, bf16[128,4736]{1,0:T(8,128)(2,1)S(1)}, u32[]{:S(2)}, u32[]{:S(2)}) collective-permute-start(bf16[128,4736]{1,0:T(8,128)(2,1)S(1)} %pack.1.refs_0_), channel_id=1, source_target_pairs={{0,1},{1,0},{2,3},{3,2},{4,5},{5,4},{6,7},{7,6},{8,9},{9,8},{10,11... | collective-permute-start | bytes 3637256 | tf_op jit(solution)/shard_map/ppermute | solution.py:58
  21.7 12.7 %collective-permute-start.9 = (bf16[64,2048]{1,0:T(8,128)(2,1)S(1)}, bf16[64,2048]{1,0:T(8,128)(2,1)S(1)}, u32[]{:S(2)}, u32[]{:S(2)}) collective-permute-start(bf16[64,2048]{1,0:T(8,128)(2,1)S(1)} %collective-permute-done.3.refs_4_), channel_id=1, source_target_pairs={{0,4},{2,6},{8,0},{10,2},{16,8},{18,10},{24,16},{26,18},{28,24},{3... | collective-permute-start | bytes 786440 | tf_op jit(solution)/shard_map/ppermute | solution.py:375
  22.2 12.8 %collective-permute-start.8 = (bf16[64,2048]{1,0:T(8,128)(2,1)S(1)}, bf16[64,2048]{1,0:T(8,128)(2,1)S(1)}, u32[]{:S(2)}, u32[]{:S(2)}) collective-permute-start(bf16[64,2048]{1,0:T(8,128)(2,1)S(1)} %collective-permute-done.1.refs_3_), channel_id=1, source_target_pairs={{0,8},{2,10},{8,16},{10,18},{16,24},{18,26},{24,28},{26,30},{28,20... | collective-permute-start | bytes 786440 | tf_op jit(solution)/shard_map/ppermute | solution.py:371
  28.8 11.2 %collective-permute-start.11 = (bf16[64,2048]{1,0:T(8,128)(2,1)S(1)}, bf16[64,2048]{1,0:T(8,128)(2,1)S(1)}, u32[]{:S(2)}, u32[]{:S(2)}) collective-permute-start(bf16[64,2048]{1,0:T(8,128)(2,1)S(1)} %collective-permute-done.7.refs_6_), channel_id=1, source_target_pairs={{0,4},{2,6},{8,0},{10,2},{16,8},{18,10},{24,16},{26,18},{28,24},{3... | collective-permute-start | bytes 786440 | tf_op jit(solution)/shard_map/ppermute | solution.py:375
  29.4 11.2 %collective-permute-start.10 = (bf16[64,2048]{1,0:T(8,128)(2,1)S(1)}, bf16[64,2048]{1,0:T(8,128)(2,1)S(1)}, u32[]{:S(2)}, u32[]{:S(2)}) collective-permute-start(bf16[64,2048]{1,0:T(8,128)(2,1)S(1)} %collective-permute-done.6.refs_5_), channel_id=1, source_target_pairs={{0,8},{2,10},{8,16},{10,18},{16,24},{18,26},{24,28},{26,30},{28,20... | collective-permute-start | bytes 786440 | tf_op jit(solution)/shard_map/ppermute | solution.py:371
  35.0 12.1 %collective-permute-start.12 = (bf16[64,2048]{1,0:T(8,128)(2,1)S(1)}, bf16[64,2048]{1,0:T(8,128)(2,1)S(1)}, u32[]{:S(2)}, u32[]{:S(2)}) collective-permute-start(bf16[64,2048]{1,0:T(8,128)(2,1)S(1)} %collective-permute-done.8.refs_7_), channel_id=1, source_target_pairs={{0,8},{2,10},{8,16},{10,18},{16,24},{18,26},{24,28},{26,30},{28,20... | collective-permute-start | bytes 786440 | tf_op jit(solution)/shard_map/ppermute | solution.py:371
  78.1 11.4 %collective-permute-start.32 = (bf16[64,2048]{1,0:T(8,128)(2,1)S(1)}, bf16[64,2048]{1,0:T(8,128)(2,1)S(1)}, u32[]{:S(2)}, u32[]{:S(2)}) collective-permute-start(bf16[64,2048]{1,0:T(8,128)(2,1)S(1)} %get-tuple-element.94), channel_id=1, source_target_pairs={{0,4},{2,6},{8,0},{10,2},{16,8},{18,10},{24,16},{26,18},{28,24},{3... | collective-permute-start | bytes 786440 | tf_op jit(solution)/shard_map/ppermute | solution.py:456
  80.2 11.5 %collective-permute-start.34 = (f32[2,136,128]{2,1,0:T(8,128)S(1)}, f32[2,136,128]{2,1,0:T(8,128)S(1)}, u32[]{:S(2)}, u32[]{:S(2)}) collective-permute-start(f32[2,136,128]{2,1,0:T(8,128)S(1)} %slice_add_fusion), channel_id=1, source_target_pairs={{0,4},{2,6},{4,0},{6,2},{8,12},{10,14},{12,8},{14,10},{16,20},{18,... | collective-permute-start | bytes 417800 | tf_op jit(solution)/shard_map/ppermute | solution.py:49
  83.5 13.9 %collective-permute-start.29 = (bf16[64,2048]{1,0:T(8,128)(2,1)S(1)}, bf16[64,2048]{1,0:T(8,128)(2,1)S(1)}, u32[]{:S(2)}, u32[]{:S(2)}) collective-permute-start(bf16[64,2048]{1,0:T(8,128)(2,1)S(1)} %get-tuple-element.91), channel_id=1, source_target_pairs={{0,8},{2,10},{8,16},{10,18},{16,24},{18,26},{24,28},{26,30},{28,20... | collective-permute-start | bytes 786440 | tf_op jit(solution)/shard_map/ppermute | solution.py:456
  85.1 12.4 %collective-permute-start.26 = (bf16[64,2048]{1,0:T(8,128)(2,1)S(1)}, bf16[64,2048]{1,0:T(8,128)(2,1)S(1)}, u32[]{:S(2)}, u32[]{:S(2)}) collective-permute-start(bf16[64,2048]{1,0:T(8,128)(2,1)S(1)} %get-tuple-element.88), channel_id=1, source_target_pairs={{0,4},{2,6},{8,0},{10,2},{16,8},{18,10},{24,16},{26,18},{28,24},{3... | collective-permute-start | bytes 786440 | tf_op jit(solution)/shard_map/ppermute | solution.py:456
  88.8 15.3 %collective-permute-start.23 = (bf16[64,2048]{1,0:T(8,128)(2,1)S(1)}, bf16[64,2048]{1,0:T(8,128)(2,1)S(1)}, u32[]{:S(2)}, u32[]{:S(2)}) collective-permute-start(bf16[64,2048]{1,0:T(8,128)(2,1)S(1)} %join.10), channel_id=1, source_target_pairs={{0,8},{2,10},{8,16},{10,18},{16,24},{18,26},{24,28},{26,30},{28,20... | collective-permute-start | bytes 786440 | tf_op jit(solution)/shard_map/ppermute | solution.py:456
  91.7 12.6 %collective-permute-start.35 = (bf16[64,2048]{1,0:T(8,128)(2,1)S(1)}, bf16[64,2048]{1,0:T(8,128)(2,1)S(1)}, u32[]{:S(2)}, u32[]{:S(2)}) collective-permute-start(bf16[64,2048]{1,0:T(8,128)(2,1)S(1)} %join.17), channel_id=1, source_target_pairs={{0,4},{2,6},{8,0},{10,2},{16,8},{18,10},{24,16},{26,18},{28,24},{3... | collective-permute-start | bytes 786440 | tf_op jit(solution)/shard_map/ppermute | solution.py:456
  91.8 12.2 %collective-permute-start.36 = (f32[2,136,128]{2,1,0:T(8,128)S(1)}, f32[2,136,128]{2,1,0:T(8,128)S(1)}, u32[]{:S(2)}, u32[]{:S(2)}) collective-permute-start(f32[2,136,128]{2,1,0:T(8,128)S(1)} %add.24), channel_id=1, source_target_pairs={{0,8},{2,10},{4,12},{6,14},{8,0},{10,2},{12,4},{14,6},{16,24},{18,... | collective-permute-start | bytes 417800 | tf_op jit(solution)/shard_map/ppermute | solution.py:49
  97.4 12.2 %collective-permute-start.30 = (bf16[64,2048]{1,0:T(8,128)(2,1)S(1)}, bf16[64,2048]{1,0:T(8,128)(2,1)S(1)}, u32[]{:S(2)}, u32[]{:S(2)}) collective-permute-start(bf16[64,2048]{1,0:T(8,128)(2,1)S(1)} %join.15), channel_id=1, source_target_pairs={{0,8},{2,10},{8,16},{10,18},{16,24},{18,26},{24,28},{26,30},{28,20... | collective-permute-start | bytes 786440 | tf_op jit(solution)/shard_map/ppermute | solution.py:456
  97.6 14.3 %collective-permute-start.27 = (bf16[64,2048]{1,0:T(8,128)(2,1)S(1)}, bf16[64,2048]{1,0:T(8,128)(2,1)S(1)}, u32[]{:S(2)}, u32[]{:S(2)}) collective-permute-start(bf16[64,2048]{1,0:T(8,128)(2,1)S(1)} %join.13), channel_id=1, source_target_pairs={{0,4},{2,6},{8,0},{10,2},{16,8},{18,10},{24,16},{26,18},{28,24},{3... | collective-permute-start | bytes 786440 | tf_op jit(solution)/shard_map/ppermute | solution.py:456
  104.1 15.7 %collective-permute-start.24 = (bf16[64,2048]{1,0:T(8,128)(2,1)S(1)}, bf16[64,2048]{1,0:T(8,128)(2,1)S(1)}, u32[]{:S(2)}, u32[]{:S(2)}) collective-permute-start(bf16[64,2048]{1,0:T(8,128)(2,1)S(1)} %join.11), channel_id=1, source_target_pairs={{0,8},{2,10},{8,16},{10,18},{16,24},{18,26},{24,28},{26,30},{28,20... | collective-permute-start | bytes 786440 | tf_op jit(solution)/shard_map/ppermute | solution.py:456
  104.4 16.2 %collective-permute-start.37 = (bf16[64,2048]{1,0:T(8,128)(2,1)S(1)}, bf16[64,2048]{1,0:T(8,128)(2,1)S(1)}, u32[]{:S(2)}, u32[]{:S(2)}) collective-permute-start(bf16[64,2048]{1,0:T(8,128)(2,1)S(1)} %join.18), channel_id=1, source_target_pairs={{0,4},{2,6},{8,0},{10,2},{16,8},{18,10},{24,16},{26,18},{28,24},{3... | collective-permute-start | bytes 786440 | tf_op jit(solution)/shard_map/ppermute | solution.py:456
  106.5 13.3 %collective-permute-start.38 = (f32[2,136,128]{2,1,0:T(8,128)S(1)}, f32[2,136,128]{2,1,0:T(8,128)S(1)}, u32[]{:S(2)}, u32[]{:S(2)}) collective-permute-start(f32[2,136,128]{2,1,0:T(8,128)S(1)} %add.25), channel_id=1, source_target_pairs={{0,16},{2,18},{4,20},{6,22},{8,24},{10,26},{12,28},{14,30},{16,0},... | collective-permute-start | bytes 417800 | tf_op jit(solution)/shard_map/ppermute | solution.py:49
  109.7 17.3 %collective-permute-start.31 = (bf16[64,2048]{1,0:T(8,128)(2,1)S(1)}, bf16[64,2048]{1,0:T(8,128)(2,1)S(1)}, u32[]{:S(2)}, u32[]{:S(2)}) collective-permute-start(bf16[64,2048]{1,0:T(8,128)(2,1)S(1)} %join.16), channel_id=1, source_target_pairs={{0,8},{2,10},{8,16},{10,18},{16,24},{18,26},{24,28},{26,30},{28,20... | collective-permute-start | bytes 786440 | tf_op jit(solution)/shard_map/ppermute | solution.py:456
  112.6 14.5 %collective-permute-start.28 = (bf16[64,2048]{1,0:T(8,128)(2,1)}, bf16[64,2048]{1,0:T(8,128)(2,1)S(1)}, u32[]{:S(2)}, u32[]{:S(2)}) collective-permute-start(bf16[64,2048]{1,0:T(8,128)(2,1)} %join.14), channel_id=1, source_target_pairs={{0,4},{2,6},{8,0},{10,2},{16,8},{18,10},{24,16},{26,18},{28,24},{3... | collective-permute-start | bytes 786440 | tf_op jit(solution)/shard_map/ppermute | solution.py:456
  (24 other events, 143.9 us)

commit v9 on v8

--- a/solution.py
+++ b/solution.py
@@ -215,12 +215,14 @@
 
 
 def own_quarter():
-    return 2 * lax.rem(lax.axis_index("rows"), 2)
+    row = lax.axis_index("rows")
+    return 2 * lax.rem(row, 2) + lax.rem(row // 2, 2)
 
 
 def turned_quarter(mine, index):
-    turned = index // 2 + mine // 2 - 2 * (index // 2) * (mine // 2)
-    return 2 * turned + index % 2
+    core, x = index // 2, index % 2
+    core = core + mine // 2 - 2 * core * (mine // 2)
+    return 2 * core + x + lax.rem(mine, 2) - 2 * x * lax.rem(mine, 2)
 
 
 def weights_kernel(ws, x_own, agg_own, grad, self_own, sums):
@@ -440,16 +442,17 @@
         )
         return out
 
-    total = sums[:2] + swap(after(sums[2:], scaled_pair), rows, 1)
-    total = total + swap(total, rows, 2)
+    near = sums[:2] + swap(after(sums[2:], scaled_pair), rows, 1)
+    total = near[0] + swap(near[1], rows, 2)
     bit, sends = 4, 0
 
     def ring(value, pairs):
         nonlocal total, bit, sends
         sends += 1
-        if sends >= 6 and sends % 4 == 2 and bit < 2 * rows:
+        due = sends in (3, 5) or (sends >= 10 and sends % 4 == 2)
+        if due and bit < 2 * rows:
             value = after(value, total)
-            total = after(total, value)
+            total = after(total, value) if sends >= 10 else total
             if bit < rows:
                 total = total + swap(total, rows, bit)
             bit *= 2
@@ -472,11 +475,12 @@
             flow = 1 - i
             up[i] = ring(joined(up[i], mine[i]), forward)
             down[flow] = ring(joined(down[flow], mine[2 + flow]), backward)
-    far = swap(total, rows, 1)
+    near = jnp.stack([total, swap(total, rows, 2)])
+    far = swap(near, rows, 1)
     grad_self, grad_neigh, total = call(
         collect_kernel, "collect",
         [((hid, every), wide), ((hid, every), wide), ((8, every), wide)],
-        [VMEM] * 2, [VMEM] * 3, [], 4, 0, 16 * hid * every, total, far,
+        [VMEM] * 2, [VMEM] * 3, [], 4, 0, 16 * hid * every, near, far,
     )
     grad_bias = lax.dynamic_slice_in_dim(total[0], lax.axis_index("feat") * hid, hid)
     (grad_features,) = call(

time: 129 us -> 130 us (level)
  starting transfers between devices: 37.1 us -> 43.7 us
  waiting for transfers between devices: 53.6 us -> 47.5 us
    ppermute x9 -> x10, waiting for transfers between devices: 16.8 us -> 11.4 us  [swap(): return lax.ppermute(value, 'rows', [(r, r ^ bit) for r in range(rows)])]
    ppermute x14, starting transfers between devices: 13.8 us -> 18.9 us  [ring(): return lax.ppermute(value, 'rows', pairs)]
    ppermute x9 -> x10, starting transfers between devices: 4.95 us -> 6.47 us  [swap(): return lax.ppermute(value, 'rows', [(r, r ^ bit) for r in range(rows)])]
  transfers between devices with their start and end apart: 41 -> 42, of which waited for: 22 -> 21; matrix products, arithmetic and copies ran while one was open for 1% -> 1% of each run, Pallas kernels for 22% -> 22%
where the time goes in v9:
time: 130 us
  waiting for transfers between devices  47.5 us (37%)
  starting transfers between devices  43.7 us (34%)
  Pallas kernels  32.7 us (25%)
  local copies, waits for them, and re-layouts  4.64 us (4%)
    pallas_call x26, Pallas kernels, call(): pl.pallas_call(kernel, out_shape=[jax.ShapeDtypeStruct(shape, kind) for s...  32.7 us
    ppermute x7, waiting for transfers between devices, shards(): down[side] = lax.ppermute(down[side], 'rows', backward)  19.7 us
    ppermute x14, starting transfers between devices, ring(): return lax.ppermute(value, 'rows', pairs)  18.9 us
    ppermute x7, starting transfers between devices, shards(): up[side] = lax.ppermute(up[side], 'rows', forward)  11.8 us
    ppermute x10, waiting for transfers between devices, swap(): return lax.ppermute(value, 'rows', [(r, r ^ bit) for r in range(rows)])  11.4 us
    ppermute x4, waiting for transfers between devices, send(): return lax.ppermute(value, ('rows', 'feat'), pairs)  7.36 us
    ppermute x10, starting transfers between devices, swap(): return lax.ppermute(value, 'rows', [(r, r ^ bit) for r in range(rows)])  6.47 us
    ppermute x14, waiting for transfers between devices, ring(): return lax.ppermute(value, 'rows', pairs)  5.21 us
  transfers between devices with their start and end apart: 42, of which 21 were waited for; matrix products, arithmetic and copies ran while one was open for 1% of the time, Pallas kernels for 22%

profile of v9, /device:TPU:0, one launch (start us, length us, event | category | flops | bytes accessed | tf_op | source)
XLA Modules:
  0.0 129.6 jit_solution(3857905672206067751)
XLA Ops:
  2.2 2.7 %collective-permute-start = (bf16[64,2048]{1,0:T(8,128)(2,1)S(1)}, bf16[64,2048]{1,0:T(8,128)(2,1)S(1)}, u32[]{:S(2)}, u32[]{:S(2)}) collective-permute-start(bf16[64,2048]{1,0:T(8,128)(2,1)S(1)} %get-tuple-element.106.refs_0_), channel_id=1, source_target_pairs={{0,8},{2,10},{8,16},{10,18},{16,24},{18,26},{24,28},{26,30},{28,20... | collective-permute-start | bytes 786440 | tf_op jit(solution)/shard_map/ppermute | solution.py:373
  6.6 2.8 %copy-done = bf16[16,12,128,128]{3,2,1,0:T(8,128)(2,1)S(1)} copy-done((bf16[16,12,128,128]{3,2,1,0:T(8,128)(2,1)S(1)}, bf16[16,12,128,128]{3,2,1,0:T(8,128)(2,1)}, u32[]{:S(2)}) %copy-start) | copy-done | bytes 6291480
  10.1 3.2 %table.1 = s32[384]{0:T(512)S(1)} custom-call(s32[16,12]{1,0:T(8,128)S(1)} %copy-done.5), custom_call_target="tpu_custom_call" | custom-call | bytes 1536 | tf_op jit(solution)/shard_map/table/pallas_call | solution.py:309
  14.0 3.1 %collective-permute-done.1.refs_3_ = bf16[64,2048]{1,0:T(8,128)(2,1)S(1)} collective-permute-done((bf16[64,2048]{1,0:T(8,128)(2,1)S(1)}, bf16[64,2048]{1,0:T(8,128)(2,1)S(1)}, u32[]{:S(2)}, u32[]{:S(2)}) %collective-permute-start.1) | collective-permute-done | bytes 262176 | tf_op jit(solution)/shard_map/ppermute | solution.py:373
  23.7 2.8 %load.3.tiles.pair = bf16[16,12,128,128]{3,2,1,0:T(8,128)(2,1)S(1)} custom-call(bf16[16,12,128,128]{3,2,1,0:T(8,128)(2,1)} %collective-permute-done.4.source), custom_call_target="tpu_custom_call" | custom-call | bytes 12582912 | tf_op jit(solution)/shard_map/load/pallas_call | solution.py:309
  26.5 2.3 %collective-permute-done.7.refs_6_ = bf16[64,2048]{1,0:T(8,128)(2,1)S(1)} collective-permute-done((bf16[64,2048]{1,0:T(8,128)(2,1)S(1)}, bf16[64,2048]{1,0:T(8,128)(2,1)S(1)}, u32[]{:S(2)}, u32[]{:S(2)}) %collective-permute-start.7) | collective-permute-done | bytes 262176 | tf_op jit(solution)/shard_map/ppermute | solution.py:377
  30.9 3.5 %collective-permute-done.9.refs_8_ = bf16[64,2048]{1,0:T(8,128)(2,1)S(1)} collective-permute-done((bf16[64,2048]{1,0:T(8,128)(2,1)S(1)}, bf16[64,2048]{1,0:T(8,128)(2,1)S(1)}, u32[]{:S(2)}, u32[]{:S(2)}) %collective-permute-start.9) | collective-permute-done | bytes 262176 | tf_op jit(solution)/shard_map/ppermute | solution.py:377
  36.5 3.5 %collective-permute-done.11.refs_10_ = bf16[64,2048]{1,0:T(8,128)(2,1)S(1)} collective-permute-done((bf16[64,2048]{1,0:T(8,128)(2,1)S(1)}, bf16[64,2048]{1,0:T(8,128)(2,1)S(1)}, u32[]{:S(2)}, u32[]{:S(2)}) %collective-permute-start.11) | collective-permute-done | bytes 262176 | tf_op jit(solution)/shard_map/ppermute | solution.py:377
  40.6 4.4 %collective-permute-done.13.refs_12_ = bf16[64,2048]{1,0:T(8,128)(2,1)S(1)} collective-permute-done((bf16[64,2048]{1,0:T(8,128)(2,1)S(1)}, bf16[64,2048]{1,0:T(8,128)(2,1)S(1)}, u32[]{:S(2)}, u32[]{:S(2)}) %collective-permute-start.13) | collective-permute-done | bytes 262176 | tf_op jit(solution)/shard_map/ppermute | solution.py:377
  48.2 4.5 %collective-permute-done.16.refs_15_ = bf16[64,2048]{1,0:T(8,128)(2,1)S(1)} collective-permute-done((bf16[64,2048]{1,0:T(8,128)(2,1)S(1)}, bf16[64,2048]{1,0:T(8,128)(2,1)S(1)}, u32[]{:S(2)}, u32[]{:S(2)}) %collective-permute-start.16) | collective-permute-done | bytes 262176 | tf_op jit(solution)/shard_map/ppermute | solution.py:377
  52.8 4.4 %aggregate.3 = (bf16[64,2048]{1,0:T(8,128)(2,1)S(1)}, f32[1,2048]{1,0:T(1,128)}) custom-call(s32[384]{0:T(512)S(1)} %collective-permute-done.18.table.table_pair, bf16[16,12,128,128]{3,2,1,0:T(8,128)(2,1)S(1)} %load.3.tiles.pair, bf16[64,2048]{1,0:T(8,128)(2,1)S(1)} %get-tuple-element.106.refs_0_, bf16[64,2048]{1,0:T(8,128)(2,1)S(1)} %collective-permute-done.refs_1_, ...), custom_call_target="tpu_custom_call" | custom-call | flops 402653184 | bytes 10485760 | tf_op jit(solution)/shard_map/aggregate/pallas_call | solution.py:309
  57.9 3.8 %aggregate.2 = (bf16[64,2048]{1,0:T(8,128)(2,1)S(1)}, f32[1,2048]{1,0:T(1,128)S(1)}) custom-call(s32[384]{0:T(512)S(1)} %table.1, bf16[16,12,128,128]{3,2,1,0:T(8,128)(2,1)S(1)} %load.2.tiles.adj, bf16[64,2048]{1,0:T(8,128)(2,1)S(1)} %get-tuple-element.106.refs_0_, bf16[64,2048]{1,0:T(8,128)(2,1)S(1)} %collective-permute-done.refs_1_, ...), custom_call_target="tpu_custom_call" | custom-call | flops 402653184 | bytes 10485760 | tf_op jit(solution)/shard_map/aggregate/pallas_call | solution.py:309
  65.5 6.2 %collective-permute-done.17.refs_1_ = bf16[64,2048]{1,0:T(8,128)(2,1)S(1)} collective-permute-done((bf16[64,2048]{1,0:T(8,128)(2,1)S(1)}, bf16[64,2048]{1,0:T(8,128)(2,1)S(1)}, u32[]{:S(2)}, u32[]{:S(2)}) %collective-permute-start.17) | collective-permute-done | bytes 262176 | tf_op jit(solution)/shard_map/ppermute | solution.py:58
  71.6 3.0 %middle.1 = (bf16[128,2048]{1,0:T(8,128)(2,1)}, bf16[256,2048]{1,0:T(8,128)(2,1)S(1)}, bf16[128,2048]{1,0:T(8,128)(2,1)S(1)}, bf16[128,2048]{1,0:T(8,128)(2,1)S(1)}) custom-call(bf16[256,256]{1,0:T(8,128)(2,1)S(1)} %get-tuple-element.56.turned, bf16[128,256]{1,0:T(8,128)(2,1)S(1)} %copy-done.3, f32[1,2048]{1,0:T(1,128)S(1)} %get-tuple-element.69.inverse, ...), custom_call_target="tpu_custom_call" | custom-call | flops 402653184 | bytes 7340032 | tf_op jit(solution)/shard_map/middle/pallas_call | solution.py:309
  91.6 2.1 %collective-permute-start.26 = (bf16[64,2048]{1,0:T(8,128)(2,1)S(1)}, bf16[64,2048]{1,0:T(8,128)(2,1)S(1)}, u32[]{:S(2)}, u32[]{:S(2)}) collective-permute-start(bf16[64,2048]{1,0:T(8,128)(2,1)S(1)} %join.10), channel_id=1, source_target_pairs={{0,8},{2,10},{8,16},{10,18},{16,24},{18,26},{24,28},{26,30},{28,20... | collective-permute-start | bytes 786440 | tf_op jit(solution)/shard_map/ppermute | solution.py:459
  93.7 2.6 %collective-permute-start.37 = (f32[136,128]{1,0:T(8,128)S(1)}, f32[136,128]{1,0:T(8,128)S(1)}, u32[]{:S(2)}, u32[]{:S(2)}) collective-permute-start(f32[136,128]{1,0:T(8,128)S(1)} %add.25), channel_id=1, source_target_pairs={{0,16},{2,18},{4,20},{6,22},{8,24},{10,26},{12,28},{14,30},{16,0},... | collective-permute-start | bytes 208904 | tf_op jit(solution)/shard_map/ppermute | solution.py:49
  98.5 5.9 %collective-permute-done.37 = f32[136,128]{1,0:T(8,128)S(1)} collective-permute-done((f32[136,128]{1,0:T(8,128)S(1)}, f32[136,128]{1,0:T(8,128)S(1)}, u32[]{:S(2)}, u32[]{:S(2)}) %collective-permute-start.37) | collective-permute-done | bytes 69664 | tf_op jit(solution)/shard_map/ppermute | solution.py:49
  104.5 2.7 %collective-permute-start.33 = (bf16[64,2048]{1,0:T(8,128)(2,1)S(1)}, bf16[64,2048]{1,0:T(8,128)(2,1)S(1)}, u32[]{:S(2)}, u32[]{:S(2)}) collective-permute-start(bf16[64,2048]{1,0:T(8,128)(2,1)S(1)} %join.15), channel_id=1, source_target_pairs={{0,8},{2,10},{8,16},{10,18},{16,24},{18,26},{24,28},{26,30},{28,20... | collective-permute-start | bytes 786440 | tf_op jit(solution)/shard_map/ppermute | solution.py:459
  107.4 2.1 %collective-permute-start.27 = (bf16[64,2048]{1,0:T(8,128)(2,1)S(1)}, bf16[64,2048]{1,0:T(8,128)(2,1)S(1)}, u32[]{:S(2)}, u32[]{:S(2)}) collective-permute-start(bf16[64,2048]{1,0:T(8,128)(2,1)S(1)} %join.11), channel_id=1, source_target_pairs={{0,8},{2,10},{8,16},{10,18},{16,24},{18,26},{24,28},{26,30},{28,20... | collective-permute-start | bytes 786440 | tf_op jit(solution)/shard_map/ppermute | solution.py:459
  109.5 2.3 %spread.4 = (f32[64,2048]{1,0:T(8,128)S(1)}, f32[64,2048]{1,0:T(8,128)S(1)}, f32[64,2048]{1,0:T(8,128)S(1)}, f32[64,2048]{1,0:T(8,128)S(1)}, f32[64,2048]{1,0:T(8,128)S(1)}, /*index=5*/f32[64,2048]{1,0:T(8,128)S(1)}) custom-call(s32[384]{0:T(512)S(1)} %table.1, s32[384]{0:T(512)S(1)} %collective-permute-done.18.table.table_pair, ...), custom_call_target="tpu_custom_call" | custom-call | flops 301989888 | bytes 6291456 | tf_op jit(solution)/shard_map/spread/pallas_call | solution.py:309
  111.9 2.0 %collective-permute-start.31 = (bf16[64,2048]{1,0:T(8,128)(2,1)S(1)}, bf16[64,2048]{1,0:T(8,128)(2,1)S(1)}, u32[]{:S(2)}, u32[]{:S(2)}) collective-permute-start(bf16[64,2048]{1,0:T(8,128)(2,1)S(1)} %join.14), channel_id=1, source_target_pairs={{0,4},{2,6},{8,0},{10,2},{16,8},{18,10},{24,16},{26,18},{28,24},{3... | collective-permute-start | bytes 786440 | tf_op jit(solution)/shard_map/ppermute | solution.py:459
  114.7 2.5 %collective-permute-start.34 = (bf16[64,2048]{1,0:T(8,128)(2,1)}, bf16[64,2048]{1,0:T(8,128)(2,1)S(1)}, u32[]{:S(2)}, u32[]{:S(2)}) collective-permute-start(bf16[64,2048]{1,0:T(8,128)(2,1)} %join.16), channel_id=1, source_target_pairs={{0,8},{2,10},{8,16},{10,18},{16,24},{18,26},{24,28},{26,30},{28,20... | collective-permute-start | bytes 786440 | tf_op jit(solution)/shard_map/ppermute | solution.py:459
  120.4 2.5 %collective-permute-start.28 = (bf16[64,2048]{1,0:T(8,128)(2,1)}, bf16[64,2048]{1,0:T(8,128)(2,1)S(1)}, u32[]{:S(2)}, u32[]{:S(2)}) collective-permute-start(bf16[64,2048]{1,0:T(8,128)(2,1)} %join.12), channel_id=1, source_target_pairs={{0,8},{2,10},{8,16},{10,18},{16,24},{18,26},{24,28},{26,30},{28,20... | collective-permute-start | bytes 786440 | tf_op jit(solution)/shard_map/ppermute | solution.py:459
  126.6 1.9 %collective-permute-done.28.a_low = bf16[64,2048]{1,0:T(8,128)(2,1)S(1)} collective-permute-done((bf16[64,2048]{1,0:T(8,128)(2,1)}, bf16[64,2048]{1,0:T(8,128)(2,1)S(1)}, u32[]{:S(2)}, u32[]{:S(2)}) %collective-permute-start.28) | collective-permute-done | bytes 262176 | tf_op jit(solution)/shard_map/ppermute | solution.py:459
  (110 shorter events, 51.7 us)
Async XLA Ops:
  0.6 17.5 %collective-permute-start.4 = (bf16[16,12,128,128]{3,2,1,0:T(8,128)(2,1)}, bf16[16,12,128,128]{3,2,1,0:T(8,128)(2,1)}, u32[]{:S(2)}, u32[]{:S(2)}) collective-permute-start(bf16[16,12,128,128]{3,2,1,0:T(8,128)(2,1)} %source.1), channel_id=1, source_target_pairs={{0,2},{2,0},{4,6},{6,4},{8,10},{10,8},{12,14},{14,12},{16,18},{18,... | collective-permute-start | bytes 18874376 | tf_op jit(solution)/shard_map/ppermute | solution.py:49
  2.2 11.4 %collective-permute-start = (bf16[64,2048]{1,0:T(8,128)(2,1)S(1)}, bf16[64,2048]{1,0:T(8,128)(2,1)S(1)}, u32[]{:S(2)}, u32[]{:S(2)}) collective-permute-start(bf16[64,2048]{1,0:T(8,128)(2,1)S(1)} %get-tuple-element.106.refs_0_), channel_id=1, source_target_pairs={{0,8},{2,10},{8,16},{10,18},{16,24},{18,26},{24,28},{26,30},{28,20... | collective-permute-start | bytes 786440 | tf_op jit(solution)/shard_map/ppermute | solution.py:373
  4.9 12.3 %collective-permute-start.1 = (bf16[64,2048]{1,0:T(8,128)(2,1)S(1)}, bf16[64,2048]{1,0:T(8,128)(2,1)S(1)}, u32[]{:S(2)}, u32[]{:S(2)}) collective-permute-start(bf16[64,2048]{1,0:T(8,128)(2,1)S(1)} %get-tuple-element.68), channel_id=1, source_target_pairs={{0,10},{2,8},{8,18},{10,16},{16,26},{18,24},{24,30},{26,28},{28,22... | collective-permute-start | bytes 786440 | tf_op jit(solution)/shard_map/ppermute | solution.py:373
  6.4 11.7 %collective-permute-start.3 = (bf16[64,2048]{1,0:T(8,128)(2,1)S(1)}, bf16[64,2048]{1,0:T(8,128)(2,1)S(1)}, u32[]{:S(2)}, u32[]{:S(2)}) collective-permute-start(bf16[64,2048]{1,0:T(8,128)(2,1)S(1)} %get-tuple-element.68), channel_id=1, source_target_pairs={{0,6},{2,4},{8,2},{10,0},{16,10},{18,8},{24,18},{26,16},{28,26},{3... | collective-permute-start | bytes 786440 | tf_op jit(solution)/shard_map/ppermute | solution.py:377
  18.2 45.3 %collective-permute-start.5 = (bf16[128,4736]{1,0:T(8,128)(2,1)S(1)}, bf16[128,4736]{1,0:T(8,128)(2,1)S(1)}, u32[]{:S(2)}, u32[]{:S(2)}) collective-permute-start(bf16[128,4736]{1,0:T(8,128)(2,1)S(1)} %pack.1.refs_0_), channel_id=1, source_target_pairs={{0,1},{1,0},{2,3},{3,2},{4,5},{5,4},{6,7},{7,6},{8,9},{9,8},{10,11... | collective-permute-start | bytes 3637256 | tf_op jit(solution)/shard_map/ppermute | solution.py:58
  21.7 12.7 %collective-permute-start.9 = (bf16[64,2048]{1,0:T(8,128)(2,1)S(1)}, bf16[64,2048]{1,0:T(8,128)(2,1)S(1)}, u32[]{:S(2)}, u32[]{:S(2)}) collective-permute-start(bf16[64,2048]{1,0:T(8,128)(2,1)S(1)} %collective-permute-done.3.refs_4_), channel_id=1, source_target_pairs={{0,4},{2,6},{8,0},{10,2},{16,8},{18,10},{24,16},{26,18},{28,24},{3... | collective-permute-start | bytes 786440 | tf_op jit(solution)/shard_map/ppermute | solution.py:377
  22.2 12.8 %collective-permute-start.8 = (bf16[64,2048]{1,0:T(8,128)(2,1)S(1)}, bf16[64,2048]{1,0:T(8,128)(2,1)S(1)}, u32[]{:S(2)}, u32[]{:S(2)}) collective-permute-start(bf16[64,2048]{1,0:T(8,128)(2,1)S(1)} %collective-permute-done.1.refs_3_), channel_id=1, source_target_pairs={{0,8},{2,10},{8,16},{10,18},{16,24},{18,26},{24,28},{26,30},{28,20... | collective-permute-start | bytes 786440 | tf_op jit(solution)/shard_map/ppermute | solution.py:373
  28.8 11.2 %collective-permute-start.11 = (bf16[64,2048]{1,0:T(8,128)(2,1)S(1)}, bf16[64,2048]{1,0:T(8,128)(2,1)S(1)}, u32[]{:S(2)}, u32[]{:S(2)}) collective-permute-start(bf16[64,2048]{1,0:T(8,128)(2,1)S(1)} %collective-permute-done.7.refs_6_), channel_id=1, source_target_pairs={{0,4},{2,6},{8,0},{10,2},{16,8},{18,10},{24,16},{26,18},{28,24},{3... | collective-permute-start | bytes 786440 | tf_op jit(solution)/shard_map/ppermute | solution.py:377
  29.4 11.2 %collective-permute-start.10 = (bf16[64,2048]{1,0:T(8,128)(2,1)S(1)}, bf16[64,2048]{1,0:T(8,128)(2,1)S(1)}, u32[]{:S(2)}, u32[]{:S(2)}) collective-permute-start(bf16[64,2048]{1,0:T(8,128)(2,1)S(1)} %collective-permute-done.6.refs_5_), channel_id=1, source_target_pairs={{0,8},{2,10},{8,16},{10,18},{16,24},{18,26},{24,28},{26,30},{28,20... | collective-permute-start | bytes 786440 | tf_op jit(solution)/shard_map/ppermute | solution.py:373
  34.4 10.6 %collective-permute-start.13 = (bf16[64,2048]{1,0:T(8,128)(2,1)S(1)}, bf16[64,2048]{1,0:T(8,128)(2,1)S(1)}, u32[]{:S(2)}, u32[]{:S(2)}) collective-permute-start(bf16[64,2048]{1,0:T(8,128)(2,1)S(1)} %collective-permute-done.9.refs_8_), channel_id=1, source_target_pairs={{0,4},{2,6},{8,0},{10,2},{16,8},{18,10},{24,16},{26,18},{28,24},{3... | collective-permute-start | bytes 786440 | tf_op jit(solution)/shard_map/ppermute | solution.py:377
  35.0 12.1 %collective-permute-start.12 = (bf16[64,2048]{1,0:T(8,128)(2,1)S(1)}, bf16[64,2048]{1,0:T(8,128)(2,1)S(1)}, u32[]{:S(2)}, u32[]{:S(2)}) collective-permute-start(bf16[64,2048]{1,0:T(8,128)(2,1)S(1)} %collective-permute-done.8.refs_7_), channel_id=1, source_target_pairs={{0,8},{2,10},{8,16},{10,18},{16,24},{18,26},{24,28},{26,30},{28,20... | collective-permute-start | bytes 786440 | tf_op jit(solution)/shard_map/ppermute | solution.py:373
  61.7 9.9 %collective-permute-start.17 = (bf16[64,2048]{1,0:T(8,128)(2,1)S(1)}, bf16[64,2048]{1,0:T(8,128)(2,1)S(1)}, u32[]{:S(2)}, u32[]{:S(2)}) collective-permute-start(bf16[64,2048]{1,0:T(8,128)(2,1)S(1)} %get-tuple-element.72.refs_0_), channel_id=1, source_target_pairs={{0,1},{1,0},{2,3},{3,2},{4,5},{5,4},{6,7},{7,6},{8,9},{9,8},{10,11... | collective-permute-start | bytes 786440 | tf_op jit(solution)/shard_map/ppermute | solution.py:58
  86.3 11.7 %collective-permute-start.29 = (bf16[64,2048]{1,0:T(8,128)(2,1)S(1)}, bf16[64,2048]{1,0:T(8,128)(2,1)S(1)}, u32[]{:S(2)}, u32[]{:S(2)}) collective-permute-start(bf16[64,2048]{1,0:T(8,128)(2,1)S(1)} %get-tuple-element.89), channel_id=1, source_target_pairs={{0,4},{2,6},{8,0},{10,2},{16,8},{18,10},{24,16},{26,18},{28,24},{3... | collective-permute-start | bytes 786440 | tf_op jit(solution)/shard_map/ppermute | solution.py:459
  87.2 17.2 %collective-permute-start.32 = (bf16[64,2048]{1,0:T(8,128)(2,1)S(1)}, bf16[64,2048]{1,0:T(8,128)(2,1)S(1)}, u32[]{:S(2)}, u32[]{:S(2)}) collective-permute-start(bf16[64,2048]{1,0:T(8,128)(2,1)S(1)} %get-tuple-element.93), channel_id=1, source_target_pairs={{0,8},{2,10},{8,16},{10,18},{16,24},{18,26},{24,28},{26,30},{28,20... | collective-permute-start | bytes 786440 | tf_op jit(solution)/shard_map/ppermute | solution.py:459
  90.1 17.1 %collective-permute-start.36 = (bf16[64,2048]{1,0:T(8,128)(2,1)S(1)}, bf16[64,2048]{1,0:T(8,128)(2,1)S(1)}, u32[]{:S(2)}, u32[]{:S(2)}) collective-permute-start(bf16[64,2048]{1,0:T(8,128)(2,1)S(1)} %join.17), channel_id=1, source_target_pairs={{0,4},{2,6},{8,0},{10,2},{16,8},{18,10},{24,16},{26,18},{28,24},{3... | collective-permute-start | bytes 786440 | tf_op jit(solution)/shard_map/ppermute | solution.py:459
  91.6 15.8 %collective-permute-start.26 = (bf16[64,2048]{1,0:T(8,128)(2,1)S(1)}, bf16[64,2048]{1,0:T(8,128)(2,1)S(1)}, u32[]{:S(2)}, u32[]{:S(2)}) collective-permute-start(bf16[64,2048]{1,0:T(8,128)(2,1)S(1)} %join.10), channel_id=1, source_target_pairs={{0,8},{2,10},{8,16},{10,18},{16,24},{18,26},{24,28},{26,30},{28,20... | collective-permute-start | bytes 786440 | tf_op jit(solution)/shard_map/ppermute | solution.py:459
  93.7 10.7 %collective-permute-start.37 = (f32[136,128]{1,0:T(8,128)S(1)}, f32[136,128]{1,0:T(8,128)S(1)}, u32[]{:S(2)}, u32[]{:S(2)}) collective-permute-start(f32[136,128]{1,0:T(8,128)S(1)} %add.25), channel_id=1, source_target_pairs={{0,16},{2,18},{4,20},{6,22},{8,24},{10,26},{12,28},{14,30},{16,0},... | collective-permute-start | bytes 208904 | tf_op jit(solution)/shard_map/ppermute | solution.py:49
  98.2 13.7 %collective-permute-start.30 = (bf16[64,2048]{1,0:T(8,128)(2,1)S(1)}, bf16[64,2048]{1,0:T(8,128)(2,1)S(1)}, u32[]{:S(2)}, u32[]{:S(2)}) collective-permute-start(bf16[64,2048]{1,0:T(8,128)(2,1)S(1)} %join.13), channel_id=1, source_target_pairs={{0,4},{2,6},{8,0},{10,2},{16,8},{18,10},{24,16},{26,18},{28,24},{3... | collective-permute-start | bytes 786440 | tf_op jit(solution)/shard_map/ppermute | solution.py:459
  104.5 9.5 %collective-permute-start.33 = (bf16[64,2048]{1,0:T(8,128)(2,1)S(1)}, bf16[64,2048]{1,0:T(8,128)(2,1)S(1)}, u32[]{:S(2)}, u32[]{:S(2)}) collective-permute-start(bf16[64,2048]{1,0:T(8,128)(2,1)S(1)} %join.15), channel_id=1, source_target_pairs={{0,8},{2,10},{8,16},{10,18},{16,24},{18,26},{24,28},{26,30},{28,20... | collective-permute-start | bytes 786440 | tf_op jit(solution)/shard_map/ppermute | solution.py:459
  107.3 9.9 %collective-permute-start.38 = (bf16[64,2048]{1,0:T(8,128)(2,1)S(1)}, bf16[64,2048]{1,0:T(8,128)(2,1)S(1)}, u32[]{:S(2)}, u32[]{:S(2)}) collective-permute-start(bf16[64,2048]{1,0:T(8,128)(2,1)S(1)} %join.18), channel_id=1, source_target_pairs={{0,4},{2,6},{8,0},{10,2},{16,8},{18,10},{24,16},{26,18},{28,24},{3... | collective-permute-start | bytes 786440 | tf_op jit(solution)/shard_map/ppermute | solution.py:459
  107.4 12.2 %collective-permute-start.27 = (bf16[64,2048]{1,0:T(8,128)(2,1)S(1)}, bf16[64,2048]{1,0:T(8,128)(2,1)S(1)}, u32[]{:S(2)}, u32[]{:S(2)}) collective-permute-start(bf16[64,2048]{1,0:T(8,128)(2,1)S(1)} %join.11), channel_id=1, source_target_pairs={{0,8},{2,10},{8,16},{10,18},{16,24},{18,26},{24,28},{26,30},{28,20... | collective-permute-start | bytes 786440 | tf_op jit(solution)/shard_map/ppermute | solution.py:459
  109.5 13.4 %collective-permute-start.40 = (f32[136,128]{1,0:T(8,128)S(1)}, f32[136,128]{1,0:T(8,128)S(1)}, u32[]{:S(2)}, u32[]{:S(2)}) collective-permute-start(f32[136,128]{1,0:T(8,128)S(1)} %add.26), channel_id=1, source_target_pairs={{0,4},{2,6},{4,0},{6,2},{8,12},{10,14},{12,8},{14,10},{16,20},{18,... | collective-permute-start | bytes 208904 | tf_op jit(solution)/shard_map/ppermute | solution.py:49
  111.9 14.7 %collective-permute-start.31 = (bf16[64,2048]{1,0:T(8,128)(2,1)S(1)}, bf16[64,2048]{1,0:T(8,128)(2,1)S(1)}, u32[]{:S(2)}, u32[]{:S(2)}) collective-permute-start(bf16[64,2048]{1,0:T(8,128)(2,1)S(1)} %join.14), channel_id=1, source_target_pairs={{0,4},{2,6},{8,0},{10,2},{16,8},{18,10},{24,16},{26,18},{28,24},{3... | collective-permute-start | bytes 786440 | tf_op jit(solution)/shard_map/ppermute | solution.py:459
  114.7 11.9 %collective-permute-start.34 = (bf16[64,2048]{1,0:T(8,128)(2,1)}, bf16[64,2048]{1,0:T(8,128)(2,1)S(1)}, u32[]{:S(2)}, u32[]{:S(2)}) collective-permute-start(bf16[64,2048]{1,0:T(8,128)(2,1)} %join.16), channel_id=1, source_target_pairs={{0,8},{2,10},{8,16},{10,18},{16,24},{18,26},{24,28},{26,30},{28,20... | collective-permute-start | bytes 786440 | tf_op jit(solution)/shard_map/ppermute | solution.py:459
  (25 other events, 147.5 us)

commit v10 on v9

--- a/solution.py
+++ b/solution.py
@@ -423,14 +423,14 @@
         [VMEM] * 2, [VMEM], [], 4, 0, 8 * hid * width, scaled, scaled_pair,
     )
 
-    def spread(offsets, kinds):
+    def spread(offsets, kinds, gate=None):
         n = 2 * CAP * len(offsets)
         return call(
             bind(spread_kernel, (rows, offsets, kinds)), "spread",
             [((half, width), kind) for kind in kinds],
             [SMEM] * 2 + [VMEM] * 3, [VMEM] * len(kinds), [pltpu.VMEM((hid, width), wide)],
             9, 2 * n * hid * tile * tile, 8 * hid * width * len(offsets),
-            table, table_pair, tiles, pair, held,
+            table, table_pair, tiles, pair, held if gate is None else after(held, gate),
         )
 
     def joined(arrived, mine):
@@ -449,32 +449,32 @@
     def ring(value, pairs):
         nonlocal total, bit, sends
         sends += 1
-        due = sends in (3, 5) or (sends >= 10 and sends % 4 == 2)
-        if due and bit < 2 * rows:
+        if sends % 7 == 5 and bit < rows:
+            total = total + after(swap(total, rows, bit), value)
+            bit *= 2
+        if sends == 9:
             value = after(value, total)
-            total = after(total, value) if sends >= 10 else total
-            if bit < rows:
-                total = total + swap(total, rows, bit)
-            bit *= 2
         return lax.ppermute(value, "rows", pairs)
 
     up, down = [None, None], [None, None]
     forward, backward = ring_pairs(rows, 1), ring_pairs(rows, -1)
-    for level in range(top, 0, -1):
-        if level == top:
-            low, high = spread((top,), (narrow, narrow))
-            up[0] = ring(low, forward)
-            down[1] = ring(high, backward)
-            continue
-        kinds = tuple(narrow if arrived is None else wide for arrived in up + down)
-        offsets = (level, -level)
-        if level == 1:
-            offsets, kinds = (1, -1, 0), kinds + (wide, wide)
-        mine = spread(offsets, kinds)
+    low, high = spread((top,), (narrow, narrow))
+    up[0], down[1] = ring(low, forward), ring(high, backward)
+    mine = spread((top - 1, 1 - top), (wide, narrow, narrow, wide))
+    for level in range(top - 1, 0, -1):
+        offsets = (level - 1, 1 - level) if level > 1 else (0,)
+        later = spread(offsets, (wide, wide) * len(offsets))
         for i in (1, 0):
             flow = 1 - i
-            up[i] = ring(joined(up[i], mine[i]), forward)
+            value = joined(up[i], mine[i])
+            if i == 1 and level > 1:
+                value = after(value, later[0])
+            up[i] = ring(value, forward)
             down[flow] = ring(joined(down[flow], mine[2 + flow]), backward)
+        mine = later
+    while bit < rows:
+        total = total + swap(total, rows, bit)
+        bit *= 2
     near = jnp.stack([total, swap(total, rows, 2)])
     far = swap(near, rows, 1)
     grad_self, grad_neigh, total = call(
@@ -485,7 +485,7 @@
     grad_bias = lax.dynamic_slice_in_dim(total[0], lax.axis_index("feat") * hid, hid)
     (grad_features,) = call(
         finish_kernel, "finish", [((hid, width), narrow)], [VMEM] * 7, [VMEM], [], 6, 0,
-        8 * hid * width, self_own, mine[4], mine[5], up[0], down[0], up[1], down[1],
+        8 * hid * width, self_own, *mine, up[0], down[0], up[1], down[1],
     )
     return (activation, grad_features, grad_self, grad_neigh, grad_bias)
 

time: 130 us -> 131 us (level)
  local copies, waits for them, and re-layouts: 4.64 us -> 10.2 us
  waiting for transfers between devices: 47.5 us -> 44.7 us
  starting transfers between devices: 43.7 us -> 42 us
    unnamed x14 -> x22, local copies, waits for them, and re-layouts: 3.04 us -> 8.61 us
    ppermute x14, starting transfers between devices: 18.9 us -> 15.8 us  [ring(): return lax.ppermute(value, 'rows', pairs)]
    ppermute x10, waiting for transfers between devices: 11.4 us -> 9.79 us  [swap(): return lax.ppermute(value, 'rows', [(r, r ^ bit) for r in range(rows)])]
    ppermute x10, starting transfers between devices: 6.47 us -> 7.86 us  [swap(): return lax.ppermute(value, 'rows', [(r, r ^ bit) for r in range(rows)])]
    pallas_call x26 -> x27, Pallas kernels: 32.7 us -> 33.2 us  [call(): pl.pallas_call(kernel, out_shape=[jax.ShapeDtypeStruct(shape, kind) for s...]
  transfers between devices with their start and end apart: 42 -> 42, of which waited for: 21 -> 19; matrix products, arithmetic and copies ran while one was open for 1% -> 1% of each run, Pallas kernels for 22% -> 22%
where the time goes in v10:
time: 131 us
  waiting for transfers between devices  44.7 us (34%)
  starting transfers between devices  42 us (32%)
  Pallas kernels  33.2 us (25%)
  local copies, waits for them, and re-layouts  10.2 us (8%)
    pallas_call x27, Pallas kernels, call(): pl.pallas_call(kernel, out_shape=[jax.ShapeDtypeStruct(shape, kind) for s...  33.2 us
    ppermute x7, waiting for transfers between devices, shards(): down[side] = lax.ppermute(down[side], 'rows', backward)  19.7 us
    ppermute x14, starting transfers between devices, ring(): return lax.ppermute(value, 'rows', pairs)  15.8 us
    ppermute x7, starting transfers between devices, shards(): up[side] = lax.ppermute(up[side], 'rows', forward)  11.8 us
    ppermute x10, waiting for transfers between devices, swap(): return lax.ppermute(value, 'rows', [(r, r ^ bit) for r in range(rows)])  9.79 us
    unnamed x22, local copies, waits for them, and re-layouts  8.61 us
    ppermute x10, starting transfers between devices, swap(): return lax.ppermute(value, 'rows', [(r, r ^ bit) for r in range(rows)])  7.86 us
    ppermute x4, waiting for transfers between devices, send(): return lax.ppermute(value, ('rows', 'feat'), pairs)  7.36 us
  transfers between devices with their start and end apart: 42, of which 19 were waited for; matrix products, arithmetic and copies ran while one was open for 1% of the time, Pallas kernels for 22%

profile of v10, /device:TPU:0, one launch (start us, length us, event | category | flops | bytes accessed | tf_op | source)
XLA Modules:
  0.0 131.1 jit_solution(12661392482847021272)
XLA Ops:
  2.2 2.7 %collective-permute-start = (bf16[64,2048]{1,0:T(8,128)(2,1)S(1)}, bf16[64,2048]{1,0:T(8,128)(2,1)S(1)}, u32[]{:S(2)}, u32[]{:S(2)}) collective-permute-start(bf16[64,2048]{1,0:T(8,128)(2,1)S(1)} %get-tuple-element.108.refs_0_), channel_id=1, source_target_pairs={{0,8},{2,10},{8,16},{10,18},{16,24},{18,26},{24,28},{26,30},{28,20... | collective-permute-start | bytes 786440 | tf_op jit(solution)/shard_map/ppermute | solution.py:373
  6.6 2.8 %copy-done.4 = bf16[16,12,128,128]{3,2,1,0:T(8,128)(2,1)S(1)} copy-done((bf16[16,12,128,128]{3,2,1,0:T(8,128)(2,1)S(1)}, bf16[16,12,128,128]{3,2,1,0:T(8,128)(2,1)}, u32[]{:S(2)}) %copy-start.4) | copy-done | bytes 6291480
  10.1 3.2 %table.1 = s32[384]{0:T(512)S(1)} custom-call(s32[16,12]{1,0:T(8,128)S(1)} %copy-done.9), custom_call_target="tpu_custom_call" | custom-call | bytes 1536 | tf_op jit(solution)/shard_map/table/pallas_call | solution.py:309
  14.0 3.1 %collective-permute-done.1.refs_3_ = bf16[64,2048]{1,0:T(8,128)(2,1)S(1)} collective-permute-done((bf16[64,2048]{1,0:T(8,128)(2,1)S(1)}, bf16[64,2048]{1,0:T(8,128)(2,1)S(1)}, u32[]{:S(2)}, u32[]{:S(2)}) %collective-permute-start.1) | collective-permute-done | bytes 262176 | tf_op jit(solution)/shard_map/ppermute | solution.py:373
  23.7 2.8 %load.3.tiles.pair = bf16[16,12,128,128]{3,2,1,0:T(8,128)(2,1)S(1)} custom-call(bf16[16,12,128,128]{3,2,1,0:T(8,128)(2,1)} %collective-permute-done.4.source), custom_call_target="tpu_custom_call" | custom-call | bytes 12582912 | tf_op jit(solution)/shard_map/load/pallas_call | solution.py:309
  26.5 2.3 %collective-permute-done.7.refs_6_ = bf16[64,2048]{1,0:T(8,128)(2,1)S(1)} collective-permute-done((bf16[64,2048]{1,0:T(8,128)(2,1)S(1)}, bf16[64,2048]{1,0:T(8,128)(2,1)S(1)}, u32[]{:S(2)}, u32[]{:S(2)}) %collective-permute-start.7) | collective-permute-done | bytes 262176 | tf_op jit(solution)/shard_map/ppermute | solution.py:377
  30.9 3.5 %collective-permute-done.9.refs_8_ = bf16[64,2048]{1,0:T(8,128)(2,1)S(1)} collective-permute-done((bf16[64,2048]{1,0:T(8,128)(2,1)S(1)}, bf16[64,2048]{1,0:T(8,128)(2,1)S(1)}, u32[]{:S(2)}, u32[]{:S(2)}) %collective-permute-start.9) | collective-permute-done | bytes 262176 | tf_op jit(solution)/shard_map/ppermute | solution.py:377
  36.5 3.5 %collective-permute-done.11.refs_10_ = bf16[64,2048]{1,0:T(8,128)(2,1)S(1)} collective-permute-done((bf16[64,2048]{1,0:T(8,128)(2,1)S(1)}, bf16[64,2048]{1,0:T(8,128)(2,1)S(1)}, u32[]{:S(2)}, u32[]{:S(2)}) %collective-permute-start.11) | collective-permute-done | bytes 262176 | tf_op jit(solution)/shard_map/ppermute | solution.py:377
  40.6 4.4 %collective-permute-done.13.refs_12_ = bf16[64,2048]{1,0:T(8,128)(2,1)S(1)} collective-permute-done((bf16[64,2048]{1,0:T(8,128)(2,1)S(1)}, bf16[64,2048]{1,0:T(8,128)(2,1)S(1)}, u32[]{:S(2)}, u32[]{:S(2)}) %collective-permute-start.13) | collective-permute-done | bytes 262176 | tf_op jit(solution)/shard_map/ppermute | solution.py:377
  48.2 4.5 %collective-permute-done.16.refs_15_ = bf16[64,2048]{1,0:T(8,128)(2,1)S(1)} collective-permute-done((bf16[64,2048]{1,0:T(8,128)(2,1)S(1)}, bf16[64,2048]{1,0:T(8,128)(2,1)S(1)}, u32[]{:S(2)}, u32[]{:S(2)}) %collective-permute-start.16) | collective-permute-done | bytes 262176 | tf_op jit(solution)/shard_map/ppermute | solution.py:377
  52.8 4.4 %aggregate.3 = (bf16[64,2048]{1,0:T(8,128)(2,1)S(1)}, f32[1,2048]{1,0:T(1,128)}) custom-call(s32[384]{0:T(512)S(1)} %collective-permute-done.18.table.table_pair, bf16[16,12,128,128]{3,2,1,0:T(8,128)(2,1)S(1)} %load.3.tiles.pair, bf16[64,2048]{1,0:T(8,128)(2,1)S(1)} %get-tuple-element.108.refs_0_, bf16[64,2048]{1,0:T(8,128)(2,1)S(1)} %collective-permute-done.refs_1_, ...), custom_call_target="tpu_custom_call" | custom-call | flops 402653184 | bytes 10485760 | tf_op jit(solution)/shard_map/aggregate/pallas_call | solution.py:309
  57.9 3.9 %aggregate.2 = (bf16[64,2048]{1,0:T(8,128)(2,1)S(1)}, f32[1,2048]{1,0:T(1,128)S(1)}) custom-call(s32[384]{0:T(512)S(1)} %table.1, bf16[16,12,128,128]{3,2,1,0:T(8,128)(2,1)S(1)} %load.2.tiles.adj, bf16[64,2048]{1,0:T(8,128)(2,1)S(1)} %get-tuple-element.108.refs_0_, bf16[64,2048]{1,0:T(8,128)(2,1)S(1)} %collective-permute-done.refs_1_, ...), custom_call_target="tpu_custom_call" | custom-call | flops 402653184 | bytes 10485760 | tf_op jit(solution)/shard_map/aggregate/pallas_call | solution.py:309
  65.4 6.2 %collective-permute-done.17.refs_1_ = bf16[64,2048]{1,0:T(8,128)(2,1)S(1)} collective-permute-done((bf16[64,2048]{1,0:T(8,128)(2,1)S(1)}, bf16[64,2048]{1,0:T(8,128)(2,1)S(1)}, u32[]{:S(2)}, u32[]{:S(2)}) %collective-permute-start.17) | collective-permute-done | bytes 262176 | tf_op jit(solution)/shard_map/ppermute | solution.py:58
  71.6 3.0 %middle.1 = (bf16[128,2048]{1,0:T(8,128)(2,1)}, bf16[256,2048]{1,0:T(8,128)(2,1)S(1)}, bf16[128,2048]{1,0:T(8,128)(2,1)S(1)}, bf16[128,2048]{1,0:T(8,128)(2,1)S(1)}) custom-call(bf16[256,256]{1,0:T(8,128)(2,1)S(1)} %get-tuple-element.57.turned, bf16[128,256]{1,0:T(8,128)(2,1)S(1)} %copy-done.7, f32[1,2048]{1,0:T(1,128)S(1)} %get-tuple-element.70.inverse, ...), custom_call_target="tpu_custom_call" | custom-call | flops 402653184 | bytes 7340032 | tf_op jit(solution)/shard_map/middle/pallas_call | solution.py:309
  84.1 1.8 %spread.8 = (f32[64,2048]{1,0:T(8,128)S(1)}, f32[64,2048]{1,0:T(8,128)S(1)}, f32[64,2048]{1,0:T(8,128)S(1)}, f32[64,2048]{1,0:T(8,128)S(1)}) custom-call(s32[384]{0:T(512)S(1)} %table.1, s32[384]{0:T(512)S(1)} %collective-permute-done.18.table.table_pair, bf16[16,12,128,128]{3,2,1,0:T(8,128)(2,1)S(1)} %load.2.tiles.adj, ...), custom_call_target="tpu_custom_call" | custom-call | flops 201326592 | bytes 4194304 | tf_op jit(solution)/shard_map/spread/pallas_call | solution.py:309
  94.6 2.1 %collective-permute-start.30 = (bf16[64,2048]{1,0:T(8,128)(2,1)S(1)}, bf16[64,2048]{1,0:T(8,128)(2,1)S(1)}, u32[]{:S(2)}, u32[]{:S(2)}) collective-permute-start(bf16[64,2048]{1,0:T(8,128)(2,1)S(1)} %join.13), channel_id=1, source_target_pairs={{0,4},{2,6},{8,0},{10,2},{16,8},{18,10},{24,16},{26,18},{28,24},{3... | collective-permute-start | bytes 786440 | tf_op jit(solution)/shard_map/ppermute | solution.py:457
  96.7 1.8 %spread.9 = (f32[64,2048]{1,0:T(8,128)S(1)}, f32[64,2048]{1,0:T(8,128)S(1)}, f32[64,2048]{1,0:T(8,128)S(1)}, f32[64,2048]{1,0:T(8,128)S(1)}) custom-call(s32[384]{0:T(512)S(1)} %table.1, s32[384]{0:T(512)S(1)} %collective-permute-done.18.table.table_pair, bf16[16,12,128,128]{3,2,1,0:T(8,128)(2,1)S(1)} %load.2.tiles.adj, ...), custom_call_target="tpu_custom_call" | custom-call | flops 201326592 | bytes 4194304 | tf_op jit(solution)/shard_map/spread/pallas_call | solution.py:309
  98.8 2.9 %collective-permute-done.26 = f32[136,128]{1,0:T(8,128)S(1)} collective-permute-done((f32[136,128]{1,0:T(8,128)S(1)}, f32[136,128]{1,0:T(8,128)S(1)}, u32[]{:S(2)}, u32[]{:S(2)}) %collective-permute-start.26) | collective-permute-done | bytes 69664 | tf_op jit(solution)/shard_map/ppermute | solution.py:49
  101.8 2.3 %collective-permute-start.37 = (bf16[64,2048]{1,0:T(8,128)(2,1)S(1)}, bf16[64,2048]{1,0:T(8,128)(2,1)S(1)}, u32[]{:S(2)}, u32[]{:S(2)}) collective-permute-start(bf16[64,2048]{1,0:T(8,128)(2,1)S(1)} %join.18), channel_id=1, source_target_pairs={{0,4},{2,6},{8,0},{10,2},{16,8},{18,10},{24,16},{26,18},{28,24},{3... | collective-permute-start | bytes 786440 | tf_op jit(solution)/shard_map/ppermute | solution.py:457
  104.2 2.3 %collective-permute-start.39 = (f32[136,128]{1,0:T(8,128)S(1)}, f32[136,128]{1,0:T(8,128)S(1)}, u32[]{:S(2)}, u32[]{:S(2)}) collective-permute-start(f32[136,128]{1,0:T(8,128)S(1)} %add.25), channel_id=1, source_target_pairs={{0,16},{2,18},{4,20},{6,22},{8,24},{10,26},{12,28},{14,30},{16,0},... | collective-permute-start | bytes 208904 | tf_op jit(solution)/shard_map/ppermute | solution.py:49
  108.1 5.1 %collective-permute-done.39 = f32[136,128]{1,0:T(8,128)S(1)} collective-permute-done((f32[136,128]{1,0:T(8,128)S(1)}, f32[136,128]{1,0:T(8,128)S(1)}, u32[]{:S(2)}, u32[]{:S(2)}) %collective-permute-start.39) | collective-permute-done | bytes 69664 | tf_op jit(solution)/shard_map/ppermute | solution.py:49
  116.1 2.3 %collective-permute-start.34 = (bf16[64,2048]{1,0:T(8,128)(2,1)}, bf16[64,2048]{1,0:T(8,128)(2,1)S(1)}, u32[]{:S(2)}, u32[]{:S(2)}) collective-permute-start(bf16[64,2048]{1,0:T(8,128)(2,1)} %join.16), channel_id=1, source_target_pairs={{0,8},{2,10},{8,16},{10,18},{16,24},{18,26},{24,28},{26,30},{28,20... | collective-permute-start | bytes 786440 | tf_op jit(solution)/shard_map/ppermute | solution.py:457
  122.0 2.8 %copy-done.1 = bf16[16,12,128,128]{3,2,1,0:T(8,128)(2,1)S(1)} copy-done((bf16[16,12,128,128]{3,2,1,0:T(8,128)(2,1)S(1)}, bf16[16,12,128,128]{3,2,1,0:T(8,128)(2,1)}, u32[]{:S(2)}) %copy-start.1) | copy-done | bytes 6291480
  124.7 2.8 %copy-done.3 = bf16[16,12,128,128]{3,2,1,0:T(8,128)(2,1)S(1)} copy-done((bf16[16,12,128,128]{3,2,1,0:T(8,128)(2,1)S(1)}, bf16[16,12,128,128]{3,2,1,0:T(8,128)(2,1)}, u32[]{:S(2)}) %copy-start.3) | copy-done | bytes 6291480
  (119 shorter events, 53.8 us)
Async XLA Ops:
  0.6 17.5 %collective-permute-start.4 = (bf16[16,12,128,128]{3,2,1,0:T(8,128)(2,1)}, bf16[16,12,128,128]{3,2,1,0:T(8,128)(2,1)}, u32[]{:S(2)}, u32[]{:S(2)}) collective-permute-start(bf16[16,12,128,128]{3,2,1,0:T(8,128)(2,1)} %source.1), channel_id=1, source_target_pairs={{0,2},{2,0},{4,6},{6,4},{8,10},{10,8},{12,14},{14,12},{16,18},{18,... | collective-permute-start | bytes 18874376 | tf_op jit(solution)/shard_map/ppermute | solution.py:49
  2.2 11.4 %collective-permute-start = (bf16[64,2048]{1,0:T(8,128)(2,1)S(1)}, bf16[64,2048]{1,0:T(8,128)(2,1)S(1)}, u32[]{:S(2)}, u32[]{:S(2)}) collective-permute-start(bf16[64,2048]{1,0:T(8,128)(2,1)S(1)} %get-tuple-element.108.refs_0_), channel_id=1, source_target_pairs={{0,8},{2,10},{8,16},{10,18},{16,24},{18,26},{24,28},{26,30},{28,20... | collective-permute-start | bytes 786440 | tf_op jit(solution)/shard_map/ppermute | solution.py:373
  4.9 12.3 %collective-permute-start.1 = (bf16[64,2048]{1,0:T(8,128)(2,1)S(1)}, bf16[64,2048]{1,0:T(8,128)(2,1)S(1)}, u32[]{:S(2)}, u32[]{:S(2)}) collective-permute-start(bf16[64,2048]{1,0:T(8,128)(2,1)S(1)} %get-tuple-element.69), channel_id=1, source_target_pairs={{0,10},{2,8},{8,18},{10,16},{16,26},{18,24},{24,30},{26,28},{28,22... | collective-permute-start | bytes 786440 | tf_op jit(solution)/shard_map/ppermute | solution.py:373
  6.4 11.7 %collective-permute-start.3 = (bf16[64,2048]{1,0:T(8,128)(2,1)S(1)}, bf16[64,2048]{1,0:T(8,128)(2,1)S(1)}, u32[]{:S(2)}, u32[]{:S(2)}) collective-permute-start(bf16[64,2048]{1,0:T(8,128)(2,1)S(1)} %get-tuple-element.69), channel_id=1, source_target_pairs={{0,6},{2,4},{8,2},{10,0},{16,10},{18,8},{24,18},{26,16},{28,26},{3... | collective-permute-start | bytes 786440 | tf_op jit(solution)/shard_map/ppermute | solution.py:377
  18.2 45.2 %collective-permute-start.5 = (bf16[128,4736]{1,0:T(8,128)(2,1)S(1)}, bf16[128,4736]{1,0:T(8,128)(2,1)S(1)}, u32[]{:S(2)}, u32[]{:S(2)}) collective-permute-start(bf16[128,4736]{1,0:T(8,128)(2,1)S(1)} %pack.1.refs_0_), channel_id=1, source_target_pairs={{0,1},{1,0},{2,3},{3,2},{4,5},{5,4},{6,7},{7,6},{8,9},{9,8},{10,11... | collective-permute-start | bytes 3637256 | tf_op jit(solution)/shard_map/ppermute | solution.py:58
  21.7 12.7 %collective-permute-start.9 = (bf16[64,2048]{1,0:T(8,128)(2,1)S(1)}, bf16[64,2048]{1,0:T(8,128)(2,1)S(1)}, u32[]{:S(2)}, u32[]{:S(2)}) collective-permute-start(bf16[64,2048]{1,0:T(8,128)(2,1)S(1)} %collective-permute-done.3.refs_4_), channel_id=1, source_target_pairs={{0,4},{2,6},{8,0},{10,2},{16,8},{18,10},{24,16},{26,18},{28,24},{3... | collective-permute-start | bytes 786440 | tf_op jit(solution)/shard_map/ppermute | solution.py:377
  22.2 12.8 %collective-permute-start.8 = (bf16[64,2048]{1,0:T(8,128)(2,1)S(1)}, bf16[64,2048]{1,0:T(8,128)(2,1)S(1)}, u32[]{:S(2)}, u32[]{:S(2)}) collective-permute-start(bf16[64,2048]{1,0:T(8,128)(2,1)S(1)} %collective-permute-done.1.refs_3_), channel_id=1, source_target_pairs={{0,8},{2,10},{8,16},{10,18},{16,24},{18,26},{24,28},{26,30},{28,20... | collective-permute-start | bytes 786440 | tf_op jit(solution)/shard_map/ppermute | solution.py:373
  28.8 11.2 %collective-permute-start.11 = (bf16[64,2048]{1,0:T(8,128)(2,1)S(1)}, bf16[64,2048]{1,0:T(8,128)(2,1)S(1)}, u32[]{:S(2)}, u32[]{:S(2)}) collective-permute-start(bf16[64,2048]{1,0:T(8,128)(2,1)S(1)} %collective-permute-done.7.refs_6_), channel_id=1, source_target_pairs={{0,4},{2,6},{8,0},{10,2},{16,8},{18,10},{24,16},{26,18},{28,24},{3... | collective-permute-start | bytes 786440 | tf_op jit(solution)/shard_map/ppermute | solution.py:377
  29.4 11.2 %collective-permute-start.10 = (bf16[64,2048]{1,0:T(8,128)(2,1)S(1)}, bf16[64,2048]{1,0:T(8,128)(2,1)S(1)}, u32[]{:S(2)}, u32[]{:S(2)}) collective-permute-start(bf16[64,2048]{1,0:T(8,128)(2,1)S(1)} %collective-permute-done.6.refs_5_), channel_id=1, source_target_pairs={{0,8},{2,10},{8,16},{10,18},{16,24},{18,26},{24,28},{26,30},{28,20... | collective-permute-start | bytes 786440 | tf_op jit(solution)/shard_map/ppermute | solution.py:373
  34.4 10.6 %collective-permute-start.13 = (bf16[64,2048]{1,0:T(8,128)(2,1)S(1)}, bf16[64,2048]{1,0:T(8,128)(2,1)S(1)}, u32[]{:S(2)}, u32[]{:S(2)}) collective-permute-start(bf16[64,2048]{1,0:T(8,128)(2,1)S(1)} %collective-permute-done.9.refs_8_), channel_id=1, source_target_pairs={{0,4},{2,6},{8,0},{10,2},{16,8},{18,10},{24,16},{26,18},{28,24},{3... | collective-permute-start | bytes 786440 | tf_op jit(solution)/shard_map/ppermute | solution.py:377
  35.0 12.1 %collective-permute-start.12 = (bf16[64,2048]{1,0:T(8,128)(2,1)S(1)}, bf16[64,2048]{1,0:T(8,128)(2,1)S(1)}, u32[]{:S(2)}, u32[]{:S(2)}) collective-permute-start(bf16[64,2048]{1,0:T(8,128)(2,1)S(1)} %collective-permute-done.8.refs_7_), channel_id=1, source_target_pairs={{0,8},{2,10},{8,16},{10,18},{16,24},{18,26},{24,28},{26,30},{28,20... | collective-permute-start | bytes 786440 | tf_op jit(solution)/shard_map/ppermute | solution.py:373
  78.1 11.4 %collective-permute-start.22 = (bf16[64,2048]{1,0:T(8,128)(2,1)S(1)}, bf16[64,2048]{1,0:T(8,128)(2,1)S(1)}, u32[]{:S(2)}, u32[]{:S(2)}) collective-permute-start(bf16[64,2048]{1,0:T(8,128)(2,1)S(1)} %get-tuple-element.83), channel_id=1, source_target_pairs={{0,8},{2,10},{8,16},{10,18},{16,24},{18,26},{24,28},{26,30},{28,20... | collective-permute-start | bytes 786440 | tf_op jit(solution)/shard_map/ppermute | solution.py:457
  80.2 11.0 %collective-permute-start.25 = (f32[136,128]{1,0:T(8,128)S(1)}, f32[136,128]{1,0:T(8,128)S(1)}, u32[]{:S(2)}, u32[]{:S(2)}) collective-permute-start(f32[136,128]{1,0:T(8,128)S(1)} %slice_bitcast_fusion), channel_id=1, source_target_pairs={{0,4},{2,6},{4,0},{6,2},{8,12},{10,14},{12,8},{14,10},{16,20},{18,... | collective-permute-start | bytes 208904 | tf_op jit(solution)/shard_map/ppermute | solution.py:49
  83.5 11.1 %collective-permute-start.29 = (bf16[64,2048]{1,0:T(8,128)(2,1)S(1)}, bf16[64,2048]{1,0:T(8,128)(2,1)S(1)}, u32[]{:S(2)}, u32[]{:S(2)}) collective-permute-start(bf16[64,2048]{1,0:T(8,128)(2,1)S(1)} %get-tuple-element.91), channel_id=1, source_target_pairs={{0,4},{2,6},{8,0},{10,2},{16,8},{18,10},{24,16},{26,18},{28,24},{3... | collective-permute-start | bytes 786440 | tf_op jit(solution)/shard_map/ppermute | solution.py:457
  85.9 12.6 %collective-permute-start.32 = (bf16[64,2048]{1,0:T(8,128)(2,1)S(1)}, bf16[64,2048]{1,0:T(8,128)(2,1)S(1)}, u32[]{:S(2)}, u32[]{:S(2)}) collective-permute-start(bf16[64,2048]{1,0:T(8,128)(2,1)S(1)} %get-tuple-element.95), channel_id=1, source_target_pairs={{0,8},{2,10},{8,16},{10,18},{16,24},{18,26},{24,28},{26,30},{28,20... | collective-permute-start | bytes 786440 | tf_op jit(solution)/shard_map/ppermute | solution.py:457
  89.0 12.7 %collective-permute-start.36 = (bf16[64,2048]{1,0:T(8,128)(2,1)S(1)}, bf16[64,2048]{1,0:T(8,128)(2,1)S(1)}, u32[]{:S(2)}, u32[]{:S(2)}) collective-permute-start(bf16[64,2048]{1,0:T(8,128)(2,1)S(1)} %join.17), channel_id=1, source_target_pairs={{0,4},{2,6},{8,0},{10,2},{16,8},{18,10},{24,16},{26,18},{28,24},{3... | collective-permute-start | bytes 786440 | tf_op jit(solution)/shard_map/ppermute | solution.py:457
  89.5 14.6 %collective-permute-start.23 = (bf16[64,2048]{1,0:T(8,128)(2,1)S(1)}, bf16[64,2048]{1,0:T(8,128)(2,1)S(1)}, u32[]{:S(2)}, u32[]{:S(2)}) collective-permute-start(bf16[64,2048]{1,0:T(8,128)(2,1)S(1)} %join.10), channel_id=1, source_target_pairs={{0,8},{2,10},{8,16},{10,18},{16,24},{18,26},{24,28},{26,30},{28,20... | collective-permute-start | bytes 786440 | tf_op jit(solution)/shard_map/ppermute | solution.py:457
  94.6 12.7 %collective-permute-start.30 = (bf16[64,2048]{1,0:T(8,128)(2,1)S(1)}, bf16[64,2048]{1,0:T(8,128)(2,1)S(1)}, u32[]{:S(2)}, u32[]{:S(2)}) collective-permute-start(bf16[64,2048]{1,0:T(8,128)(2,1)S(1)} %join.13), channel_id=1, source_target_pairs={{0,4},{2,6},{8,0},{10,2},{16,8},{18,10},{24,16},{26,18},{28,24},{3... | collective-permute-start | bytes 786440 | tf_op jit(solution)/shard_map/ppermute | solution.py:457
  98.6 16.7 %collective-permute-start.33 = (bf16[64,2048]{1,0:T(8,128)(2,1)S(1)}, bf16[64,2048]{1,0:T(8,128)(2,1)S(1)}, u32[]{:S(2)}, u32[]{:S(2)}) collective-permute-start(bf16[64,2048]{1,0:T(8,128)(2,1)S(1)} %join.15), channel_id=1, source_target_pairs={{0,8},{2,10},{8,16},{10,18},{16,24},{18,26},{24,28},{26,30},{28,20... | collective-permute-start | bytes 786440 | tf_op jit(solution)/shard_map/ppermute | solution.py:457
  101.8 16.5 %collective-permute-start.37 = (bf16[64,2048]{1,0:T(8,128)(2,1)S(1)}, bf16[64,2048]{1,0:T(8,128)(2,1)S(1)}, u32[]{:S(2)}, u32[]{:S(2)}) collective-permute-start(bf16[64,2048]{1,0:T(8,128)(2,1)S(1)} %join.18), channel_id=1, source_target_pairs={{0,4},{2,6},{8,0},{10,2},{16,8},{18,10},{24,16},{26,18},{28,24},{3... | collective-permute-start | bytes 786440 | tf_op jit(solution)/shard_map/ppermute | solution.py:457
  104.2 15.6 %collective-permute-start.27 = (bf16[64,2048]{1,0:T(8,128)(2,1)S(1)}, bf16[64,2048]{1,0:T(8,128)(2,1)S(1)}, u32[]{:S(2)}, u32[]{:S(2)}) collective-permute-start(bf16[64,2048]{1,0:T(8,128)(2,1)S(1)} %join.11), channel_id=1, source_target_pairs={{0,8},{2,10},{8,16},{10,18},{16,24},{18,26},{24,28},{26,30},{28,20... | collective-permute-start | bytes 786440 | tf_op jit(solution)/shard_map/ppermute | solution.py:457
  114.8 15.3 %collective-permute-start.31 = (bf16[64,2048]{1,0:T(8,128)(2,1)}, bf16[64,2048]{1,0:T(8,128)(2,1)S(1)}, u32[]{:S(2)}, u32[]{:S(2)}) collective-permute-start(bf16[64,2048]{1,0:T(8,128)(2,1)} %join.14), channel_id=1, source_target_pairs={{0,4},{2,6},{8,0},{10,2},{16,8},{18,10},{24,16},{26,18},{28,24},{3... | collective-permute-start | bytes 786440 | tf_op jit(solution)/shard_map/ppermute | solution.py:457
  116.1 14.0 %collective-permute-start.34 = (bf16[64,2048]{1,0:T(8,128)(2,1)}, bf16[64,2048]{1,0:T(8,128)(2,1)S(1)}, u32[]{:S(2)}, u32[]{:S(2)}) collective-permute-start(bf16[64,2048]{1,0:T(8,128)(2,1)} %join.16), channel_id=1, source_target_pairs={{0,8},{2,10},{8,16},{10,18},{16,24},{18,26},{24,28},{26,30},{28,20... | collective-permute-start | bytes 786440 | tf_op jit(solution)/shard_map/ppermute | solution.py:457
  119.1 11.0 %collective-permute-start.38 = (bf16[64,2048]{1,0:T(8,128)(2,1)}, bf16[64,2048]{1,0:T(8,128)(2,1)S(1)}, u32[]{:S(2)}, u32[]{:S(2)}) collective-permute-start(bf16[64,2048]{1,0:T(8,128)(2,1)} %join.19), channel_id=1, source_target_pairs={{0,4},{2,6},{8,0},{10,2},{16,8},{18,10},{24,16},{26,18},{28,24},{3... | collective-permute-start | bytes 786440 | tf_op jit(solution)/shard_map/ppermute | solution.py:457
  (29 other events, 325.5 us)

commit v11 on v10

--- a/solution.py
+++ b/solution.py
@@ -467,7 +467,7 @@
         for i in (1, 0):
             flow = 1 - i
             value = joined(up[i], mine[i])
-            if i == 1 and level > 1:
+            if i == (1 if level > 1 else 0):
                 value = after(value, later[0])
             up[i] = ring(value, forward)
             down[flow] = ring(joined(down[flow], mine[2 + flow]), backward)

time: 131 us -> 132 us (level)
  waiting for transfers between devices: 44.7 us -> 50.9 us
  local copies, waits for them, and re-layouts: 10.2 us -> 4.64 us
    unnamed x22 -> x14, local copies, waits for them, and re-layouts: 8.61 us -> 3.04 us
    ppermute x14, waiting for transfers between devices: 4.01 us -> 8.03 us  [ring(): return lax.ppermute(value, 'rows', pairs)]
    ppermute x10, waiting for transfers between devices: 9.79 us -> 12 us  [swap(): return lax.ppermute(value, 'rows', [(r, r ^ bit) for r in range(rows)])]
  transfers between devices with their start and end apart: 42 -> 42, of which waited for: 19 -> 23; matrix products, arithmetic and copies ran while one was open for 1% -> 1% of each run, Pallas kernels for 22% -> 22%
where the time goes in v11:
time: 132 us
  waiting for transfers between devices  50.9 us (39%)
  starting transfers between devices  42.1 us (32%)
  Pallas kernels  33.4 us (25%)
  local copies, waits for them, and re-layouts  4.64 us (4%)
    pallas_call x27, Pallas kernels, call(): pl.pallas_call(kernel, out_shape=[jax.ShapeDtypeStruct(shape, kind) for s...  33.4 us
    ppermute x7, waiting for transfers between devices, shards(): down[side] = lax.ppermute(down[side], 'rows', backward)  19.7 us
    ppermute x14, starting transfers between devices, ring(): return lax.ppermute(value, 'rows', pairs)  15.8 us
    ppermute x10, waiting for transfers between devices, swap(): return lax.ppermute(value, 'rows', [(r, r ^ bit) for r in range(rows)])  12 us
    ppermute x7, starting transfers between devices, shards(): up[side] = lax.ppermute(up[side], 'rows', forward)  11.8 us
    ppermute x14, waiting for transfers between devices, ring(): return lax.ppermute(value, 'rows', pairs)  8.03 us
    ppermute x10, starting transfers between devices, swap(): return lax.ppermute(value, 'rows', [(r, r ^ bit) for r in range(rows)])  7.89 us
    ppermute x4, waiting for transfers between devices, send(): return lax.ppermute(value, ('rows', 'feat'), pairs)  7.36 us
  transfers between devices with their start and end apart: 42, of which 23 were waited for; matrix products, arithmetic and copies ran while one was open for 1% of the time, Pallas kernels for 22%

profile of v11, /device:TPU:0, one launch (start us, length us, event | category | flops | bytes accessed | tf_op | source)
XLA Modules:
  0.0 132.0 jit_solution(4674847166866888774)
XLA Ops:
  2.2 2.7 %collective-permute-start = (bf16[64,2048]{1,0:T(8,128)(2,1)S(1)}, bf16[64,2048]{1,0:T(8,128)(2,1)S(1)}, u32[]{:S(2)}, u32[]{:S(2)}) collective-permute-start(bf16[64,2048]{1,0:T(8,128)(2,1)S(1)} %get-tuple-element.110.refs_0_), channel_id=1, source_target_pairs={{0,8},{2,10},{8,16},{10,18},{16,24},{18,26},{24,28},{26,30},{28,20... | collective-permute-start | bytes 786440 | tf_op jit(solution)/shard_map/ppermute | solution.py:373
  6.6 2.8 %copy-done = bf16[16,12,128,128]{3,2,1,0:T(8,128)(2,1)S(1)} copy-done((bf16[16,12,128,128]{3,2,1,0:T(8,128)(2,1)S(1)}, bf16[16,12,128,128]{3,2,1,0:T(8,128)(2,1)}, u32[]{:S(2)}) %copy-start) | copy-done | bytes 6291480
  10.1 3.2 %table.1 = s32[384]{0:T(512)S(1)} custom-call(s32[16,12]{1,0:T(8,128)S(1)} %copy-done.5), custom_call_target="tpu_custom_call" | custom-call | bytes 1536 | tf_op jit(solution)/shard_map/table/pallas_call | solution.py:309
  14.0 3.1 %collective-permute-done.1.refs_3_ = bf16[64,2048]{1,0:T(8,128)(2,1)S(1)} collective-permute-done((bf16[64,2048]{1,0:T(8,128)(2,1)S(1)}, bf16[64,2048]{1,0:T(8,128)(2,1)S(1)}, u32[]{:S(2)}, u32[]{:S(2)}) %collective-permute-start.1) | collective-permute-done | bytes 262176 | tf_op jit(solution)/shard_map/ppermute | solution.py:373
  23.7 2.8 %load.3.tiles.pair = bf16[16,12,128,128]{3,2,1,0:T(8,128)(2,1)S(1)} custom-call(bf16[16,12,128,128]{3,2,1,0:T(8,128)(2,1)} %collective-permute-done.4.source), custom_call_target="tpu_custom_call" | custom-call | bytes 12582912 | tf_op jit(solution)/shard_map/load/pallas_call | solution.py:309
  26.5 2.3 %collective-permute-done.7.refs_6_ = bf16[64,2048]{1,0:T(8,128)(2,1)S(1)} collective-permute-done((bf16[64,2048]{1,0:T(8,128)(2,1)S(1)}, bf16[64,2048]{1,0:T(8,128)(2,1)S(1)}, u32[]{:S(2)}, u32[]{:S(2)}) %collective-permute-start.7) | collective-permute-done | bytes 262176 | tf_op jit(solution)/shard_map/ppermute | solution.py:377
  30.9 3.5 %collective-permute-done.9.refs_8_ = bf16[64,2048]{1,0:T(8,128)(2,1)S(1)} collective-permute-done((bf16[64,2048]{1,0:T(8,128)(2,1)S(1)}, bf16[64,2048]{1,0:T(8,128)(2,1)S(1)}, u32[]{:S(2)}, u32[]{:S(2)}) %collective-permute-start.9) | collective-permute-done | bytes 262176 | tf_op jit(solution)/shard_map/ppermute | solution.py:377
  36.5 3.5 %collective-permute-done.11.refs_10_ = bf16[64,2048]{1,0:T(8,128)(2,1)S(1)} collective-permute-done((bf16[64,2048]{1,0:T(8,128)(2,1)S(1)}, bf16[64,2048]{1,0:T(8,128)(2,1)S(1)}, u32[]{:S(2)}, u32[]{:S(2)}) %collective-permute-start.11) | collective-permute-done | bytes 262176 | tf_op jit(solution)/shard_map/ppermute | solution.py:377
  40.6 4.4 %collective-permute-done.13.refs_12_ = bf16[64,2048]{1,0:T(8,128)(2,1)S(1)} collective-permute-done((bf16[64,2048]{1,0:T(8,128)(2,1)S(1)}, bf16[64,2048]{1,0:T(8,128)(2,1)S(1)}, u32[]{:S(2)}, u32[]{:S(2)}) %collective-permute-start.13) | collective-permute-done | bytes 262176 | tf_op jit(solution)/shard_map/ppermute | solution.py:377
  48.2 4.5 %collective-permute-done.16.refs_15_ = bf16[64,2048]{1,0:T(8,128)(2,1)S(1)} collective-permute-done((bf16[64,2048]{1,0:T(8,128)(2,1)S(1)}, bf16[64,2048]{1,0:T(8,128)(2,1)S(1)}, u32[]{:S(2)}, u32[]{:S(2)}) %collective-permute-start.16) | collective-permute-done | bytes 262176 | tf_op jit(solution)/shard_map/ppermute | solution.py:377
  52.8 4.4 %aggregate.3 = (bf16[64,2048]{1,0:T(8,128)(2,1)S(1)}, f32[1,2048]{1,0:T(1,128)}) custom-call(s32[384]{0:T(512)S(1)} %collective-permute-done.18.table.table_pair, bf16[16,12,128,128]{3,2,1,0:T(8,128)(2,1)S(1)} %load.3.tiles.pair, bf16[64,2048]{1,0:T(8,128)(2,1)S(1)} %get-tuple-element.110.refs_0_, bf16[64,2048]{1,0:T(8,128)(2,1)S(1)} %collective-permute-done.refs_1_, ...), custom_call_target="tpu_custom_call" | custom-call | flops 402653184 | bytes 10485760 | tf_op jit(solution)/shard_map/aggregate/pallas_call | solution.py:309
  57.9 3.9 %aggregate.2 = (bf16[64,2048]{1,0:T(8,128)(2,1)S(1)}, f32[1,2048]{1,0:T(1,128)S(1)}) custom-call(s32[384]{0:T(512)S(1)} %table.1, bf16[16,12,128,128]{3,2,1,0:T(8,128)(2,1)S(1)} %load.2.tiles.adj, bf16[64,2048]{1,0:T(8,128)(2,1)S(1)} %get-tuple-element.110.refs_0_, bf16[64,2048]{1,0:T(8,128)(2,1)S(1)} %collective-permute-done.refs_1_, ...), custom_call_target="tpu_custom_call" | custom-call | flops 402653184 | bytes 10485760 | tf_op jit(solution)/shard_map/aggregate/pallas_call | solution.py:309
  65.5 6.2 %collective-permute-done.17.refs_1_ = bf16[64,2048]{1,0:T(8,128)(2,1)S(1)} collective-permute-done((bf16[64,2048]{1,0:T(8,128)(2,1)S(1)}, bf16[64,2048]{1,0:T(8,128)(2,1)S(1)}, u32[]{:S(2)}, u32[]{:S(2)}) %collective-permute-start.17) | collective-permute-done | bytes 262176 | tf_op jit(solution)/shard_map/ppermute | solution.py:58
  71.6 3.0 %middle.1 = (bf16[128,2048]{1,0:T(8,128)(2,1)}, bf16[256,2048]{1,0:T(8,128)(2,1)S(1)}, bf16[128,2048]{1,0:T(8,128)(2,1)S(1)}, bf16[128,2048]{1,0:T(8,128)(2,1)S(1)}) custom-call(bf16[256,256]{1,0:T(8,128)(2,1)S(1)} %get-tuple-element.58.turned, bf16[128,256]{1,0:T(8,128)(2,1)S(1)} %copy-done.3, f32[1,2048]{1,0:T(1,128)S(1)} %get-tuple-element.71.inverse, ...), custom_call_target="tpu_custom_call" | custom-call | flops 402653184 | bytes 7340032 | tf_op jit(solution)/shard_map/middle/pallas_call | solution.py:309
  81.7 1.8 %spread.7 = (f32[64,2048]{1,0:T(8,128)S(1)}, bf16[64,2048]{1,0:T(8,128)(2,1)S(1)}, bf16[64,2048]{1,0:T(8,128)(2,1)S(1)}, f32[64,2048]{1,0:T(8,128)S(1)}) custom-call(s32[384]{0:T(512)S(1)} %table.1, s32[384]{0:T(512)S(1)} %collective-permute-done.18.table.table_pair, bf16[16,12,128,128]{3,2,1,0:T(8,128)(2,1)S(1)} %load.2.tiles.adj, ...), custom_call_target="tpu_custom_call" | custom-call | flops 201326592 | bytes 4194304 | tf_op jit(solution)/shard_map/spread/pallas_call | solution.py:309
  84.1 1.8 %spread.8 = (f32[64,2048]{1,0:T(8,128)S(1)}, f32[64,2048]{1,0:T(8,128)S(1)}, f32[64,2048]{1,0:T(8,128)S(1)}, f32[64,2048]{1,0:T(8,128)S(1)}) custom-call(s32[384]{0:T(512)S(1)} %table.1, s32[384]{0:T(512)S(1)} %collective-permute-done.18.table.table_pair, bf16[16,12,128,128]{3,2,1,0:T(8,128)(2,1)S(1)} %load.2.tiles.adj, ...), custom_call_target="tpu_custom_call" | custom-call | flops 201326592 | bytes 4194304 | tf_op jit(solution)/shard_map/spread/pallas_call | solution.py:309
  94.6 2.1 %collective-permute-start.30 = (bf16[64,2048]{1,0:T(8,128)(2,1)S(1)}, bf16[64,2048]{1,0:T(8,128)(2,1)S(1)}, u32[]{:S(2)}, u32[]{:S(2)}) collective-permute-start(bf16[64,2048]{1,0:T(8,128)(2,1)S(1)} %join.13), channel_id=1, source_target_pairs={{0,4},{2,6},{8,0},{10,2},{16,8},{18,10},{24,16},{26,18},{28,24},{3... | collective-permute-start | bytes 786440 | tf_op jit(solution)/shard_map/ppermute | solution.py:457
  96.7 1.8 %spread.9 = (f32[64,2048]{1,0:T(8,128)S(1)}, f32[64,2048]{1,0:T(8,128)S(1)}, f32[64,2048]{1,0:T(8,128)S(1)}, f32[64,2048]{1,0:T(8,128)S(1)}) custom-call(s32[384]{0:T(512)S(1)} %table.1, s32[384]{0:T(512)S(1)} %collective-permute-done.18.table.table_pair, bf16[16,12,128,128]{3,2,1,0:T(8,128)(2,1)S(1)} %load.2.tiles.adj, ...), custom_call_target="tpu_custom_call" | custom-call | flops 201326592 | bytes 4194304 | tf_op jit(solution)/shard_map/spread/pallas_call | solution.py:309
  98.8 2.9 %collective-permute-done.26 = f32[136,128]{1,0:T(8,128)S(1)} collective-permute-done((f32[136,128]{1,0:T(8,128)S(1)}, f32[136,128]{1,0:T(8,128)S(1)}, u32[]{:S(2)}, u32[]{:S(2)}) %collective-permute-start.26) | collective-permute-done | bytes 69664 | tf_op jit(solution)/shard_map/ppermute | solution.py:49
  101.8 2.3 %collective-permute-start.37 = (bf16[64,2048]{1,0:T(8,128)(2,1)S(1)}, bf16[64,2048]{1,0:T(8,128)(2,1)S(1)}, u32[]{:S(2)}, u32[]{:S(2)}) collective-permute-start(bf16[64,2048]{1,0:T(8,128)(2,1)S(1)} %join.18), channel_id=1, source_target_pairs={{0,4},{2,6},{8,0},{10,2},{16,8},{18,10},{24,16},{26,18},{28,24},{3... | collective-permute-start | bytes 786440 | tf_op jit(solution)/shard_map/ppermute | solution.py:457
  104.2 2.3 %collective-permute-start.39 = (f32[136,128]{1,0:T(8,128)S(1)}, f32[136,128]{1,0:T(8,128)S(1)}, u32[]{:S(2)}, u32[]{:S(2)}) collective-permute-start(f32[136,128]{1,0:T(8,128)S(1)} %add.25), channel_id=1, source_target_pairs={{0,16},{2,18},{4,20},{6,22},{8,24},{10,26},{12,28},{14,30},{16,0},... | collective-permute-start | bytes 208904 | tf_op jit(solution)/shard_map/ppermute | solution.py:49
  107.4 5.8 %collective-permute-done.39 = f32[136,128]{1,0:T(8,128)S(1)} collective-permute-done((f32[136,128]{1,0:T(8,128)S(1)}, f32[136,128]{1,0:T(8,128)S(1)}, u32[]{:S(2)}, u32[]{:S(2)}) %collective-permute-start.39) | collective-permute-done | bytes 69664 | tf_op jit(solution)/shard_map/ppermute | solution.py:49
  117.3 2.3 %collective-permute-start.34 = (bf16[64,2048]{1,0:T(8,128)(2,1)}, bf16[64,2048]{1,0:T(8,128)(2,1)S(1)}, u32[]{:S(2)}, u32[]{:S(2)}) collective-permute-start(bf16[64,2048]{1,0:T(8,128)(2,1)} %join.16), channel_id=1, source_target_pairs={{0,8},{2,10},{8,16},{10,18},{16,24},{18,26},{24,28},{26,30},{28,20... | collective-permute-start | bytes 786440 | tf_op jit(solution)/shard_map/ppermute | solution.py:457
  129.1 1.9 %collective-permute-done.28.a_low = bf16[64,2048]{1,0:T(8,128)(2,1)S(1)} collective-permute-done((bf16[64,2048]{1,0:T(8,128)(2,1)}, bf16[64,2048]{1,0:T(8,128)(2,1)S(1)}, u32[]{:S(2)}, u32[]{:S(2)}) %collective-permute-start.28) | collective-permute-done | bytes 262176 | tf_op jit(solution)/shard_map/ppermute | solution.py:457
  (111 shorter events, 55.7 us)
Async XLA Ops:
  0.6 17.5 %collective-permute-start.4 = (bf16[16,12,128,128]{3,2,1,0:T(8,128)(2,1)}, bf16[16,12,128,128]{3,2,1,0:T(8,128)(2,1)}, u32[]{:S(2)}, u32[]{:S(2)}) collective-permute-start(bf16[16,12,128,128]{3,2,1,0:T(8,128)(2,1)} %source.1), channel_id=1, source_target_pairs={{0,2},{2,0},{4,6},{6,4},{8,10},{10,8},{12,14},{14,12},{16,18},{18,... | collective-permute-start | bytes 18874376 | tf_op jit(solution)/shard_map/ppermute | solution.py:49
  2.2 11.4 %collective-permute-start = (bf16[64,2048]{1,0:T(8,128)(2,1)S(1)}, bf16[64,2048]{1,0:T(8,128)(2,1)S(1)}, u32[]{:S(2)}, u32[]{:S(2)}) collective-permute-start(bf16[64,2048]{1,0:T(8,128)(2,1)S(1)} %get-tuple-element.110.refs_0_), channel_id=1, source_target_pairs={{0,8},{2,10},{8,16},{10,18},{16,24},{18,26},{24,28},{26,30},{28,20... | collective-permute-start | bytes 786440 | tf_op jit(solution)/shard_map/ppermute | solution.py:373
  4.9 12.3 %collective-permute-start.1 = (bf16[64,2048]{1,0:T(8,128)(2,1)S(1)}, bf16[64,2048]{1,0:T(8,128)(2,1)S(1)}, u32[]{:S(2)}, u32[]{:S(2)}) collective-permute-start(bf16[64,2048]{1,0:T(8,128)(2,1)S(1)} %get-tuple-element.70), channel_id=1, source_target_pairs={{0,10},{2,8},{8,18},{10,16},{16,26},{18,24},{24,30},{26,28},{28,22... | collective-permute-start | bytes 786440 | tf_op jit(solution)/shard_map/ppermute | solution.py:373
  6.4 11.7 %collective-permute-start.3 = (bf16[64,2048]{1,0:T(8,128)(2,1)S(1)}, bf16[64,2048]{1,0:T(8,128)(2,1)S(1)}, u32[]{:S(2)}, u32[]{:S(2)}) collective-permute-start(bf16[64,2048]{1,0:T(8,128)(2,1)S(1)} %get-tuple-element.70), channel_id=1, source_target_pairs={{0,6},{2,4},{8,2},{10,0},{16,10},{18,8},{24,18},{26,16},{28,26},{3... | collective-permute-start | bytes 786440 | tf_op jit(solution)/shard_map/ppermute | solution.py:377
  18.2 45.3 %collective-permute-start.5 = (bf16[128,4736]{1,0:T(8,128)(2,1)S(1)}, bf16[128,4736]{1,0:T(8,128)(2,1)S(1)}, u32[]{:S(2)}, u32[]{:S(2)}) collective-permute-start(bf16[128,4736]{1,0:T(8,128)(2,1)S(1)} %pack.1.refs_0_), channel_id=1, source_target_pairs={{0,1},{1,0},{2,3},{3,2},{4,5},{5,4},{6,7},{7,6},{8,9},{9,8},{10,11... | collective-permute-start | bytes 3637256 | tf_op jit(solution)/shard_map/ppermute | solution.py:58
  21.7 12.7 %collective-permute-start.9 = (bf16[64,2048]{1,0:T(8,128)(2,1)S(1)}, bf16[64,2048]{1,0:T(8,128)(2,1)S(1)}, u32[]{:S(2)}, u32[]{:S(2)}) collective-permute-start(bf16[64,2048]{1,0:T(8,128)(2,1)S(1)} %collective-permute-done.3.refs_4_), channel_id=1, source_target_pairs={{0,4},{2,6},{8,0},{10,2},{16,8},{18,10},{24,16},{26,18},{28,24},{3... | collective-permute-start | bytes 786440 | tf_op jit(solution)/shard_map/ppermute | solution.py:377
  22.2 12.8 %collective-permute-start.8 = (bf16[64,2048]{1,0:T(8,128)(2,1)S(1)}, bf16[64,2048]{1,0:T(8,128)(2,1)S(1)}, u32[]{:S(2)}, u32[]{:S(2)}) collective-permute-start(bf16[64,2048]{1,0:T(8,128)(2,1)S(1)} %collective-permute-done.1.refs_3_), channel_id=1, source_target_pairs={{0,8},{2,10},{8,16},{10,18},{16,24},{18,26},{24,28},{26,30},{28,20... | collective-permute-start | bytes 786440 | tf_op jit(solution)/shard_map/ppermute | solution.py:373
  28.8 11.2 %collective-permute-start.11 = (bf16[64,2048]{1,0:T(8,128)(2,1)S(1)}, bf16[64,2048]{1,0:T(8,128)(2,1)S(1)}, u32[]{:S(2)}, u32[]{:S(2)}) collective-permute-start(bf16[64,2048]{1,0:T(8,128)(2,1)S(1)} %collective-permute-done.7.refs_6_), channel_id=1, source_target_pairs={{0,4},{2,6},{8,0},{10,2},{16,8},{18,10},{24,16},{26,18},{28,24},{3... | collective-permute-start | bytes 786440 | tf_op jit(solution)/shard_map/ppermute | solution.py:377
  29.4 11.2 %collective-permute-start.10 = (bf16[64,2048]{1,0:T(8,128)(2,1)S(1)}, bf16[64,2048]{1,0:T(8,128)(2,1)S(1)}, u32[]{:S(2)}, u32[]{:S(2)}) collective-permute-start(bf16[64,2048]{1,0:T(8,128)(2,1)S(1)} %collective-permute-done.6.refs_5_), channel_id=1, source_target_pairs={{0,8},{2,10},{8,16},{10,18},{16,24},{18,26},{24,28},{26,30},{28,20... | collective-permute-start | bytes 786440 | tf_op jit(solution)/shard_map/ppermute | solution.py:373
  34.4 10.6 %collective-permute-start.13 = (bf16[64,2048]{1,0:T(8,128)(2,1)S(1)}, bf16[64,2048]{1,0:T(8,128)(2,1)S(1)}, u32[]{:S(2)}, u32[]{:S(2)}) collective-permute-start(bf16[64,2048]{1,0:T(8,128)(2,1)S(1)} %collective-permute-done.9.refs_8_), channel_id=1, source_target_pairs={{0,4},{2,6},{8,0},{10,2},{16,8},{18,10},{24,16},{26,18},{28,24},{3... | collective-permute-start | bytes 786440 | tf_op jit(solution)/shard_map/ppermute | solution.py:377
  35.0 12.1 %collective-permute-start.12 = (bf16[64,2048]{1,0:T(8,128)(2,1)S(1)}, bf16[64,2048]{1,0:T(8,128)(2,1)S(1)}, u32[]{:S(2)}, u32[]{:S(2)}) collective-permute-start(bf16[64,2048]{1,0:T(8,128)(2,1)S(1)} %collective-permute-done.8.refs_7_), channel_id=1, source_target_pairs={{0,8},{2,10},{8,16},{10,18},{16,24},{18,26},{24,28},{26,30},{28,20... | collective-permute-start | bytes 786440 | tf_op jit(solution)/shard_map/ppermute | solution.py:373
  78.1 11.4 %collective-permute-start.22 = (bf16[64,2048]{1,0:T(8,128)(2,1)S(1)}, bf16[64,2048]{1,0:T(8,128)(2,1)S(1)}, u32[]{:S(2)}, u32[]{:S(2)}) collective-permute-start(bf16[64,2048]{1,0:T(8,128)(2,1)S(1)} %get-tuple-element.84), channel_id=1, source_target_pairs={{0,8},{2,10},{8,16},{10,18},{16,24},{18,26},{24,28},{26,30},{28,20... | collective-permute-start | bytes 786440 | tf_op jit(solution)/shard_map/ppermute | solution.py:457
  80.2 11.0 %collective-permute-start.25 = (f32[136,128]{1,0:T(8,128)S(1)}, f32[136,128]{1,0:T(8,128)S(1)}, u32[]{:S(2)}, u32[]{:S(2)}) collective-permute-start(f32[136,128]{1,0:T(8,128)S(1)} %slice_bitcast_fusion), channel_id=1, source_target_pairs={{0,4},{2,6},{4,0},{6,2},{8,12},{10,14},{12,8},{14,10},{16,20},{18,... | collective-permute-start | bytes 208904 | tf_op jit(solution)/shard_map/ppermute | solution.py:49
  83.5 11.1 %collective-permute-start.29 = (bf16[64,2048]{1,0:T(8,128)(2,1)S(1)}, bf16[64,2048]{1,0:T(8,128)(2,1)S(1)}, u32[]{:S(2)}, u32[]{:S(2)}) collective-permute-start(bf16[64,2048]{1,0:T(8,128)(2,1)S(1)} %get-tuple-element.93), channel_id=1, source_target_pairs={{0,4},{2,6},{8,0},{10,2},{16,8},{18,10},{24,16},{26,18},{28,24},{3... | collective-permute-start | bytes 786440 | tf_op jit(solution)/shard_map/ppermute | solution.py:457
  85.9 12.6 %collective-permute-start.32 = (bf16[64,2048]{1,0:T(8,128)(2,1)S(1)}, bf16[64,2048]{1,0:T(8,128)(2,1)S(1)}, u32[]{:S(2)}, u32[]{:S(2)}) collective-permute-start(bf16[64,2048]{1,0:T(8,128)(2,1)S(1)} %get-tuple-element.97), channel_id=1, source_target_pairs={{0,8},{2,10},{8,16},{10,18},{16,24},{18,26},{24,28},{26,30},{28,20... | collective-permute-start | bytes 786440 | tf_op jit(solution)/shard_map/ppermute | solution.py:457
  89.0 12.7 %collective-permute-start.36 = (bf16[64,2048]{1,0:T(8,128)(2,1)S(1)}, bf16[64,2048]{1,0:T(8,128)(2,1)S(1)}, u32[]{:S(2)}, u32[]{:S(2)}) collective-permute-start(bf16[64,2048]{1,0:T(8,128)(2,1)S(1)} %join.17), channel_id=1, source_target_pairs={{0,4},{2,6},{8,0},{10,2},{16,8},{18,10},{24,16},{26,18},{28,24},{3... | collective-permute-start | bytes 786440 | tf_op jit(solution)/shard_map/ppermute | solution.py:457
  89.5 14.6 %collective-permute-start.23 = (bf16[64,2048]{1,0:T(8,128)(2,1)S(1)}, bf16[64,2048]{1,0:T(8,128)(2,1)S(1)}, u32[]{:S(2)}, u32[]{:S(2)}) collective-permute-start(bf16[64,2048]{1,0:T(8,128)(2,1)S(1)} %join.10), channel_id=1, source_target_pairs={{0,8},{2,10},{8,16},{10,18},{16,24},{18,26},{24,28},{26,30},{28,20... | collective-permute-start | bytes 786440 | tf_op jit(solution)/shard_map/ppermute | solution.py:457
  91.2 10.5 %collective-permute-start.26 = (f32[136,128]{1,0:T(8,128)S(1)}, f32[136,128]{1,0:T(8,128)S(1)}, u32[]{:S(2)}, u32[]{:S(2)}) collective-permute-start(f32[136,128]{1,0:T(8,128)S(1)} %fusion), channel_id=1, source_target_pairs={{0,8},{2,10},{4,12},{6,14},{8,0},{10,2},{12,4},{14,6},{16,24},{18,... | collective-permute-start | bytes 208904 | tf_op jit(solution)/shard_map/ppermute | solution.py:49
  94.6 12.7 %collective-permute-start.30 = (bf16[64,2048]{1,0:T(8,128)(2,1)S(1)}, bf16[64,2048]{1,0:T(8,128)(2,1)S(1)}, u32[]{:S(2)}, u32[]{:S(2)}) collective-permute-start(bf16[64,2048]{1,0:T(8,128)(2,1)S(1)} %join.13), channel_id=1, source_target_pairs={{0,4},{2,6},{8,0},{10,2},{16,8},{18,10},{24,16},{26,18},{28,24},{3... | collective-permute-start | bytes 786440 | tf_op jit(solution)/shard_map/ppermute | solution.py:457
  98.6 18.0 %collective-permute-start.33 = (bf16[64,2048]{1,0:T(8,128)(2,1)S(1)}, bf16[64,2048]{1,0:T(8,128)(2,1)S(1)}, u32[]{:S(2)}, u32[]{:S(2)}) collective-permute-start(bf16[64,2048]{1,0:T(8,128)(2,1)S(1)} %join.15), channel_id=1, source_target_pairs={{0,8},{2,10},{8,16},{10,18},{16,24},{18,26},{24,28},{26,30},{28,20... | collective-permute-start | bytes 786440 | tf_op jit(solution)/shard_map/ppermute | solution.py:457
  101.8 17.8 %collective-permute-start.37 = (bf16[64,2048]{1,0:T(8,128)(2,1)S(1)}, bf16[64,2048]{1,0:T(8,128)(2,1)S(1)}, u32[]{:S(2)}, u32[]{:S(2)}) collective-permute-start(bf16[64,2048]{1,0:T(8,128)(2,1)S(1)} %join.18), channel_id=1, source_target_pairs={{0,4},{2,6},{8,0},{10,2},{16,8},{18,10},{24,16},{26,18},{28,24},{3... | collective-permute-start | bytes 786440 | tf_op jit(solution)/shard_map/ppermute | solution.py:457
  104.2 16.9 %collective-permute-start.27 = (bf16[64,2048]{1,0:T(8,128)(2,1)S(1)}, bf16[64,2048]{1,0:T(8,128)(2,1)S(1)}, u32[]{:S(2)}, u32[]{:S(2)}) collective-permute-start(bf16[64,2048]{1,0:T(8,128)(2,1)S(1)} %join.11), channel_id=1, source_target_pairs={{0,8},{2,10},{8,16},{10,18},{16,24},{18,26},{24,28},{26,30},{28,20... | collective-permute-start | bytes 786440 | tf_op jit(solution)/shard_map/ppermute | solution.py:457
  116.1 11.6 %collective-permute-start.31 = (bf16[64,2048]{1,0:T(8,128)(2,1)S(1)}, bf16[64,2048]{1,0:T(8,128)(2,1)S(1)}, u32[]{:S(2)}, u32[]{:S(2)}) collective-permute-start(bf16[64,2048]{1,0:T(8,128)(2,1)S(1)} %join.14), channel_id=1, source_target_pairs={{0,4},{2,6},{8,0},{10,2},{16,8},{18,10},{24,16},{26,18},{28,24},{3... | collective-permute-start | bytes 786440 | tf_op jit(solution)/shard_map/ppermute | solution.py:457
  117.3 10.4 %collective-permute-start.34 = (bf16[64,2048]{1,0:T(8,128)(2,1)}, bf16[64,2048]{1,0:T(8,128)(2,1)S(1)}, u32[]{:S(2)}, u32[]{:S(2)}) collective-permute-start(bf16[64,2048]{1,0:T(8,128)(2,1)} %join.16), channel_id=1, source_target_pairs={{0,8},{2,10},{8,16},{10,18},{16,24},{18,26},{24,28},{26,30},{28,20... | collective-permute-start | bytes 786440 | tf_op jit(solution)/shard_map/ppermute | solution.py:457
  (25 other events, 156.9 us)

commit v12 on v8

--- a/solution.py
+++ b/solution.py
@@ -352,8 +352,8 @@
     pair, tiles = swap(adjacency, rows), load(adjacency)
     for step in range(1, top + 1):
         if step == 2:
-            up, down, pair, pack, tiles, table = lax.optimization_barrier(
-                (up, down, pair, pack, tiles, table)
+            up[1], down[1], pair, pack, tiles, table = lax.optimization_barrier(
+                (up[1], down[1], pair, pack, tiles, table)
             )
             packs = [pack] + [send(pack, k, 0, rows, feats) for k in range(1, feats)]
         if step == 3:

time: 129 us -> 130 us (level)
  starting transfers between devices: 37.1 us -> 39.4 us
  waiting for transfers between devices: 53.6 us -> 52 us
    ppermute x7, waiting for transfers between devices: 3.85 us -> 13.2 us  [shards(): up[side] = lax.ppermute(up[side], 'rows', forward)]
    ppermute x7, waiting for transfers between devices: 19.7 us -> 11 us  [shards(): down[side] = lax.ppermute(down[side], 'rows', backward)]
    ppermute x9, waiting for transfers between devices: 16.8 us -> 14.6 us  [swap(): return lax.ppermute(value, 'rows', [(r, r ^ bit) for r in range(rows)])]
  transfers between devices with their start and end apart: 41 -> 41, of which waited for: 22 -> 21; matrix products, arithmetic and copies ran while one was open for 1% -> 1% of each run, Pallas kernels for 22% -> 22%
where the time goes in v12:
time: 130 us
  waiting for transfers between devices  52 us (40%)
  starting transfers between devices  39.4 us (30%)
  Pallas kernels  32.6 us (25%)
  local copies, waits for them, and re-layouts  4.64 us (4%)
    pallas_call x26, Pallas kernels, call(): pl.pallas_call(kernel, out_shape=[jax.ShapeDtypeStruct(shape, kind) for s...  32.6 us
    ppermute x14, starting transfers between devices, ring(): return lax.ppermute(value, 'rows', pairs)  14.7 us
    ppermute x9, waiting for transfers between devices, swap(): return lax.ppermute(value, 'rows', [(r, r ^ bit) for r in range(rows)])  14.6 us
    ppermute x7, waiting for transfers between devices, shards(): up[side] = lax.ppermute(up[side], 'rows', forward)  13.2 us
    ppermute x7, starting transfers between devices, shards(): up[side] = lax.ppermute(up[side], 'rows', forward)  12.5 us
    ppermute x7, waiting for transfers between devices, shards(): down[side] = lax.ppermute(down[side], 'rows', backward)  11 us
    ppermute x4, waiting for transfers between devices, send(): return lax.ppermute(value, ('rows', 'feat'), pairs)  7.36 us
    ppermute x14, waiting for transfers between devices, ring(): return lax.ppermute(value, 'rows', pairs)  5.85 us
  transfers between devices with their start and end apart: 41, of which 21 were waited for; matrix products, arithmetic and copies ran while one was open for 1% of the time, Pallas kernels for 22%

profile of v12, /device:TPU:0, one launch (start us, length us, event | category | flops | bytes accessed | tf_op | source)
XLA Modules:
  0.0 129.7 jit_solution(550914022397290435)
XLA Ops:
  2.2 2.7 %collective-permute-start = (bf16[64,2048]{1,0:T(8,128)(2,1)S(1)}, bf16[64,2048]{1,0:T(8,128)(2,1)S(1)}, u32[]{:S(2)}, u32[]{:S(2)}) collective-permute-start(bf16[64,2048]{1,0:T(8,128)(2,1)S(1)} %get-tuple-element.66), channel_id=1, source_target_pairs={{0,10},{2,8},{8,18},{10,16},{16,26},{18,24},{24,30},{26,28},{28,22... | collective-permute-start | bytes 786440 | tf_op jit(solution)/shard_map/ppermute | solution.py:371
  7.0 2.8 %copy-done = bf16[16,12,128,128]{3,2,1,0:T(8,128)(2,1)S(1)} copy-done((bf16[16,12,128,128]{3,2,1,0:T(8,128)(2,1)S(1)}, bf16[16,12,128,128]{3,2,1,0:T(8,128)(2,1)}, u32[]{:S(2)}) %copy-start) | copy-done | bytes 6291480
  10.5 3.2 %table.1 = s32[384]{0:T(512)S(1)} custom-call(s32[16,12]{1,0:T(8,128)S(1)} %copy-done.5), custom_call_target="tpu_custom_call" | custom-call | bytes 1536 | tf_op jit(solution)/shard_map/table/pallas_call | solution.py:307
  21.1 2.8 %load.3.tiles.pair = bf16[16,12,128,128]{3,2,1,0:T(8,128)(2,1)S(1)} custom-call(bf16[16,12,128,128]{3,2,1,0:T(8,128)(2,1)} %collective-permute-done.2.source), custom_call_target="tpu_custom_call" | custom-call | bytes 12582912 | tf_op jit(solution)/shard_map/load/pallas_call | solution.py:307
  28.6 1.8 %collective-permute-start.8 = (bf16[64,2048]{1,0:T(8,128)(2,1)S(1)}, bf16[64,2048]{1,0:T(8,128)(2,1)S(1)}, u32[]{:S(2)}, u32[]{:S(2)}) collective-permute-start(bf16[64,2048]{1,0:T(8,128)(2,1)S(1)} %collective-permute-done.refs_3_), channel_id=1, source_target_pairs={{0,8},{2,10},{8,16},{10,18},{16,24},{18,26},{24,28},{26,30},{28,20... | collective-permute-start | bytes 786440 | tf_op jit(solution)/shard_map/ppermute | solution.py:371
  30.4 3.6 %collective-permute-done.9.refs_8_ = bf16[64,2048]{1,0:T(8,128)(2,1)S(1)} collective-permute-done((bf16[64,2048]{1,0:T(8,128)(2,1)S(1)}, bf16[64,2048]{1,0:T(8,128)(2,1)S(1)}, u32[]{:S(2)}, u32[]{:S(2)}) %collective-permute-start.9) | collective-permute-done | bytes 262176 | tf_op jit(solution)/shard_map/ppermute | solution.py:375
  34.7 4.9 %collective-permute-done.11.refs_10_ = bf16[64,2048]{1,0:T(8,128)(2,1)S(1)} collective-permute-done((bf16[64,2048]{1,0:T(8,128)(2,1)S(1)}, bf16[64,2048]{1,0:T(8,128)(2,1)S(1)}, u32[]{:S(2)}, u32[]{:S(2)}) %collective-permute-start.11) | collective-permute-done | bytes 262176 | tf_op jit(solution)/shard_map/ppermute | solution.py:375
  44.4 4.9 %collective-permute-done.12.refs_11_ = bf16[64,2048]{1,0:T(8,128)(2,1)S(1)} collective-permute-done((bf16[64,2048]{1,0:T(8,128)(2,1)S(1)}, bf16[64,2048]{1,0:T(8,128)(2,1)S(1)}, u32[]{:S(2)}, u32[]{:S(2)}) %collective-permute-start.12) | collective-permute-done | bytes 262176 | tf_op jit(solution)/shard_map/ppermute | solution.py:371
  49.3 4.7 %collective-permute-done.15.refs_14_ = bf16[64,2048]{1,0:T(8,128)(2,1)S(1)} collective-permute-done((bf16[64,2048]{1,0:T(8,128)(2,1)S(1)}, bf16[64,2048]{1,0:T(8,128)(2,1)S(1)}, u32[]{:S(2)}, u32[]{:S(2)}) %collective-permute-start.15) | collective-permute-done | bytes 262176 | tf_op jit(solution)/shard_map/ppermute | solution.py:371
  54.0 4.4 %aggregate.3 = (bf16[64,2048]{1,0:T(8,128)(2,1)S(1)}, f32[1,2048]{1,0:T(1,128)}) custom-call(s32[384]{0:T(512)S(1)} %collective-permute-done.18.table.table_pair, bf16[16,12,128,128]{3,2,1,0:T(8,128)(2,1)S(1)} %load.3.tiles.pair, bf16[64,2048]{1,0:T(8,128)(2,1)S(1)} %get-tuple-element.105.refs_0_, bf16[64,2048]{1,0:T(8,128)(2,1)S(1)} %collective-permute-done.4.refs_1_, ...), custom_call_target="tpu_custom_call" | custom-call | flops 402653184 | bytes 10485760 | tf_op jit(solution)/shard_map/aggregate/pallas_call | solution.py:307
  60.1 3.9 %aggregate.2 = (bf16[64,2048]{1,0:T(8,128)(2,1)S(1)}, f32[1,2048]{1,0:T(1,128)S(1)}) custom-call(s32[384]{0:T(512)S(1)} %table.1, bf16[16,12,128,128]{3,2,1,0:T(8,128)(2,1)S(1)} %load.2.tiles.adj, bf16[64,2048]{1,0:T(8,128)(2,1)S(1)} %get-tuple-element.105.refs_0_, bf16[64,2048]{1,0:T(8,128)(2,1)S(1)} %collective-permute-done.4.refs_1_, ...), custom_call_target="tpu_custom_call" | custom-call | flops 402653184 | bytes 10485760 | tf_op jit(solution)/shard_map/aggregate/pallas_call | solution.py:307
  66.8 6.0 %collective-permute-done.17.refs_1_ = bf16[64,2048]{1,0:T(8,128)(2,1)S(1)} collective-permute-done((bf16[64,2048]{1,0:T(8,128)(2,1)S(1)}, bf16[64,2048]{1,0:T(8,128)(2,1)S(1)}, u32[]{:S(2)}, u32[]{:S(2)}) %collective-permute-start.17) | collective-permute-done | bytes 262176 | tf_op jit(solution)/shard_map/ppermute | solution.py:58
  72.8 3.0 %middle.1 = (bf16[128,2048]{1,0:T(8,128)(2,1)}, bf16[256,2048]{1,0:T(8,128)(2,1)S(1)}, bf16[128,2048]{1,0:T(8,128)(2,1)S(1)}, bf16[128,2048]{1,0:T(8,128)(2,1)S(1)}) custom-call(bf16[256,256]{1,0:T(8,128)(2,1)S(1)} %get-tuple-element.56.turned, bf16[128,256]{1,0:T(8,128)(2,1)S(1)} %copy-done.3, f32[1,2048]{1,0:T(1,128)S(1)} %get-tuple-element.67.inverse, ...), custom_call_target="tpu_custom_call" | custom-call | flops 402653184 | bytes 7340032 | tf_op jit(solution)/shard_map/middle/pallas_call | solution.py:307
  85.5 3.2 %collective-permute-done.22.arrived = bf16[64,2048]{1,0:T(8,128)(2,1)S(1)} collective-permute-done((bf16[64,2048]{1,0:T(8,128)(2,1)S(1)}, bf16[64,2048]{1,0:T(8,128)(2,1)S(1)}, u32[]{:S(2)}, u32[]{:S(2)}) %collective-permute-start.22) | collective-permute-done | bytes 262176 | tf_op jit(solution)/shard_map/ppermute | solution.py:456
  88.8 1.8 %collective-permute-start.23 = (bf16[64,2048]{1,0:T(8,128)(2,1)S(1)}, bf16[64,2048]{1,0:T(8,128)(2,1)S(1)}, u32[]{:S(2)}, u32[]{:S(2)}) collective-permute-start(bf16[64,2048]{1,0:T(8,128)(2,1)S(1)} %join.10), channel_id=1, source_target_pairs={{0,8},{2,10},{8,16},{10,18},{16,24},{18,26},{24,28},{26,30},{28,20... | collective-permute-start | bytes 786440 | tf_op jit(solution)/shard_map/ppermute | solution.py:456
  91.8 2.0 %collective-permute-start.36 = (f32[2,136,128]{2,1,0:T(8,128)S(1)}, f32[2,136,128]{2,1,0:T(8,128)S(1)}, u32[]{:S(2)}, u32[]{:S(2)}) collective-permute-start(f32[2,136,128]{2,1,0:T(8,128)S(1)} %add.24), channel_id=1, source_target_pairs={{0,8},{2,10},{4,12},{6,14},{8,0},{10,2},{12,4},{14,6},{16,24},{18,... | collective-permute-start | bytes 417800 | tf_op jit(solution)/shard_map/ppermute | solution.py:49
  93.8 1.8 %spread.7 = (f32[64,2048]{1,0:T(8,128)S(1)}, f32[64,2048]{1,0:T(8,128)S(1)}, f32[64,2048]{1,0:T(8,128)S(1)}, f32[64,2048]{1,0:T(8,128)S(1)}) custom-call(s32[384]{0:T(512)S(1)} %table.1, s32[384]{0:T(512)S(1)} %collective-permute-done.18.table.table_pair, bf16[16,12,128,128]{3,2,1,0:T(8,128)(2,1)S(1)} %load.2.tiles.adj, ...), custom_call_target="tpu_custom_call" | custom-call | flops 201326592 | bytes 4194304 | tf_op jit(solution)/shard_map/spread/pallas_call | solution.py:307
  97.5 2.1 %collective-permute-start.27 = (bf16[64,2048]{1,0:T(8,128)(2,1)S(1)}, bf16[64,2048]{1,0:T(8,128)(2,1)S(1)}, u32[]{:S(2)}, u32[]{:S(2)}) collective-permute-start(bf16[64,2048]{1,0:T(8,128)(2,1)S(1)} %join.13), channel_id=1, source_target_pairs={{0,4},{2,6},{8,0},{10,2},{16,8},{18,10},{24,16},{26,18},{28,24},{3... | collective-permute-start | bytes 786440 | tf_op jit(solution)/shard_map/ppermute | solution.py:456
  99.6 4.4 %collective-permute-done.36 = f32[2,136,128]{2,1,0:T(8,128)S(1)} collective-permute-done((f32[2,136,128]{2,1,0:T(8,128)S(1)}, f32[2,136,128]{2,1,0:T(8,128)S(1)}, u32[]{:S(2)}, u32[]{:S(2)}) %collective-permute-start.36) | collective-permute-done | bytes 139296 | tf_op jit(solution)/shard_map/ppermute | solution.py:49
  106.5 1.8 %collective-permute-start.38 = (f32[2,136,128]{2,1,0:T(8,128)S(1)}, f32[2,136,128]{2,1,0:T(8,128)S(1)}, u32[]{:S(2)}, u32[]{:S(2)}) collective-permute-start(f32[2,136,128]{2,1,0:T(8,128)S(1)} %add.25), channel_id=1, source_target_pairs={{0,16},{2,18},{4,20},{6,22},{8,24},{10,26},{12,28},{14,30},{16,0},... | collective-permute-start | bytes 417800 | tf_op jit(solution)/shard_map/ppermute | solution.py:49
  108.2 2.3 %spread.4 = (f32[64,2048]{1,0:T(8,128)S(1)}, f32[64,2048]{1,0:T(8,128)S(1)}, f32[64,2048]{1,0:T(8,128)S(1)}, f32[64,2048]{1,0:T(8,128)S(1)}, f32[64,2048]{1,0:T(8,128)S(1)}, /*index=5*/f32[64,2048]{1,0:T(8,128)S(1)}) custom-call(s32[384]{0:T(512)S(1)} %table.1, s32[384]{0:T(512)S(1)} %collective-permute-done.18.table.table_pair, ...), custom_call_target="tpu_custom_call" | custom-call | flops 301989888 | bytes 6291456 | tf_op jit(solution)/shard_map/spread/pallas_call | solution.py:307
  110.6 2.2 %collective-permute-start.31 = (bf16[64,2048]{1,0:T(8,128)(2,1)S(1)}, bf16[64,2048]{1,0:T(8,128)(2,1)S(1)}, u32[]{:S(2)}, u32[]{:S(2)}) collective-permute-start(bf16[64,2048]{1,0:T(8,128)(2,1)S(1)} %join.16), channel_id=1, source_target_pairs={{0,8},{2,10},{8,16},{10,18},{16,24},{18,26},{24,28},{26,30},{28,20... | collective-permute-start | bytes 786440 | tf_op jit(solution)/shard_map/ppermute | solution.py:456
  113.6 7.0 %collective-permute-done.38 = f32[2,136,128]{2,1,0:T(8,128)S(1)} collective-permute-done((f32[2,136,128]{2,1,0:T(8,128)S(1)}, f32[2,136,128]{2,1,0:T(8,128)S(1)}, u32[]{:S(2)}, u32[]{:S(2)}) %collective-permute-start.38) | collective-permute-done | bytes 139296 | tf_op jit(solution)/shard_map/ppermute | solution.py:49
  122.1 2.0 %collective-permute-start.39 = (bf16[64,2048]{1,0:T(8,128)(2,1)}, bf16[64,2048]{1,0:T(8,128)(2,1)S(1)}, u32[]{:S(2)}, u32[]{:S(2)}) collective-permute-start(bf16[64,2048]{1,0:T(8,128)(2,1)} %join.19), channel_id=1, source_target_pairs={{0,4},{2,6},{8,0},{10,2},{16,8},{18,10},{24,16},{26,18},{28,24},{3... | collective-permute-start | bytes 786440 | tf_op jit(solution)/shard_map/ppermute | solution.py:456
  (106 shorter events, 49.5 us)
Async XLA Ops:
  0.6 13.4 %collective-permute-start.2 = (bf16[16,12,128,128]{3,2,1,0:T(8,128)(2,1)}, bf16[16,12,128,128]{3,2,1,0:T(8,128)(2,1)}, u32[]{:S(2)}, u32[]{:S(2)}) collective-permute-start(bf16[16,12,128,128]{3,2,1,0:T(8,128)(2,1)} %source.1), channel_id=1, source_target_pairs={{0,2},{2,0},{4,6},{6,4},{8,10},{10,8},{12,14},{14,12},{16,18},{18,... | collective-permute-start | bytes 18874376 | tf_op jit(solution)/shard_map/ppermute | solution.py:49
  2.2 11.8 %collective-permute-start = (bf16[64,2048]{1,0:T(8,128)(2,1)S(1)}, bf16[64,2048]{1,0:T(8,128)(2,1)S(1)}, u32[]{:S(2)}, u32[]{:S(2)}) collective-permute-start(bf16[64,2048]{1,0:T(8,128)(2,1)S(1)} %get-tuple-element.66), channel_id=1, source_target_pairs={{0,10},{2,8},{8,18},{10,16},{16,26},{18,24},{24,30},{26,28},{28,22... | collective-permute-start | bytes 786440 | tf_op jit(solution)/shard_map/ppermute | solution.py:371
  5.0 12.4 %collective-permute-start.4 = (bf16[64,2048]{1,0:T(8,128)(2,1)S(1)}, bf16[64,2048]{1,0:T(8,128)(2,1)S(1)}, u32[]{:S(2)}, u32[]{:S(2)}) collective-permute-start(bf16[64,2048]{1,0:T(8,128)(2,1)S(1)} %get-tuple-element.105.refs_0_), channel_id=1, source_target_pairs={{0,8},{2,10},{8,16},{10,18},{16,24},{18,26},{24,28},{26,30},{28,20... | collective-permute-start | bytes 786440 | tf_op jit(solution)/shard_map/ppermute | solution.py:371
  6.6 12.6 %collective-permute-start.5 = (bf16[64,2048]{1,0:T(8,128)(2,1)S(1)}, bf16[64,2048]{1,0:T(8,128)(2,1)S(1)}, u32[]{:S(2)}, u32[]{:S(2)}) collective-permute-start(bf16[64,2048]{1,0:T(8,128)(2,1)S(1)} %get-tuple-element.105.refs_0_), channel_id=1, source_target_pairs={{0,4},{2,6},{8,0},{10,2},{16,8},{18,10},{24,16},{26,18},{28,24},{3... | collective-permute-start | bytes 786440 | tf_op jit(solution)/shard_map/ppermute | solution.py:375
  14.0 50.5 %collective-permute-start.3 = (bf16[128,4736]{1,0:T(8,128)(2,1)S(1)}, bf16[128,4736]{1,0:T(8,128)(2,1)S(1)}, u32[]{:S(2)}, u32[]{:S(2)}) collective-permute-start(bf16[128,4736]{1,0:T(8,128)(2,1)S(1)} %pack.1.refs_0_), channel_id=1, source_target_pairs={{0,1},{1,0},{2,3},{3,2},{4,5},{5,4},{6,7},{7,6},{8,9},{9,8},{10,11... | collective-permute-start | bytes 3637256 | tf_op jit(solution)/shard_map/ppermute | solution.py:58
  19.4 14.6 %collective-permute-start.9 = (bf16[64,2048]{1,0:T(8,128)(2,1)S(1)}, bf16[64,2048]{1,0:T(8,128)(2,1)S(1)}, u32[]{:S(2)}, u32[]{:S(2)}) collective-permute-start(bf16[64,2048]{1,0:T(8,128)(2,1)S(1)} %collective-permute-done.1.refs_4_), channel_id=1, source_target_pairs={{0,4},{2,6},{8,0},{10,2},{16,8},{18,10},{24,16},{26,18},{28,24},{3... | collective-permute-start | bytes 786440 | tf_op jit(solution)/shard_map/ppermute | solution.py:375
  28.4 11.2 %collective-permute-start.11 = (bf16[64,2048]{1,0:T(8,128)(2,1)S(1)}, bf16[64,2048]{1,0:T(8,128)(2,1)S(1)}, u32[]{:S(2)}, u32[]{:S(2)}) collective-permute-start(bf16[64,2048]{1,0:T(8,128)(2,1)S(1)} %collective-permute-done.7.refs_6_), channel_id=1, source_target_pairs={{0,4},{2,6},{8,0},{10,2},{16,8},{18,10},{24,16},{26,18},{28,24},{3... | collective-permute-start | bytes 786440 | tf_op jit(solution)/shard_map/ppermute | solution.py:375
  28.6 11.6 %collective-permute-start.8 = (bf16[64,2048]{1,0:T(8,128)(2,1)S(1)}, bf16[64,2048]{1,0:T(8,128)(2,1)S(1)}, u32[]{:S(2)}, u32[]{:S(2)}) collective-permute-start(bf16[64,2048]{1,0:T(8,128)(2,1)S(1)} %collective-permute-done.refs_3_), channel_id=1, source_target_pairs={{0,8},{2,10},{8,16},{10,18},{16,24},{18,26},{24,28},{26,30},{28,20... | collective-permute-start | bytes 786440 | tf_op jit(solution)/shard_map/ppermute | solution.py:371
  34.0 10.2 %collective-permute-start.13 = (bf16[64,2048]{1,0:T(8,128)(2,1)S(1)}, bf16[64,2048]{1,0:T(8,128)(2,1)S(1)}, u32[]{:S(2)}, u32[]{:S(2)}) collective-permute-start(bf16[64,2048]{1,0:T(8,128)(2,1)S(1)} %collective-permute-done.9.refs_8_), channel_id=1, source_target_pairs={{0,4},{2,6},{8,0},{10,2},{16,8},{18,10},{24,16},{26,18},{28,24},{3... | collective-permute-start | bytes 786440 | tf_op jit(solution)/shard_map/ppermute | solution.py:375
  41.7 12.3 %collective-permute-start.15 = (bf16[64,2048]{1,0:T(8,128)(2,1)S(1)}, bf16[64,2048]{1,0:T(8,128)(2,1)S(1)}, u32[]{:S(2)}, u32[]{:S(2)}) collective-permute-start(bf16[64,2048]{1,0:T(8,128)(2,1)S(1)} %collective-permute-done.10.refs_9_), channel_id=1, source_target_pairs={{0,8},{2,10},{8,16},{10,18},{16,24},{18,26},{24,28},{26,30},{28,20... | collective-permute-start | bytes 786440 | tf_op jit(solution)/shard_map/ppermute | solution.py:371
  79.2 11.4 %collective-permute-start.32 = (bf16[64,2048]{1,0:T(8,128)(2,1)S(1)}, bf16[64,2048]{1,0:T(8,128)(2,1)S(1)}, u32[]{:S(2)}, u32[]{:S(2)}) collective-permute-start(bf16[64,2048]{1,0:T(8,128)(2,1)S(1)} %get-tuple-element.90), channel_id=1, source_target_pairs={{0,4},{2,6},{8,0},{10,2},{16,8},{18,10},{24,16},{26,18},{28,24},{3... | collective-permute-start | bytes 786440 | tf_op jit(solution)/shard_map/ppermute | solution.py:456
  81.3 10.3 %collective-permute-start.34 = (f32[2,136,128]{2,1,0:T(8,128)S(1)}, f32[2,136,128]{2,1,0:T(8,128)S(1)}, u32[]{:S(2)}, u32[]{:S(2)}) collective-permute-start(f32[2,136,128]{2,1,0:T(8,128)S(1)} %slice_add_fusion), channel_id=1, source_target_pairs={{0,4},{2,6},{4,0},{6,2},{8,12},{10,14},{12,8},{14,10},{16,20},{18,... | collective-permute-start | bytes 417800 | tf_op jit(solution)/shard_map/ppermute | solution.py:49
  83.4 13.9 %collective-permute-start.29 = (bf16[64,2048]{1,0:T(8,128)(2,1)S(1)}, bf16[64,2048]{1,0:T(8,128)(2,1)S(1)}, u32[]{:S(2)}, u32[]{:S(2)}) collective-permute-start(bf16[64,2048]{1,0:T(8,128)(2,1)S(1)} %get-tuple-element.87), channel_id=1, source_target_pairs={{0,8},{2,10},{8,16},{10,18},{16,24},{18,26},{24,28},{26,30},{28,20... | collective-permute-start | bytes 786440 | tf_op jit(solution)/shard_map/ppermute | solution.py:456
  85.2 12.3 %collective-permute-start.26 = (bf16[64,2048]{1,0:T(8,128)(2,1)S(1)}, bf16[64,2048]{1,0:T(8,128)(2,1)S(1)}, u32[]{:S(2)}, u32[]{:S(2)}) collective-permute-start(bf16[64,2048]{1,0:T(8,128)(2,1)S(1)} %get-tuple-element.84), channel_id=1, source_target_pairs={{0,4},{2,6},{8,0},{10,2},{16,8},{18,10},{24,16},{26,18},{28,24},{3... | collective-permute-start | bytes 786440 | tf_op jit(solution)/shard_map/ppermute | solution.py:456
  88.8 15.3 %collective-permute-start.23 = (bf16[64,2048]{1,0:T(8,128)(2,1)S(1)}, bf16[64,2048]{1,0:T(8,128)(2,1)S(1)}, u32[]{:S(2)}, u32[]{:S(2)}) collective-permute-start(bf16[64,2048]{1,0:T(8,128)(2,1)S(1)} %join.10), channel_id=1, source_target_pairs={{0,8},{2,10},{8,16},{10,18},{16,24},{18,26},{24,28},{26,30},{28,20... | collective-permute-start | bytes 786440 | tf_op jit(solution)/shard_map/ppermute | solution.py:456
  91.7 13.3 %collective-permute-start.35 = (bf16[64,2048]{1,0:T(8,128)(2,1)S(1)}, bf16[64,2048]{1,0:T(8,128)(2,1)S(1)}, u32[]{:S(2)}, u32[]{:S(2)}) collective-permute-start(bf16[64,2048]{1,0:T(8,128)(2,1)S(1)} %join.17), channel_id=1, source_target_pairs={{0,4},{2,6},{8,0},{10,2},{16,8},{18,10},{24,16},{26,18},{28,24},{3... | collective-permute-start | bytes 786440 | tf_op jit(solution)/shard_map/ppermute | solution.py:456
  91.8 12.2 %collective-permute-start.36 = (f32[2,136,128]{2,1,0:T(8,128)S(1)}, f32[2,136,128]{2,1,0:T(8,128)S(1)}, u32[]{:S(2)}, u32[]{:S(2)}) collective-permute-start(f32[2,136,128]{2,1,0:T(8,128)S(1)} %add.24), channel_id=1, source_target_pairs={{0,8},{2,10},{4,12},{6,14},{8,0},{10,2},{12,4},{14,6},{16,24},{18,... | collective-permute-start | bytes 417800 | tf_op jit(solution)/shard_map/ppermute | solution.py:49
  97.4 13.2 %collective-permute-start.30 = (bf16[64,2048]{1,0:T(8,128)(2,1)S(1)}, bf16[64,2048]{1,0:T(8,128)(2,1)S(1)}, u32[]{:S(2)}, u32[]{:S(2)}) collective-permute-start(bf16[64,2048]{1,0:T(8,128)(2,1)S(1)} %join.15), channel_id=1, source_target_pairs={{0,8},{2,10},{8,16},{10,18},{16,24},{18,26},{24,28},{26,30},{28,20... | collective-permute-start | bytes 786440 | tf_op jit(solution)/shard_map/ppermute | solution.py:456
  97.5 15.3 %collective-permute-start.27 = (bf16[64,2048]{1,0:T(8,128)(2,1)S(1)}, bf16[64,2048]{1,0:T(8,128)(2,1)S(1)}, u32[]{:S(2)}, u32[]{:S(2)}) collective-permute-start(bf16[64,2048]{1,0:T(8,128)(2,1)S(1)} %join.13), channel_id=1, source_target_pairs={{0,4},{2,6},{8,0},{10,2},{16,8},{18,10},{24,16},{26,18},{28,24},{3... | collective-permute-start | bytes 786440 | tf_op jit(solution)/shard_map/ppermute | solution.py:456
  104.1 16.5 %collective-permute-start.24 = (bf16[64,2048]{1,0:T(8,128)(2,1)S(1)}, bf16[64,2048]{1,0:T(8,128)(2,1)S(1)}, u32[]{:S(2)}, u32[]{:S(2)}) collective-permute-start(bf16[64,2048]{1,0:T(8,128)(2,1)S(1)} %join.11), channel_id=1, source_target_pairs={{0,8},{2,10},{8,16},{10,18},{16,24},{18,26},{24,28},{26,30},{28,20... | collective-permute-start | bytes 786440 | tf_op jit(solution)/shard_map/ppermute | solution.py:456
  105.1 16.2 %collective-permute-start.37 = (bf16[64,2048]{1,0:T(8,128)(2,1)S(1)}, bf16[64,2048]{1,0:T(8,128)(2,1)S(1)}, u32[]{:S(2)}, u32[]{:S(2)}) collective-permute-start(bf16[64,2048]{1,0:T(8,128)(2,1)S(1)} %join.18), channel_id=1, source_target_pairs={{0,4},{2,6},{8,0},{10,2},{16,8},{18,10},{24,16},{26,18},{28,24},{3... | collective-permute-start | bytes 786440 | tf_op jit(solution)/shard_map/ppermute | solution.py:456
  106.5 14.1 %collective-permute-start.38 = (f32[2,136,128]{2,1,0:T(8,128)S(1)}, f32[2,136,128]{2,1,0:T(8,128)S(1)}, u32[]{:S(2)}, u32[]{:S(2)}) collective-permute-start(f32[2,136,128]{2,1,0:T(8,128)S(1)} %add.25), channel_id=1, source_target_pairs={{0,16},{2,18},{4,20},{6,22},{8,24},{10,26},{12,28},{14,30},{16,0},... | collective-permute-start | bytes 417800 | tf_op jit(solution)/shard_map/ppermute | solution.py:49
  110.6 17.1 %collective-permute-start.31 = (bf16[64,2048]{1,0:T(8,128)(2,1)S(1)}, bf16[64,2048]{1,0:T(8,128)(2,1)S(1)}, u32[]{:S(2)}, u32[]{:S(2)}) collective-permute-start(bf16[64,2048]{1,0:T(8,128)(2,1)S(1)} %join.16), channel_id=1, source_target_pairs={{0,8},{2,10},{8,16},{10,18},{16,24},{18,26},{24,28},{26,30},{28,20... | collective-permute-start | bytes 786440 | tf_op jit(solution)/shard_map/ppermute | solution.py:456
  113.6 14.2 %collective-permute-start.28 = (bf16[64,2048]{1,0:T(8,128)(2,1)}, bf16[64,2048]{1,0:T(8,128)(2,1)S(1)}, u32[]{:S(2)}, u32[]{:S(2)}) collective-permute-start(bf16[64,2048]{1,0:T(8,128)(2,1)} %join.14), channel_id=1, source_target_pairs={{0,4},{2,6},{8,0},{10,2},{16,8},{18,10},{24,16},{26,18},{28,24},{3... | collective-permute-start | bytes 786440 | tf_op jit(solution)/shard_map/ppermute | solution.py:456
  (24 other events, 142.9 us)

commit v13 on v8

--- a/solution.py
+++ b/solution.py
@@ -441,17 +441,20 @@
         return out
 
     total = sums[:2] + swap(after(sums[2:], scaled_pair), rows, 1)
-    total = total + swap(total, rows, 2)
-    bit, sends = 4, 0
+    arriving, bit, sends = swap(total, rows, 2), 4, 0
 
     def ring(value, pairs):
-        nonlocal total, bit, sends
+        nonlocal total, arriving, bit, sends
         sends += 1
-        if sends >= 6 and sends % 4 == 2 and bit < 2 * rows:
-            value = after(value, total)
-            total = after(total, value)
+        if sends >= 6 and sends % 4 == 2 and arriving is not None:
+            if sends == 6:
+                total = total + arriving
+                value = after(value, total)
+            else:
+                total = total + after(arriving, value)
+            arriving = None
             if bit < rows:
-                total = total + swap(total, rows, bit)
+                arriving = swap(total, rows, bit)
             bit *= 2
         return lax.ppermute(value, "rows", pairs)
 

time: 129 us -> 128 us (level)
    ppermute x9, waiting for transfers between devices: 16.8 us -> 5.49 us  [swap(): return lax.ppermute(value, 'rows', [(r, r ^ bit) for r in range(rows)])]
    ppermute x14, waiting for transfers between devices: 5.85 us -> 16.2 us  [ring(): return lax.ppermute(value, 'rows', pairs)]
  transfers between devices with their start and end apart: 41 -> 41, of which waited for: 22 -> 25; matrix products, arithmetic and copies ran while one was open for 1% -> 1% of each run, Pallas kernels for 22% -> 22%
where the time goes in v13:
time: 128 us
  waiting for transfers between devices  52.6 us (41%)
  starting transfers between devices  36.9 us (29%)
  Pallas kernels  32.7 us (26%)
  local copies, waits for them, and re-layouts  4.64 us (4%)
    pallas_call x26, Pallas kernels, call(): pl.pallas_call(kernel, out_shape=[jax.ShapeDtypeStruct(shape, kind) for s...  32.7 us
    ppermute x7, waiting for transfers between devices, shards(): down[side] = lax.ppermute(down[side], 'rows', backward)  19.7 us
    ppermute x14, waiting for transfers between devices, ring(): return lax.ppermute(value, 'rows', pairs)  16.2 us
    ppermute x14, starting transfers between devices, ring(): return lax.ppermute(value, 'rows', pairs)  13.9 us
    ppermute x7, starting transfers between devices, shards(): up[side] = lax.ppermute(up[side], 'rows', forward)  11.8 us
    ppermute x4, waiting for transfers between devices, send(): return lax.ppermute(value, ('rows', 'feat'), pairs)  7.36 us
    ppermute x9, waiting for transfers between devices, swap(): return lax.ppermute(value, 'rows', [(r, r ^ bit) for r in range(rows)])  5.49 us
    ppermute x9, starting transfers between devices, swap(): return lax.ppermute(value, 'rows', [(r, r ^ bit) for r in range(rows)])  4.65 us
  transfers between devices with their start and end apart: 41, of which 25 were waited for; matrix products, arithmetic and copies ran while one was open for 1% of the time, Pallas kernels for 22%

profile of v13, /device:TPU:0, one launch (start us, length us, event | category | flops | bytes accessed | tf_op | source)
XLA Modules:
  0.0 127.8 jit_solution(14062799125285711542)
XLA Ops:
  2.2 2.7 %collective-permute-start = (bf16[64,2048]{1,0:T(8,128)(2,1)S(1)}, bf16[64,2048]{1,0:T(8,128)(2,1)S(1)}, u32[]{:S(2)}, u32[]{:S(2)}) collective-permute-start(bf16[64,2048]{1,0:T(8,128)(2,1)S(1)} %get-tuple-element.104.refs_0_), channel_id=1, source_target_pairs={{0,8},{2,10},{8,16},{10,18},{16,24},{18,26},{24,28},{26,30},{28,20... | collective-permute-start | bytes 786440 | tf_op jit(solution)/shard_map/ppermute | solution.py:371
  6.6 2.8 %copy-done = bf16[16,12,128,128]{3,2,1,0:T(8,128)(2,1)S(1)} copy-done((bf16[16,12,128,128]{3,2,1,0:T(8,128)(2,1)S(1)}, bf16[16,12,128,128]{3,2,1,0:T(8,128)(2,1)}, u32[]{:S(2)}) %copy-start) | copy-done | bytes 6291480
  10.1 3.2 %table.1 = s32[384]{0:T(512)S(1)} custom-call(s32[16,12]{1,0:T(8,128)S(1)} %copy-done.5), custom_call_target="tpu_custom_call" | custom-call | bytes 1536 | tf_op jit(solution)/shard_map/table/pallas_call | solution.py:307
  14.0 3.1 %collective-permute-done.1.refs_3_ = bf16[64,2048]{1,0:T(8,128)(2,1)S(1)} collective-permute-done((bf16[64,2048]{1,0:T(8,128)(2,1)S(1)}, bf16[64,2048]{1,0:T(8,128)(2,1)S(1)}, u32[]{:S(2)}, u32[]{:S(2)}) %collective-permute-start.1) | collective-permute-done | bytes 262176 | tf_op jit(solution)/shard_map/ppermute | solution.py:371
  23.7 2.8 %load.3.tiles.pair = bf16[16,12,128,128]{3,2,1,0:T(8,128)(2,1)S(1)} custom-call(bf16[16,12,128,128]{3,2,1,0:T(8,128)(2,1)} %collective-permute-done.4.source), custom_call_target="tpu_custom_call" | custom-call | bytes 12582912 | tf_op jit(solution)/shard_map/load/pallas_call | solution.py:307
  26.5 2.3 %collective-permute-done.7.refs_6_ = bf16[64,2048]{1,0:T(8,128)(2,1)S(1)} collective-permute-done((bf16[64,2048]{1,0:T(8,128)(2,1)S(1)}, bf16[64,2048]{1,0:T(8,128)(2,1)S(1)}, u32[]{:S(2)}, u32[]{:S(2)}) %collective-permute-start.7) | collective-permute-done | bytes 262176 | tf_op jit(solution)/shard_map/ppermute | solution.py:375
  30.9 3.5 %collective-permute-done.9.refs_8_ = bf16[64,2048]{1,0:T(8,128)(2,1)S(1)} collective-permute-done((bf16[64,2048]{1,0:T(8,128)(2,1)S(1)}, bf16[64,2048]{1,0:T(8,128)(2,1)S(1)}, u32[]{:S(2)}, u32[]{:S(2)}) %collective-permute-start.9) | collective-permute-done | bytes 262176 | tf_op jit(solution)/shard_map/ppermute | solution.py:375
  36.5 3.5 %collective-permute-done.11.refs_10_ = bf16[64,2048]{1,0:T(8,128)(2,1)S(1)} collective-permute-done((bf16[64,2048]{1,0:T(8,128)(2,1)S(1)}, bf16[64,2048]{1,0:T(8,128)(2,1)S(1)}, u32[]{:S(2)}, u32[]{:S(2)}) %collective-permute-start.11) | collective-permute-done | bytes 262176 | tf_op jit(solution)/shard_map/ppermute | solution.py:375
  40.6 4.4 %collective-permute-done.13.refs_12_ = bf16[64,2048]{1,0:T(8,128)(2,1)S(1)} collective-permute-done((bf16[64,2048]{1,0:T(8,128)(2,1)S(1)}, bf16[64,2048]{1,0:T(8,128)(2,1)S(1)}, u32[]{:S(2)}, u32[]{:S(2)}) %collective-permute-start.13) | collective-permute-done | bytes 262176 | tf_op jit(solution)/shard_map/ppermute | solution.py:375
  48.2 4.5 %collective-permute-done.16.refs_15_ = bf16[64,2048]{1,0:T(8,128)(2,1)S(1)} collective-permute-done((bf16[64,2048]{1,0:T(8,128)(2,1)S(1)}, bf16[64,2048]{1,0:T(8,128)(2,1)S(1)}, u32[]{:S(2)}, u32[]{:S(2)}) %collective-permute-start.16) | collective-permute-done | bytes 262176 | tf_op jit(solution)/shard_map/ppermute | solution.py:375
  52.8 4.5 %aggregate.3 = (bf16[64,2048]{1,0:T(8,128)(2,1)S(1)}, f32[1,2048]{1,0:T(1,128)}) custom-call(s32[384]{0:T(512)S(1)} %collective-permute-done.18.table.table_pair, bf16[16,12,128,128]{3,2,1,0:T(8,128)(2,1)S(1)} %load.3.tiles.pair, bf16[64,2048]{1,0:T(8,128)(2,1)S(1)} %get-tuple-element.104.refs_0_, bf16[64,2048]{1,0:T(8,128)(2,1)S(1)} %collective-permute-done.refs_1_, ...), custom_call_target="tpu_custom_call" | custom-call | flops 402653184 | bytes 10485760 | tf_op jit(solution)/shard_map/aggregate/pallas_call | solution.py:307
  57.9 3.9 %aggregate.2 = (bf16[64,2048]{1,0:T(8,128)(2,1)S(1)}, f32[1,2048]{1,0:T(1,128)S(1)}) custom-call(s32[384]{0:T(512)S(1)} %table.1, bf16[16,12,128,128]{3,2,1,0:T(8,128)(2,1)S(1)} %load.2.tiles.adj, bf16[64,2048]{1,0:T(8,128)(2,1)S(1)} %get-tuple-element.104.refs_0_, bf16[64,2048]{1,0:T(8,128)(2,1)S(1)} %collective-permute-done.refs_1_, ...), custom_call_target="tpu_custom_call" | custom-call | flops 402653184 | bytes 10485760 | tf_op jit(solution)/shard_map/aggregate/pallas_call | solution.py:307
  65.5 6.2 %collective-permute-done.17.refs_1_ = bf16[64,2048]{1,0:T(8,128)(2,1)S(1)} collective-permute-done((bf16[64,2048]{1,0:T(8,128)(2,1)S(1)}, bf16[64,2048]{1,0:T(8,128)(2,1)S(1)}, u32[]{:S(2)}, u32[]{:S(2)}) %collective-permute-start.17) | collective-permute-done | bytes 262176 | tf_op jit(solution)/shard_map/ppermute | solution.py:58
  71.7 3.0 %middle.1 = (bf16[128,2048]{1,0:T(8,128)(2,1)}, bf16[256,2048]{1,0:T(8,128)(2,1)S(1)}, bf16[128,2048]{1,0:T(8,128)(2,1)S(1)}, bf16[128,2048]{1,0:T(8,128)(2,1)S(1)}) custom-call(bf16[256,256]{1,0:T(8,128)(2,1)S(1)} %get-tuple-element.55.turned, bf16[128,256]{1,0:T(8,128)(2,1)S(1)} %copy-done.3, f32[1,2048]{1,0:T(1,128)S(1)} %get-tuple-element.68.inverse, ...), custom_call_target="tpu_custom_call" | custom-call | flops 402653184 | bytes 7340032 | tf_op jit(solution)/shard_map/middle/pallas_call | solution.py:307
  85.5 3.2 %collective-permute-done.22.arrived = bf16[64,2048]{1,0:T(8,128)(2,1)S(1)} collective-permute-done((bf16[64,2048]{1,0:T(8,128)(2,1)S(1)}, bf16[64,2048]{1,0:T(8,128)(2,1)S(1)}, u32[]{:S(2)}, u32[]{:S(2)}) %collective-permute-start.22) | collective-permute-done | bytes 262176 | tf_op jit(solution)/shard_map/ppermute | solution.py:459
  89.5 2.2 %collective-permute-done.34 = f32[2,136,128]{2,1,0:T(8,128)S(1)} collective-permute-done((f32[2,136,128]{2,1,0:T(8,128)S(1)}, f32[2,136,128]{2,1,0:T(8,128)S(1)}, u32[]{:S(2)}, u32[]{:S(2)}) %collective-permute-start.34) | collective-permute-done | bytes 139296 | tf_op jit(solution)/shard_map/ppermute | solution.py:49
  91.8 2.0 %collective-permute-start.38 = (f32[2,136,128]{2,1,0:T(8,128)S(1)}, f32[2,136,128]{2,1,0:T(8,128)S(1)}, u32[]{:S(2)}, u32[]{:S(2)}) collective-permute-start(f32[2,136,128]{2,1,0:T(8,128)S(1)} %add.24), channel_id=1, source_target_pairs={{0,8},{2,10},{4,12},{6,14},{8,0},{10,2},{12,4},{14,6},{16,24},{18,... | collective-permute-start | bytes 417800 | tf_op jit(solution)/shard_map/ppermute | solution.py:49
  97.6 2.1 %collective-permute-start.27 = (bf16[64,2048]{1,0:T(8,128)(2,1)S(1)}, bf16[64,2048]{1,0:T(8,128)(2,1)S(1)}, u32[]{:S(2)}, u32[]{:S(2)}) collective-permute-start(bf16[64,2048]{1,0:T(8,128)(2,1)S(1)} %join.13), channel_id=1, source_target_pairs={{0,4},{2,6},{8,0},{10,2},{16,8},{18,10},{24,16},{26,18},{28,24},{3... | collective-permute-start | bytes 786440 | tf_op jit(solution)/shard_map/ppermute | solution.py:459
  99.6 3.3 %collective-permute-done.23.arrived = bf16[64,2048]{1,0:T(8,128)(2,1)S(1)} collective-permute-done((bf16[64,2048]{1,0:T(8,128)(2,1)S(1)}, bf16[64,2048]{1,0:T(8,128)(2,1)S(1)}, u32[]{:S(2)}, u32[]{:S(2)}) %collective-permute-start.23) | collective-permute-done | bytes 262176 | tf_op jit(solution)/shard_map/ppermute | solution.py:459
  103.3 2.1 %collective-permute-start.36 = (bf16[64,2048]{1,0:T(8,128)(2,1)S(1)}, bf16[64,2048]{1,0:T(8,128)(2,1)S(1)}, u32[]{:S(2)}, u32[]{:S(2)}) collective-permute-start(bf16[64,2048]{1,0:T(8,128)(2,1)S(1)} %join.18), channel_id=1, source_target_pairs={{0,4},{2,6},{8,0},{10,2},{16,8},{18,10},{24,16},{26,18},{28,24},{3... | collective-permute-start | bytes 786440 | tf_op jit(solution)/shard_map/ppermute | solution.py:459
  105.9 2.3 %spread.4 = (f32[64,2048]{1,0:T(8,128)S(1)}, f32[64,2048]{1,0:T(8,128)S(1)}, f32[64,2048]{1,0:T(8,128)S(1)}, f32[64,2048]{1,0:T(8,128)S(1)}, f32[64,2048]{1,0:T(8,128)S(1)}, /*index=5*/f32[64,2048]{1,0:T(8,128)S(1)}) custom-call(s32[384]{0:T(512)S(1)} %table.1, s32[384]{0:T(512)S(1)} %collective-permute-done.18.table.table_pair, ...), custom_call_target="tpu_custom_call" | custom-call | flops 301989888 | bytes 6291456 | tf_op jit(solution)/shard_map/spread/pallas_call | solution.py:307
  108.6 2.2 %collective-permute-start.31 = (bf16[64,2048]{1,0:T(8,128)(2,1)S(1)}, bf16[64,2048]{1,0:T(8,128)(2,1)S(1)}, u32[]{:S(2)}, u32[]{:S(2)}) collective-permute-start(bf16[64,2048]{1,0:T(8,128)(2,1)S(1)} %join.16), channel_id=1, source_target_pairs={{0,8},{2,10},{8,16},{10,18},{16,24},{18,26},{24,28},{26,30},{28,20... | collective-permute-start | bytes 786440 | tf_op jit(solution)/shard_map/ppermute | solution.py:459
  111.8 2.4 %collective-permute-done.24.arrived = bf16[64,2048]{1,0:T(8,128)(2,1)S(1)} collective-permute-done((bf16[64,2048]{1,0:T(8,128)(2,1)S(1)}, bf16[64,2048]{1,0:T(8,128)(2,1)S(1)}, u32[]{:S(2)}, u32[]{:S(2)}) %collective-permute-start.24) | collective-permute-done | bytes 262176 | tf_op jit(solution)/shard_map/ppermute | solution.py:459
  115.5 2.2 %collective-permute-done.36.arrived = bf16[64,2048]{1,0:T(8,128)(2,1)S(1)} collective-permute-done((bf16[64,2048]{1,0:T(8,128)(2,1)S(1)}, bf16[64,2048]{1,0:T(8,128)(2,1)S(1)}, u32[]{:S(2)}, u32[]{:S(2)}) %collective-permute-start.36) | collective-permute-done | bytes 262176 | tf_op jit(solution)/shard_map/ppermute | solution.py:459
  (106 shorter events, 52.6 us)
Async XLA Ops:
  0.6 17.5 %collective-permute-start.4 = (bf16[16,12,128,128]{3,2,1,0:T(8,128)(2,1)}, bf16[16,12,128,128]{3,2,1,0:T(8,128)(2,1)}, u32[]{:S(2)}, u32[]{:S(2)}) collective-permute-start(bf16[16,12,128,128]{3,2,1,0:T(8,128)(2,1)} %source.1), channel_id=1, source_target_pairs={{0,2},{2,0},{4,6},{6,4},{8,10},{10,8},{12,14},{14,12},{16,18},{18,... | collective-permute-start | bytes 18874376 | tf_op jit(solution)/shard_map/ppermute | solution.py:49
  2.2 11.4 %collective-permute-start = (bf16[64,2048]{1,0:T(8,128)(2,1)S(1)}, bf16[64,2048]{1,0:T(8,128)(2,1)S(1)}, u32[]{:S(2)}, u32[]{:S(2)}) collective-permute-start(bf16[64,2048]{1,0:T(8,128)(2,1)S(1)} %get-tuple-element.104.refs_0_), channel_id=1, source_target_pairs={{0,8},{2,10},{8,16},{10,18},{16,24},{18,26},{24,28},{26,30},{28,20... | collective-permute-start | bytes 786440 | tf_op jit(solution)/shard_map/ppermute | solution.py:371
  4.9 12.3 %collective-permute-start.1 = (bf16[64,2048]{1,0:T(8,128)(2,1)S(1)}, bf16[64,2048]{1,0:T(8,128)(2,1)S(1)}, u32[]{:S(2)}, u32[]{:S(2)}) collective-permute-start(bf16[64,2048]{1,0:T(8,128)(2,1)S(1)} %get-tuple-element.67), channel_id=1, source_target_pairs={{0,10},{2,8},{8,18},{10,16},{16,26},{18,24},{24,30},{26,28},{28,22... | collective-permute-start | bytes 786440 | tf_op jit(solution)/shard_map/ppermute | solution.py:371
  6.4 11.7 %collective-permute-start.3 = (bf16[64,2048]{1,0:T(8,128)(2,1)S(1)}, bf16[64,2048]{1,0:T(8,128)(2,1)S(1)}, u32[]{:S(2)}, u32[]{:S(2)}) collective-permute-start(bf16[64,2048]{1,0:T(8,128)(2,1)S(1)} %get-tuple-element.67), channel_id=1, source_target_pairs={{0,6},{2,4},{8,2},{10,0},{16,10},{18,8},{24,18},{26,16},{28,26},{3... | collective-permute-start | bytes 786440 | tf_op jit(solution)/shard_map/ppermute | solution.py:375
  18.2 45.3 %collective-permute-start.5 = (bf16[128,4736]{1,0:T(8,128)(2,1)S(1)}, bf16[128,4736]{1,0:T(8,128)(2,1)S(1)}, u32[]{:S(2)}, u32[]{:S(2)}) collective-permute-start(bf16[128,4736]{1,0:T(8,128)(2,1)S(1)} %pack.1.refs_0_), channel_id=1, source_target_pairs={{0,1},{1,0},{2,3},{3,2},{4,5},{5,4},{6,7},{7,6},{8,9},{9,8},{10,11... | collective-permute-start | bytes 3637256 | tf_op jit(solution)/shard_map/ppermute | solution.py:58
  21.7 12.7 %collective-permute-start.9 = (bf16[64,2048]{1,0:T(8,128)(2,1)S(1)}, bf16[64,2048]{1,0:T(8,128)(2,1)S(1)}, u32[]{:S(2)}, u32[]{:S(2)}) collective-permute-start(bf16[64,2048]{1,0:T(8,128)(2,1)S(1)} %collective-permute-done.3.refs_4_), channel_id=1, source_target_pairs={{0,4},{2,6},{8,0},{10,2},{16,8},{18,10},{24,16},{26,18},{28,24},{3... | collective-permute-start | bytes 786440 | tf_op jit(solution)/shard_map/ppermute | solution.py:375
  22.2 12.8 %collective-permute-start.8 = (bf16[64,2048]{1,0:T(8,128)(2,1)S(1)}, bf16[64,2048]{1,0:T(8,128)(2,1)S(1)}, u32[]{:S(2)}, u32[]{:S(2)}) collective-permute-start(bf16[64,2048]{1,0:T(8,128)(2,1)S(1)} %collective-permute-done.1.refs_3_), channel_id=1, source_target_pairs={{0,8},{2,10},{8,16},{10,18},{16,24},{18,26},{24,28},{26,30},{28,20... | collective-permute-start | bytes 786440 | tf_op jit(solution)/shard_map/ppermute | solution.py:371
  28.8 11.2 %collective-permute-start.11 = (bf16[64,2048]{1,0:T(8,128)(2,1)S(1)}, bf16[64,2048]{1,0:T(8,128)(2,1)S(1)}, u32[]{:S(2)}, u32[]{:S(2)}) collective-permute-start(bf16[64,2048]{1,0:T(8,128)(2,1)S(1)} %collective-permute-done.7.refs_6_), channel_id=1, source_target_pairs={{0,4},{2,6},{8,0},{10,2},{16,8},{18,10},{24,16},{26,18},{28,24},{3... | collective-permute-start | bytes 786440 | tf_op jit(solution)/shard_map/ppermute | solution.py:375
  29.4 11.2 %collective-permute-start.10 = (bf16[64,2048]{1,0:T(8,128)(2,1)S(1)}, bf16[64,2048]{1,0:T(8,128)(2,1)S(1)}, u32[]{:S(2)}, u32[]{:S(2)}) collective-permute-start(bf16[64,2048]{1,0:T(8,128)(2,1)S(1)} %collective-permute-done.6.refs_5_), channel_id=1, source_target_pairs={{0,8},{2,10},{8,16},{10,18},{16,24},{18,26},{24,28},{26,30},{28,20... | collective-permute-start | bytes 786440 | tf_op jit(solution)/shard_map/ppermute | solution.py:371
  35.0 12.1 %collective-permute-start.12 = (bf16[64,2048]{1,0:T(8,128)(2,1)S(1)}, bf16[64,2048]{1,0:T(8,128)(2,1)S(1)}, u32[]{:S(2)}, u32[]{:S(2)}) collective-permute-start(bf16[64,2048]{1,0:T(8,128)(2,1)S(1)} %collective-permute-done.8.refs_7_), channel_id=1, source_target_pairs={{0,8},{2,10},{8,16},{10,18},{16,24},{18,26},{24,28},{26,30},{28,20... | collective-permute-start | bytes 786440 | tf_op jit(solution)/shard_map/ppermute | solution.py:371
  78.1 11.4 %collective-permute-start.32 = (bf16[64,2048]{1,0:T(8,128)(2,1)S(1)}, bf16[64,2048]{1,0:T(8,128)(2,1)S(1)}, u32[]{:S(2)}, u32[]{:S(2)}) collective-permute-start(bf16[64,2048]{1,0:T(8,128)(2,1)S(1)} %get-tuple-element.91), channel_id=1, source_target_pairs={{0,4},{2,6},{8,0},{10,2},{16,8},{18,10},{24,16},{26,18},{28,24},{3... | collective-permute-start | bytes 786440 | tf_op jit(solution)/shard_map/ppermute | solution.py:459
  80.2 11.5 %collective-permute-start.34 = (f32[2,136,128]{2,1,0:T(8,128)S(1)}, f32[2,136,128]{2,1,0:T(8,128)S(1)}, u32[]{:S(2)}, u32[]{:S(2)}) collective-permute-start(f32[2,136,128]{2,1,0:T(8,128)S(1)} %slice_add_fusion), channel_id=1, source_target_pairs={{0,4},{2,6},{4,0},{6,2},{8,12},{10,14},{12,8},{14,10},{16,20},{18,... | collective-permute-start | bytes 417800 | tf_op jit(solution)/shard_map/ppermute | solution.py:49
  83.5 13.9 %collective-permute-start.29 = (bf16[64,2048]{1,0:T(8,128)(2,1)S(1)}, bf16[64,2048]{1,0:T(8,128)(2,1)S(1)}, u32[]{:S(2)}, u32[]{:S(2)}) collective-permute-start(bf16[64,2048]{1,0:T(8,128)(2,1)S(1)} %get-tuple-element.88), channel_id=1, source_target_pairs={{0,8},{2,10},{8,16},{10,18},{16,24},{18,26},{24,28},{26,30},{28,20... | collective-permute-start | bytes 786440 | tf_op jit(solution)/shard_map/ppermute | solution.py:459
  85.1 12.4 %collective-permute-start.26 = (bf16[64,2048]{1,0:T(8,128)(2,1)S(1)}, bf16[64,2048]{1,0:T(8,128)(2,1)S(1)}, u32[]{:S(2)}, u32[]{:S(2)}) collective-permute-start(bf16[64,2048]{1,0:T(8,128)(2,1)S(1)} %get-tuple-element.85), channel_id=1, source_target_pairs={{0,4},{2,6},{8,0},{10,2},{16,8},{18,10},{24,16},{26,18},{28,24},{3... | collective-permute-start | bytes 786440 | tf_op jit(solution)/shard_map/ppermute | solution.py:459
  88.8 14.2 %collective-permute-start.23 = (bf16[64,2048]{1,0:T(8,128)(2,1)S(1)}, bf16[64,2048]{1,0:T(8,128)(2,1)S(1)}, u32[]{:S(2)}, u32[]{:S(2)}) collective-permute-start(bf16[64,2048]{1,0:T(8,128)(2,1)S(1)} %join.10), channel_id=1, source_target_pairs={{0,8},{2,10},{8,16},{10,18},{16,24},{18,26},{24,28},{26,30},{28,20... | collective-permute-start | bytes 786440 | tf_op jit(solution)/shard_map/ppermute | solution.py:459
  91.7 11.5 %collective-permute-start.35 = (bf16[64,2048]{1,0:T(8,128)(2,1)S(1)}, bf16[64,2048]{1,0:T(8,128)(2,1)S(1)}, u32[]{:S(2)}, u32[]{:S(2)}) collective-permute-start(bf16[64,2048]{1,0:T(8,128)(2,1)S(1)} %join.17), channel_id=1, source_target_pairs={{0,4},{2,6},{8,0},{10,2},{16,8},{18,10},{24,16},{26,18},{28,24},{3... | collective-permute-start | bytes 786440 | tf_op jit(solution)/shard_map/ppermute | solution.py:459
  91.8 13.6 %collective-permute-start.38 = (f32[2,136,128]{2,1,0:T(8,128)S(1)}, f32[2,136,128]{2,1,0:T(8,128)S(1)}, u32[]{:S(2)}, u32[]{:S(2)}) collective-permute-start(f32[2,136,128]{2,1,0:T(8,128)S(1)} %add.24), channel_id=1, source_target_pairs={{0,8},{2,10},{4,12},{6,14},{8,0},{10,2},{12,4},{14,6},{16,24},{18,... | collective-permute-start | bytes 417800 | tf_op jit(solution)/shard_map/ppermute | solution.py:49
  97.4 11.2 %collective-permute-start.30 = (bf16[64,2048]{1,0:T(8,128)(2,1)S(1)}, bf16[64,2048]{1,0:T(8,128)(2,1)S(1)}, u32[]{:S(2)}, u32[]{:S(2)}) collective-permute-start(bf16[64,2048]{1,0:T(8,128)(2,1)S(1)} %join.15), channel_id=1, source_target_pairs={{0,8},{2,10},{8,16},{10,18},{16,24},{18,26},{24,28},{26,30},{28,20... | collective-permute-start | bytes 786440 | tf_op jit(solution)/shard_map/ppermute | solution.py:459
  97.6 13.5 %collective-permute-start.27 = (bf16[64,2048]{1,0:T(8,128)(2,1)S(1)}, bf16[64,2048]{1,0:T(8,128)(2,1)S(1)}, u32[]{:S(2)}, u32[]{:S(2)}) collective-permute-start(bf16[64,2048]{1,0:T(8,128)(2,1)S(1)} %join.13), channel_id=1, source_target_pairs={{0,4},{2,6},{8,0},{10,2},{16,8},{18,10},{24,16},{26,18},{28,24},{3... | collective-permute-start | bytes 786440 | tf_op jit(solution)/shard_map/ppermute | solution.py:459
  103.0 11.2 %collective-permute-start.24 = (bf16[64,2048]{1,0:T(8,128)(2,1)S(1)}, bf16[64,2048]{1,0:T(8,128)(2,1)S(1)}, u32[]{:S(2)}, u32[]{:S(2)}) collective-permute-start(bf16[64,2048]{1,0:T(8,128)(2,1)S(1)} %join.11), channel_id=1, source_target_pairs={{0,8},{2,10},{8,16},{10,18},{16,24},{18,26},{24,28},{26,30},{28,20... | collective-permute-start | bytes 786440 | tf_op jit(solution)/shard_map/ppermute | solution.py:459
  103.3 14.4 %collective-permute-start.36 = (bf16[64,2048]{1,0:T(8,128)(2,1)S(1)}, bf16[64,2048]{1,0:T(8,128)(2,1)S(1)}, u32[]{:S(2)}, u32[]{:S(2)}) collective-permute-start(bf16[64,2048]{1,0:T(8,128)(2,1)S(1)} %join.18), channel_id=1, source_target_pairs={{0,4},{2,6},{8,0},{10,2},{16,8},{18,10},{24,16},{26,18},{28,24},{3... | collective-permute-start | bytes 786440 | tf_op jit(solution)/shard_map/ppermute | solution.py:459
  105.4 14.8 %collective-permute-start.39 = (f32[2,136,128]{2,1,0:T(8,128)S(1)}, f32[2,136,128]{2,1,0:T(8,128)S(1)}, u32[]{:S(2)}, u32[]{:S(2)}) collective-permute-start(f32[2,136,128]{2,1,0:T(8,128)S(1)} %add.25), channel_id=1, source_target_pairs={{0,16},{2,18},{4,20},{6,22},{8,24},{10,26},{12,28},{14,30},{16,0},... | collective-permute-start | bytes 417800 | tf_op jit(solution)/shard_map/ppermute | solution.py:49
  108.6 15.4 %collective-permute-start.31 = (bf16[64,2048]{1,0:T(8,128)(2,1)S(1)}, bf16[64,2048]{1,0:T(8,128)(2,1)S(1)}, u32[]{:S(2)}, u32[]{:S(2)}) collective-permute-start(bf16[64,2048]{1,0:T(8,128)(2,1)S(1)} %join.16), channel_id=1, source_target_pairs={{0,8},{2,10},{8,16},{10,18},{16,24},{18,26},{24,28},{26,30},{28,20... | collective-permute-start | bytes 786440 | tf_op jit(solution)/shard_map/ppermute | solution.py:459
  111.7 12.3 %collective-permute-start.28 = (bf16[64,2048]{1,0:T(8,128)(2,1)}, bf16[64,2048]{1,0:T(8,128)(2,1)S(1)}, u32[]{:S(2)}, u32[]{:S(2)}) collective-permute-start(bf16[64,2048]{1,0:T(8,128)(2,1)} %join.14), channel_id=1, source_target_pairs={{0,4},{2,6},{8,0},{10,2},{16,8},{18,10},{24,16},{26,18},{28,24},{3... | collective-permute-start | bytes 786440 | tf_op jit(solution)/shard_map/ppermute | solution.py:459
  (24 other events, 150.0 us)

commit v14 on v13

--- a/solution.py
+++ b/solution.py
@@ -187,7 +187,7 @@
         inverse[:, lane] = factor
         return carry
 
-    lax.fori_loop(0, blocks, step, 0, unroll=4)
+    lax.fori_loop(0, blocks, step, 0, unroll=8)
 
 
 def middle_kernel(feats, turned, wn, inverse, base, cot, *refs):
@@ -435,7 +435,7 @@
         if arrived is None:
             return mine
         (out,) = call(
-            join_kernel, "join", [((half, width), narrow)], [VMEM] * 2, [VMEM], [], 3,
+            join_kernel, "join", [((half, width), narrow)], [VMEM] * 2, [VMEM], [], 2,
             0, 4 * hid * width, arrived, mine,
         )
         return out

time: 128 us -> 128 us (level)
  waiting for transfers between devices: 52.6 us -> 53.9 us
where the time goes in v14:
time: 128 us
  waiting for transfers between devices  53.9 us (42%)
  starting transfers between devices  36.2 us (28%)
  Pallas kernels  32 us (25%)
  local copies, waits for them, and re-layouts  4.64 us (4%)
    pallas_call x26, Pallas kernels, call(): pl.pallas_call(kernel, out_shape=[jax.ShapeDtypeStruct(shape, kind) for s...  32 us
    ppermute x7, waiting for transfers between devices, shards(): down[side] = lax.ppermute(down[side], 'rows', backward)  19.7 us
    ppermute x14, waiting for transfers between devices, ring(): return lax.ppermute(value, 'rows', pairs)  17.2 us
    ppermute x14, starting transfers between devices, ring(): return lax.ppermute(value, 'rows', pairs)  13.2 us
    ppermute x7, starting transfers between devices, shards(): up[side] = lax.ppermute(up[side], 'rows', forward)  11.8 us
    ppermute x4, waiting for transfers between devices, send(): return lax.ppermute(value, ('rows', 'feat'), pairs)  7.68 us
    ppermute x9, waiting for transfers between devices, swap(): return lax.ppermute(value, 'rows', [(r, r ^ bit) for r in range(rows)])  5.48 us
    ppermute x9, starting transfers between devices, swap(): return lax.ppermute(value, 'rows', [(r, r ^ bit) for r in range(rows)])  4.65 us
  transfers between devices with their start and end apart: 41, of which 25 were waited for; matrix products, arithmetic and copies ran while one was open for 1% of the time, Pallas kernels for 22%

profile of v14, /device:TPU:0, one launch (start us, length us, event | category | flops | bytes accessed | tf_op | source)
XLA Modules:
  0.0 127.7 jit_solution(16987268371981817843)
XLA Ops:
  2.2 2.7 %collective-permute-start = (bf16[64,2048]{1,0:T(8,128)(2,1)S(1)}, bf16[64,2048]{1,0:T(8,128)(2,1)S(1)}, u32[]{:S(2)}, u32[]{:S(2)}) collective-permute-start(bf16[64,2048]{1,0:T(8,128)(2,1)S(1)} %get-tuple-element.104.refs_0_), channel_id=1, source_target_pairs={{0,8},{2,10},{8,16},{10,18},{16,24},{18,26},{24,28},{26,30},{28,20... | collective-permute-start | bytes 786440 | tf_op jit(solution)/shard_map/ppermute | solution.py:371
  6.6 2.8 %copy-done = bf16[16,12,128,128]{3,2,1,0:T(8,128)(2,1)S(1)} copy-done((bf16[16,12,128,128]{3,2,1,0:T(8,128)(2,1)S(1)}, bf16[16,12,128,128]{3,2,1,0:T(8,128)(2,1)}, u32[]{:S(2)}) %copy-start) | copy-done | bytes 6291480
  10.1 3.2 %table.1 = s32[384]{0:T(512)S(1)} custom-call(s32[16,12]{1,0:T(8,128)S(1)} %copy-done.5), custom_call_target="tpu_custom_call" | custom-call | bytes 1536 | tf_op jit(solution)/shard_map/table/pallas_call | solution.py:307
  14.0 3.1 %collective-permute-done.1.refs_3_ = bf16[64,2048]{1,0:T(8,128)(2,1)S(1)} collective-permute-done((bf16[64,2048]{1,0:T(8,128)(2,1)S(1)}, bf16[64,2048]{1,0:T(8,128)(2,1)S(1)}, u32[]{:S(2)}, u32[]{:S(2)}) %collective-permute-start.1) | collective-permute-done | bytes 262176 | tf_op jit(solution)/shard_map/ppermute | solution.py:371
  23.7 2.8 %load.3.tiles.pair = bf16[16,12,128,128]{3,2,1,0:T(8,128)(2,1)S(1)} custom-call(bf16[16,12,128,128]{3,2,1,0:T(8,128)(2,1)} %collective-permute-done.4.source), custom_call_target="tpu_custom_call" | custom-call | bytes 12582912 | tf_op jit(solution)/shard_map/load/pallas_call | solution.py:307
  26.5 2.3 %collective-permute-done.7.refs_6_ = bf16[64,2048]{1,0:T(8,128)(2,1)S(1)} collective-permute-done((bf16[64,2048]{1,0:T(8,128)(2,1)S(1)}, bf16[64,2048]{1,0:T(8,128)(2,1)S(1)}, u32[]{:S(2)}, u32[]{:S(2)}) %collective-permute-start.7) | collective-permute-done | bytes 262176 | tf_op jit(solution)/shard_map/ppermute | solution.py:375
  30.9 3.5 %collective-permute-done.9.refs_8_ = bf16[64,2048]{1,0:T(8,128)(2,1)S(1)} collective-permute-done((bf16[64,2048]{1,0:T(8,128)(2,1)S(1)}, bf16[64,2048]{1,0:T(8,128)(2,1)S(1)}, u32[]{:S(2)}, u32[]{:S(2)}) %collective-permute-start.9) | collective-permute-done | bytes 262176 | tf_op jit(solution)/shard_map/ppermute | solution.py:375
  36.5 3.5 %collective-permute-done.11.refs_10_ = bf16[64,2048]{1,0:T(8,128)(2,1)S(1)} collective-permute-done((bf16[64,2048]{1,0:T(8,128)(2,1)S(1)}, bf16[64,2048]{1,0:T(8,128)(2,1)S(1)}, u32[]{:S(2)}, u32[]{:S(2)}) %collective-permute-start.11) | collective-permute-done | bytes 262176 | tf_op jit(solution)/shard_map/ppermute | solution.py:375
  40.6 4.4 %collective-permute-done.13.refs_12_ = bf16[64,2048]{1,0:T(8,128)(2,1)S(1)} collective-permute-done((bf16[64,2048]{1,0:T(8,128)(2,1)S(1)}, bf16[64,2048]{1,0:T(8,128)(2,1)S(1)}, u32[]{:S(2)}, u32[]{:S(2)}) %collective-permute-start.13) | collective-permute-done | bytes 262176 | tf_op jit(solution)/shard_map/ppermute | solution.py:375
  48.2 4.5 %collective-permute-done.16.refs_15_ = bf16[64,2048]{1,0:T(8,128)(2,1)S(1)} collective-permute-done((bf16[64,2048]{1,0:T(8,128)(2,1)S(1)}, bf16[64,2048]{1,0:T(8,128)(2,1)S(1)}, u32[]{:S(2)}, u32[]{:S(2)}) %collective-permute-start.16) | collective-permute-done | bytes 262176 | tf_op jit(solution)/shard_map/ppermute | solution.py:375
  52.8 4.1 %aggregate.3 = (bf16[64,2048]{1,0:T(8,128)(2,1)S(1)}, f32[1,2048]{1,0:T(1,128)}) custom-call(s32[384]{0:T(512)S(1)} %collective-permute-done.18.table.table_pair, bf16[16,12,128,128]{3,2,1,0:T(8,128)(2,1)S(1)} %load.3.tiles.pair, bf16[64,2048]{1,0:T(8,128)(2,1)S(1)} %get-tuple-element.104.refs_0_, bf16[64,2048]{1,0:T(8,128)(2,1)S(1)} %collective-permute-done.refs_1_, ...), custom_call_target="tpu_custom_call" | custom-call | flops 402653184 | bytes 10485760 | tf_op jit(solution)/shard_map/aggregate/pallas_call | solution.py:307
  57.6 3.5 %aggregate.2 = (bf16[64,2048]{1,0:T(8,128)(2,1)S(1)}, f32[1,2048]{1,0:T(1,128)S(1)}) custom-call(s32[384]{0:T(512)S(1)} %table.1, bf16[16,12,128,128]{3,2,1,0:T(8,128)(2,1)S(1)} %load.2.tiles.adj, bf16[64,2048]{1,0:T(8,128)(2,1)S(1)} %get-tuple-element.104.refs_0_, bf16[64,2048]{1,0:T(8,128)(2,1)S(1)} %collective-permute-done.refs_1_, ...), custom_call_target="tpu_custom_call" | custom-call | flops 402653184 | bytes 10485760 | tf_op jit(solution)/shard_map/aggregate/pallas_call | solution.py:307
  65.1 6.2 %collective-permute-done.17.refs_1_ = bf16[64,2048]{1,0:T(8,128)(2,1)S(1)} collective-permute-done((bf16[64,2048]{1,0:T(8,128)(2,1)S(1)}, bf16[64,2048]{1,0:T(8,128)(2,1)S(1)}, u32[]{:S(2)}, u32[]{:S(2)}) %collective-permute-start.17) | collective-permute-done | bytes 262176 | tf_op jit(solution)/shard_map/ppermute | solution.py:58
  71.3 3.0 %middle.1 = (bf16[128,2048]{1,0:T(8,128)(2,1)}, bf16[256,2048]{1,0:T(8,128)(2,1)S(1)}, bf16[128,2048]{1,0:T(8,128)(2,1)S(1)}, bf16[128,2048]{1,0:T(8,128)(2,1)S(1)}) custom-call(bf16[256,256]{1,0:T(8,128)(2,1)S(1)} %get-tuple-element.55.turned, bf16[128,256]{1,0:T(8,128)(2,1)S(1)} %copy-done.3, f32[1,2048]{1,0:T(1,128)S(1)} %get-tuple-element.68.inverse, ...), custom_call_target="tpu_custom_call" | custom-call | flops 402653184 | bytes 7340032 | tf_op jit(solution)/shard_map/middle/pallas_call | solution.py:307
  85.2 3.2 %collective-permute-done.22.arrived = bf16[64,2048]{1,0:T(8,128)(2,1)S(1)} collective-permute-done((bf16[64,2048]{1,0:T(8,128)(2,1)S(1)}, bf16[64,2048]{1,0:T(8,128)(2,1)S(1)}, u32[]{:S(2)}, u32[]{:S(2)}) %collective-permute-start.22) | collective-permute-done | bytes 262176 | tf_op jit(solution)/shard_map/ppermute | solution.py:459
  89.2 2.2 %collective-permute-done.34 = f32[2,136,128]{2,1,0:T(8,128)S(1)} collective-permute-done((f32[2,136,128]{2,1,0:T(8,128)S(1)}, f32[2,136,128]{2,1,0:T(8,128)S(1)}, u32[]{:S(2)}, u32[]{:S(2)}) %collective-permute-start.34) | collective-permute-done | bytes 139296 | tf_op jit(solution)/shard_map/ppermute | solution.py:49
  91.7 2.0 %collective-permute-start.38 = (f32[2,136,128]{2,1,0:T(8,128)S(1)}, f32[2,136,128]{2,1,0:T(8,128)S(1)}, u32[]{:S(2)}, u32[]{:S(2)}) collective-permute-start(f32[2,136,128]{2,1,0:T(8,128)S(1)} %add.24), channel_id=1, source_target_pairs={{0,8},{2,10},{4,12},{6,14},{8,0},{10,2},{12,4},{14,6},{16,24},{18,... | collective-permute-start | bytes 417800 | tf_op jit(solution)/shard_map/ppermute | solution.py:49
  97.2 2.1 %collective-permute-start.27 = (bf16[64,2048]{1,0:T(8,128)(2,1)S(1)}, bf16[64,2048]{1,0:T(8,128)(2,1)S(1)}, u32[]{:S(2)}, u32[]{:S(2)}) collective-permute-start(bf16[64,2048]{1,0:T(8,128)(2,1)S(1)} %join.13), channel_id=1, source_target_pairs={{0,4},{2,6},{8,0},{10,2},{16,8},{18,10},{24,16},{26,18},{28,24},{3... | collective-permute-start | bytes 786440 | tf_op jit(solution)/shard_map/ppermute | solution.py:459
  99.3 3.3 %collective-permute-done.23.arrived = bf16[64,2048]{1,0:T(8,128)(2,1)S(1)} collective-permute-done((bf16[64,2048]{1,0:T(8,128)(2,1)S(1)}, bf16[64,2048]{1,0:T(8,128)(2,1)S(1)}, u32[]{:S(2)}, u32[]{:S(2)}) %collective-permute-start.23) | collective-permute-done | bytes 262176 | tf_op jit(solution)/shard_map/ppermute | solution.py:459
  102.8 2.1 %collective-permute-start.36 = (bf16[64,2048]{1,0:T(8,128)(2,1)S(1)}, bf16[64,2048]{1,0:T(8,128)(2,1)S(1)}, u32[]{:S(2)}, u32[]{:S(2)}) collective-permute-start(bf16[64,2048]{1,0:T(8,128)(2,1)S(1)} %join.18), channel_id=1, source_target_pairs={{0,4},{2,6},{8,0},{10,2},{16,8},{18,10},{24,16},{26,18},{28,24},{3... | collective-permute-start | bytes 786440 | tf_op jit(solution)/shard_map/ppermute | solution.py:459
  105.4 2.3 %spread.4 = (f32[64,2048]{1,0:T(8,128)S(1)}, f32[64,2048]{1,0:T(8,128)S(1)}, f32[64,2048]{1,0:T(8,128)S(1)}, f32[64,2048]{1,0:T(8,128)S(1)}, f32[64,2048]{1,0:T(8,128)S(1)}, /*index=5*/f32[64,2048]{1,0:T(8,128)S(1)}) custom-call(s32[384]{0:T(512)S(1)} %table.1, s32[384]{0:T(512)S(1)} %collective-permute-done.18.table.table_pair, ...), custom_call_target="tpu_custom_call" | custom-call | flops 301989888 | bytes 6291456 | tf_op jit(solution)/shard_map/spread/pallas_call | solution.py:307
  108.3 2.0 %collective-permute-start.31 = (bf16[64,2048]{1,0:T(8,128)(2,1)S(1)}, bf16[64,2048]{1,0:T(8,128)(2,1)S(1)}, u32[]{:S(2)}, u32[]{:S(2)}) collective-permute-start(bf16[64,2048]{1,0:T(8,128)(2,1)S(1)} %join.16), channel_id=1, source_target_pairs={{0,8},{2,10},{8,16},{10,18},{16,24},{18,26},{24,28},{26,30},{28,20... | collective-permute-start | bytes 786440 | tf_op jit(solution)/shard_map/ppermute | solution.py:459
  111.7 2.1 %collective-permute-done.24.arrived = bf16[64,2048]{1,0:T(8,128)(2,1)S(1)} collective-permute-done((bf16[64,2048]{1,0:T(8,128)(2,1)S(1)}, bf16[64,2048]{1,0:T(8,128)(2,1)S(1)}, u32[]{:S(2)}, u32[]{:S(2)}) %collective-permute-start.24) | collective-permute-done | bytes 262176 | tf_op jit(solution)/shard_map/ppermute | solution.py:459
  115.2 2.7 %collective-permute-done.36.arrived = bf16[64,2048]{1,0:T(8,128)(2,1)S(1)} collective-permute-done((bf16[64,2048]{1,0:T(8,128)(2,1)S(1)}, bf16[64,2048]{1,0:T(8,128)(2,1)S(1)}, u32[]{:S(2)}, u32[]{:S(2)}) %collective-permute-start.36) | collective-permute-done | bytes 262176 | tf_op jit(solution)/shard_map/ppermute | solution.py:459
  (106 shorter events, 53.1 us)
Async XLA Ops:
  0.6 17.5 %collective-permute-start.4 = (bf16[16,12,128,128]{3,2,1,0:T(8,128)(2,1)}, bf16[16,12,128,128]{3,2,1,0:T(8,128)(2,1)}, u32[]{:S(2)}, u32[]{:S(2)}) collective-permute-start(bf16[16,12,128,128]{3,2,1,0:T(8,128)(2,1)} %source.1), channel_id=1, source_target_pairs={{0,2},{2,0},{4,6},{6,4},{8,10},{10,8},{12,14},{14,12},{16,18},{18,... | collective-permute-start | bytes 18874376 | tf_op jit(solution)/shard_map/ppermute | solution.py:49
  2.2 11.4 %collective-permute-start = (bf16[64,2048]{1,0:T(8,128)(2,1)S(1)}, bf16[64,2048]{1,0:T(8,128)(2,1)S(1)}, u32[]{:S(2)}, u32[]{:S(2)}) collective-permute-start(bf16[64,2048]{1,0:T(8,128)(2,1)S(1)} %get-tuple-element.104.refs_0_), channel_id=1, source_target_pairs={{0,8},{2,10},{8,16},{10,18},{16,24},{18,26},{24,28},{26,30},{28,20... | collective-permute-start | bytes 786440 | tf_op jit(solution)/shard_map/ppermute | solution.py:371
  4.9 12.3 %collective-permute-start.1 = (bf16[64,2048]{1,0:T(8,128)(2,1)S(1)}, bf16[64,2048]{1,0:T(8,128)(2,1)S(1)}, u32[]{:S(2)}, u32[]{:S(2)}) collective-permute-start(bf16[64,2048]{1,0:T(8,128)(2,1)S(1)} %get-tuple-element.67), channel_id=1, source_target_pairs={{0,10},{2,8},{8,18},{10,16},{16,26},{18,24},{24,30},{26,28},{28,22... | collective-permute-start | bytes 786440 | tf_op jit(solution)/shard_map/ppermute | solution.py:371
  6.4 11.7 %collective-permute-start.3 = (bf16[64,2048]{1,0:T(8,128)(2,1)S(1)}, bf16[64,2048]{1,0:T(8,128)(2,1)S(1)}, u32[]{:S(2)}, u32[]{:S(2)}) collective-permute-start(bf16[64,2048]{1,0:T(8,128)(2,1)S(1)} %get-tuple-element.67), channel_id=1, source_target_pairs={{0,6},{2,4},{8,2},{10,0},{16,10},{18,8},{24,18},{26,16},{28,26},{3... | collective-permute-start | bytes 786440 | tf_op jit(solution)/shard_map/ppermute | solution.py:375
  18.2 44.6 %collective-permute-start.5 = (bf16[128,4736]{1,0:T(8,128)(2,1)S(1)}, bf16[128,4736]{1,0:T(8,128)(2,1)S(1)}, u32[]{:S(2)}, u32[]{:S(2)}) collective-permute-start(bf16[128,4736]{1,0:T(8,128)(2,1)S(1)} %pack.1.refs_0_), channel_id=1, source_target_pairs={{0,1},{1,0},{2,3},{3,2},{4,5},{5,4},{6,7},{7,6},{8,9},{9,8},{10,11... | collective-permute-start | bytes 3637256 | tf_op jit(solution)/shard_map/ppermute | solution.py:58
  21.7 12.7 %collective-permute-start.9 = (bf16[64,2048]{1,0:T(8,128)(2,1)S(1)}, bf16[64,2048]{1,0:T(8,128)(2,1)S(1)}, u32[]{:S(2)}, u32[]{:S(2)}) collective-permute-start(bf16[64,2048]{1,0:T(8,128)(2,1)S(1)} %collective-permute-done.3.refs_4_), channel_id=1, source_target_pairs={{0,4},{2,6},{8,0},{10,2},{16,8},{18,10},{24,16},{26,18},{28,24},{3... | collective-permute-start | bytes 786440 | tf_op jit(solution)/shard_map/ppermute | solution.py:375
  22.2 12.8 %collective-permute-start.8 = (bf16[64,2048]{1,0:T(8,128)(2,1)S(1)}, bf16[64,2048]{1,0:T(8,128)(2,1)S(1)}, u32[]{:S(2)}, u32[]{:S(2)}) collective-permute-start(bf16[64,2048]{1,0:T(8,128)(2,1)S(1)} %collective-permute-done.1.refs_3_), channel_id=1, source_target_pairs={{0,8},{2,10},{8,16},{10,18},{16,24},{18,26},{24,28},{26,30},{28,20... | collective-permute-start | bytes 786440 | tf_op jit(solution)/shard_map/ppermute | solution.py:371
  28.8 11.2 %collective-permute-start.11 = (bf16[64,2048]{1,0:T(8,128)(2,1)S(1)}, bf16[64,2048]{1,0:T(8,128)(2,1)S(1)}, u32[]{:S(2)}, u32[]{:S(2)}) collective-permute-start(bf16[64,2048]{1,0:T(8,128)(2,1)S(1)} %collective-permute-done.7.refs_6_), channel_id=1, source_target_pairs={{0,4},{2,6},{8,0},{10,2},{16,8},{18,10},{24,16},{26,18},{28,24},{3... | collective-permute-start | bytes 786440 | tf_op jit(solution)/shard_map/ppermute | solution.py:375
  29.4 11.2 %collective-permute-start.10 = (bf16[64,2048]{1,0:T(8,128)(2,1)S(1)}, bf16[64,2048]{1,0:T(8,128)(2,1)S(1)}, u32[]{:S(2)}, u32[]{:S(2)}) collective-permute-start(bf16[64,2048]{1,0:T(8,128)(2,1)S(1)} %collective-permute-done.6.refs_5_), channel_id=1, source_target_pairs={{0,8},{2,10},{8,16},{10,18},{16,24},{18,26},{24,28},{26,30},{28,20... | collective-permute-start | bytes 786440 | tf_op jit(solution)/shard_map/ppermute | solution.py:371
  35.0 12.1 %collective-permute-start.12 = (bf16[64,2048]{1,0:T(8,128)(2,1)S(1)}, bf16[64,2048]{1,0:T(8,128)(2,1)S(1)}, u32[]{:S(2)}, u32[]{:S(2)}) collective-permute-start(bf16[64,2048]{1,0:T(8,128)(2,1)S(1)} %collective-permute-done.8.refs_7_), channel_id=1, source_target_pairs={{0,8},{2,10},{8,16},{10,18},{16,24},{18,26},{24,28},{26,30},{28,20... | collective-permute-start | bytes 786440 | tf_op jit(solution)/shard_map/ppermute | solution.py:371
  77.8 11.4 %collective-permute-start.32 = (bf16[64,2048]{1,0:T(8,128)(2,1)S(1)}, bf16[64,2048]{1,0:T(8,128)(2,1)S(1)}, u32[]{:S(2)}, u32[]{:S(2)}) collective-permute-start(bf16[64,2048]{1,0:T(8,128)(2,1)S(1)} %get-tuple-element.91), channel_id=1, source_target_pairs={{0,4},{2,6},{8,0},{10,2},{16,8},{18,10},{24,16},{26,18},{28,24},{3... | collective-permute-start | bytes 786440 | tf_op jit(solution)/shard_map/ppermute | solution.py:459
  79.9 11.5 %collective-permute-start.34 = (f32[2,136,128]{2,1,0:T(8,128)S(1)}, f32[2,136,128]{2,1,0:T(8,128)S(1)}, u32[]{:S(2)}, u32[]{:S(2)}) collective-permute-start(f32[2,136,128]{2,1,0:T(8,128)S(1)} %slice_add_fusion), channel_id=1, source_target_pairs={{0,4},{2,6},{4,0},{6,2},{8,12},{10,14},{12,8},{14,10},{16,20},{18,... | collective-permute-start | bytes 417800 | tf_op jit(solution)/shard_map/ppermute | solution.py:49
  83.1 13.9 %collective-permute-start.29 = (bf16[64,2048]{1,0:T(8,128)(2,1)S(1)}, bf16[64,2048]{1,0:T(8,128)(2,1)S(1)}, u32[]{:S(2)}, u32[]{:S(2)}) collective-permute-start(bf16[64,2048]{1,0:T(8,128)(2,1)S(1)} %get-tuple-element.88), channel_id=1, source_target_pairs={{0,8},{2,10},{8,16},{10,18},{16,24},{18,26},{24,28},{26,30},{28,20... | collective-permute-start | bytes 786440 | tf_op jit(solution)/shard_map/ppermute | solution.py:459
  84.7 12.4 %collective-permute-start.26 = (bf16[64,2048]{1,0:T(8,128)(2,1)S(1)}, bf16[64,2048]{1,0:T(8,128)(2,1)S(1)}, u32[]{:S(2)}, u32[]{:S(2)}) collective-permute-start(bf16[64,2048]{1,0:T(8,128)(2,1)S(1)} %get-tuple-element.85), channel_id=1, source_target_pairs={{0,4},{2,6},{8,0},{10,2},{16,8},{18,10},{24,16},{26,18},{28,24},{3... | collective-permute-start | bytes 786440 | tf_op jit(solution)/shard_map/ppermute | solution.py:459
  88.5 14.2 %collective-permute-start.23 = (bf16[64,2048]{1,0:T(8,128)(2,1)S(1)}, bf16[64,2048]{1,0:T(8,128)(2,1)S(1)}, u32[]{:S(2)}, u32[]{:S(2)}) collective-permute-start(bf16[64,2048]{1,0:T(8,128)(2,1)S(1)} %join.10), channel_id=1, source_target_pairs={{0,8},{2,10},{8,16},{10,18},{16,24},{18,26},{24,28},{26,30},{28,20... | collective-permute-start | bytes 786440 | tf_op jit(solution)/shard_map/ppermute | solution.py:459
  91.4 11.4 %collective-permute-start.35 = (bf16[64,2048]{1,0:T(8,128)(2,1)S(1)}, bf16[64,2048]{1,0:T(8,128)(2,1)S(1)}, u32[]{:S(2)}, u32[]{:S(2)}) collective-permute-start(bf16[64,2048]{1,0:T(8,128)(2,1)S(1)} %join.17), channel_id=1, source_target_pairs={{0,4},{2,6},{8,0},{10,2},{16,8},{18,10},{24,16},{26,18},{28,24},{3... | collective-permute-start | bytes 786440 | tf_op jit(solution)/shard_map/ppermute | solution.py:459
  91.7 13.2 %collective-permute-start.38 = (f32[2,136,128]{2,1,0:T(8,128)S(1)}, f32[2,136,128]{2,1,0:T(8,128)S(1)}, u32[]{:S(2)}, u32[]{:S(2)}) collective-permute-start(f32[2,136,128]{2,1,0:T(8,128)S(1)} %add.24), channel_id=1, source_target_pairs={{0,8},{2,10},{4,12},{6,14},{8,0},{10,2},{12,4},{14,6},{16,24},{18,... | collective-permute-start | bytes 417800 | tf_op jit(solution)/shard_map/ppermute | solution.py:49
  97.1 11.2 %collective-permute-start.30 = (bf16[64,2048]{1,0:T(8,128)(2,1)S(1)}, bf16[64,2048]{1,0:T(8,128)(2,1)S(1)}, u32[]{:S(2)}, u32[]{:S(2)}) collective-permute-start(bf16[64,2048]{1,0:T(8,128)(2,1)S(1)} %join.15), channel_id=1, source_target_pairs={{0,8},{2,10},{8,16},{10,18},{16,24},{18,26},{24,28},{26,30},{28,20... | collective-permute-start | bytes 786440 | tf_op jit(solution)/shard_map/ppermute | solution.py:459
  97.2 13.8 %collective-permute-start.27 = (bf16[64,2048]{1,0:T(8,128)(2,1)S(1)}, bf16[64,2048]{1,0:T(8,128)(2,1)S(1)}, u32[]{:S(2)}, u32[]{:S(2)}) collective-permute-start(bf16[64,2048]{1,0:T(8,128)(2,1)S(1)} %join.13), channel_id=1, source_target_pairs={{0,4},{2,6},{8,0},{10,2},{16,8},{18,10},{24,16},{26,18},{28,24},{3... | collective-permute-start | bytes 786440 | tf_op jit(solution)/shard_map/ppermute | solution.py:459
  102.7 11.2 %collective-permute-start.24 = (bf16[64,2048]{1,0:T(8,128)(2,1)S(1)}, bf16[64,2048]{1,0:T(8,128)(2,1)S(1)}, u32[]{:S(2)}, u32[]{:S(2)}) collective-permute-start(bf16[64,2048]{1,0:T(8,128)(2,1)S(1)} %join.11), channel_id=1, source_target_pairs={{0,8},{2,10},{8,16},{10,18},{16,24},{18,26},{24,28},{26,30},{28,20... | collective-permute-start | bytes 786440 | tf_op jit(solution)/shard_map/ppermute | solution.py:459
  102.8 15.1 %collective-permute-start.36 = (bf16[64,2048]{1,0:T(8,128)(2,1)S(1)}, bf16[64,2048]{1,0:T(8,128)(2,1)S(1)}, u32[]{:S(2)}, u32[]{:S(2)}) collective-permute-start(bf16[64,2048]{1,0:T(8,128)(2,1)S(1)} %join.18), channel_id=1, source_target_pairs={{0,4},{2,6},{8,0},{10,2},{16,8},{18,10},{24,16},{26,18},{28,24},{3... | collective-permute-start | bytes 786440 | tf_op jit(solution)/shard_map/ppermute | solution.py:459
  104.9 15.0 %collective-permute-start.39 = (f32[2,136,128]{2,1,0:T(8,128)S(1)}, f32[2,136,128]{2,1,0:T(8,128)S(1)}, u32[]{:S(2)}, u32[]{:S(2)}) collective-permute-start(f32[2,136,128]{2,1,0:T(8,128)S(1)} %add.25), channel_id=1, source_target_pairs={{0,16},{2,18},{4,20},{6,22},{8,24},{10,26},{12,28},{14,30},{16,0},... | collective-permute-start | bytes 417800 | tf_op jit(solution)/shard_map/ppermute | solution.py:49
  108.3 15.4 %collective-permute-start.31 = (bf16[64,2048]{1,0:T(8,128)(2,1)S(1)}, bf16[64,2048]{1,0:T(8,128)(2,1)S(1)}, u32[]{:S(2)}, u32[]{:S(2)}) collective-permute-start(bf16[64,2048]{1,0:T(8,128)(2,1)S(1)} %join.16), channel_id=1, source_target_pairs={{0,8},{2,10},{8,16},{10,18},{16,24},{18,26},{24,28},{26,30},{28,20... | collective-permute-start | bytes 786440 | tf_op jit(solution)/shard_map/ppermute | solution.py:459
  111.7 12.0 %collective-permute-start.28 = (bf16[64,2048]{1,0:T(8,128)(2,1)}, bf16[64,2048]{1,0:T(8,128)(2,1)S(1)}, u32[]{:S(2)}, u32[]{:S(2)}) collective-permute-start(bf16[64,2048]{1,0:T(8,128)(2,1)} %join.14), channel_id=1, source_target_pairs={{0,4},{2,6},{8,0},{10,2},{16,8},{18,10},{24,16},{26,18},{28,24},{3... | collective-permute-start | bytes 786440 | tf_op jit(solution)/shard_map/ppermute | solution.py:459
  (24 other events, 149.7 us)

commit v15 on v13

--- a/solution.py
+++ b/solution.py
@@ -192,7 +192,7 @@
 
 def middle_kernel(feats, turned, wn, inverse, base, cot, *refs):
     near, far, refs = refs[:feats], refs[feats : 2 * feats], refs[2 * feats :]
-    act, grad, scaled, agg_own, agg, value = refs
+    act, grad, scaled, agg_own, agg = refs
     hid, width = act.shape
     half = hid // 2
     core = lax.rem(lax.axis_index("rows"), 2)
@@ -207,11 +207,16 @@
         lane = pl.ds(c, chunk)
         pre = product(turned[...], agg[:, lane]) + base[:, lane]
         slope = jnp.exp(jnp.minimum(pre, 0.0))
-        grad[:, lane] = (cot[:, lane].astype(jnp.float32) * slope).astype(jnp.bfloat16)
-        value[...] = jnp.where(pre > 0, pre, slope - 1.0)
-        back = product(wn[...], grad[:, lane])
+        g = (cot[:, lane].astype(jnp.float32) * slope).astype(jnp.bfloat16)
+        grad[:, lane] = g
+        back = product(wn[...], g)
         scaled[:, lane] = (back * inverse[:, lane]).astype(jnp.bfloat16)
-        act[:, lane] = value[own].astype(jnp.bfloat16)
+        mine, mine_slope = pre[:hid], slope[:hid]
+        for k in range(1, feats):
+            here = lax.axis_index("feat") == k
+            mine = jnp.where(here, pre[k * hid : (k + 1) * hid], mine)
+            mine_slope = jnp.where(here, slope[k * hid : (k + 1) * hid], mine_slope)
+        act[:, lane] = jnp.where(mine > 0, mine, mine_slope - 1.0).astype(jnp.bfloat16)
 
 
 def own_quarter():
@@ -406,7 +411,7 @@
         bind(middle_kernel, feats), "middle",
         [((hid, width), narrow), ((every, width), narrow)] + [((hid, width), narrow)] * 2,
         [VMEM] * (5 + 2 * feats), [VMEM] * 4,
-        [pltpu.VMEM((every, width), narrow), pltpu.VMEM((every, min(width, 256)), wide)], 9,
+        [pltpu.VMEM((every, width), narrow)], 9,
         3 * every * every * width, 14 * every * width,
         turned, neigh_weight, inverse, base, cot_all, *near, *far,
     )

time: 128 us -> 128 us (level)
  no operation moved by 1% of the time
where the time goes in v15:
time: 128 us
  waiting for transfers between devices  52.7 us (41%)
  starting transfers between devices  36.9 us (29%)
  Pallas kernels  32.6 us (25%)
  local copies, waits for them, and re-layouts  4.64 us (4%)
    pallas_call x26, Pallas kernels, call(): pl.pallas_call(kernel, out_shape=[jax.ShapeDtypeStruct(shape, kind) for s...  32.6 us
    ppermute x7, waiting for transfers between devices, shards(): down[side] = lax.ppermute(down[side], 'rows', backward)  19.7 us
    ppermute x14, waiting for transfers between devices, ring(): return lax.ppermute(value, 'rows', pairs)  16.3 us
    ppermute x14, starting transfers between devices, ring(): return lax.ppermute(value, 'rows', pairs)  13.9 us
    ppermute x7, starting transfers between devices, shards(): up[side] = lax.ppermute(up[side], 'rows', forward)  11.8 us
    ppermute x4, waiting for transfers between devices, send(): return lax.ppermute(value, ('rows', 'feat'), pairs)  7.36 us
    ppermute x9, waiting for transfers between devices, swap(): return lax.ppermute(value, 'rows', [(r, r ^ bit) for r in range(rows)])  5.5 us
    ppermute x9, starting transfers between devices, swap(): return lax.ppermute(value, 'rows', [(r, r ^ bit) for r in range(rows)])  4.66 us
  transfers between devices with their start and end apart: 41, of which 25 were waited for; matrix products, arithmetic and copies ran while one was open for 1% of the time, Pallas kernels for 22%

profile of v15, /device:TPU:0, one launch (start us, length us, event | category | flops | bytes accessed | tf_op | source)
XLA Modules:
  0.0 127.8 jit_solution(4055320985238667483)
XLA Ops:
  2.2 2.7 %collective-permute-start = (bf16[64,2048]{1,0:T(8,128)(2,1)S(1)}, bf16[64,2048]{1,0:T(8,128)(2,1)S(1)}, u32[]{:S(2)}, u32[]{:S(2)}) collective-permute-start(bf16[64,2048]{1,0:T(8,128)(2,1)S(1)} %get-tuple-element.104.refs_0_), channel_id=1, source_target_pairs={{0,8},{2,10},{8,16},{10,18},{16,24},{18,26},{24,28},{26,30},{28,20... | collective-permute-start | bytes 786440 | tf_op jit(solution)/shard_map/ppermute | solution.py:376
  6.6 2.8 %copy-done = bf16[16,12,128,128]{3,2,1,0:T(8,128)(2,1)S(1)} copy-done((bf16[16,12,128,128]{3,2,1,0:T(8,128)(2,1)S(1)}, bf16[16,12,128,128]{3,2,1,0:T(8,128)(2,1)}, u32[]{:S(2)}) %copy-start) | copy-done | bytes 6291480
  10.1 3.2 %table.1 = s32[384]{0:T(512)S(1)} custom-call(s32[16,12]{1,0:T(8,128)S(1)} %copy-done.5), custom_call_target="tpu_custom_call" | custom-call | bytes 1536 | tf_op jit(solution)/shard_map/table/pallas_call | solution.py:312
  14.0 3.1 %collective-permute-done.1.refs_3_ = bf16[64,2048]{1,0:T(8,128)(2,1)S(1)} collective-permute-done((bf16[64,2048]{1,0:T(8,128)(2,1)S(1)}, bf16[64,2048]{1,0:T(8,128)(2,1)S(1)}, u32[]{:S(2)}, u32[]{:S(2)}) %collective-permute-start.1) | collective-permute-done | bytes 262176 | tf_op jit(solution)/shard_map/ppermute | solution.py:376
  23.7 2.8 %load.3.tiles.pair = bf16[16,12,128,128]{3,2,1,0:T(8,128)(2,1)S(1)} custom-call(bf16[16,12,128,128]{3,2,1,0:T(8,128)(2,1)} %collective-permute-done.4.source), custom_call_target="tpu_custom_call" | custom-call | bytes 12582912 | tf_op jit(solution)/shard_map/load/pallas_call | solution.py:312
  26.5 2.3 %collective-permute-done.7.refs_6_ = bf16[64,2048]{1,0:T(8,128)(2,1)S(1)} collective-permute-done((bf16[64,2048]{1,0:T(8,128)(2,1)S(1)}, bf16[64,2048]{1,0:T(8,128)(2,1)S(1)}, u32[]{:S(2)}, u32[]{:S(2)}) %collective-permute-start.7) | collective-permute-done | bytes 262176 | tf_op jit(solution)/shard_map/ppermute | solution.py:380
  30.9 3.5 %collective-permute-done.9.refs_8_ = bf16[64,2048]{1,0:T(8,128)(2,1)S(1)} collective-permute-done((bf16[64,2048]{1,0:T(8,128)(2,1)S(1)}, bf16[64,2048]{1,0:T(8,128)(2,1)S(1)}, u32[]{:S(2)}, u32[]{:S(2)}) %collective-permute-start.9) | collective-permute-done | bytes 262176 | tf_op jit(solution)/shard_map/ppermute | solution.py:380
  36.5 3.5 %collective-permute-done.11.refs_10_ = bf16[64,2048]{1,0:T(8,128)(2,1)S(1)} collective-permute-done((bf16[64,2048]{1,0:T(8,128)(2,1)S(1)}, bf16[64,2048]{1,0:T(8,128)(2,1)S(1)}, u32[]{:S(2)}, u32[]{:S(2)}) %collective-permute-start.11) | collective-permute-done | bytes 262176 | tf_op jit(solution)/shard_map/ppermute | solution.py:380
  40.6 4.4 %collective-permute-done.13.refs_12_ = bf16[64,2048]{1,0:T(8,128)(2,1)S(1)} collective-permute-done((bf16[64,2048]{1,0:T(8,128)(2,1)S(1)}, bf16[64,2048]{1,0:T(8,128)(2,1)S(1)}, u32[]{:S(2)}, u32[]{:S(2)}) %collective-permute-start.13) | collective-permute-done | bytes 262176 | tf_op jit(solution)/shard_map/ppermute | solution.py:380
  48.2 4.5 %collective-permute-done.16.refs_15_ = bf16[64,2048]{1,0:T(8,128)(2,1)S(1)} collective-permute-done((bf16[64,2048]{1,0:T(8,128)(2,1)S(1)}, bf16[64,2048]{1,0:T(8,128)(2,1)S(1)}, u32[]{:S(2)}, u32[]{:S(2)}) %collective-permute-start.16) | collective-permute-done | bytes 262176 | tf_op jit(solution)/shard_map/ppermute | solution.py:380
  52.8 4.4 %aggregate.3 = (bf16[64,2048]{1,0:T(8,128)(2,1)S(1)}, f32[1,2048]{1,0:T(1,128)}) custom-call(s32[384]{0:T(512)S(1)} %collective-permute-done.18.table.table_pair, bf16[16,12,128,128]{3,2,1,0:T(8,128)(2,1)S(1)} %load.3.tiles.pair, bf16[64,2048]{1,0:T(8,128)(2,1)S(1)} %get-tuple-element.104.refs_0_, bf16[64,2048]{1,0:T(8,128)(2,1)S(1)} %collective-permute-done.refs_1_, ...), custom_call_target="tpu_custom_call" | custom-call | flops 402653184 | bytes 10485760 | tf_op jit(solution)/shard_map/aggregate/pallas_call | solution.py:312
  57.9 3.9 %aggregate.2 = (bf16[64,2048]{1,0:T(8,128)(2,1)S(1)}, f32[1,2048]{1,0:T(1,128)S(1)}) custom-call(s32[384]{0:T(512)S(1)} %table.1, bf16[16,12,128,128]{3,2,1,0:T(8,128)(2,1)S(1)} %load.2.tiles.adj, bf16[64,2048]{1,0:T(8,128)(2,1)S(1)} %get-tuple-element.104.refs_0_, bf16[64,2048]{1,0:T(8,128)(2,1)S(1)} %collective-permute-done.refs_1_, ...), custom_call_target="tpu_custom_call" | custom-call | flops 402653184 | bytes 10485760 | tf_op jit(solution)/shard_map/aggregate/pallas_call | solution.py:312
  65.5 6.2 %collective-permute-done.17.refs_1_ = bf16[64,2048]{1,0:T(8,128)(2,1)S(1)} collective-permute-done((bf16[64,2048]{1,0:T(8,128)(2,1)S(1)}, bf16[64,2048]{1,0:T(8,128)(2,1)S(1)}, u32[]{:S(2)}, u32[]{:S(2)}) %collective-permute-start.17) | collective-permute-done | bytes 262176 | tf_op jit(solution)/shard_map/ppermute | solution.py:58
  71.6 3.0 %middle.1 = (bf16[128,2048]{1,0:T(8,128)(2,1)}, bf16[256,2048]{1,0:T(8,128)(2,1)S(1)}, bf16[128,2048]{1,0:T(8,128)(2,1)S(1)}, bf16[128,2048]{1,0:T(8,128)(2,1)S(1)}) custom-call(bf16[256,256]{1,0:T(8,128)(2,1)S(1)} %get-tuple-element.55.turned, bf16[128,256]{1,0:T(8,128)(2,1)S(1)} %copy-done.3, f32[1,2048]{1,0:T(1,128)S(1)} %get-tuple-element.68.inverse, ...), custom_call_target="tpu_custom_call" | custom-call | flops 402653184 | bytes 7340032 | tf_op jit(solution)/shard_map/middle/pallas_call | solution.py:312
  85.5 3.2 %collective-permute-done.22.arrived = bf16[64,2048]{1,0:T(8,128)(2,1)S(1)} collective-permute-done((bf16[64,2048]{1,0:T(8,128)(2,1)S(1)}, bf16[64,2048]{1,0:T(8,128)(2,1)S(1)}, u32[]{:S(2)}, u32[]{:S(2)}) %collective-permute-start.22) | collective-permute-done | bytes 262176 | tf_op jit(solution)/shard_map/ppermute | solution.py:464
  89.5 2.2 %collective-permute-done.34 = f32[2,136,128]{2,1,0:T(8,128)S(1)} collective-permute-done((f32[2,136,128]{2,1,0:T(8,128)S(1)}, f32[2,136,128]{2,1,0:T(8,128)S(1)}, u32[]{:S(2)}, u32[]{:S(2)}) %collective-permute-start.34) | collective-permute-done | bytes 139296 | tf_op jit(solution)/shard_map/ppermute | solution.py:49
  91.8 2.0 %collective-permute-start.38 = (f32[2,136,128]{2,1,0:T(8,128)S(1)}, f32[2,136,128]{2,1,0:T(8,128)S(1)}, u32[]{:S(2)}, u32[]{:S(2)}) collective-permute-start(f32[2,136,128]{2,1,0:T(8,128)S(1)} %add.24), channel_id=1, source_target_pairs={{0,8},{2,10},{4,12},{6,14},{8,0},{10,2},{12,4},{14,6},{16,24},{18,... | collective-permute-start | bytes 417800 | tf_op jit(solution)/shard_map/ppermute | solution.py:49
  97.5 2.1 %collective-permute-start.27 = (bf16[64,2048]{1,0:T(8,128)(2,1)S(1)}, bf16[64,2048]{1,0:T(8,128)(2,1)S(1)}, u32[]{:S(2)}, u32[]{:S(2)}) collective-permute-start(bf16[64,2048]{1,0:T(8,128)(2,1)S(1)} %join.13), channel_id=1, source_target_pairs={{0,4},{2,6},{8,0},{10,2},{16,8},{18,10},{24,16},{26,18},{28,24},{3... | collective-permute-start | bytes 786440 | tf_op jit(solution)/shard_map/ppermute | solution.py:464
  99.6 3.3 %collective-permute-done.23.arrived = bf16[64,2048]{1,0:T(8,128)(2,1)S(1)} collective-permute-done((bf16[64,2048]{1,0:T(8,128)(2,1)S(1)}, bf16[64,2048]{1,0:T(8,128)(2,1)S(1)}, u32[]{:S(2)}, u32[]{:S(2)}) %collective-permute-start.23) | collective-permute-done | bytes 262176 | tf_op jit(solution)/shard_map/ppermute | solution.py:464
  103.3 2.1 %collective-permute-start.36 = (bf16[64,2048]{1,0:T(8,128)(2,1)S(1)}, bf16[64,2048]{1,0:T(8,128)(2,1)S(1)}, u32[]{:S(2)}, u32[]{:S(2)}) collective-permute-start(bf16[64,2048]{1,0:T(8,128)(2,1)S(1)} %join.18), channel_id=1, source_target_pairs={{0,4},{2,6},{8,0},{10,2},{16,8},{18,10},{24,16},{26,18},{28,24},{3... | collective-permute-start | bytes 786440 | tf_op jit(solution)/shard_map/ppermute | solution.py:464
  105.8 2.3 %spread.4 = (f32[64,2048]{1,0:T(8,128)S(1)}, f32[64,2048]{1,0:T(8,128)S(1)}, f32[64,2048]{1,0:T(8,128)S(1)}, f32[64,2048]{1,0:T(8,128)S(1)}, f32[64,2048]{1,0:T(8,128)S(1)}, /*index=5*/f32[64,2048]{1,0:T(8,128)S(1)}) custom-call(s32[384]{0:T(512)S(1)} %table.1, s32[384]{0:T(512)S(1)} %collective-permute-done.18.table.table_pair, ...), custom_call_target="tpu_custom_call" | custom-call | flops 301989888 | bytes 6291456 | tf_op jit(solution)/shard_map/spread/pallas_call | solution.py:312
  108.6 2.2 %collective-permute-start.31 = (bf16[64,2048]{1,0:T(8,128)(2,1)S(1)}, bf16[64,2048]{1,0:T(8,128)(2,1)S(1)}, u32[]{:S(2)}, u32[]{:S(2)}) collective-permute-start(bf16[64,2048]{1,0:T(8,128)(2,1)S(1)} %join.16), channel_id=1, source_target_pairs={{0,8},{2,10},{8,16},{10,18},{16,24},{18,26},{24,28},{26,30},{28,20... | collective-permute-start | bytes 786440 | tf_op jit(solution)/shard_map/ppermute | solution.py:464
  111.7 2.5 %collective-permute-done.24.arrived = bf16[64,2048]{1,0:T(8,128)(2,1)S(1)} collective-permute-done((bf16[64,2048]{1,0:T(8,128)(2,1)S(1)}, bf16[64,2048]{1,0:T(8,128)(2,1)S(1)}, u32[]{:S(2)}, u32[]{:S(2)}) %collective-permute-start.24) | collective-permute-done | bytes 262176 | tf_op jit(solution)/shard_map/ppermute | solution.py:464
  115.5 2.2 %collective-permute-done.36.arrived = bf16[64,2048]{1,0:T(8,128)(2,1)S(1)} collective-permute-done((bf16[64,2048]{1,0:T(8,128)(2,1)S(1)}, bf16[64,2048]{1,0:T(8,128)(2,1)S(1)}, u32[]{:S(2)}, u32[]{:S(2)}) %collective-permute-start.36) | collective-permute-done | bytes 262176 | tf_op jit(solution)/shard_map/ppermute | solution.py:464
  (106 shorter events, 52.6 us)
Async XLA Ops:
  0.6 17.5 %collective-permute-start.4 = (bf16[16,12,128,128]{3,2,1,0:T(8,128)(2,1)}, bf16[16,12,128,128]{3,2,1,0:T(8,128)(2,1)}, u32[]{:S(2)}, u32[]{:S(2)}) collective-permute-start(bf16[16,12,128,128]{3,2,1,0:T(8,128)(2,1)} %source.1), channel_id=1, source_target_pairs={{0,2},{2,0},{4,6},{6,4},{8,10},{10,8},{12,14},{14,12},{16,18},{18,... | collective-permute-start | bytes 18874376 | tf_op jit(solution)/shard_map/ppermute | solution.py:49
  2.2 11.4 %collective-permute-start = (bf16[64,2048]{1,0:T(8,128)(2,1)S(1)}, bf16[64,2048]{1,0:T(8,128)(2,1)S(1)}, u32[]{:S(2)}, u32[]{:S(2)}) collective-permute-start(bf16[64,2048]{1,0:T(8,128)(2,1)S(1)} %get-tuple-element.104.refs_0_), channel_id=1, source_target_pairs={{0,8},{2,10},{8,16},{10,18},{16,24},{18,26},{24,28},{26,30},{28,20... | collective-permute-start | bytes 786440 | tf_op jit(solution)/shard_map/ppermute | solution.py:376
  4.9 12.3 %collective-permute-start.1 = (bf16[64,2048]{1,0:T(8,128)(2,1)S(1)}, bf16[64,2048]{1,0:T(8,128)(2,1)S(1)}, u32[]{:S(2)}, u32[]{:S(2)}) collective-permute-start(bf16[64,2048]{1,0:T(8,128)(2,1)S(1)} %get-tuple-element.67), channel_id=1, source_target_pairs={{0,10},{2,8},{8,18},{10,16},{16,26},{18,24},{24,30},{26,28},{28,22... | collective-permute-start | bytes 786440 | tf_op jit(solution)/shard_map/ppermute | solution.py:376
  6.4 11.7 %collective-permute-start.3 = (bf16[64,2048]{1,0:T(8,128)(2,1)S(1)}, bf16[64,2048]{1,0:T(8,128)(2,1)S(1)}, u32[]{:S(2)}, u32[]{:S(2)}) collective-permute-start(bf16[64,2048]{1,0:T(8,128)(2,1)S(1)} %get-tuple-element.67), channel_id=1, source_target_pairs={{0,6},{2,4},{8,2},{10,0},{16,10},{18,8},{24,18},{26,16},{28,26},{3... | collective-permute-start | bytes 786440 | tf_op jit(solution)/shard_map/ppermute | solution.py:380
  18.2 45.3 %collective-permute-start.5 = (bf16[128,4736]{1,0:T(8,128)(2,1)S(1)}, bf16[128,4736]{1,0:T(8,128)(2,1)S(1)}, u32[]{:S(2)}, u32[]{:S(2)}) collective-permute-start(bf16[128,4736]{1,0:T(8,128)(2,1)S(1)} %pack.1.refs_0_), channel_id=1, source_target_pairs={{0,1},{1,0},{2,3},{3,2},{4,5},{5,4},{6,7},{7,6},{8,9},{9,8},{10,11... | collective-permute-start | bytes 3637256 | tf_op jit(solution)/shard_map/ppermute | solution.py:58
  21.7 12.7 %collective-permute-start.9 = (bf16[64,2048]{1,0:T(8,128)(2,1)S(1)}, bf16[64,2048]{1,0:T(8,128)(2,1)S(1)}, u32[]{:S(2)}, u32[]{:S(2)}) collective-permute-start(bf16[64,2048]{1,0:T(8,128)(2,1)S(1)} %collective-permute-done.3.refs_4_), channel_id=1, source_target_pairs={{0,4},{2,6},{8,0},{10,2},{16,8},{18,10},{24,16},{26,18},{28,24},{3... | collective-permute-start | bytes 786440 | tf_op jit(solution)/shard_map/ppermute | solution.py:380
  22.2 12.8 %collective-permute-start.8 = (bf16[64,2048]{1,0:T(8,128)(2,1)S(1)}, bf16[64,2048]{1,0:T(8,128)(2,1)S(1)}, u32[]{:S(2)}, u32[]{:S(2)}) collective-permute-start(bf16[64,2048]{1,0:T(8,128)(2,1)S(1)} %collective-permute-done.1.refs_3_), channel_id=1, source_target_pairs={{0,8},{2,10},{8,16},{10,18},{16,24},{18,26},{24,28},{26,30},{28,20... | collective-permute-start | bytes 786440 | tf_op jit(solution)/shard_map/ppermute | solution.py:376
  28.8 11.2 %collective-permute-start.11 = (bf16[64,2048]{1,0:T(8,128)(2,1)S(1)}, bf16[64,2048]{1,0:T(8,128)(2,1)S(1)}, u32[]{:S(2)}, u32[]{:S(2)}) collective-permute-start(bf16[64,2048]{1,0:T(8,128)(2,1)S(1)} %collective-permute-done.7.refs_6_), channel_id=1, source_target_pairs={{0,4},{2,6},{8,0},{10,2},{16,8},{18,10},{24,16},{26,18},{28,24},{3... | collective-permute-start | bytes 786440 | tf_op jit(solution)/shard_map/ppermute | solution.py:380
  29.4 11.2 %collective-permute-start.10 = (bf16[64,2048]{1,0:T(8,128)(2,1)S(1)}, bf16[64,2048]{1,0:T(8,128)(2,1)S(1)}, u32[]{:S(2)}, u32[]{:S(2)}) collective-permute-start(bf16[64,2048]{1,0:T(8,128)(2,1)S(1)} %collective-permute-done.6.refs_5_), channel_id=1, source_target_pairs={{0,8},{2,10},{8,16},{10,18},{16,24},{18,26},{24,28},{26,30},{28,20... | collective-permute-start | bytes 786440 | tf_op jit(solution)/shard_map/ppermute | solution.py:376
  35.0 12.1 %collective-permute-start.12 = (bf16[64,2048]{1,0:T(8,128)(2,1)S(1)}, bf16[64,2048]{1,0:T(8,128)(2,1)S(1)}, u32[]{:S(2)}, u32[]{:S(2)}) collective-permute-start(bf16[64,2048]{1,0:T(8,128)(2,1)S(1)} %collective-permute-done.8.refs_7_), channel_id=1, source_target_pairs={{0,8},{2,10},{8,16},{10,18},{16,24},{18,26},{24,28},{26,30},{28,20... | collective-permute-start | bytes 786440 | tf_op jit(solution)/shard_map/ppermute | solution.py:376
  78.1 11.4 %collective-permute-start.32 = (bf16[64,2048]{1,0:T(8,128)(2,1)S(1)}, bf16[64,2048]{1,0:T(8,128)(2,1)S(1)}, u32[]{:S(2)}, u32[]{:S(2)}) collective-permute-start(bf16[64,2048]{1,0:T(8,128)(2,1)S(1)} %get-tuple-element.91), channel_id=1, source_target_pairs={{0,4},{2,6},{8,0},{10,2},{16,8},{18,10},{24,16},{26,18},{28,24},{3... | collective-permute-start | bytes 786440 | tf_op jit(solution)/shard_map/ppermute | solution.py:464
  80.2 11.5 %collective-permute-start.34 = (f32[2,136,128]{2,1,0:T(8,128)S(1)}, f32[2,136,128]{2,1,0:T(8,128)S(1)}, u32[]{:S(2)}, u32[]{:S(2)}) collective-permute-start(f32[2,136,128]{2,1,0:T(8,128)S(1)} %slice_add_fusion), channel_id=1, source_target_pairs={{0,4},{2,6},{4,0},{6,2},{8,12},{10,14},{12,8},{14,10},{16,20},{18,... | collective-permute-start | bytes 417800 | tf_op jit(solution)/shard_map/ppermute | solution.py:49
  83.4 13.9 %collective-permute-start.29 = (bf16[64,2048]{1,0:T(8,128)(2,1)S(1)}, bf16[64,2048]{1,0:T(8,128)(2,1)S(1)}, u32[]{:S(2)}, u32[]{:S(2)}) collective-permute-start(bf16[64,2048]{1,0:T(8,128)(2,1)S(1)} %get-tuple-element.88), channel_id=1, source_target_pairs={{0,8},{2,10},{8,16},{10,18},{16,24},{18,26},{24,28},{26,30},{28,20... | collective-permute-start | bytes 786440 | tf_op jit(solution)/shard_map/ppermute | solution.py:464
  85.0 12.4 %collective-permute-start.26 = (bf16[64,2048]{1,0:T(8,128)(2,1)S(1)}, bf16[64,2048]{1,0:T(8,128)(2,1)S(1)}, u32[]{:S(2)}, u32[]{:S(2)}) collective-permute-start(bf16[64,2048]{1,0:T(8,128)(2,1)S(1)} %get-tuple-element.85), channel_id=1, source_target_pairs={{0,4},{2,6},{8,0},{10,2},{16,8},{18,10},{24,16},{26,18},{28,24},{3... | collective-permute-start | bytes 786440 | tf_op jit(solution)/shard_map/ppermute | solution.py:464
  88.8 14.2 %collective-permute-start.23 = (bf16[64,2048]{1,0:T(8,128)(2,1)S(1)}, bf16[64,2048]{1,0:T(8,128)(2,1)S(1)}, u32[]{:S(2)}, u32[]{:S(2)}) collective-permute-start(bf16[64,2048]{1,0:T(8,128)(2,1)S(1)} %join.10), channel_id=1, source_target_pairs={{0,8},{2,10},{8,16},{10,18},{16,24},{18,26},{24,28},{26,30},{28,20... | collective-permute-start | bytes 786440 | tf_op jit(solution)/shard_map/ppermute | solution.py:464
  91.7 11.5 %collective-permute-start.35 = (bf16[64,2048]{1,0:T(8,128)(2,1)S(1)}, bf16[64,2048]{1,0:T(8,128)(2,1)S(1)}, u32[]{:S(2)}, u32[]{:S(2)}) collective-permute-start(bf16[64,2048]{1,0:T(8,128)(2,1)S(1)} %join.17), channel_id=1, source_target_pairs={{0,4},{2,6},{8,0},{10,2},{16,8},{18,10},{24,16},{26,18},{28,24},{3... | collective-permute-start | bytes 786440 | tf_op jit(solution)/shard_map/ppermute | solution.py:464
  91.8 13.6 %collective-permute-start.38 = (f32[2,136,128]{2,1,0:T(8,128)S(1)}, f32[2,136,128]{2,1,0:T(8,128)S(1)}, u32[]{:S(2)}, u32[]{:S(2)}) collective-permute-start(f32[2,136,128]{2,1,0:T(8,128)S(1)} %add.24), channel_id=1, source_target_pairs={{0,8},{2,10},{4,12},{6,14},{8,0},{10,2},{12,4},{14,6},{16,24},{18,... | collective-permute-start | bytes 417800 | tf_op jit(solution)/shard_map/ppermute | solution.py:49
  97.4 11.2 %collective-permute-start.30 = (bf16[64,2048]{1,0:T(8,128)(2,1)S(1)}, bf16[64,2048]{1,0:T(8,128)(2,1)S(1)}, u32[]{:S(2)}, u32[]{:S(2)}) collective-permute-start(bf16[64,2048]{1,0:T(8,128)(2,1)S(1)} %join.15), channel_id=1, source_target_pairs={{0,8},{2,10},{8,16},{10,18},{16,24},{18,26},{24,28},{26,30},{28,20... | collective-permute-start | bytes 786440 | tf_op jit(solution)/shard_map/ppermute | solution.py:464
  97.5 13.4 %collective-permute-start.27 = (bf16[64,2048]{1,0:T(8,128)(2,1)S(1)}, bf16[64,2048]{1,0:T(8,128)(2,1)S(1)}, u32[]{:S(2)}, u32[]{:S(2)}) collective-permute-start(bf16[64,2048]{1,0:T(8,128)(2,1)S(1)} %join.13), channel_id=1, source_target_pairs={{0,4},{2,6},{8,0},{10,2},{16,8},{18,10},{24,16},{26,18},{28,24},{3... | collective-permute-start | bytes 786440 | tf_op jit(solution)/shard_map/ppermute | solution.py:464
  103.0 11.2 %collective-permute-start.24 = (bf16[64,2048]{1,0:T(8,128)(2,1)S(1)}, bf16[64,2048]{1,0:T(8,128)(2,1)S(1)}, u32[]{:S(2)}, u32[]{:S(2)}) collective-permute-start(bf16[64,2048]{1,0:T(8,128)(2,1)S(1)} %join.11), channel_id=1, source_target_pairs={{0,8},{2,10},{8,16},{10,18},{16,24},{18,26},{24,28},{26,30},{28,20... | collective-permute-start | bytes 786440 | tf_op jit(solution)/shard_map/ppermute | solution.py:464
  103.3 14.3 %collective-permute-start.36 = (bf16[64,2048]{1,0:T(8,128)(2,1)S(1)}, bf16[64,2048]{1,0:T(8,128)(2,1)S(1)}, u32[]{:S(2)}, u32[]{:S(2)}) collective-permute-start(bf16[64,2048]{1,0:T(8,128)(2,1)S(1)} %join.18), channel_id=1, source_target_pairs={{0,4},{2,6},{8,0},{10,2},{16,8},{18,10},{24,16},{26,18},{28,24},{3... | collective-permute-start | bytes 786440 | tf_op jit(solution)/shard_map/ppermute | solution.py:464
  105.4 14.8 %collective-permute-start.39 = (f32[2,136,128]{2,1,0:T(8,128)S(1)}, f32[2,136,128]{2,1,0:T(8,128)S(1)}, u32[]{:S(2)}, u32[]{:S(2)}) collective-permute-start(f32[2,136,128]{2,1,0:T(8,128)S(1)} %add.25), channel_id=1, source_target_pairs={{0,16},{2,18},{4,20},{6,22},{8,24},{10,26},{12,28},{14,30},{16,0},... | collective-permute-start | bytes 417800 | tf_op jit(solution)/shard_map/ppermute | solution.py:49
  108.6 15.4 %collective-permute-start.31 = (bf16[64,2048]{1,0:T(8,128)(2,1)S(1)}, bf16[64,2048]{1,0:T(8,128)(2,1)S(1)}, u32[]{:S(2)}, u32[]{:S(2)}) collective-permute-start(bf16[64,2048]{1,0:T(8,128)(2,1)S(1)} %join.16), channel_id=1, source_target_pairs={{0,8},{2,10},{8,16},{10,18},{16,24},{18,26},{24,28},{26,30},{28,20... | collective-permute-start | bytes 786440 | tf_op jit(solution)/shard_map/ppermute | solution.py:464
  111.7 12.3 %collective-permute-start.28 = (bf16[64,2048]{1,0:T(8,128)(2,1)}, bf16[64,2048]{1,0:T(8,128)(2,1)S(1)}, u32[]{:S(2)}, u32[]{:S(2)}) collective-permute-start(bf16[64,2048]{1,0:T(8,128)(2,1)} %join.14), channel_id=1, source_target_pairs={{0,4},{2,6},{8,0},{10,2},{16,8},{18,10},{24,16},{26,18},{28,24},{3... | collective-permute-start | bytes 786440 | tf_op jit(solution)/shard_map/ppermute | solution.py:464
  (24 other events, 150.0 us)

commit v16 on v13

--- a/solution.py
+++ b/solution.py
@@ -223,7 +223,8 @@
     return 2 * turned + index % 2
 
 
-def weights_kernel(ws, x_own, agg_own, grad, self_own, sums):
+def weights_kernel(ws, x_own, agg_own, grad, act, self_own, sums, act_out):
+    act_out[...] = act[...]
     hid, every = ws.shape
     g = grad[...]
     self_own[...] = product(ws[...], g)
@@ -402,7 +403,7 @@
         ],
         8, 2 * every * every * width, 4 * every * packed, *packs,
     )
-    activation, grad, scaled, agg_own = call(
+    act, grad, scaled, agg_own = call(
         bind(middle_kernel, feats), "middle",
         [((hid, width), narrow), ((every, width), narrow)] + [((hid, width), narrow)] * 2,
         [VMEM] * (5 + 2 * feats), [VMEM] * 4,
@@ -411,10 +412,10 @@
         turned, neigh_weight, inverse, base, cot_all, *near, *far,
     )
     scaled_pair = swap(scaled, rows)
-    self_own, sums = call(
-        weights_kernel, "weights", [((hid, width), wide), ((4, hid + 8, every // 2), wide)],
-        [VMEM] * 4, [VMEM] * 2, [], 6, 6 * hid * every * width, 10 * every * width,
-        self_weight, features, agg_own, grad,
+    self_own, sums, activation = call(
+        weights_kernel, "weights", [((hid, width), wide), ((4, hid + 8, every // 2), wide), ((hid, width), narrow)],
+        [VMEM] * 5, [VMEM] * 3, [], 7, 6 * hid * every * width, 10 * every * width,
+        self_weight, features, agg_own, grad, act,
     )
     (held,) = call(
         arrange_kernel, "arrange", [((2, blocks + 1, hid, tile), narrow)],

time: 128 us -> 127 us (level)
  waiting for transfers between devices: 52.6 us -> 51.1 us
  transfers between devices with their start and end apart: 41 -> 41, of which waited for: 25 -> 23; matrix products, arithmetic and copies ran while one was open for 1% -> 1% of each run, Pallas kernels for 22% -> 23%
where the time goes in v16:
time: 127 us
  waiting for transfers between devices  51.1 us (40%)
  starting transfers between devices  37.7 us (30%)
  Pallas kernels  32.7 us (26%)
  local copies, waits for them, and re-layouts  4.64 us (4%)
    pallas_call x26, Pallas kernels, call(): pl.pallas_call(kernel, out_shape=[jax.ShapeDtypeStruct(shape, kind) for s...  32.7 us
    ppermute x7, waiting for transfers between devices, shards(): down[side] = lax.ppermute(down[side], 'rows', backward)  19.7 us
    ppermute x14, waiting for transfers between devices, ring(): return lax.ppermute(value, 'rows', pairs)  15.3 us
    ppermute x14, starting transfers between devices, ring(): return lax.ppermute(value, 'rows', pairs)  14.2 us
    ppermute x7, starting transfers between devices, shards(): up[side] = lax.ppermute(up[side], 'rows', forward)  11.8 us
    ppermute x4, waiting for transfers between devices, send(): return lax.ppermute(value, ('rows', 'feat'), pairs)  7.37 us
    ppermute x9, starting transfers between devices, swap(): return lax.ppermute(value, 'rows', [(r, r ^ bit) for r in range(rows)])  5.16 us
    ppermute x9, waiting for transfers between devices, swap(): return lax.ppermute(value, 'rows', [(r, r ^ bit) for r in range(rows)])  4.91 us
  transfers between devices with their start and end apart: 41, of which 23 were waited for; matrix products, arithmetic and copies ran while one was open for 1% of the time, Pallas kernels for 23%

profile of v16, /device:TPU:0, one launch (start us, length us, event | category | flops | bytes accessed | tf_op | source)
XLA Modules:
  0.0 127.1 jit_solution(15541817326971210358)
XLA Ops:
  2.2 2.7 %collective-permute-start = (bf16[64,2048]{1,0:T(8,128)(2,1)S(1)}, bf16[64,2048]{1,0:T(8,128)(2,1)S(1)}, u32[]{:S(2)}, u32[]{:S(2)}) collective-permute-start(bf16[64,2048]{1,0:T(8,128)(2,1)S(1)} %get-tuple-element.106.refs_0_), channel_id=1, source_target_pairs={{0,8},{2,10},{8,16},{10,18},{16,24},{18,26},{24,28},{26,30},{28,20... | collective-permute-start | bytes 786440 | tf_op jit(solution)/shard_map/ppermute | solution.py:372
  6.6 2.8 %copy-done = bf16[16,12,128,128]{3,2,1,0:T(8,128)(2,1)S(1)} copy-done((bf16[16,12,128,128]{3,2,1,0:T(8,128)(2,1)S(1)}, bf16[16,12,128,128]{3,2,1,0:T(8,128)(2,1)}, u32[]{:S(2)}) %copy-start) | copy-done | bytes 6291480
  10.1 3.2 %table.1 = s32[384]{0:T(512)S(1)} custom-call(s32[16,12]{1,0:T(8,128)S(1)} %copy-done.5), custom_call_target="tpu_custom_call" | custom-call | bytes 1536 | tf_op jit(solution)/shard_map/table/pallas_call | solution.py:308
  14.0 3.1 %collective-permute-done.1.refs_3_ = bf16[64,2048]{1,0:T(8,128)(2,1)S(1)} collective-permute-done((bf16[64,2048]{1,0:T(8,128)(2,1)S(1)}, bf16[64,2048]{1,0:T(8,128)(2,1)S(1)}, u32[]{:S(2)}, u32[]{:S(2)}) %collective-permute-start.1) | collective-permute-done | bytes 262176 | tf_op jit(solution)/shard_map/ppermute | solution.py:372
  23.7 2.8 %load.3.tiles.pair = bf16[16,12,128,128]{3,2,1,0:T(8,128)(2,1)S(1)} custom-call(bf16[16,12,128,128]{3,2,1,0:T(8,128)(2,1)} %collective-permute-done.4.source), custom_call_target="tpu_custom_call" | custom-call | bytes 12582912 | tf_op jit(solution)/shard_map/load/pallas_call | solution.py:308
  26.5 2.3 %collective-permute-done.7.refs_6_ = bf16[64,2048]{1,0:T(8,128)(2,1)S(1)} collective-permute-done((bf16[64,2048]{1,0:T(8,128)(2,1)S(1)}, bf16[64,2048]{1,0:T(8,128)(2,1)S(1)}, u32[]{:S(2)}, u32[]{:S(2)}) %collective-permute-start.7) | collective-permute-done | bytes 262176 | tf_op jit(solution)/shard_map/ppermute | solution.py:376
  30.9 3.5 %collective-permute-done.9.refs_8_ = bf16[64,2048]{1,0:T(8,128)(2,1)S(1)} collective-permute-done((bf16[64,2048]{1,0:T(8,128)(2,1)S(1)}, bf16[64,2048]{1,0:T(8,128)(2,1)S(1)}, u32[]{:S(2)}, u32[]{:S(2)}) %collective-permute-start.9) | collective-permute-done | bytes 262176 | tf_op jit(solution)/shard_map/ppermute | solution.py:376
  36.5 3.5 %collective-permute-done.11.refs_10_ = bf16[64,2048]{1,0:T(8,128)(2,1)S(1)} collective-permute-done((bf16[64,2048]{1,0:T(8,128)(2,1)S(1)}, bf16[64,2048]{1,0:T(8,128)(2,1)S(1)}, u32[]{:S(2)}, u32[]{:S(2)}) %collective-permute-start.11) | collective-permute-done | bytes 262176 | tf_op jit(solution)/shard_map/ppermute | solution.py:376
  40.6 4.4 %collective-permute-done.13.refs_12_ = bf16[64,2048]{1,0:T(8,128)(2,1)S(1)} collective-permute-done((bf16[64,2048]{1,0:T(8,128)(2,1)S(1)}, bf16[64,2048]{1,0:T(8,128)(2,1)S(1)}, u32[]{:S(2)}, u32[]{:S(2)}) %collective-permute-start.13) | collective-permute-done | bytes 262176 | tf_op jit(solution)/shard_map/ppermute | solution.py:376
  48.2 4.5 %collective-permute-done.16.refs_15_ = bf16[64,2048]{1,0:T(8,128)(2,1)S(1)} collective-permute-done((bf16[64,2048]{1,0:T(8,128)(2,1)S(1)}, bf16[64,2048]{1,0:T(8,128)(2,1)S(1)}, u32[]{:S(2)}, u32[]{:S(2)}) %collective-permute-start.16) | collective-permute-done | bytes 262176 | tf_op jit(solution)/shard_map/ppermute | solution.py:376
  52.8 4.4 %aggregate.3 = (bf16[64,2048]{1,0:T(8,128)(2,1)S(1)}, f32[1,2048]{1,0:T(1,128)}) custom-call(s32[384]{0:T(512)S(1)} %collective-permute-done.18.table.table_pair, bf16[16,12,128,128]{3,2,1,0:T(8,128)(2,1)S(1)} %load.3.tiles.pair, bf16[64,2048]{1,0:T(8,128)(2,1)S(1)} %get-tuple-element.106.refs_0_, bf16[64,2048]{1,0:T(8,128)(2,1)S(1)} %collective-permute-done.refs_1_, ...), custom_call_target="tpu_custom_call" | custom-call | flops 402653184 | bytes 10485760 | tf_op jit(solution)/shard_map/aggregate/pallas_call | solution.py:308
  57.9 3.9 %aggregate.2 = (bf16[64,2048]{1,0:T(8,128)(2,1)S(1)}, f32[1,2048]{1,0:T(1,128)S(1)}) custom-call(s32[384]{0:T(512)S(1)} %table.1, bf16[16,12,128,128]{3,2,1,0:T(8,128)(2,1)S(1)} %load.2.tiles.adj, bf16[64,2048]{1,0:T(8,128)(2,1)S(1)} %get-tuple-element.106.refs_0_, bf16[64,2048]{1,0:T(8,128)(2,1)S(1)} %collective-permute-done.refs_1_, ...), custom_call_target="tpu_custom_call" | custom-call | flops 402653184 | bytes 10485760 | tf_op jit(solution)/shard_map/aggregate/pallas_call | solution.py:308
  65.4 6.2 %collective-permute-done.17.refs_1_ = bf16[64,2048]{1,0:T(8,128)(2,1)S(1)} collective-permute-done((bf16[64,2048]{1,0:T(8,128)(2,1)S(1)}, bf16[64,2048]{1,0:T(8,128)(2,1)S(1)}, u32[]{:S(2)}, u32[]{:S(2)}) %collective-permute-start.17) | collective-permute-done | bytes 262176 | tf_op jit(solution)/shard_map/ppermute | solution.py:58
  71.6 2.3 %middle.1 = (bf16[128,2048]{1,0:T(8,128)(2,1)S(1)}, bf16[256,2048]{1,0:T(8,128)(2,1)S(1)}, bf16[128,2048]{1,0:T(8,128)(2,1)S(1)}, bf16[128,2048]{1,0:T(8,128)(2,1)S(1)}) custom-call(bf16[256,256]{1,0:T(8,128)(2,1)S(1)} %get-tuple-element.56.turned, bf16[128,256]{1,0:T(8,128)(2,1)S(1)} %copy-done.3, f32[1,2048]{1,0:T(1,128)S(1)} %get-tuple-element.69.inverse, ...), custom_call_target="tpu_custom_call" | custom-call | flops 402653184 | bytes 7340032 | tf_op jit(solution)/shard_map/middle/pallas_call | solution.py:308
  85.3 3.3 %collective-permute-done.22.arrived = bf16[64,2048]{1,0:T(8,128)(2,1)S(1)} collective-permute-done((bf16[64,2048]{1,0:T(8,128)(2,1)S(1)}, bf16[64,2048]{1,0:T(8,128)(2,1)S(1)}, u32[]{:S(2)}, u32[]{:S(2)}) %collective-permute-start.22) | collective-permute-done | bytes 262176 | tf_op jit(solution)/shard_map/ppermute | solution.py:460
  89.3 2.3 %collective-permute-done.34 = f32[2,136,128]{2,1,0:T(8,128)S(1)} collective-permute-done((f32[2,136,128]{2,1,0:T(8,128)S(1)}, f32[2,136,128]{2,1,0:T(8,128)S(1)}, u32[]{:S(2)}, u32[]{:S(2)}) %collective-permute-start.34) | collective-permute-done | bytes 139296 | tf_op jit(solution)/shard_map/ppermute | solution.py:49
  91.7 2.0 %collective-permute-start.38 = (f32[2,136,128]{2,1,0:T(8,128)S(1)}, f32[2,136,128]{2,1,0:T(8,128)S(1)}, u32[]{:S(2)}, u32[]{:S(2)}) collective-permute-start(f32[2,136,128]{2,1,0:T(8,128)S(1)} %add.24), channel_id=1, source_target_pairs={{0,8},{2,10},{4,12},{6,14},{8,0},{10,2},{12,4},{14,6},{16,24},{18,... | collective-permute-start | bytes 417800 | tf_op jit(solution)/shard_map/ppermute | solution.py:49
  97.4 2.1 %collective-permute-start.27 = (bf16[64,2048]{1,0:T(8,128)(2,1)S(1)}, bf16[64,2048]{1,0:T(8,128)(2,1)S(1)}, u32[]{:S(2)}, u32[]{:S(2)}) collective-permute-start(bf16[64,2048]{1,0:T(8,128)(2,1)S(1)} %join.13), channel_id=1, source_target_pairs={{0,4},{2,6},{8,0},{10,2},{16,8},{18,10},{24,16},{26,18},{28,24},{3... | collective-permute-start | bytes 786440 | tf_op jit(solution)/shard_map/ppermute | solution.py:460
  99.5 3.3 %collective-permute-done.23.arrived = bf16[64,2048]{1,0:T(8,128)(2,1)S(1)} collective-permute-done((bf16[64,2048]{1,0:T(8,128)(2,1)S(1)}, bf16[64,2048]{1,0:T(8,128)(2,1)S(1)}, u32[]{:S(2)}, u32[]{:S(2)}) %collective-permute-start.23) | collective-permute-done | bytes 262176 | tf_op jit(solution)/shard_map/ppermute | solution.py:460
  103.2 2.1 %collective-permute-start.36 = (bf16[64,2048]{1,0:T(8,128)(2,1)S(1)}, bf16[64,2048]{1,0:T(8,128)(2,1)S(1)}, u32[]{:S(2)}, u32[]{:S(2)}) collective-permute-start(bf16[64,2048]{1,0:T(8,128)(2,1)S(1)} %join.18), channel_id=1, source_target_pairs={{0,4},{2,6},{8,0},{10,2},{16,8},{18,10},{24,16},{26,18},{28,24},{3... | collective-permute-start | bytes 786440 | tf_op jit(solution)/shard_map/ppermute | solution.py:460
  105.7 2.3 %spread.4 = (f32[64,2048]{1,0:T(8,128)S(1)}, f32[64,2048]{1,0:T(8,128)S(1)}, f32[64,2048]{1,0:T(8,128)S(1)}, f32[64,2048]{1,0:T(8,128)S(1)}, f32[64,2048]{1,0:T(8,128)S(1)}, /*index=5*/f32[64,2048]{1,0:T(8,128)S(1)}) custom-call(s32[384]{0:T(512)S(1)} %table.1, s32[384]{0:T(512)S(1)} %collective-permute-done.18.table.table_pair, ...), custom_call_target="tpu_custom_call" | custom-call | flops 301989888 | bytes 6291456 | tf_op jit(solution)/shard_map/spread/pallas_call | solution.py:308
  108.5 2.2 %collective-permute-start.31 = (bf16[64,2048]{1,0:T(8,128)(2,1)S(1)}, bf16[64,2048]{1,0:T(8,128)(2,1)S(1)}, u32[]{:S(2)}, u32[]{:S(2)}) collective-permute-start(bf16[64,2048]{1,0:T(8,128)(2,1)S(1)} %join.16), channel_id=1, source_target_pairs={{0,8},{2,10},{8,16},{10,18},{16,24},{18,26},{24,28},{26,30},{28,20... | collective-permute-start | bytes 786440 | tf_op jit(solution)/shard_map/ppermute | solution.py:460
  111.5 2.6 %collective-permute-done.24.arrived = bf16[64,2048]{1,0:T(8,128)(2,1)S(1)} collective-permute-done((bf16[64,2048]{1,0:T(8,128)(2,1)S(1)}, bf16[64,2048]{1,0:T(8,128)(2,1)S(1)}, u32[]{:S(2)}, u32[]{:S(2)}) %collective-permute-start.24) | collective-permute-done | bytes 262176 | tf_op jit(solution)/shard_map/ppermute | solution.py:460
  117.9 2.2 %collective-permute-start.37 = (bf16[64,2048]{1,0:T(8,128)(2,1)}, bf16[64,2048]{1,0:T(8,128)(2,1)S(1)}, u32[]{:S(2)}, u32[]{:S(2)}) collective-permute-start(bf16[64,2048]{1,0:T(8,128)(2,1)} %join.19), channel_id=1, source_target_pairs={{0,4},{2,6},{8,0},{10,2},{16,8},{18,10},{24,16},{26,18},{28,24},{3... | collective-permute-start | bytes 786440 | tf_op jit(solution)/shard_map/ppermute | solution.py:460
  (106 shorter events, 52.2 us)
Async XLA Ops:
  0.6 17.5 %collective-permute-start.4 = (bf16[16,12,128,128]{3,2,1,0:T(8,128)(2,1)}, bf16[16,12,128,128]{3,2,1,0:T(8,128)(2,1)}, u32[]{:S(2)}, u32[]{:S(2)}) collective-permute-start(bf16[16,12,128,128]{3,2,1,0:T(8,128)(2,1)} %source.1), channel_id=1, source_target_pairs={{0,2},{2,0},{4,6},{6,4},{8,10},{10,8},{12,14},{14,12},{16,18},{18,... | collective-permute-start | bytes 18874376 | tf_op jit(solution)/shard_map/ppermute | solution.py:49
  2.2 11.4 %collective-permute-start = (bf16[64,2048]{1,0:T(8,128)(2,1)S(1)}, bf16[64,2048]{1,0:T(8,128)(2,1)S(1)}, u32[]{:S(2)}, u32[]{:S(2)}) collective-permute-start(bf16[64,2048]{1,0:T(8,128)(2,1)S(1)} %get-tuple-element.106.refs_0_), channel_id=1, source_target_pairs={{0,8},{2,10},{8,16},{10,18},{16,24},{18,26},{24,28},{26,30},{28,20... | collective-permute-start | bytes 786440 | tf_op jit(solution)/shard_map/ppermute | solution.py:372
  4.9 12.3 %collective-permute-start.1 = (bf16[64,2048]{1,0:T(8,128)(2,1)S(1)}, bf16[64,2048]{1,0:T(8,128)(2,1)S(1)}, u32[]{:S(2)}, u32[]{:S(2)}) collective-permute-start(bf16[64,2048]{1,0:T(8,128)(2,1)S(1)} %get-tuple-element.68), channel_id=1, source_target_pairs={{0,10},{2,8},{8,18},{10,16},{16,26},{18,24},{24,30},{26,28},{28,22... | collective-permute-start | bytes 786440 | tf_op jit(solution)/shard_map/ppermute | solution.py:372
  6.4 11.7 %collective-permute-start.3 = (bf16[64,2048]{1,0:T(8,128)(2,1)S(1)}, bf16[64,2048]{1,0:T(8,128)(2,1)S(1)}, u32[]{:S(2)}, u32[]{:S(2)}) collective-permute-start(bf16[64,2048]{1,0:T(8,128)(2,1)S(1)} %get-tuple-element.68), channel_id=1, source_target_pairs={{0,6},{2,4},{8,2},{10,0},{16,10},{18,8},{24,18},{26,16},{28,26},{3... | collective-permute-start | bytes 786440 | tf_op jit(solution)/shard_map/ppermute | solution.py:376
  18.2 45.3 %collective-permute-start.5 = (bf16[128,4736]{1,0:T(8,128)(2,1)S(1)}, bf16[128,4736]{1,0:T(8,128)(2,1)S(1)}, u32[]{:S(2)}, u32[]{:S(2)}) collective-permute-start(bf16[128,4736]{1,0:T(8,128)(2,1)S(1)} %pack.1.refs_0_), channel_id=1, source_target_pairs={{0,1},{1,0},{2,3},{3,2},{4,5},{5,4},{6,7},{7,6},{8,9},{9,8},{10,11... | collective-permute-start | bytes 3637256 | tf_op jit(solution)/shard_map/ppermute | solution.py:58
  21.7 12.7 %collective-permute-start.9 = (bf16[64,2048]{1,0:T(8,128)(2,1)S(1)}, bf16[64,2048]{1,0:T(8,128)(2,1)S(1)}, u32[]{:S(2)}, u32[]{:S(2)}) collective-permute-start(bf16[64,2048]{1,0:T(8,128)(2,1)S(1)} %collective-permute-done.3.refs_4_), channel_id=1, source_target_pairs={{0,4},{2,6},{8,0},{10,2},{16,8},{18,10},{24,16},{26,18},{28,24},{3... | collective-permute-start | bytes 786440 | tf_op jit(solution)/shard_map/ppermute | solution.py:376
  22.2 12.8 %collective-permute-start.8 = (bf16[64,2048]{1,0:T(8,128)(2,1)S(1)}, bf16[64,2048]{1,0:T(8,128)(2,1)S(1)}, u32[]{:S(2)}, u32[]{:S(2)}) collective-permute-start(bf16[64,2048]{1,0:T(8,128)(2,1)S(1)} %collective-permute-done.1.refs_3_), channel_id=1, source_target_pairs={{0,8},{2,10},{8,16},{10,18},{16,24},{18,26},{24,28},{26,30},{28,20... | collective-permute-start | bytes 786440 | tf_op jit(solution)/shard_map/ppermute | solution.py:372
  28.8 11.2 %collective-permute-start.11 = (bf16[64,2048]{1,0:T(8,128)(2,1)S(1)}, bf16[64,2048]{1,0:T(8,128)(2,1)S(1)}, u32[]{:S(2)}, u32[]{:S(2)}) collective-permute-start(bf16[64,2048]{1,0:T(8,128)(2,1)S(1)} %collective-permute-done.7.refs_6_), channel_id=1, source_target_pairs={{0,4},{2,6},{8,0},{10,2},{16,8},{18,10},{24,16},{26,18},{28,24},{3... | collective-permute-start | bytes 786440 | tf_op jit(solution)/shard_map/ppermute | solution.py:376
  29.4 11.2 %collective-permute-start.10 = (bf16[64,2048]{1,0:T(8,128)(2,1)S(1)}, bf16[64,2048]{1,0:T(8,128)(2,1)S(1)}, u32[]{:S(2)}, u32[]{:S(2)}) collective-permute-start(bf16[64,2048]{1,0:T(8,128)(2,1)S(1)} %collective-permute-done.6.refs_5_), channel_id=1, source_target_pairs={{0,8},{2,10},{8,16},{10,18},{16,24},{18,26},{24,28},{26,30},{28,20... | collective-permute-start | bytes 786440 | tf_op jit(solution)/shard_map/ppermute | solution.py:372
  35.0 12.1 %collective-permute-start.12 = (bf16[64,2048]{1,0:T(8,128)(2,1)S(1)}, bf16[64,2048]{1,0:T(8,128)(2,1)S(1)}, u32[]{:S(2)}, u32[]{:S(2)}) collective-permute-start(bf16[64,2048]{1,0:T(8,128)(2,1)S(1)} %collective-permute-done.8.refs_7_), channel_id=1, source_target_pairs={{0,8},{2,10},{8,16},{10,18},{16,24},{18,26},{24,28},{26,30},{28,20... | collective-permute-start | bytes 786440 | tf_op jit(solution)/shard_map/ppermute | solution.py:372
  77.9 11.3 %collective-permute-start.32 = (bf16[64,2048]{1,0:T(8,128)(2,1)S(1)}, bf16[64,2048]{1,0:T(8,128)(2,1)S(1)}, u32[]{:S(2)}, u32[]{:S(2)}) collective-permute-start(bf16[64,2048]{1,0:T(8,128)(2,1)S(1)} %get-tuple-element.93), channel_id=1, source_target_pairs={{0,4},{2,6},{8,0},{10,2},{16,8},{18,10},{24,16},{26,18},{28,24},{3... | collective-permute-start | bytes 786440 | tf_op jit(solution)/shard_map/ppermute | solution.py:460
  80.0 11.6 %collective-permute-start.34 = (f32[2,136,128]{2,1,0:T(8,128)S(1)}, f32[2,136,128]{2,1,0:T(8,128)S(1)}, u32[]{:S(2)}, u32[]{:S(2)}) collective-permute-start(f32[2,136,128]{2,1,0:T(8,128)S(1)} %slice_add_fusion), channel_id=1, source_target_pairs={{0,4},{2,6},{4,0},{6,2},{8,12},{10,14},{12,8},{14,10},{16,20},{18,... | collective-permute-start | bytes 417800 | tf_op jit(solution)/shard_map/ppermute | solution.py:49
  83.3 13.9 %collective-permute-start.29 = (bf16[64,2048]{1,0:T(8,128)(2,1)S(1)}, bf16[64,2048]{1,0:T(8,128)(2,1)S(1)}, u32[]{:S(2)}, u32[]{:S(2)}) collective-permute-start(bf16[64,2048]{1,0:T(8,128)(2,1)S(1)} %get-tuple-element.90), channel_id=1, source_target_pairs={{0,8},{2,10},{8,16},{10,18},{16,24},{18,26},{24,28},{26,30},{28,20... | collective-permute-start | bytes 786440 | tf_op jit(solution)/shard_map/ppermute | solution.py:460
  84.9 12.4 %collective-permute-start.26 = (bf16[64,2048]{1,0:T(8,128)(2,1)S(1)}, bf16[64,2048]{1,0:T(8,128)(2,1)S(1)}, u32[]{:S(2)}, u32[]{:S(2)}) collective-permute-start(bf16[64,2048]{1,0:T(8,128)(2,1)S(1)} %get-tuple-element.87), channel_id=1, source_target_pairs={{0,4},{2,6},{8,0},{10,2},{16,8},{18,10},{24,16},{26,18},{28,24},{3... | collective-permute-start | bytes 786440 | tf_op jit(solution)/shard_map/ppermute | solution.py:460
  88.7 14.2 %collective-permute-start.23 = (bf16[64,2048]{1,0:T(8,128)(2,1)S(1)}, bf16[64,2048]{1,0:T(8,128)(2,1)S(1)}, u32[]{:S(2)}, u32[]{:S(2)}) collective-permute-start(bf16[64,2048]{1,0:T(8,128)(2,1)S(1)} %join.10), channel_id=1, source_target_pairs={{0,8},{2,10},{8,16},{10,18},{16,24},{18,26},{24,28},{26,30},{28,20... | collective-permute-start | bytes 786440 | tf_op jit(solution)/shard_map/ppermute | solution.py:460
  91.6 11.5 %collective-permute-start.35 = (bf16[64,2048]{1,0:T(8,128)(2,1)S(1)}, bf16[64,2048]{1,0:T(8,128)(2,1)S(1)}, u32[]{:S(2)}, u32[]{:S(2)}) collective-permute-start(bf16[64,2048]{1,0:T(8,128)(2,1)S(1)} %join.17), channel_id=1, source_target_pairs={{0,4},{2,6},{8,0},{10,2},{16,8},{18,10},{24,16},{26,18},{28,24},{3... | collective-permute-start | bytes 786440 | tf_op jit(solution)/shard_map/ppermute | solution.py:460
  91.7 13.6 %collective-permute-start.38 = (f32[2,136,128]{2,1,0:T(8,128)S(1)}, f32[2,136,128]{2,1,0:T(8,128)S(1)}, u32[]{:S(2)}, u32[]{:S(2)}) collective-permute-start(f32[2,136,128]{2,1,0:T(8,128)S(1)} %add.24), channel_id=1, source_target_pairs={{0,8},{2,10},{4,12},{6,14},{8,0},{10,2},{12,4},{14,6},{16,24},{18,... | collective-permute-start | bytes 417800 | tf_op jit(solution)/shard_map/ppermute | solution.py:49
  97.3 11.2 %collective-permute-start.30 = (bf16[64,2048]{1,0:T(8,128)(2,1)S(1)}, bf16[64,2048]{1,0:T(8,128)(2,1)S(1)}, u32[]{:S(2)}, u32[]{:S(2)}) collective-permute-start(bf16[64,2048]{1,0:T(8,128)(2,1)S(1)} %join.15), channel_id=1, source_target_pairs={{0,8},{2,10},{8,16},{10,18},{16,24},{18,26},{24,28},{26,30},{28,20... | collective-permute-start | bytes 786440 | tf_op jit(solution)/shard_map/ppermute | solution.py:460
  97.4 13.3 %collective-permute-start.27 = (bf16[64,2048]{1,0:T(8,128)(2,1)S(1)}, bf16[64,2048]{1,0:T(8,128)(2,1)S(1)}, u32[]{:S(2)}, u32[]{:S(2)}) collective-permute-start(bf16[64,2048]{1,0:T(8,128)(2,1)S(1)} %join.13), channel_id=1, source_target_pairs={{0,4},{2,6},{8,0},{10,2},{16,8},{18,10},{24,16},{26,18},{28,24},{3... | collective-permute-start | bytes 786440 | tf_op jit(solution)/shard_map/ppermute | solution.py:460
  102.9 11.2 %collective-permute-start.24 = (bf16[64,2048]{1,0:T(8,128)(2,1)S(1)}, bf16[64,2048]{1,0:T(8,128)(2,1)S(1)}, u32[]{:S(2)}, u32[]{:S(2)}) collective-permute-start(bf16[64,2048]{1,0:T(8,128)(2,1)S(1)} %join.11), channel_id=1, source_target_pairs={{0,8},{2,10},{8,16},{10,18},{16,24},{18,26},{24,28},{26,30},{28,20... | collective-permute-start | bytes 786440 | tf_op jit(solution)/shard_map/ppermute | solution.py:460
  103.2 13.9 %collective-permute-start.36 = (bf16[64,2048]{1,0:T(8,128)(2,1)S(1)}, bf16[64,2048]{1,0:T(8,128)(2,1)S(1)}, u32[]{:S(2)}, u32[]{:S(2)}) collective-permute-start(bf16[64,2048]{1,0:T(8,128)(2,1)S(1)} %join.18), channel_id=1, source_target_pairs={{0,4},{2,6},{8,0},{10,2},{16,8},{18,10},{24,16},{26,18},{28,24},{3... | collective-permute-start | bytes 786440 | tf_op jit(solution)/shard_map/ppermute | solution.py:460
  105.3 14.8 %collective-permute-start.39 = (f32[2,136,128]{2,1,0:T(8,128)S(1)}, f32[2,136,128]{2,1,0:T(8,128)S(1)}, u32[]{:S(2)}, u32[]{:S(2)}) collective-permute-start(f32[2,136,128]{2,1,0:T(8,128)S(1)} %add.25), channel_id=1, source_target_pairs={{0,16},{2,18},{4,20},{6,22},{8,24},{10,26},{12,28},{14,30},{16,0},... | collective-permute-start | bytes 417800 | tf_op jit(solution)/shard_map/ppermute | solution.py:49
  108.5 15.4 %collective-permute-start.31 = (bf16[64,2048]{1,0:T(8,128)(2,1)S(1)}, bf16[64,2048]{1,0:T(8,128)(2,1)S(1)}, u32[]{:S(2)}, u32[]{:S(2)}) collective-permute-start(bf16[64,2048]{1,0:T(8,128)(2,1)S(1)} %join.16), channel_id=1, source_target_pairs={{0,8},{2,10},{8,16},{10,18},{16,24},{18,26},{24,28},{26,30},{28,20... | collective-permute-start | bytes 786440 | tf_op jit(solution)/shard_map/ppermute | solution.py:460
  111.4 12.5 %collective-permute-start.28 = (bf16[64,2048]{1,0:T(8,128)(2,1)}, bf16[64,2048]{1,0:T(8,128)(2,1)S(1)}, u32[]{:S(2)}, u32[]{:S(2)}) collective-permute-start(bf16[64,2048]{1,0:T(8,128)(2,1)} %join.14), channel_id=1, source_target_pairs={{0,4},{2,6},{8,0},{10,2},{16,8},{18,10},{24,16},{26,18},{28,24},{3... | collective-permute-start | bytes 786440 | tf_op jit(solution)/shard_map/ppermute | solution.py:460
  (24 other events, 149.9 us)
